TPU v7x, 32 devices: a whole 2x2x4 slice. The times are simulated.
32 devices in a mesh: groups: 2 (over x), gx: 16 (over z, y, core).
Axes of the slice: x: 2, y: 2, z: 4, core: 2. Of those that a mesh axis runs over, the one named last changes fastest.
Arguments:
- point_feats: bfloat16 [16384, 64], P(('groups', 'gx')), parts along dimension 0, may hold values from -6 to 6
- pair_point: int32 [32, 16, 128], P(('groups', 'gx')), parts along dimension 0, may hold values from 0 to 511
- pair_cell: int32 [16, 32, 128], P(None, ('groups', 'gx')), parts along dimension 1, may hold values from 0 to 16383
- kernel: float32 [32, 16, 128], P(('groups', 'gx')), parts along dimension 0, may hold values from 0.1 to 1
- counts: int32 [32, 16], P(('groups', 'gx')), parts along dimension 0, may hold values from 1 to 128, as said below
- area: float32 [16384], P(('groups', 'gx')), parts along dimension 0, may hold values from 0.3 to 3
- normals: float32 [2, 16384], P(None, ('groups', 'gx')), parts along dimension 1, may hold values from -4 to 4
- targets: float32 [4], P('groups'), parts along dimension 0, may hold values from -4 to 4
- spec_weight: bfloat16 [1024, 64, 64], P('gx'), may hold values from -0.75 to 0.75
- skip_weight: bfloat16 [64, 64], replicated, may hold values from -0.75 to 0.75
- skip_bias: float32 [64], replicated, may hold values from -3 to 3
- head_weight: bfloat16 [64, 64], replicated, may hold values from -0.75 to 0.75
- head_bias: float32 [64], replicated, may hold values from -3 to 3
- out_weight: float32 [64], replicated, may hold values from -0.75 to 0.75
Outputs:
- pressure: float32 [16384], P(('groups', 'gx')), parts along dimension 0
- forces: float32 [4], P('groups'), parts along dimension 0
- spec_grad: float32 [2048, 64, 64], P(('groups', 'gx')), parts along dimension 0
- skip_grad: float32 [128, 64], P('groups'), parts along dimension 0
- out_grad: float32 [128], P('groups'), parts along dimension 0
There are 2 independent parts, one for each index of `groups`. A program takes and returns all parts, laid end to end along the dimension named above; an argument that names none is the same for every part. Nothing has to cross between parts.
Inputs may be any that keep to these rules, and one draw needn't show every extreme that they name: counts[s, d] valid slots lead each block; some block of every draw is full. `pair_cell`: cells of the destination slab, numbered x-plane, then y, then z.
All inputs are finite; a program needn't handle non-finite values.
Results may differ from a plain program's by a relative error of at most 0.0055.
The roundings to bfloat16 on the way count: a program that leaves them out, or rounds other values in their place, can miss the bound.
Values may be sent and summed in bfloat16 or wider, within the bound.
No kernel may reach another device: no remote copies, remote signals or barrier semaphores. Data moves between devices by JAX's collectives and lax.ppermute only.
A program may use at most 128 MiB of HBM per device.

v0:
```python
import math

import jax
import jax.numpy as jnp
from jax import lax
from jax.sharding import PartitionSpec as P

GX = 128
GY = 128
MODES = 32
ZL = 1
NMODE = 1024


def fourier_rows(length, number):
    places = jnp.arange(length, dtype=jnp.float32)
    order = jnp.arange(number)
    half = number // 2
    freqs = jnp.where(order < half, order, order - half + 1).astype(jnp.float32)
    angles = 2.0 * math.pi / length * freqs[:, None] * places[None, :]
    table = jnp.where((order < half)[:, None], jnp.cos(angles), jnp.sin(angles))
    return (table * math.sqrt(2.0 / length)).astype(jnp.bfloat16)


def gelu_value(values):
    return 0.5 * values * (1.0 + lax.erf(values * (1.0 / math.sqrt(2.0))))


def gelu_slope(values):
    return 0.5 * (1.0 + lax.erf(values * (1.0 / math.sqrt(2.0)))) + values * jnp.exp(
        -0.5 * values * values
    ) * (1.0 / math.sqrt(2.0 * math.pi))


def per_device(
    point_feats,
    pair_point,
    pair_cell,
    kernel,
    counts,
    area,
    normals,
    targets,
    spec_weight,
    skip_weight,
    skip_bias,
    head_weight,
    head_bias,
    out_weight,
):
    devices = lax.axis_size("gx")
    local_points, width = point_feats.shape
    block_slots = pair_point.shape[2]
    row_count = GX // devices
    depth = ZL * devices
    slab_cells = row_count * GY * depth
    valid_mask = jnp.arange(block_slots)[None, :] < counts[0][:, None]
    point_rows = pair_point[0]
    pair_weight = jnp.where(valid_mask, kernel[0], jnp.float32(0.0))
    sender_weight = pair_weight * area[point_rows]
    contrib = (sender_weight[..., None] * point_feats[point_rows].astype(jnp.float32)).astype(
        jnp.bfloat16
    )
    arrived = lax.all_to_all(contrib, "gx", split_axis=0, concat_axis=0, tiled=True)
    cell_rows = pair_cell[:, 0, :].reshape(-1)
    latent = jax.ops.segment_sum(
        arrived.reshape(-1, width).astype(jnp.float32), cell_rows, num_segments=slab_cells
    ).astype(jnp.bfloat16)
    col_table = fourier_rows(GY, MODES)
    row_table = fourier_rows(GX, MODES)
    volume = latent.reshape(row_count, GY, depth * width)
    along_y = jnp.einsum(
        "by,xyk->xbk", col_table, volume, preferred_element_type=jnp.float32
    ).astype(jnp.bfloat16)
    columns = lax.all_to_all(along_y, "gx", split_axis=2, concat_axis=0, tiled=True)
    spectrum = jnp.einsum(
        "ax,xbk->abk", row_table, columns, preferred_element_type=jnp.float32
    ).astype(jnp.bfloat16)
    mode_rows = lax.all_to_all(
        spectrum.reshape(NMODE, ZL * width), "gx", split_axis=0, concat_axis=1, tiled=True
    )
    own_modes = mode_rows.shape[0]
    mixed_rows = jnp.einsum(
        "mzc,mcd->mzd",
        mode_rows.reshape(own_modes, depth, width),
        spec_weight,
        preferred_element_type=jnp.float32,
    ).astype(jnp.bfloat16)
    mixed = lax.all_to_all(
        mixed_rows.reshape(own_modes, depth * width), "gx", split_axis=1, concat_axis=0, tiled=True
    )
    back_x = jnp.einsum(
        "ax,abk->xbk",
        row_table,
        mixed.reshape(MODES, MODES, ZL * width),
        preferred_element_type=jnp.float32,
    ).astype(jnp.bfloat16)
    slabs = lax.all_to_all(back_x, "gx", split_axis=0, concat_axis=2, tiled=True)
    spatial = jnp.einsum(
        "by,xbk->xyk", col_table, slabs, preferred_element_type=jnp.float32
    ).reshape(slab_cells, width)
    pre = spatial + jnp.dot(latent, skip_weight, preferred_element_type=jnp.float32) + skip_bias
    features = gelu_value(pre).astype(jnp.bfloat16)
    picked = features[cell_rows].reshape(devices, block_slots, width)
    returned = lax.all_to_all(picked, "gx", split_axis=0, concat_axis=0, tiled=True)
    point_latent = jax.ops.segment_sum(
        (pair_weight[..., None] * returned.astype(jnp.float32)).reshape(-1, width),
        point_rows.reshape(-1),
        num_segments=local_points,
    )
    head_matrix = head_weight.astype(jnp.float32)
    head_pre = jnp.dot(point_latent, head_matrix, precision=lax.Precision.HIGHEST) + head_bias
    head = gelu_value(head_pre)
    pressure = jnp.dot(head, out_weight, precision=lax.Precision.HIGHEST)
    weighted = pressure * area
    scale = 1.0 / math.sqrt(local_points * devices)
    totals = lax.psum(
        jnp.stack([jnp.sum(weighted * normals[0]), jnp.sum(weighted * normals[1])]), "gx"
    )
    forces = scale * totals
    misfit = forces - targets
    point_grad = 2.0 * scale * (misfit[0] * normals[0] + misfit[1] * normals[1]) * area
    out_part = jnp.dot(point_grad, head, precision=lax.Precision.HIGHEST)
    head_grad = point_grad[:, None] * out_weight[None, :] * gelu_slope(head_pre)
    latent_grad = jnp.dot(head_grad, head_matrix.T, precision=lax.Precision.HIGHEST).astype(
        jnp.bfloat16
    )
    grad_pairs = (pair_weight[..., None] * latent_grad[point_rows].astype(jnp.float32)).astype(
        jnp.bfloat16
    )
    grad_arrived = lax.all_to_all(grad_pairs, "gx", split_axis=0, concat_axis=0, tiled=True)
    cell_grad = jax.ops.segment_sum(
        grad_arrived.reshape(-1, width).astype(jnp.float32), cell_rows, num_segments=slab_cells
    )
    pre_grad = (cell_grad * gelu_slope(pre)).astype(jnp.bfloat16)
    skip_part = jnp.dot(latent.T, pre_grad, preferred_element_type=jnp.float32)
    grad_y = jnp.einsum(
        "by,xyk->xbk",
        col_table,
        pre_grad.reshape(row_count, GY, depth * width),
        preferred_element_type=jnp.float32,
    ).astype(jnp.bfloat16)
    grad_columns = lax.all_to_all(grad_y, "gx", split_axis=2, concat_axis=0, tiled=True)
    grad_spec = jnp.einsum(
        "ax,xbk->abk", row_table, grad_columns, preferred_element_type=jnp.float32
    ).astype(jnp.bfloat16)
    grad_rows = lax.all_to_all(
        grad_spec.reshape(NMODE, ZL * width), "gx", split_axis=0, concat_axis=1, tiled=True
    )
    own_modes = grad_rows.shape[0]
    spec_grad = jnp.einsum(
        "mzc,mzd->mcd",
        mode_rows.reshape(own_modes, depth, width),
        grad_rows.reshape(own_modes, depth, width),
        preferred_element_type=jnp.float32,
    )
    out_grad, skip_grad = lax.psum((out_part, skip_part), "gx")
    return (pressure, forces, spec_grad, skip_grad, out_grad)


def solution(mesh):
    in_specs = (
        P(("groups", "gx"), None),
        P(("groups", "gx"), None, None),
        P(None, ("groups", "gx"), None),
        P(("groups", "gx"), None, None),
        P(("groups", "gx"), None),
        P(("groups", "gx")),
        P(None, ("groups", "gx")),
        P("groups"),
        P("gx", None, None),
        P(),
        P(),
        P(),
        P(),
        P(),
    )
    out_specs = (
        P(("groups", "gx")),
        P("groups"),
        P(("groups", "gx"), None, None),
        P("groups", None),
        P("groups"),
    )
    return jax.shard_map(
        per_device, mesh=mesh, in_specs=in_specs, out_specs=out_specs, check_vma=False
    )
```

profile of v0, /device:TPU:0, one launch (start us, length us, event | category | flops | bytes accessed | tf_op | source)
XLA Modules:
  0.0 421.3 jit_solution(12792961737609167166)
XLA Ops:
  2.4 13.2 %gather_fusion = f32[2048]{0:T(1024)S(1)} fusion(f32[512]{0:T(512)S(1)} %copy-done.2, s32[2048]{0:T(1024)S(1)} %fusion.47), kind=kCustom, calls=%fused_computation | custom fusion | bytes 24576 | tf_op jit(solution)/shard_map/gather | solution.py:60
  15.7 6.2 %gather_fusion.1 = bf16[2048,64]{1,0:T(8,128)(2,1)S(1)} fusion(bf16[512,64]{1,0:T(8,128)(2,1)S(1)} %copy.71, s32[2048]{0:T(1024)S(1)} %fusion.47), kind=kCustom, calls=%fused_computation.1 | custom fusion | bytes 532480 | tf_op jit(solution)/shard_map/gather | solution.py:61
  22.9 7.4 %all-to-all-start = ((bf16[16,128,64]{1,2,0:T(8,128)(2,1)}), bf16[16,128,64]{1,2,0:T(8,128)(2,1)S(1)}, u32[]{:S(2)}, u32[]{:S(2)}) async-start(bf16[16,128,64]{1,2,0:T(8,128)(2,1)} %multiply_convert_fusion.2), calls=%async_computation | async-start | bytes 524288 | tf_op jit(solution)/shard_map/all_to_all | solution.py:64
  30.4 10.0 %all-to-all-done = bf16[16,128,64]{1,2,0:T(8,128)(2,1)S(1)} async-done(((bf16[16,128,64]{1,2,0:T(8,128)(2,1)}), bf16[16,128,64]{1,2,0:T(8,128)(2,1)S(1)}, u32[]{:S(2)}, u32[]{:S(2)}) %all-to-all-start) | async-done | bytes 262176 | tf_op jit(solution)/shard_map/all_to_all | solution.py:64
  40.6 15.2 %scatter_custom_fusion = f32[16384,64]{1,0:T(8,128)} fusion(s32[2048]{0:T(1024)S(1)} %bitcast.124, f32[2048,64]{1,0:T(8,128)S(1)} %bitcast.109, f32[]{:T(128)} %constant.15.clone.1), kind=kCustom, calls=%fused_computation.20 | custom fusion | flops 131072 | bytes 4194308 | tf_op jit(solution)/shard_map/scatter-add | solution.py:66
  55.8 5.1 %convert_element_type.102 = bf16[16384,64]{1,0:T(8,128)(2,1)} convert(f32[16384,64]{1,0:T(8,128)} %scatter_custom_fusion) | non-fusion elementwise | flops 1048576 | bytes 6291456 | tf_op jit(solution)/shard_map/convert_element_type | solution.py:68
  60.9 5.5 %reshape.185 = bf16[8,128,1024]{2,1,0:T(8,128)(2,1)S(1)} reshape(bf16[16384,64]{1,0:T(8,128)(2,1)} %convert_element_type.102) | data formatting | bytes 4194304 | tf_op jit(solution)/shard_map/reshape | solution.py:71
  73.0 18.7 %all_to_all.114 = bf16[16,2,8192]{2,1,0:T(2,128)(2,1)} all-to-all(bf16[16,2,8192]{2,1,0:T(2,128)(2,1)} %reshape.268), channel_id=1, replica_groups=mesh['groups'=2,'gx'=16] {'gx'}, dimensions={0} | all-to-all | bytes 1048576 | tf_op jit(solution)/shard_map/all_to_all | solution.py:75
  98.8 11.8 %all_to_all.115 = bf16[16,2,2048]{2,1,0:T(2,128)(2,1)S(1)} all-to-all(bf16[16,2,2048]{2,1,0:T(2,128)(2,1)S(1)} %reshape.270), channel_id=1, replica_groups=mesh['groups'=2,'gx'=16] {'gx'}, dimensions={0} | all-to-all | bytes 262144 | tf_op jit(solution)/shard_map/all_to_all | solution.py:79
  111.5 10.8 %all_to_all.116 = bf16[16,2,2048]{2,1,0:T(2,128)(2,1)S(1)} all-to-all(bf16[16,2,2048]{2,1,0:T(2,128)(2,1)S(1)} %reshape.272), channel_id=1, replica_groups=mesh['groups'=2,'gx'=16] {'gx'}, dimensions={0} | all-to-all | bytes 262144 | tf_op jit(solution)/shard_map/all_to_all | solution.py:89
  126.1 3.6 all-to-all-start.4
  129.7 14.4 %all-to-all-done.4 = bf16[16,2,8192]{2,1,0:T(2,128)(2,1)S(1)} async-done(((bf16[16,2,8192]{2,1,0:T(2,128)(2,1)}), bf16[16,2,8192]{2,1,0:T(2,128)(2,1)S(1)}, u32[]{:S(2)}, u32[]{:S(2)}) %all-to-all-start.4) | async-done | bytes 524320 | tf_op jit(solution)/shard_map/all_to_all | solution.py:98
  148.9 5.3 %copy.84 = f32[8,128,1024]{2,1,0:T(8,128)} copy(f32[8,128,1024]{1,2,0:T(8,128)} %convolution_bitcast_fusion) | data formatting | bytes 8388608 | tf_op jit(solution)/shard_map/by,xbk->xyk/transpose | solution.py:99
  154.3 7.3 %reshape.187 = f32[16384,64]{1,0:T(8,128)} reshape(f32[8,128,1024]{2,1,0:T(8,128)} %copy.84) | data formatting | bytes 8388608 | tf_op jit(solution)/shard_map/reshape | solution.py:101
  161.5 6.8 %copy.85 = f32[16384,64]{0,1:T(8,128)} copy(f32[16384,64]{1,0:T(8,128)} %reshape.187) | data formatting | bytes 8388608 | tf_op jit(solution)/shard_map/reshape | solution.py:101
  168.3 7.1 %multiply_convert_fusion = (bf16[16384,64]{0,1:T(8,128)(2,1)S(1)}, f32[16384,64]{0,1:T(8,128)}) fusion(f32[64]{0:T(128)S(1)} %copy-done.9, f32[16384,64]{0,1:T(8,128)} %copy.85, bf16[16384,64]{1,0:T(8,128)(2,1)} %convert_element_type.102, bf16[64,64]{1,0:T(8,128)(2,1)S(1)} %copy-done.3), kind=kOutput, calls=%fused_computation.16 | convolution fusion | flops 141557760 | bytes 12591360 | tf_op jit(solution)/shard_map/dot_general | solution.py:102
  178.6 8.4 %gather_fusion.2 = bf16[2048,64]{1,0:T(8,128)(2,1)S(1)} fusion(bf16[16384,64]{1,0:T(8,128)(2,1)} %copy.86, s32[2048]{0:T(1024)S(1)} %broadcast_clamp_fusion), kind=kCustom, calls=%fused_computation.2 | custom fusion | bytes 532480 | tf_op jit(solution)/shard_map/gather | solution.py:104
  187.9 4.0 all-to-all-start.5
  191.9 10.0 %all-to-all-done.5 = bf16[16,128,64]{1,2,0:T(8,128)(2,1)S(1)} async-done(((bf16[16,128,64]{1,2,0:T(8,128)(2,1)}), bf16[16,128,64]{1,2,0:T(8,128)(2,1)S(1)}, u32[]{:S(2)}, u32[]{:S(2)}) %all-to-all-start.5) | async-done | bytes 262176 | tf_op jit(solution)/shard_map/all_to_all | solution.py:105
  202.4 21.6 %scatter_custom_fusion.1 = f32[512,64]{1,0:T(8,128)S(1)} fusion(s32[2048]{0:T(1024)} %bitcast.123, f32[2048,64]{1,0:T(8,128)S(1)} %bitcast.110, f32[]{:T(128)} %constant.15.clone.1), kind=kCustom, calls=%fused_computation.57 | custom fusion | flops 131072 | bytes 131584 | tf_op jit(solution)/shard_map/scatter-add | solution.py:106
  226.5 30.8 %psum.21 = f32[2]{0:T(128)S(1)} all-reduce(f32[2]{0:T(128)S(1)} %pad_maximum_fusion), channel_id=1, replica_groups=mesh['groups'=2,'gx'=16] {'gx'}, use_global_device_ids=true, to_apply=%region_4.5 | all-reduce | flops 2 | bytes 16 | tf_op jit(solution)/shard_map/psum | solution.py:117
  260.2 6.2 %gather_fusion.3 = bf16[2048,64]{1,0:T(8,128)(2,1)S(1)} fusion(bf16[512,64]{1,0:T(8,128)(2,1)S(1)} %copy.90, s32[2048]{0:T(1024)S(1)} %fusion.47), kind=kCustom, calls=%fused_computation.3 | custom fusion | bytes 532480 | tf_op jit(solution)/shard_map/gather | solution.py:128
  266.6 12.6 %all_to_all.117 = bf16[16,128,64]{1,2,0:T(8,128)(2,1)S(1)} all-to-all(bf16[16,128,64]{1,2,0:T(8,128)(2,1)S(1)} %multiply_convert_fusion.1), channel_id=1, replica_groups=mesh['groups'=2,'gx'=16] {'gx'}, dimensions={0} | all-to-all | bytes 524288 | tf_op jit(solution)/shard_map/all_to_all | solution.py:131
  279.5 15.2 %scatter_custom_fusion.2 = f32[16384,64]{1,0:T(8,128)} fusion(s32[2048]{0:T(1024)S(1)} %bitcast.125, f32[2048,64]{1,0:T(8,128)S(1)} %bitcast.108, f32[]{:T(128)} %constant.15.clone.1), kind=kCustom, calls=%fused_computation.18 | custom fusion | flops 131072 | bytes 4194308 | tf_op jit(solution)/shard_map/scatter-add | solution.py:132
  294.7 6.8 %copy.94 = f32[16384,64]{0,1:T(8,128)} copy(f32[16384,64]{1,0:T(8,128)} %scatter_custom_fusion.2) | data formatting | bytes 8388608 | tf_op jit(solution)/shard_map/scatter-add | solution.py:132
  301.4 4.3 %fusion.6 = bf16[16384,64]{0,1:T(8,128)(2,1)S(1)} fusion(f32[16384,64]{0,1:T(8,128)} %copy.94, f32[16384,64]{0,1:T(8,128)} %get-tuple-element.18), kind=kLoop, calls=%fused_computation.15 | loop fusion | flops 10485760 | bytes 10485760 | tf_op jit(solution)/shard_map/convert_element_type | solution.py:135
  309.0 6.5 %reshape.190 = bf16[8,128,1024]{2,1,0:T(8,128)(2,1)} reshape(bf16[16384,64]{1,0:T(8,128)(2,1)} %copy.95) | data formatting | bytes 4194304 | tf_op jit(solution)/shard_map/reshape | solution.py:140
  320.0 4.5 %reshape.276 = bf16[16,2,8192]{2,1,0:T(2,128)(2,1)} reshape(bf16[1024,8,32]{2,1,0:T(8,128)(2,1)} %bitcast.100) | data formatting | bytes 1048576
  328.3 14.2 %all-to-all-done.7 = bf16[16,2,8192]{2,1,0:T(2,128)(2,1)S(1)} async-done(((bf16[16,2,8192]{2,1,0:T(2,128)(2,1)}), bf16[16,2,8192]{2,1,0:T(2,128)(2,1)S(1)}, u32[]{:S(2)}, u32[]{:S(2)}) %all-to-all-start.7) | async-done | bytes 524320 | tf_op jit(solution)/shard_map/all_to_all | solution.py:143
  348.4 4.0 all-to-all-start.8
  352.4 4.1 fusion.83
  356.6 62.5 %all-reduce = (f32[64,64]{1,0:T(8,128)}, f32[64]{0:T(128)}) all-reduce(f32[64,64]{1,0:T(8,128)} %fusion.83, f32[64]{0:T(128)S(1)} %convolution_bitcast_fusion.1), channel_id=1, replica_groups=mesh['groups'=2,'gx'=16] {'gx'}, use_global_device_ids=true, to_apply=%region_6.7 | all-reduce | flops 4160 | bytes 33280 | tf_op jit(solution)/shard_map/psum | solution.py:157
  (88 shorter events, 55.9 us)
Async XLA Ops:
  0.6 110.1 %copy-start = (bf16[64,64,64]{2,1,0:T(8,128)(2,1)S(1)}, bf16[64,64,64]{2,1,0:T(8,128)(2,1)}, u32[]{:S(2)}) copy-start(bf16[64,64,64]{2,1,0:T(8,128)(2,1)} %param.22) | copy-start | bytes 1572868
  0.6 1.8 copy-start.2
  15.6 6.4 %copy-start.7 = (f32[1,16,128]{2,1,0:T(8,128)S(1)}, f32[1,16,128]{2,1,0:T(8,128)}, u32[]{:S(2)}) copy-start(f32[1,16,128]{2,1,0:T(8,128)} %param.17) | copy-start | bytes 24580
  15.7 6.4 %copy-start.10 = (s32[1,16]{1,0:T(1,128)S(1)}, s32[1,16]{1,0:T(1,128)}, u32[]{:S(2)}) copy-start(s32[1,16]{1,0:T(1,128)} %param.18) | copy-start | bytes 196
  15.7 24.9 %copy-start.6 = (s32[16,1,128]{2,1,0:T(1,128)S(1)}, s32[16,1,128]{2,1,0:T(1,128)}, u32[]{:S(2)}) copy-start(s32[16,1,128]{2,1,0:T(1,128)} %param.16) | copy-start | bytes 24580
  22.9 17.4 %all-to-all-start = ((bf16[16,128,64]{1,2,0:T(8,128)(2,1)}), bf16[16,128,64]{1,2,0:T(8,128)(2,1)S(1)}, u32[]{:S(2)}, u32[]{:S(2)}) async-start(bf16[16,128,64]{1,2,0:T(8,128)(2,1)} %multiply_convert_fusion.2), calls=%async_computation | async-start | bytes 524288 | tf_op jit(solution)/shard_map/all_to_all | solution.py:64
  126.1 18.0 %all-to-all-start.4 = ((bf16[16,2,8192]{2,1,0:T(2,128)(2,1)}), bf16[16,2,8192]{2,1,0:T(2,128)(2,1)S(1)}, u32[]{:S(2)}, u32[]{:S(2)}) async-start(bf16[16,2,8192]{2,1,0:T(2,128)(2,1)} %reshape.274), calls=%async_computation.4 | async-start | bytes 1048576 | tf_op jit(solution)/shard_map/all_to_all | solution.py:98
  161.5 6.8 %copy-start.3 = (bf16[64,64]{1,0:T(8,128)(2,1)S(1)}, bf16[64,64]{1,0:T(8,128)(2,1)}, u32[]{:S(2)}) copy-start(bf16[64,64]{1,0:T(8,128)(2,1)} %param.23) | copy-start | bytes 24580
  161.5 6.8 %copy-start.9 = (f32[64]{0:T(128)S(1)}, f32[64]{0:T(128)}, u32[]{:S(2)}) copy-start(f32[64]{0:T(128)} %param.24) | copy-start | bytes 772
  178.6 13.3 %copy-start.8 = (f32[2,512]{1,0:T(2,128)S(1)}, f32[2,512]{1,0:T(2,128)}, u32[]{:S(2)}) copy-start(f32[2,512]{1,0:T(2,128)} %param.20) | copy-start | bytes 12292
  178.6 45.4 %copy-start.4 = (bf16[64,64]{1,0:T(8,128)(2,1)S(1)}, bf16[64,64]{1,0:T(8,128)(2,1)}, u32[]{:S(2)}) copy-start(bf16[64,64]{1,0:T(8,128)(2,1)} %param.25) | copy-start | bytes 24580
  178.6 45.4 %copy-start.11 = (f32[64]{0:T(128)S(1)}, f32[64]{0:T(128)}, u32[]{:S(2)}) copy-start(f32[64]{0:T(128)} %param.26) | copy-start | bytes 772
  178.6 45.8 %copy-start.12 = (f32[64]{0:T(128)S(1)}, f32[64]{0:T(128)}, u32[]{:S(2)}) copy-start(f32[64]{0:T(128)} %param.27) | copy-start | bytes 772
  178.6 78.8 %copy-start.13 = (f32[2]{0:T(128)S(1)}, f32[2]{0:T(128)}, u32[]{:S(2)}) copy-start(f32[2]{0:T(128)} %param.21) | copy-start | bytes 28
  187.9 14.1 %all-to-all-start.5 = ((bf16[16,128,64]{1,2,0:T(8,128)(2,1)}), bf16[16,128,64]{1,2,0:T(8,128)(2,1)S(1)}, u32[]{:S(2)}, u32[]{:S(2)}) async-start(bf16[16,128,64]{1,2,0:T(8,128)(2,1)} %copy.87), calls=%async_computation.5 | async-start | bytes 524288 | tf_op jit(solution)/shard_map/all_to_all | solution.py:105
  224.5 55.0 %copy-start.5 = (f32[1,512]{1,0:T(1,128)}, f32[1,512]{1,0:T(1,128)S(1)}, u32[]{:S(2)}) copy-start(f32[1,512]{1,0:T(1,128)S(1)} %fusion.38) | copy-start | bytes 6148
  324.5 18.0 %all-to-all-start.7 = ((bf16[16,2,8192]{2,1,0:T(2,128)(2,1)}), bf16[16,2,8192]{2,1,0:T(2,128)(2,1)S(1)}, u32[]{:S(2)}, u32[]{:S(2)}) async-start(bf16[16,2,8192]{2,1,0:T(2,128)(2,1)} %reshape.276), calls=%async_computation.7 | async-start | bytes 1048576 | tf_op jit(solution)/shard_map/all_to_all | solution.py:143
  348.4 70.7 %all-to-all-start.8 = ((bf16[16,2,2048]{2,1,0:T(2,128)(2,1)}), bf16[16,2,2048]{2,1,0:T(2,128)(2,1)S(1)}, u32[]{:S(2)}, u32[]{:S(2)}) async-start(bf16[16,2,2048]{2,1,0:T(2,128)(2,1)} %reshape.278), calls=%async_computation.8 | async-start | bytes 262144 | tf_op jit(solution)/shard_map/all_to_all | solution.py:147
  352.4 68.7 %copy-start.1 = (bf16[64,64,64]{2,1,0:T(8,128)(2,1)S(1)}, bf16[64,64,64]{2,1,0:T(8,128)(2,1)}, u32[]{:S(2)}) copy-start(bf16[64,64,64]{2,1,0:T(8,128)(2,1)} %param.22) | copy-start | bytes 1572868
where the time goes:
time: 426 us; the launch traced here: 421 us
  blocking collectives  147 us (35%)
  local copies, waits for them, and re-layouts  111 us (26%)
  other arithmetic  67 us (16%)
  waiting for transfers between devices  48.7 us (11%)
  matrix products  23.4 us (5%)
  starting transfers between devices  22.6 us (5%)
    psum x1, blocking collectives, per_device(): out_grad, skip_grad = lax.psum((out_part, skip_part), 'gx')  62.5 us
    psum x1, blocking collectives, per_device(): lax.psum(jnp.stack([jnp.sum(weighted * normals[0]), jnp.sum(weighted * no...  30.8 us
    scatter-add x1, other arithmetic, per_device(): jax.ops.segment_sum((pair_weight[..., None] * returned.astype(jnp.float32...  21.6 us
    all_to_all x1, blocking collectives, per_device(): lax.all_to_all(along_y, 'gx', split_axis=2, concat_axis=0, tiled=True)  18.7 us
    unnamed x41, local copies, waits for them, and re-layouts  17.5 us
    scatter-add x1, other arithmetic, per_device(): jax.ops.segment_sum(arrived.reshape(-1, width).astype(jnp.float32), cell_...  15.2 us
    scatter-add x1, other arithmetic, per_device(): jax.ops.segment_sum(grad_arrived.reshape(-1, width).astype(jnp.float32),...  15.2 us
    all_to_all x1, waiting for transfers between devices, per_device(): lax.all_to_all(back_x, 'gx', split_axis=0, concat_axis=2, tiled=True)  14.4 us
  transfers between devices with their start and end apart: 5, of which 4 were waited for; matrix products, arithmetic and copies ran while one was open for 1% of the time, Pallas kernels for 0%

commit v1 on v0

--- a/solution.py
+++ b/solution.py
@@ -1,8 +1,13 @@
+import functools
 import math
 
 import jax
 import jax.numpy as jnp
+import ml_dtypes
+import numpy as np
 from jax import lax
+from jax.experimental import pallas as pl
+from jax.experimental.pallas import tpu as pltpu
 from jax.sharding import PartitionSpec as P
 
 GX = 128
@@ -32,7 +37,7 @@
     ) * (1.0 / math.sqrt(2.0 * math.pi))
 
 
-def per_device(
+def general_step(
     point_feats,
     pair_point,
     pair_cell,
@@ -158,7 +163,554 @@
     return (pressure, forces, spec_grad, skip_grad, out_grad)
 
 
+F32 = jnp.float32
+BF16 = jnp.bfloat16
+LANES = 128
+WIDTH = 64
+
+
+def host_rows(length, number):
+    places = np.arange(length, dtype=np.float32)
+    order = np.arange(number)
+    half = number // 2
+    freqs = np.where(order < half, order, order - half + 1).astype(np.float32)
+    angles = np.float32(2.0 * math.pi / length) * freqs[:, None] * places[None, :]
+    table = np.where((order < half)[:, None], np.cos(angles), np.sin(angles))
+    table = table.astype(np.float32) * np.float32(math.sqrt(2.0 / length))
+    return table.astype(ml_dtypes.bfloat16)
+
+
+def three_parts(values):
+    first = values.astype(BF16)
+    rest = values - first.astype(F32)
+    second = rest.astype(BF16)
+    third = (rest - second.astype(F32)).astype(BF16)
+    return first, second, third
+
+
+def mm(left, right):
+    return jnp.dot(left, right, preferred_element_type=F32)
+
+
+def mm_nt(left, right):
+    return lax.dot_general(left, right, (((1,), (1,)), ((), ())), preferred_element_type=F32)
+
+
+def mm_tn(left, right):
+    return lax.dot_general(left, right, (((0,), (0,)), ((), ())), preferred_element_type=F32)
+
+
+def two_rows(ref, pair):
+    return jnp.concatenate([ref[2 * pair : 2 * pair + 1, :], ref[2 * pair + 1 : 2 * pair + 2, :]], axis=1)
+
+
+def source_kernel(group_ref, count_ref, point_ref, kern_ref, area_ref, feat_ref, weight_ref, msg_ref, pw_ref):
+    devices = point_ref.shape[0]
+    points = feat_ref.shape[1]
+    low = MODES // devices
+    first, second, third = three_parts(area_ref[...])
+    place = lax.broadcasted_iota(jnp.int32, (16, points), 0)
+    extra = jnp.where(
+        place == 0,
+        first.astype(F32),
+        jnp.where(place == 1, second.astype(F32), jnp.where(place == 2, third.astype(F32), 0.0)),
+    ).astype(BF16)
+    table = jnp.concatenate([feat_ref[...], extra], axis=0)
+    rows = lax.broadcasted_iota(jnp.int32, (points, 2 * LANES), 0)
+    lane = lax.broadcasted_iota(jnp.int32, (1, LANES), 1)
+    offset = group_ref[0] * MODES
+    for pair in range(devices // 2):
+        hot = jnp.where(rows == two_rows(point_ref, pair), 1.0, 0.0).astype(BF16)
+        got = mm(table, hot)
+        spread = got[WIDTH : WIDTH + 1] + got[WIDTH + 1 : WIDTH + 2] + got[WIDTH + 2 : WIDTH + 3]
+        for half in range(2):
+            dest = 2 * pair + half
+            cut = slice(half * LANES, (half + 1) * LANES)
+            weight = jnp.where(lane < count_ref[0, dest], kern_ref[dest : dest + 1, :], 0.0)
+            pw_ref[dest : dest + 1, :] = weight
+            msg_ref[dest, 0:WIDTH, :] = ((weight * spread[:, cut]) * got[0:WIDTH, cut]).astype(BF16)
+            msg_ref[dest, WIDTH : 2 * WIDTH, :] = jnp.concatenate(
+                [weight_ref[offset + low * dest], weight_ref[offset + low * dest + 1]], axis=1
+            )
+
+
+def place_kernel(depth, cell_ref, by_ref, col_ref, lp_ref, zr_ref):
+    devices = cell_ref.shape[0]
+    zbits = depth.bit_length() - 1
+    rows = by_ref.shape[0]
+    slab = rows // MODES
+    yrow = lax.broadcasted_iota(jnp.int32, (GY, LANES), 0)
+    xrow = jnp.bitwise_and(lax.broadcasted_iota(jnp.int32, (rows, LANES), 0), slab - 1)
+    up = lax.broadcasted_iota(jnp.int32, (LANES, LANES), 0) < lax.broadcasted_iota(
+        jnp.int32, (LANES, LANES), 1
+    )
+    for block in range(devices):
+        cells = cell_ref[block : block + 1, :]
+        cut = slice(block * LANES, (block + 1) * LANES)
+        col_ref[cut, :] = jnp.broadcast_to(cells.astype(F32), (LANES, LANES)).T
+        ypos = jnp.bitwise_and(jnp.right_shift(cells, zbits), GY - 1)
+        xpos = jnp.right_shift(cells, zbits + GY.bit_length() - 1)
+        hot = jnp.where(yrow == ypos, 1.0, 0.0).astype(BF16)
+        lp_ref[:, cut] = jnp.where(xrow == xpos, mm(by_ref[...], hot), 0.0).astype(BF16)
+    for block in range(devices):
+        cells = cell_ref[block : block + 1, :]
+        row = cells.astype(F32)
+        cut = slice(block * LANES, (block + 1) * LANES)
+        same = jnp.where(jnp.logical_and(col_ref[cut, :] == row, up), 1.0, 0.0)
+        seen = jnp.max(same, axis=0, keepdims=True)
+        if block:
+            before = jnp.where(col_ref[0 : block * LANES, :] == row, 1.0, 0.0)
+            seen = jnp.maximum(seen, jnp.max(before, axis=0, keepdims=True))
+        zr_ref[block : block + 1, :] = jnp.where(
+            seen > 0.0, -1, jnp.bitwise_and(cells, depth - 1)
+        )
+
+
+def equal_cells(col_ref, cell_ref, same_ref, pair):
+    for half in range(2):
+        row = cell_ref[2 * pair + half : 2 * pair + half + 1, :].astype(F32)
+        same_ref[:, half * LANES : (half + 1) * LANES] = jnp.where(
+            col_ref[...] == row, 1.0, 0.0
+        ).astype(BF16)
+
+
+def spread_depth(values, zpos, rp_ref, pair):
+    cut = slice(pair * 2 * LANES, (pair + 1) * 2 * LANES)
+    for level in range(rp_ref.shape[0] // WIDTH):
+        rp_ref[level * WIDTH : (level + 1) * WIDTH, cut] = jnp.where(
+            zpos == level, values, 0.0
+        ).astype(BF16)
+
+
+def slab_rows(lp_ref, rp_ref, msg_ref):
+    devices = msg_ref.shape[0]
+    step = lp_ref.shape[0] // devices
+    for quad in range(rp_ref.shape[0] // (4 * WIDTH)):
+        out = mm_nt(lp_ref[...], rp_ref[quad * 4 * WIDTH : (quad + 1) * 4 * WIDTH, :]).astype(BF16)
+        for half in range(2):
+            level = 2 * quad + half
+            for dest in range(devices):
+                msg_ref[dest, level * step : (level + 1) * step, :] = out[
+                    dest * step : (dest + 1) * step, half * LANES : (half + 1) * LANES
+                ]
+
+
+def cell_kernel(rx_ref, cell_ref, zr_ref, col_ref, lp_ref, msg_ref, lat_ref, xs_ref, same_a, same_b, rp_ref):
+    devices = rx_ref.shape[0]
+    for block in range(devices):
+        xs_ref[:, block * LANES : (block + 1) * LANES] = rx_ref[block, 0:WIDTH, :]
+    for pair in range(devices // 2):
+        same_ref = (same_a, same_b)[pair % 2]
+        equal_cells(col_ref, cell_ref, same_ref, pair)
+        latent = mm(xs_ref[...], same_ref[...])
+        lat_ref[:, pair * 2 * LANES : (pair + 1) * 2 * LANES] = latent.astype(BF16)
+        spread_depth(latent, two_rows(zr_ref, pair), rp_ref, pair)
+    slab_rows(lp_ref, rp_ref, msg_ref)
+
+
+def to_modes(rx_ref, table_ref, sp_ref):
+    levels = sp_ref.shape[0] // table_ref.shape[0]
+    step = table_ref.shape[1] // rx_ref.shape[0]
+    for level in range(levels):
+        block = rx_ref[:, level * step : (level + 1) * step, :].reshape(table_ref.shape[1], LANES)
+        coeffs = mm(table_ref[...], block).astype(BF16).astype(F32)
+        sp_ref[pl.ds(level, table_ref.shape[0], stride=levels), :] = coeffs
+
+
+def swap_halves(values):
+    return pltpu.roll(values, WIDTH, 1)
+
+
+def mode_kernel(group_ref, rx_ref, own_ref, other_ref, table_ref, back_ref, msg_ref, spec_ref, sp_ref, mx_ref):
+    devices = rx_ref.shape[0]
+    own_rows = spec_ref.shape[1]
+    modes = table_ref.shape[0]
+    levels = sp_ref.shape[0] // modes
+    step = back_ref.shape[0] // devices
+    to_modes(rx_ref, table_ref, sp_ref)
+    for dest in range(devices):
+        spec_ref[dest] = sp_ref[dest * own_rows : (dest + 1) * own_rows, :].astype(BF16)
+    left = lax.broadcasted_iota(jnp.int32, (levels, LANES), 1) < WIDTH
+    for order in range(MODES):
+        source, which = order // 2, order % 2
+        mine = jnp.full((WIDTH, LANES), group_ref[0], jnp.int32) == which
+        weight = jnp.where(
+            mine,
+            own_ref[source, WIDTH : 2 * WIDTH, :].astype(F32),
+            other_ref[source].astype(F32),
+        ).astype(BF16)
+        at = order * 2 * levels
+        even = sp_ref[at : at + levels, :]
+        odd = sp_ref[at + levels : at + 2 * levels, :]
+        rows = jnp.concatenate([even, swap_halves(even), odd, swap_halves(odd)], axis=0)
+        out = mm(rows[:, 0:WIDTH].astype(BF16), weight)
+        mx_ref[at : at + levels, :] = jnp.where(
+            left, out[0:levels], swap_halves(out[levels : 2 * levels])
+        )
+        mx_ref[at + levels : at + 2 * levels, :] = jnp.where(
+            left, swap_halves(out[2 * levels : 3 * levels]), out[3 * levels : 4 * levels]
+        )
+    for level in range(levels):
+        mixed = mx_ref[pl.ds(level, modes, stride=levels), :].astype(BF16)
+        out = mm(back_ref[...], mixed).astype(BF16)
+        for dest in range(devices):
+            msg_ref[dest, level * step : (level + 1) * step, :] = out[dest * step : (dest + 1) * step]
+
+
+def pre_kernel(depth, rx_ref, lp_ref, lat_ref, cell_ref, skip_ref, bias_ref, msg_ref, pre_ref, rt_ref):
+    devices = rx_ref.shape[0]
+    rows = lp_ref.shape[0]
+    step = rows // devices
+    for level in range(rt_ref.shape[0] // LANES):
+        block = rx_ref[:, level * step : (level + 1) * step, :].reshape(rows, LANES)
+        rt_ref[level * LANES : (level + 1) * LANES, :] = block.T
+    for pair in range(devices // 2):
+        cut = slice(pair * 2 * LANES, (pair + 1) * 2 * LANES)
+        zpos = jnp.bitwise_and(two_rows(cell_ref, pair), depth - 1)
+        field = mm(rt_ref[...], lp_ref[:, cut])
+        total = jnp.where(zpos == 0, field[0:WIDTH], 0.0)
+        for level in range(1, depth):
+            total += jnp.where(zpos == level, field[level * WIDTH : (level + 1) * WIDTH], 0.0)
+        pre = total + mm_tn(skip_ref[...], lat_ref[:, cut]) + bias_ref[...]
+        pre_ref[:, cut] = pre
+        feats = gelu_value(pre).astype(BF16)
+        for half in range(2):
+            msg_ref[2 * pair + half] = feats[:, half * LANES : (half + 1) * LANES]
+
+
+def slope_kernel(pre_ref, slope_ref):
+    slope_ref[...] = gelu_slope(pre_ref[...])
+
+
+def head_kernel(rx_ref, point_ref, pw_ref, head_ref, bias_ref, out_ref, area_ref, normal_ref, pres_ref, part_ref, hp_ref, value_ref, hot_ref):
+    devices = rx_ref.shape[0]
+    points = area_ref.shape[1]
+    rows = lax.broadcasted_iota(jnp.int32, (points, LANES), 0)
+    for block in range(devices):
+        cut = slice(block * LANES, (block + 1) * LANES)
+        parts = three_parts(pw_ref[block : block + 1, :] * rx_ref[block].astype(F32))
+        for index, part in enumerate(parts):
+            value_ref[index * WIDTH : (index + 1) * WIDTH, cut] = part
+        hot_ref[:, cut] = jnp.where(rows == point_ref[block : block + 1, :], 1.0, 0.0).astype(BF16)
+    sums = mm_nt(value_ref[...], hot_ref[...])
+    latent = sums[0:WIDTH] + sums[WIDTH : 2 * WIDTH] + sums[2 * WIDTH : 3 * WIDTH]
+    first, second, third = three_parts(latent)
+    weight = head_ref[...]
+    head_pre = mm_tn(weight, first) + mm_tn(weight, second) + mm_tn(weight, third) + bias_ref[...]
+    hp_ref[...] = head_pre
+    pressure = jnp.sum(gelu_value(head_pre) * out_ref[...], axis=0, keepdims=True)
+    pres_ref[...] = pressure
+    weighted = pressure * area_ref[...]
+    drag = jnp.sum(weighted * normal_ref[0:1, :], axis=1, keepdims=True)
+    lift = jnp.sum(weighted * normal_ref[1:2, :], axis=1, keepdims=True)
+    lane = lax.broadcasted_iota(jnp.int32, (1, LANES), 1)
+    row = jnp.where(lane == 0, drag, jnp.where(lane == 1, lift, 0.0))
+    for dest in range(devices):
+        part_ref[dest] = row
+
+
+def pair_kernel(hp_ref, point_ref, head_ref, out_ref, area_ref, normal_ref, up_ref, na_ref, head_out):
+    devices = point_ref.shape[0]
+    points = area_ref.shape[1]
+    head_pre = hp_ref[...]
+    head_out[...] = gelu_value(head_pre)
+    base = out_ref[...] * gelu_slope(head_pre)
+    first, second, third = three_parts(base)
+    weight = head_ref[...]
+    grad = mm(weight, first) + mm(weight, second) + mm(weight, third)
+    parts = three_parts(grad)
+    place = lax.broadcasted_iota(jnp.int32, (16, points), 0)
+    extra = jnp.zeros((16, points), F32)
+    for which in range(2):
+        scaled = three_parts(normal_ref[which : which + 1, :] * area_ref[...])
+        for index, part in enumerate(scaled):
+            extra = jnp.where(place == 3 * which + index, part.astype(F32), extra)
+    table = jnp.concatenate(list(parts) + [extra.astype(BF16)], axis=0)
+    rows = lax.broadcasted_iota(jnp.int32, (points, 2 * LANES), 0)
+    for pair in range(devices // 2):
+        hot = jnp.where(rows == two_rows(point_ref, pair), 1.0, 0.0).astype(BF16)
+        got = mm(table, hot)
+        up_ref[:, pair * 2 * LANES : (pair + 1) * 2 * LANES] = (
+            got[0:WIDTH] + got[WIDTH : 2 * WIDTH] + got[2 * WIDTH : 3 * WIDTH]
+        )
+        tail = got[3 * WIDTH : 3 * WIDTH + 16]
+        for which in range(2):
+            at = 3 * which
+            value = tail[at : at + 1] + tail[at + 1 : at + 2] + tail[at + 2 : at + 3]
+            for half in range(2):
+                na_ref[which, 2 * pair + half : 2 * pair + half + 1, :] = value[
+                    :, half * LANES : (half + 1) * LANES
+                ]
+
+
+def grad_kernel(scale, target_ref, part_ref, up_ref, na_ref, pw_ref, head_ref, area_ref, normal_ref, msg_ref, force_ref, outp_ref):
+    devices = part_ref.shape[0]
+    totals = part_ref[0]
+    for source in range(1, devices):
+        totals += part_ref[source]
+    forces = scale * totals
+    force_ref[...] = forces
+    drag = forces[:, 0:1] - target_ref[0]
+    lift = forces[:, 1:2] - target_ref[1]
+    twice = 2.0 * scale
+    for dest in range(devices):
+        along = twice * (drag * na_ref[0, dest : dest + 1, :] + lift * na_ref[1, dest : dest + 1, :])
+        grad = (along * up_ref[:, dest * LANES : (dest + 1) * LANES]).astype(BF16).astype(F32)
+        msg_ref[dest] = (pw_ref[dest : dest + 1, :] * grad).astype(BF16)
+    point_grad = twice * (drag * normal_ref[0:1, :] + lift * normal_ref[1:2, :]) * area_ref[...]
+    spread = jnp.broadcast_to(point_grad, (8, point_grad.shape[1]))
+    found = lax.dot_general(
+        spread,
+        head_ref[...],
+        (((1,), (1,)), ((), ())),
+        precision=lax.Precision.HIGHEST,
+        preferred_element_type=F32,
+    )
+    outp_ref[...] = jnp.where(lax.broadcasted_iota(jnp.int32, found.shape, 0) == 0, found, 0.0)
+
+
+def fold_rows(values):
+    first, second, third = three_parts(values)
+    upper = jnp.concatenate([first.astype(F32), second.astype(F32)], axis=1)
+    lower = jnp.concatenate([third.astype(F32), jnp.zeros_like(values)], axis=1)
+    return upper, lower
+
+
+def back_kernel(rx_ref, cell_ref, zr_ref, col_ref, lp_ref, lat_ref, slope_ref, outp_ref, msg_ref, xs_ref, pg_ref, same_a, same_b, rp_ref):
+    devices = rx_ref.shape[0]
+    main = lp_ref.shape[0] // devices * (rp_ref.shape[0] // LANES)
+    for block in range(devices):
+        xs_ref[:, block * LANES : (block + 1) * LANES] = rx_ref[block]
+    for pair in range(devices // 2):
+        cut = slice(pair * 2 * LANES, (pair + 1) * 2 * LANES)
+        same_ref = (same_a, same_b)[pair % 2]
+        equal_cells(col_ref, cell_ref, same_ref, pair)
+        grad = mm(xs_ref[...], same_ref[...]) * slope_ref[:, cut]
+        zpos = two_rows(zr_ref, pair)
+        pg_ref[:, cut] = jnp.where(zpos >= 0, grad, 0.0).astype(BF16)
+        spread_depth(grad, zpos, rp_ref, pair)
+    slab_rows(lp_ref, rp_ref, msg_ref)
+    skip = mm_nt(lat_ref[...], pg_ref[...])
+    upper, lower = fold_rows(jnp.concatenate([skip, outp_ref[...]], axis=0))
+    blocks = upper.shape[0] // 8
+    for dest in range(devices):
+        if dest < blocks:
+            cut = slice(8 * dest, 8 * dest + 8)
+            rows = jnp.concatenate([upper[cut], lower[cut]], axis=0)
+        else:
+            rows = jnp.zeros((16, LANES), F32)
+        msg_ref[dest, main : main + 16, :] = rows.astype(BF16)
+
+
+def spec_kernel(rx_ref, table_ref, spec_ref, msg_ref, sp_ref):
+    devices = rx_ref.shape[0]
+    own_rows = spec_ref.shape[1]
+    main = rx_ref.shape[1] - 16
+    to_modes(rx_ref, table_ref, sp_ref)
+    total = rx_ref[0, main : main + 16, :].astype(F32)
+    for source in range(1, devices):
+        total += rx_ref[source, main : main + 16, :].astype(F32)
+    upper, lower = total[0:8], total[8:16]
+    left = lax.broadcasted_iota(jnp.int32, (8, LANES), 1) < WIDTH
+    value = jnp.where(left, upper + swap_halves(upper) + lower, 0.0)
+    first, second, third = three_parts(value)
+    upper = first.astype(F32) + swap_halves(second.astype(F32))
+    rows = jnp.concatenate([upper, third.astype(F32)], axis=0).astype(BF16)
+    for dest in range(devices):
+        msg_ref[dest, 0:own_rows, :] = spec_ref[dest]
+        msg_ref[dest, own_rows : 2 * own_rows, :] = sp_ref[
+            dest * own_rows : (dest + 1) * own_rows, :
+        ].astype(BF16)
+        msg_ref[dest, 2 * own_rows : 2 * own_rows + 16, :] = rows
+
+
+def final_kernel(rx_ref, spec_ref, skip_ref, out_ref):
+    devices = rx_ref.shape[0]
+    own_rows = (rx_ref.shape[1] - 16) // 2
+    for source in range(devices):
+        for which in range(own_rows // 16):
+            at = which * 16
+            coeffs = rx_ref[source, at : at + 16, :].astype(F32)
+            grads = rx_ref[source, own_rows + at : own_rows + at + 16, :].astype(F32)
+            for low in range(2):
+                cut = slice(8 * low, 8 * low + 8)
+                left, right = coeffs[cut], grads[cut]
+                left = jnp.concatenate([left, swap_halves(left)], axis=0)[:, 0:WIDTH]
+                right = jnp.concatenate([right, swap_halves(right)], axis=0)[:, 0:WIDTH]
+                spec_ref[which * MODES + 2 * source + low] = mm_tn(
+                    left.astype(BF16), right.astype(BF16)
+                )
+    for source in range(WIDTH // 8 + 1):
+        rows = rx_ref[source, 2 * own_rows : 2 * own_rows + 16, :].astype(F32)
+        value = (rows[0:8] + swap_halves(rows[0:8]) + rows[8:16])[:, 0:WIDTH]
+        if source < WIDTH // 8:
+            skip_ref[8 * source : 8 * source + 8, :] = value
+        else:
+            out_ref[...] = value
+
+
+def run(kernel, outs, ins, flops, scratch=(), smem=0):
+    vmem = pl.BlockSpec(memory_space=pltpu.VMEM)
+    moved = sum(math.prod(a.shape) * a.dtype.itemsize for a in list(ins) + list(outs))
+    return pl.pallas_call(
+        kernel,
+        out_shape=tuple(outs),
+        in_specs=[pl.BlockSpec(memory_space=pltpu.SMEM)] * smem + [vmem] * (len(ins) - smem),
+        out_specs=tuple([vmem] * len(outs)),
+        scratch_shapes=list(scratch),
+        compiler_params=pltpu.CompilerParams(vmem_limit_bytes=48 * 1024 * 1024),
+        cost_estimate=pl.CostEstimate(flops=flops, bytes_accessed=moved, transcendentals=0),
+    )(*ins)
+
+
+def slab_step(
+    point_feats,
+    pair_point,
+    pair_cell,
+    kernel,
+    counts,
+    area,
+    normals,
+    targets,
+    spec_weight,
+    skip_weight,
+    skip_bias,
+    head_weight,
+    head_bias,
+    out_weight,
+):
+    n = lax.axis_size("gx")
+    points = point_feats.shape[0]
+    slots = n * LANES
+    slab = GX // n
+    low = MODES // n
+    depth = ZL * n
+    levels = depth * WIDTH // LANES
+    rows = MODES * slab
+    main = levels * slab * low
+    own_rows = low * low * levels
+    shape = jax.ShapeDtypeStruct
+
+    by = host_rows(GY, MODES)
+    bx = host_rows(GX, MODES)
+    by_rows = jnp.asarray(np.repeat(by, slab, axis=0))
+    table = np.zeros((MODES, low, n, low, slab), ml_dtypes.bfloat16)
+    for index in range(low):
+        table[:, index, :, index, :] = bx.reshape(MODES, n, slab)
+    table = table.reshape(MODES * low, rows)
+    back = jnp.asarray(np.ascontiguousarray(table.T))
+    table = jnp.asarray(table)
+
+    def exchange(message):
+        return lax.all_to_all(message, "gx", split_axis=0, concat_axis=0, tiled=True)
+
+    group = lax.axis_index("groups").astype(jnp.int32).reshape(1)
+    point_rows = pair_point[0]
+    cells = pair_cell[:, 0, :]
+    area_row = area.reshape(1, points)
+    msg, pw = run(
+        source_kernel,
+        [shape((n, 2 * WIDTH, LANES), BF16), shape((n, LANES), F32)],
+        [group, counts, point_rows, kernel[0], area_row, point_feats.T, spec_weight],
+        2 * 80 * points * slots,
+        smem=2,
+    )
+    rx = exchange(msg)
+    col, lp, zr = run(
+        functools.partial(place_kernel, depth),
+        [shape((slots, LANES), F32), shape((rows, slots), BF16), shape((n, LANES), jnp.int32)],
+        [cells, by_rows],
+        2 * rows * LANES * slots,
+    )
+    other = lax.ppermute(rx[:, WIDTH : 2 * WIDTH, :], "groups", [(0, 1), (1, 0)])
+    sum_scratch = [
+        pltpu.VMEM((slots, 2 * LANES), BF16),
+        pltpu.VMEM((slots, 2 * LANES), BF16),
+        pltpu.VMEM((depth * WIDTH, slots), BF16),
+    ]
+    big = 2 * WIDTH * slots * slots + 2 * rows * slots * depth * WIDTH
+    msg, lat = run(
+        cell_kernel,
+        [shape((n, main, LANES), BF16), shape((WIDTH, slots), BF16)],
+        [rx, cells, zr, col, lp],
+        big,
+        scratch=[pltpu.VMEM((WIDTH, slots), BF16)] + sum_scratch,
+    )
+    columns = exchange(msg)
+    msg, spec = run(
+        mode_kernel,
+        [shape((n, main, LANES), BF16), shape((n, own_rows, LANES), BF16)],
+        [group, columns, rx, other, table, back],
+        4 * MODES * low * rows * depth * WIDTH,
+        scratch=[pltpu.VMEM((MODES * low * levels, LANES), F32)] * 2,
+        smem=1,
+    )
+    slabs = exchange(msg)
+    msg, pre = run(
+        functools.partial(pre_kernel, depth),
+        [shape((n, WIDTH, LANES), BF16), shape((WIDTH, slots), F32)],
+        [slabs, lp, lat, cells, skip_weight, skip_bias.reshape(WIDTH, 1)],
+        2 * rows * slots * depth * WIDTH,
+        scratch=[pltpu.VMEM((depth * WIDTH, rows), BF16)],
+    )
+    returned = exchange(msg)
+    (slope,) = run(slope_kernel, [shape(pre.shape, F32)], [pre], 100 * WIDTH * slots)
+    out_col = out_weight.reshape(WIDTH, 1)
+    pressure, part, head_pre = run(
+        head_kernel,
+        [shape((1, points), F32), shape((n, 1, LANES), F32), shape((WIDTH, points), F32)],
+        [returned, point_rows, pw, head_weight, head_bias.reshape(WIDTH, 1), out_col, area_row, normals],
+        2 * 3 * WIDTH * points * slots,
+        scratch=[pltpu.VMEM((3 * WIDTH, slots), BF16), pltpu.VMEM((points, slots), BF16)],
+    )
+    parts = exchange(part)
+    up, na, head = run(
+        pair_kernel,
+        [shape((WIDTH, slots), F32), shape((2, n, LANES), F32), shape((WIDTH, points), F32)],
+        [head_pre, point_rows, head_weight, out_col, area_row, normals],
+        2 * 208 * points * slots,
+    )
+    scale = 1.0 / math.sqrt(points * n)
+    msg, forces, outp = run(
+        functools.partial(grad_kernel, scale),
+        [shape((n, WIDTH, LANES), BF16), shape((1, LANES), F32), shape((8, WIDTH), F32)],
+        [targets, parts, up, na, pw, head, area_row, normals],
+        10 * WIDTH * slots,
+        smem=1,
+    )
+    grads = exchange(msg)
+    (msg,) = run(
+        back_kernel,
+        [shape((n, main + 16, LANES), BF16)],
+        [grads, cells, zr, col, lp, lat, slope, outp],
+        big,
+        scratch=[pltpu.VMEM((WIDTH, slots), BF16)] * 2 + sum_scratch,
+    )
+    grad_columns = exchange(msg)
+    (msg,) = run(
+        spec_kernel,
+        [shape((n, 2 * own_rows + 16, LANES), BF16)],
+        [grad_columns, table, spec],
+        2 * MODES * low * rows * depth * WIDTH,
+        scratch=[pltpu.VMEM((MODES * low * levels, LANES), F32)],
+    )
+    finals = exchange(msg)
+    spec_grad, skip_grad, out_grad = run(
+        final_kernel,
+        [
+            shape((spec_weight.shape[0], WIDTH, WIDTH), F32),
+            shape((WIDTH, WIDTH), F32),
+            shape((8, WIDTH), F32),
+        ],
+        [finals],
+        2 * NMODE * WIDTH * WIDTH * depth // n,
+    )
+    return (pressure.reshape(points), forces[0, 0:2], spec_grad, skip_grad, out_grad[0])
+
+
 def solution(mesh):
+    fits = mesh.shape["gx"] == 16 and mesh.shape["groups"] == 2
+    per_device = slab_step if fits else general_step
     in_specs = (
         P(("groups", "gx"), None),
         P(("groups", "gx"), None, None),

time: 426 us -> 164 us (0.38)
  blocking collectives: 147 us -> 20 us
  local copies, waits for them, and re-layouts: 111 us -> 10.8 us
  other arithmetic: 67 us -> 0 us
  waiting for transfers between devices: 48.7 us -> 74.8 us
  Pallas kernels: 0 us -> 24.5 us
  matrix products: 23.4 us -> 0 us
  starting transfers between devices: 22.6 us -> 32.2 us
    psum x2 -> x0, blocking collectives: 93.3 us -> none  [the longest x1 62.5 us: per_device(): out_grad, skip_grad = lax.psum((out_part, skip_part), 'gx')]
    scatter-add x3 -> x0, other arithmetic: 52 us -> none  [the longest x1 21.6 us: per_device(): jax.ops.segment_sum((pair_weight[..., None] * returned.astype(jnp.float32...]
    gather x4 -> x0, local copies, waits for them, and re-layouts: 34 us -> none  [the longest x1 13.2 us: per_device(): sender_weight = pair_weight * area[point_rows]]
    all_to_all x4 -> x1, blocking collectives: 53.8 us -> 20 us  [exchange(): lax.all_to_all(message, 'gx', split_axis=0, concat_axis=0, tiled=True)]
    reshape x6 -> x3, local copies, waits for them, and re-layouts: 27.3 us -> 0.29 us  [the longest x1 0.1 us: slab_step(): skip_bias.reshape(WIDTH, 1)]
    pallas_call x0 -> x12, Pallas kernels: none -> 24.5 us  [run(): pl.pallas_call(kernel, out_shape=tuple(outs), in_specs=[pl.BlockSpec(memo...]
    dot_general x14 -> x0, matrix products: 23.4 us -> none  [the longest x1 7.06 us: per_device(): jnp.dot(latent, skip_weight, preferred_element_type=jnp.float32)]
    all_to_all x5 -> x7, waiting for transfers between devices: 48.7 us -> 67.6 us  [exchange(): lax.all_to_all(message, 'gx', split_axis=0, concat_axis=0, tiled=True)]
  transfers between devices with their start and end apart: 5 -> 8, of which waited for: 4 -> 8; matrix products, arithmetic and copies ran while one was open for 1% -> 1% of each run, Pallas kernels for 0% -> 1%
where the time goes in v1:
time: 164 us; the launch traced here: 163 us
  waiting for transfers between devices  74.8 us (46%)
  starting transfers between devices  32.2 us (20%)
  Pallas kernels  24.5 us (15%)
  blocking collectives  20 us (12%)
  local copies, waits for them, and re-layouts  10.8 us (7%)
    all_to_all x7, waiting for transfers between devices, exchange(): lax.all_to_all(message, 'gx', split_axis=0, concat_axis=0, tiled=True)  67.6 us
    all_to_all x7, starting transfers between devices, exchange(): lax.all_to_all(message, 'gx', split_axis=0, concat_axis=0, tiled=True)  30.7 us
    pallas_call x12, Pallas kernels, run(): pl.pallas_call(kernel, out_shape=tuple(outs), in_specs=[pl.BlockSpec(memo...  24.5 us
    all_to_all x1, blocking collectives, exchange(): lax.all_to_all(message, 'gx', split_axis=0, concat_axis=0, tiled=True)  20 us
    unnamed x46, local copies, waits for them, and re-layouts  9.48 us
    ppermute x1, waiting for transfers between devices, slab_step(): other = lax.ppermute(rx[:, WIDTH:2 * WIDTH, :], 'groups', [(0, 1), (1, 0)])  7.14 us
  transfers between devices with their start and end apart: 8, of which 8 were waited for; matrix products, arithmetic and copies ran while one was open for 1% of the time, Pallas kernels for 1%

profile of v1, /device:TPU:0, one launch (start us, length us, event | category | flops | bytes accessed | tf_op | source)
XLA Modules:
  0.0 163.2 jit_solution(8844711832583808615)
XLA Ops:
  0.7 1.2 copy-done
  5.4 1.9 %shard_map.200 = (bf16[16,128,128]{2,1,0:T(8,128)(2,1)}, f32[16,128]{1,0:T(8,128)S(1)}) custom-call(s32[1]{0:T(128)} %bitcast.group_ref, s32[1,16]{1,0:T(1,128)S(1)} %copy-done.10, s32[16,128]{1,0:T(8,128)S(1)} %bitcast.16, f32[16,128]{1,0:T(8,128)S(1)} %bitcast.15, f32[1,512]{1,0:T(1,128)S(1)} %bitcast.19, bf16[64,512]{1,0:T(8,128)(2,1)S(1)} %bitcast.14, ...), custom_call_target="tpu_custom_call" | custom-call | flops 167772160 | bytes 1140804 | tf_op jit(solution)/shard_map/pallas_call | solution.py:555
  7.3 7.4 %all-to-all-start = ((bf16[16,128,128]{2,1,0:T(8,128)(2,1)}), bf16[16,128,128]{2,1,0:T(8,128)(2,1)S(1)}, u32[]{:S(2)}, u32[]{:S(2)}) async-start(bf16[16,128,128]{2,1,0:T(8,128)(2,1)} %get-tuple-element.28), calls=%async_computation | async-start | bytes 1048576 | tf_op jit(solution)/shard_map/all_to_all | solution.py:605
  14.7 1.3 shard_map.201
  16.1 1.0 copy-done.16
  17.0 12.1 %all-to-all-done.rx_ref.own_ref = bf16[16,128,128]{2,1,0:T(8,128)(2,1)S(1)} async-done(((bf16[16,128,128]{2,1,0:T(8,128)(2,1)}), bf16[16,128,128]{2,1,0:T(8,128)(2,1)S(1)}, u32[]{:S(2)}, u32[]{:S(2)}) %all-to-all-start) | async-done | bytes 524320 | tf_op jit(solution)/shard_map/all_to_all | solution.py:605
  29.2 1.2 copy-done.17
  30.4 5.2 %shard_map.202 = (bf16[16,128,128]{2,1,0:T(8,128)(2,1)}, bf16[64,2048]{1,0:T(8,128)(2,1)S(1)}) custom-call(bf16[16,128,128]{2,1,0:T(8,128)(2,1)S(1)} %all-to-all-done.rx_ref.own_ref, s32[16,128]{1,0:T(8,128)S(1)} %bitcast.24, s32[16,128]{1,0:T(8,128)S(1)} %get-tuple-element.29.zr_ref, f32[2048,128]{1,0:T(8,128)S(1)} %get-tuple-element.30.col_ref, ...), custom_call_target="tpu_custom_call" | custom-call | flops 1610612736 | bytes 3424256 | tf_op jit(solution)/shard_map/pallas_call | solution.py:555
  35.6 4.2 %all-to-all-start.1 = ((bf16[16,128,128]{2,1,0:T(8,128)(2,1)}), bf16[16,128,128]{2,1,0:T(8,128)(2,1)S(1)}, u32[]{:S(2)}, u32[]{:S(2)}) async-start(bf16[16,128,128]{2,1,0:T(8,128)(2,1)} %get-tuple-element.32), calls=%async_computation.1 | async-start | bytes 1048576 | tf_op jit(solution)/shard_map/all_to_all | solution.py:605
  39.8 1.6 collective-permute-start
  41.4 7.1 %collective-permute-done.other_ref = bf16[16,64,128]{2,1,0:T(8,128)(2,1)S(1)} collective-permute-done((bf16[16,64,128]{2,1,0:T(8,128)(2,1)S(1)}, bf16[16,64,128]{2,1,0:T(8,128)(2,1)S(1)}, u32[]{:S(2)}, u32[]{:S(2)}) %collective-permute-start) | collective-permute-done | bytes 262176 | tf_op jit(solution)/shard_map/ppermute | solution.py:625
  48.5 5.7 %all-to-all-done.1.rx_ref = bf16[16,128,128]{2,1,0:T(8,128)(2,1)S(1)} async-done(((bf16[16,128,128]{2,1,0:T(8,128)(2,1)}), bf16[16,128,128]{2,1,0:T(8,128)(2,1)S(1)}, u32[]{:S(2)}, u32[]{:S(2)}) %all-to-all-start.1) | async-done | bytes 524320 | tf_op jit(solution)/shard_map/all_to_all | solution.py:605
  54.3 1.7 %shard_map.203 = (bf16[16,128,128]{2,1,0:T(8,128)(2,1)}, bf16[16,32,128]{2,1,0:T(8,128)(2,1)S(1)}) custom-call(s32[1]{0:T(128)} %bitcast.group_ref, bf16[16,128,128]{2,1,0:T(8,128)(2,1)S(1)} %all-to-all-done.1.rx_ref, bf16[16,128,128]{2,1,0:T(8,128)(2,1)S(1)} %all-to-all-done.rx_ref.own_ref, bf16[16,64,128]{2,1,0:T(8,128)(2,1)S(1)} %collective-permute-done.other_ref, ...), custom_call_target="tpu_custom_call" | custom-call | flops 67108864 | bytes 2031620 | tf_op jit(solution)/shard_map/pallas_call | solution.py:555
  56.0 4.1 %all-to-all-start.2 = ((bf16[16,128,128]{2,1,0:T(8,128)(2,1)}), bf16[16,128,128]{2,1,0:T(8,128)(2,1)S(1)}, u32[]{:S(2)}, u32[]{:S(2)}) async-start(bf16[16,128,128]{2,1,0:T(8,128)(2,1)} %get-tuple-element.33), calls=%async_computation.2 | async-start | bytes 1048576 | tf_op jit(solution)/shard_map/all_to_all | solution.py:605
  60.2 14.4 %all-to-all-done.2.rx_ref = bf16[16,128,128]{2,1,0:T(8,128)(2,1)S(1)} async-done(((bf16[16,128,128]{2,1,0:T(8,128)(2,1)}), bf16[16,128,128]{2,1,0:T(8,128)(2,1)S(1)}, u32[]{:S(2)}, u32[]{:S(2)}) %all-to-all-start.2) | async-done | bytes 524320 | tf_op jit(solution)/shard_map/all_to_all | solution.py:605
  74.6 1.2 copy-done.18
  75.8 2.2 %shard_map.204 = (bf16[16,64,128]{2,1,0:T(8,128)(2,1)}, f32[64,2048]{1,0:T(8,128)S(1)}) custom-call(bf16[16,128,128]{2,1,0:T(8,128)(2,1)S(1)} %all-to-all-done.2.rx_ref, bf16[256,2048]{1,0:T(8,128)(2,1)S(1)} %copy-done.18, bf16[64,2048]{1,0:T(8,128)(2,1)S(1)} %get-tuple-element.34.lat_ref, s32[16,128]{1,0:T(8,128)S(1)} %bitcast.25, ...), custom_call_target="tpu_custom_call" | custom-call | flops 1073741824 | bytes 2638080 | tf_op jit(solution)/shard_map/pallas_call | solution.py:555
  78.0 4.2 %all-to-all-start.3 = ((bf16[16,64,128]{2,1,0:T(8,128)(2,1)}), bf16[16,64,128]{2,1,0:T(8,128)(2,1)S(1)}, u32[]{:S(2)}, u32[]{:S(2)}) async-start(bf16[16,64,128]{2,1,0:T(8,128)(2,1)} %get-tuple-element.35), calls=%async_computation.3 | async-start | bytes 524288 | tf_op jit(solution)/shard_map/all_to_all | solution.py:605
  82.5 9.8 %all-to-all-done.3.rx_ref = bf16[16,64,128]{2,1,0:T(8,128)(2,1)S(1)} async-done(((bf16[16,64,128]{2,1,0:T(8,128)(2,1)}), bf16[16,64,128]{2,1,0:T(8,128)(2,1)S(1)}, u32[]{:S(2)}, u32[]{:S(2)}) %all-to-all-start.3) | async-done | bytes 262176 | tf_op jit(solution)/shard_map/all_to_all | solution.py:605
  92.3 2.2 %shard_map.205 = (f32[1,512]{1,0:T(1,128)}, f32[16,1,128]{2,1,0:T(1,128)}, f32[64,512]{1,0:T(8,128)S(1)}) custom-call(bf16[16,64,128]{2,1,0:T(8,128)(2,1)S(1)} %all-to-all-done.3.rx_ref, s32[16,128]{1,0:T(8,128)S(1)} %bitcast.17, f32[16,128]{1,0:T(8,128)S(1)} %get-tuple-element.36.pw_ref, bf16[64,64]{1,0:T(8,128)(2,1)S(1)} %copy-done.13, ...), custom_call_target="tpu_custom_call" | custom-call | flops 402653184 | bytes 434688 | tf_op jit(solution)/shard_map/pallas_call | solution.py:555
  94.5 3.5 %all-to-all-start.4 = ((f32[16,1,128]{2,1,0:T(1,128)}), f32[16,1,128]{2,1,0:T(1,128)S(1)}, u32[]{:S(2)}, u32[]{:S(2)}) async-start(f32[16,1,128]{2,1,0:T(1,128)} %get-tuple-element.38), calls=%async_computation.4 | async-start | bytes 16384 | tf_op jit(solution)/shard_map/all_to_all | solution.py:605
  98.9 5.4 %all-to-all-done.4.part_ref = f32[16,1,128]{2,1,0:T(1,128)S(1)} async-done(((f32[16,1,128]{2,1,0:T(1,128)}), f32[16,1,128]{2,1,0:T(1,128)S(1)}, u32[]{:S(2)}, u32[]{:S(2)}) %all-to-all-start.4) | async-done | bytes 8224 | tf_op jit(solution)/shard_map/all_to_all | solution.py:605
  104.3 1.4 shard_map.207
  105.7 3.7 %all-to-all-start.5 = ((bf16[16,64,128]{2,1,0:T(8,128)(2,1)}), bf16[16,64,128]{2,1,0:T(8,128)(2,1)S(1)}, u32[]{:S(2)}, u32[]{:S(2)}) async-start(bf16[16,64,128]{2,1,0:T(8,128)(2,1)} %get-tuple-element.44), calls=%async_computation.5 | async-start | bytes 524288 | tf_op jit(solution)/shard_map/all_to_all | solution.py:605
  109.7 9.6 %all-to-all-done.5.rx_ref = bf16[16,64,128]{2,1,0:T(8,128)(2,1)S(1)} async-done(((bf16[16,64,128]{2,1,0:T(8,128)(2,1)}), bf16[16,64,128]{2,1,0:T(8,128)(2,1)S(1)}, u32[]{:S(2)}, u32[]{:S(2)}) %all-to-all-start.5) | async-done | bytes 262176 | tf_op jit(solution)/shard_map/all_to_all | solution.py:605
  119.3 1.2 copy-done.19
  120.5 4.5 %shard_map.209 = bf16[16,144,128]{2,1,0:T(8,128)(2,1)S(1)} custom-call(bf16[16,64,128]{2,1,0:T(8,128)(2,1)S(1)} %all-to-all-done.5.rx_ref, s32[16,128]{1,0:T(8,128)S(1)} %bitcast.26, s32[16,128]{1,0:T(8,128)S(1)} %get-tuple-element.29.zr_ref, f32[2048,128]{1,0:T(8,128)S(1)} %get-tuple-element.30.col_ref, bf16[256,2048]{1,0:T(8,128)(2,1)S(1)} %copy-done.19, ...), custom_call_target="tpu_custom_call" | custom-call | flops 1610612736 | bytes 3753984 | tf_op jit(solution)/shard_map/pallas_call | solution.py:555
  125.0 20.0 %all_to_all.40.rx_ref = bf16[16,144,128]{2,1,0:T(8,128)(2,1)S(1)} all-to-all(bf16[16,144,128]{2,1,0:T(8,128)(2,1)S(1)} %shard_map.209), channel_id=1, replica_groups=mesh['groups'=2,'gx'=16] {'gx'}, dimensions={0} | all-to-all | bytes 1179648 | tf_op jit(solution)/shard_map/all_to_all | solution.py:605
  145.1 1.0 shard_map.210
  146.0 3.5 %all-to-all-start.7 = ((bf16[16,80,128]{2,1,0:T(8,128)(2,1)}), bf16[16,80,128]{2,1,0:T(8,128)(2,1)S(1)}, u32[]{:S(2)}, u32[]{:S(2)}) async-start(bf16[16,80,128]{2,1,0:T(8,128)(2,1)} %shard_map.210), calls=%async_computation.7 | async-start | bytes 655360 | tf_op jit(solution)/shard_map/all_to_all | solution.py:605
  150.1 10.5 %all-to-all-done.7.rx_ref = bf16[16,80,128]{2,1,0:T(8,128)(2,1)S(1)} async-done(((bf16[16,80,128]{2,1,0:T(8,128)(2,1)}), bf16[16,80,128]{2,1,0:T(8,128)(2,1)S(1)}, u32[]{:S(2)}, u32[]{:S(2)}) %all-to-all-start.7) | async-done | bytes 327712 | tf_op jit(solution)/shard_map/all_to_all | solution.py:605
  160.6 2.0 %shard_map.211 = (f32[64,64,64]{2,1,0:T(8,128)}, f32[64,64]{1,0:T(8,128)}, f32[8,64]{1,0:T(8,128)S(1)}) custom-call(bf16[16,80,128]{2,1,0:T(8,128)(2,1)S(1)} %all-to-all-done.7.rx_ref), custom_call_target="tpu_custom_call" | custom-call | flops 8388608 | bytes 1394688 | tf_op jit(solution)/shard_map/pallas_call | solution.py:555
  (49 shorter events, 6.1 us)
Async XLA Ops:
  0.6 14.1 %copy-start.14 = (s32[16,1,128]{2,1,0:T(1,128)S(1)}, s32[16,1,128]{2,1,0:T(1,128)}, u32[]{:S(2)}) copy-start(s32[16,1,128]{2,1,0:T(1,128)} %param.19) | copy-start | bytes 24580
  0.6 1.2 copy-start
  1.9 0.8 copy-start.2
  2.7 0.7 copy-start.4
  3.4 0.7 copy-start.5
  4.1 0.7 copy-start.7
  4.8 0.7 copy-start.10
  5.4 9.3 %copy-start.15 = (bf16[256,128]{1,0:T(8,128)(2,1)S(1)}, bf16[256,128]{1,0:T(8,128)(2,1)}, u32[]{:S(2)}) copy-start(bf16[256,128]{1,0:T(8,128)(2,1)} %constant.12.clone.by_ref) | copy-start | bytes 196612
  7.3 21.9 %all-to-all-start = ((bf16[16,128,128]{2,1,0:T(8,128)(2,1)}), bf16[16,128,128]{2,1,0:T(8,128)(2,1)S(1)}, u32[]{:S(2)}, u32[]{:S(2)}) async-start(bf16[16,128,128]{2,1,0:T(8,128)(2,1)} %get-tuple-element.28), calls=%async_computation | async-start | bytes 1048576 | tf_op jit(solution)/shard_map/all_to_all | solution.py:605
  16.1 1.0 copy-start.16
  29.2 1.2 copy-start.17
  30.4 23.9 %copy-start.1 = (bf16[64,256]{1,0:T(8,128)(2,1)S(1)}, bf16[64,256]{1,0:T(8,128)(2,1)}, u32[]{:S(2)}) copy-start(bf16[64,256]{1,0:T(8,128)(2,1)} %constant.14.clone.table_ref) | copy-start | bytes 98308
  30.4 23.9 %copy-start.3 = (bf16[256,64]{1,0:T(8,128)(2,1)S(1)}, bf16[256,64]{1,0:T(8,128)(2,1)}, u32[]{:S(2)}) copy-start(bf16[256,64]{1,0:T(8,128)(2,1)} %constant.13.clone.back_ref) | copy-start | bytes 98308
  35.6 24.5 %copy-start.20 = (f32[64]{0:T(128)S(1)}, f32[64]{0:T(128)}, u32[]{:S(2)}) copy-start(f32[64]{0:T(128)} %param.27) | copy-start | bytes 772
  35.6 39.0 %copy-start.12 = (bf16[64,64]{1,0:T(8,128)(2,1)S(1)}, bf16[64,64]{1,0:T(8,128)(2,1)}, u32[]{:S(2)}) copy-start(bf16[64,64]{1,0:T(8,128)(2,1)} %skip_ref.1) | copy-start | bytes 24580
  35.6 18.7 %all-to-all-start.1 = ((bf16[16,128,128]{2,1,0:T(8,128)(2,1)}), bf16[16,128,128]{2,1,0:T(8,128)(2,1)S(1)}, u32[]{:S(2)}, u32[]{:S(2)}) async-start(bf16[16,128,128]{2,1,0:T(8,128)(2,1)} %get-tuple-element.32), calls=%async_computation.1 | async-start | bytes 1048576 | tf_op jit(solution)/shard_map/all_to_all | solution.py:605
  39.8 8.7 %collective-permute-start = (bf16[16,64,128]{2,1,0:T(8,128)(2,1)S(1)}, bf16[16,64,128]{2,1,0:T(8,128)(2,1)S(1)}, u32[]{:S(2)}, u32[]{:S(2)}) collective-permute-start(bf16[16,64,128]{2,1,0:T(8,128)(2,1)S(1)} %slice.12), channel_id=1, source_target_pairs={{0,16},{16,0},{1,17},{17,1},{2,18},{18,2},{3,19},{19,3},{4,20},{20... | collective-permute-start | bytes 786440 | tf_op jit(solution)/shard_map/ppermute | solution.py:625
  56.0 18.6 %all-to-all-start.2 = ((bf16[16,128,128]{2,1,0:T(8,128)(2,1)}), bf16[16,128,128]{2,1,0:T(8,128)(2,1)S(1)}, u32[]{:S(2)}, u32[]{:S(2)}) async-start(bf16[16,128,128]{2,1,0:T(8,128)(2,1)} %get-tuple-element.33), calls=%async_computation.2 | async-start | bytes 1048576 | tf_op jit(solution)/shard_map/all_to_all | solution.py:605
  74.6 1.2 copy-start.18
  75.8 6.5 %copy-start.21 = (f32[64]{0:T(128)S(1)}, f32[64]{0:T(128)}, u32[]{:S(2)}) copy-start(f32[64]{0:T(128)} %param.30) | copy-start | bytes 772
  75.8 6.6 %copy-start.22 = (f32[64]{0:T(128)S(1)}, f32[64]{0:T(128)}, u32[]{:S(2)}) copy-start(f32[64]{0:T(128)} %param.29) | copy-start | bytes 772
  75.8 16.5 %copy-start.6 = (s32[1,16,128]{2,1,0:T(8,128)S(1)}, s32[1,16,128]{2,1,0:T(8,128)}, u32[]{:S(2)}) copy-start(s32[1,16,128]{2,1,0:T(8,128)} %param.18) | copy-start | bytes 24580
  75.8 16.5 %copy-start.8 = (f32[512]{0:T(512)S(1)}, f32[512]{0:T(512)}, u32[]{:S(2)}) copy-start(f32[512]{0:T(512)} %param.22) | copy-start | bytes 6148
  75.8 16.5 %copy-start.9 = (f32[2,512]{1,0:T(2,128)S(1)}, f32[2,512]{1,0:T(2,128)}, u32[]{:S(2)}) copy-start(f32[2,512]{1,0:T(2,128)} %normal_ref.5) | copy-start | bytes 12292
  75.8 16.5 %copy-start.13 = (bf16[64,64]{1,0:T(8,128)(2,1)S(1)}, bf16[64,64]{1,0:T(8,128)(2,1)}, u32[]{:S(2)}) copy-start(bf16[64,64]{1,0:T(8,128)(2,1)} %head_ref.3) | copy-start | bytes 24580
  78.0 26.3 %copy-start.11 = (f32[2]{0:T(128)S(1)}, f32[2]{0:T(128)}, u32[]{:S(2)}) copy-start(f32[2]{0:T(128)} %target_ref.1) | copy-start | bytes 28
  78.0 14.3 %all-to-all-start.3 = ((bf16[16,64,128]{2,1,0:T(8,128)(2,1)}), bf16[16,64,128]{2,1,0:T(8,128)(2,1)S(1)}, u32[]{:S(2)}, u32[]{:S(2)}) async-start(bf16[16,64,128]{2,1,0:T(8,128)(2,1)} %get-tuple-element.35), calls=%async_computation.3 | async-start | bytes 524288 | tf_op jit(solution)/shard_map/all_to_all | solution.py:605
  94.5 9.8 %all-to-all-start.4 = ((f32[16,1,128]{2,1,0:T(1,128)}), f32[16,1,128]{2,1,0:T(1,128)S(1)}, u32[]{:S(2)}, u32[]{:S(2)}) async-start(f32[16,1,128]{2,1,0:T(1,128)} %get-tuple-element.38), calls=%async_computation.4 | async-start | bytes 16384 | tf_op jit(solution)/shard_map/all_to_all | solution.py:605
  105.7 13.5 %all-to-all-start.5 = ((bf16[16,64,128]{2,1,0:T(8,128)(2,1)}), bf16[16,64,128]{2,1,0:T(8,128)(2,1)S(1)}, u32[]{:S(2)}, u32[]{:S(2)}) async-start(bf16[16,64,128]{2,1,0:T(8,128)(2,1)} %get-tuple-element.44), calls=%async_computation.5 | async-start | bytes 524288 | tf_op jit(solution)/shard_map/all_to_all | solution.py:605
  119.3 1.2 copy-start.19
  146.0 14.6 %all-to-all-start.7 = ((bf16[16,80,128]{2,1,0:T(8,128)(2,1)}), bf16[16,80,128]{2,1,0:T(8,128)(2,1)S(1)}, u32[]{:S(2)}, u32[]{:S(2)}) async-start(bf16[16,80,128]{2,1,0:T(8,128)(2,1)} %shard_map.210), calls=%async_computation.7 | async-start | bytes 655360 | tf_op jit(solution)/shard_map/all_to_all | solution.py:605

commit v2 on v1

--- a/solution.py
+++ b/solution.py
@@ -204,10 +204,25 @@
     return jnp.concatenate([ref[2 * pair : 2 * pair + 1, :], ref[2 * pair + 1 : 2 * pair + 2, :]], axis=1)
 
 
-def source_kernel(group_ref, count_ref, point_ref, kern_ref, area_ref, feat_ref, weight_ref, msg_ref, pw_ref):
-    devices = point_ref.shape[0]
-    points = feat_ref.shape[1]
+def source_kernel(group_ref, count_hbm, point_hbm, kern_hbm, area_hbm, feat_hbm, weight_hbm, msg_ref, pw_ref, count_ref, point_ref, kern_ref, area_ref, feat_ref, weight_ref, sems):
+    devices, points = point_ref.shape[0], feat_ref.shape[1]
     low = MODES // devices
+    pieces = (
+        (point_hbm, point_ref),
+        (area_hbm, area_ref),
+        (feat_hbm, feat_ref),
+        (kern_hbm, kern_ref),
+        (count_hbm, count_ref),
+        (weight_hbm.at[pl.ds(group_ref[0] * MODES, MODES)], weight_ref),
+    )
+    copies = [
+        pltpu.make_async_copy(source, place, sems.at[index])
+        for index, (source, place) in enumerate(pieces)
+    ]
+    for copy in copies:
+        copy.start()
+    for copy in copies[:-1]:
+        copy.wait()
     first, second, third = three_parts(area_ref[...])
     place = lax.broadcasted_iota(jnp.int32, (16, points), 0)
     extra = jnp.where(
@@ -218,7 +233,6 @@
     table = jnp.concatenate([feat_ref[...], extra], axis=0)
     rows = lax.broadcasted_iota(jnp.int32, (points, 2 * LANES), 0)
     lane = lax.broadcasted_iota(jnp.int32, (1, LANES), 1)
-    offset = group_ref[0] * MODES
     for pair in range(devices // 2):
         hot = jnp.where(rows == two_rows(point_ref, pair), 1.0, 0.0).astype(BF16)
         got = mm(table, hot)
@@ -226,15 +240,18 @@
         for half in range(2):
             dest = 2 * pair + half
             cut = slice(half * LANES, (half + 1) * LANES)
-            weight = jnp.where(lane < count_ref[0, dest], kern_ref[dest : dest + 1, :], 0.0)
+            valid = lane < count_ref[0:1, dest : dest + 1]
+            weight = jnp.where(valid, kern_ref[dest : dest + 1, :], 0.0)
             pw_ref[dest : dest + 1, :] = weight
             msg_ref[dest, 0:WIDTH, :] = ((weight * spread[:, cut]) * got[0:WIDTH, cut]).astype(BF16)
-            msg_ref[dest, WIDTH : 2 * WIDTH, :] = jnp.concatenate(
-                [weight_ref[offset + low * dest], weight_ref[offset + low * dest + 1]], axis=1
-            )
-
-
-def place_kernel(depth, cell_ref, by_ref, col_ref, lp_ref, zr_ref):
+    copies[-1].wait()
+    for dest in range(devices):
+        msg_ref[dest, WIDTH : 2 * WIDTH, :] = jnp.concatenate(
+            [weight_ref[low * dest], weight_ref[low * dest + 1]], axis=1
+        )
+
+
+def place_kernel(depth, cell_ref, by_ref, same_ref, lp_ref, zr_ref, col_ref):
     devices = cell_ref.shape[0]
     zbits = depth.bit_length() - 1
     rows = by_ref.shape[0]
@@ -264,14 +281,23 @@
         zr_ref[block : block + 1, :] = jnp.where(
             seen > 0.0, -1, jnp.bitwise_and(cells, depth - 1)
         )
-
-
-def equal_cells(col_ref, cell_ref, same_ref, pair):
-    for half in range(2):
-        row = cell_ref[2 * pair + half : 2 * pair + half + 1, :].astype(F32)
-        same_ref[:, half * LANES : (half + 1) * LANES] = jnp.where(
+    equal_cells(cell_ref, col_ref, same_ref)
+
+
+def equal_cells(cell_ref, col_ref, same_ref):
+    for block in range(cell_ref.shape[0]):
+        row = cell_ref[block : block + 1, :].astype(F32)
+        same_ref[:, block * LANES : (block + 1) * LANES] = jnp.where(
             col_ref[...] == row, 1.0, 0.0
         ).astype(BF16)
+
+
+def same_kernel(cell_ref, after_ref, same_ref, col_ref):
+    for block in range(cell_ref.shape[0]):
+        row = cell_ref[block : block + 1, :].astype(F32)
+        cut = slice(block * LANES, (block + 1) * LANES)
+        col_ref[cut, :] = jnp.broadcast_to(row, (LANES, LANES)).T
+    equal_cells(cell_ref, col_ref, same_ref)
 
 
 def spread_depth(values, zpos, rp_ref, pair):
@@ -295,15 +321,14 @@
                 ]
 
 
-def cell_kernel(rx_ref, cell_ref, zr_ref, col_ref, lp_ref, msg_ref, lat_ref, xs_ref, same_a, same_b, rp_ref):
+def cell_kernel(rx_ref, same_ref, zr_ref, lp_ref, msg_ref, lat_ref, xs_ref, rp_ref):
     devices = rx_ref.shape[0]
     for block in range(devices):
         xs_ref[:, block * LANES : (block + 1) * LANES] = rx_ref[block, 0:WIDTH, :]
     for pair in range(devices // 2):
-        same_ref = (same_a, same_b)[pair % 2]
-        equal_cells(col_ref, cell_ref, same_ref, pair)
-        latent = mm(xs_ref[...], same_ref[...])
-        lat_ref[:, pair * 2 * LANES : (pair + 1) * 2 * LANES] = latent.astype(BF16)
+        cut = slice(pair * 2 * LANES, (pair + 1) * 2 * LANES)
+        latent = mm(xs_ref[...], same_ref[:, cut])
+        lat_ref[:, cut] = latent.astype(BF16)
         spread_depth(latent, two_rows(zr_ref, pair), rp_ref, pair)
     slab_rows(lp_ref, rp_ref, msg_ref)
 
@@ -382,7 +407,7 @@
     slope_ref[...] = gelu_slope(pre_ref[...])
 
 
-def head_kernel(rx_ref, point_ref, pw_ref, head_ref, bias_ref, out_ref, area_ref, normal_ref, pres_ref, part_ref, hp_ref, value_ref, hot_ref):
+def head_kernel(rx_ref, point_ref, pw_ref, head_ref, bias_ref, out_ref, area_ref, normal_ref, pres_ref, msg_ref, value_ref, hot_ref):
     devices = rx_ref.shape[0]
     points = area_ref.shape[1]
     rows = lax.broadcasted_iota(jnp.int32, (points, LANES), 0)
@@ -397,76 +422,48 @@
     first, second, third = three_parts(latent)
     weight = head_ref[...]
     head_pre = mm_tn(weight, first) + mm_tn(weight, second) + mm_tn(weight, third) + bias_ref[...]
-    hp_ref[...] = head_pre
-    pressure = jnp.sum(gelu_value(head_pre) * out_ref[...], axis=0, keepdims=True)
+    head = gelu_value(head_pre)
+    pressure = jnp.sum(head * out_ref[...], axis=0, keepdims=True)
     pres_ref[...] = pressure
-    weighted = pressure * area_ref[...]
-    drag = jnp.sum(weighted * normal_ref[0:1, :], axis=1, keepdims=True)
-    lift = jnp.sum(weighted * normal_ref[1:2, :], axis=1, keepdims=True)
-    lane = lax.broadcasted_iota(jnp.int32, (1, LANES), 1)
-    row = jnp.where(lane == 0, drag, jnp.where(lane == 1, lift, 0.0))
-    for dest in range(devices):
-        part_ref[dest] = row
-
-
-def pair_kernel(hp_ref, point_ref, head_ref, out_ref, area_ref, normal_ref, up_ref, na_ref, head_out):
-    devices = point_ref.shape[0]
-    points = area_ref.shape[1]
-    head_pre = hp_ref[...]
-    head_out[...] = gelu_value(head_pre)
-    base = out_ref[...] * gelu_slope(head_pre)
-    first, second, third = three_parts(base)
-    weight = head_ref[...]
+    along = [normal_ref[which : which + 1, :] * area_ref[...] for which in range(2)]
+    first, second, third = three_parts(out_ref[...] * gelu_slope(head_pre))
     grad = mm(weight, first) + mm(weight, second) + mm(weight, third)
-    parts = three_parts(grad)
     place = lax.broadcasted_iota(jnp.int32, (16, points), 0)
     extra = jnp.zeros((16, points), F32)
     for which in range(2):
-        scaled = three_parts(normal_ref[which : which + 1, :] * area_ref[...])
-        for index, part in enumerate(scaled):
-            extra = jnp.where(place == 3 * which + index, part.astype(F32), extra)
-    table = jnp.concatenate(list(parts) + [extra.astype(BF16)], axis=0)
-    rows = lax.broadcasted_iota(jnp.int32, (points, 2 * LANES), 0)
-    for pair in range(devices // 2):
-        hot = jnp.where(rows == two_rows(point_ref, pair), 1.0, 0.0).astype(BF16)
-        got = mm(table, hot)
-        up_ref[:, pair * 2 * LANES : (pair + 1) * 2 * LANES] = (
-            got[0:WIDTH] + got[WIDTH : 2 * WIDTH] + got[2 * WIDTH : 3 * WIDTH]
-        )
-        tail = got[3 * WIDTH : 3 * WIDTH + 16]
-        for which in range(2):
-            at = 3 * which
-            value = tail[at : at + 1] + tail[at + 1 : at + 2] + tail[at + 2 : at + 3]
-            for half in range(2):
-                na_ref[which, 2 * pair + half : 2 * pair + half + 1, :] = value[
-                    :, half * LANES : (half + 1) * LANES
-                ]
-
-
-def grad_kernel(scale, target_ref, part_ref, up_ref, na_ref, pw_ref, head_ref, area_ref, normal_ref, msg_ref, force_ref, outp_ref):
-    devices = part_ref.shape[0]
-    totals = part_ref[0]
-    for source in range(1, devices):
-        totals += part_ref[source]
-    forces = scale * totals
-    force_ref[...] = forces
-    drag = forces[:, 0:1] - target_ref[0]
-    lift = forces[:, 1:2] - target_ref[1]
-    twice = 2.0 * scale
-    for dest in range(devices):
-        along = twice * (drag * na_ref[0, dest : dest + 1, :] + lift * na_ref[1, dest : dest + 1, :])
-        grad = (along * up_ref[:, dest * LANES : (dest + 1) * LANES]).astype(BF16).astype(F32)
-        msg_ref[dest] = (pw_ref[dest : dest + 1, :] * grad).astype(BF16)
-    point_grad = twice * (drag * normal_ref[0:1, :] + lift * normal_ref[1:2, :]) * area_ref[...]
-    spread = jnp.broadcast_to(point_grad, (8, point_grad.shape[1]))
-    found = lax.dot_general(
-        spread,
-        head_ref[...],
+        for index, part in enumerate(three_parts(along[which])):
+            extra = jnp.where(place == 3 + 3 * which + index, part.astype(F32), extra)
+    upper = grad.astype(BF16)
+    lower = (grad - upper.astype(F32)).astype(BF16)
+    table = jnp.concatenate([upper, lower, extra.astype(BF16)], axis=0)
+    lane = lax.broadcasted_iota(jnp.int32, (1, LANES), 1)
+    partial = []
+    for which in range(2):
+        force = jnp.sum(pressure * area_ref[...] * normal_ref[which : which + 1, :], axis=1, keepdims=True)
+        partial.append(force)
+    force_row = jnp.where(lane == 0, partial[0], jnp.where(lane == 1, partial[1], 0.0))
+    out_rows = lax.dot_general(
+        jnp.concatenate([along[0], along[1], jnp.zeros((6, points), F32)], axis=0),
+        head,
         (((1,), (1,)), ((), ())),
         precision=lax.Precision.HIGHEST,
         preferred_element_type=F32,
     )
-    outp_ref[...] = jnp.where(lax.broadcasted_iota(jnp.int32, found.shape, 0) == 0, found, 0.0)
+    out_row = jnp.concatenate([out_rows[0:1], out_rows[1:2]], axis=1)
+    place = lax.broadcasted_iota(jnp.int32, (16, LANES), 0)
+    common = jnp.zeros((16, LANES), F32)
+    for index, part in enumerate(three_parts(out_row)):
+        common = jnp.where(place == 9 + index, part.astype(F32), common)
+    for index, part in enumerate(three_parts(force_row)):
+        common = jnp.where(place == 12 + index, part.astype(F32), common)
+    for block in range(devices):
+        cut = slice(block * LANES, (block + 1) * LANES)
+        got = mm(table, hot_ref[:, cut])
+        msg_ref[block, 0 : 2 * WIDTH, :] = got[0 : 2 * WIDTH].astype(BF16)
+        tail = got[2 * WIDTH : 2 * WIDTH + 16] + common
+        for index, part in enumerate(three_parts(pw_ref[block : block + 1, :])):
+            tail = jnp.where(place == index, part.astype(F32), tail)
+        msg_ref[block, 2 * WIDTH : 2 * WIDTH + 16, :] = tail.astype(BF16)
 
 
 def fold_rows(values):
@@ -476,22 +473,37 @@
     return upper, lower
 
 
-def back_kernel(rx_ref, cell_ref, zr_ref, col_ref, lp_ref, lat_ref, slope_ref, outp_ref, msg_ref, xs_ref, pg_ref, same_a, same_b, rp_ref):
+def back_kernel(scale, rx_ref, target_ref, same_ref, zr_ref, lp_ref, lat_ref, slope_ref, msg_ref, force_ref, outg_ref, xs_ref, pg_ref, rp_ref):
     devices = rx_ref.shape[0]
     main = lp_ref.shape[0] // devices * (rp_ref.shape[0] // LANES)
+    extra = slice(2 * WIDTH, 2 * WIDTH + 16)
+    total = rx_ref[0, extra, :].astype(F32)
+    for block in range(1, devices):
+        total += rx_ref[block, extra, :].astype(F32)
+    forces = scale * (total[12:13] + total[13:14] + total[14:15])
+    force_ref[...] = forces[:, 0:2]
+    misfit = forces[:, 0:2] - target_ref[...]
+    drag, lift = misfit[:, 0:1], misfit[:, 1:2]
+    twice = 2.0 * scale
+    out_row = total[9:10] + total[10:11] + total[11:12]
+    outg_ref[...] = twice * (drag * out_row[:, 0:WIDTH] + lift * out_row[:, WIDTH : 2 * WIDTH])
     for block in range(devices):
-        xs_ref[:, block * LANES : (block + 1) * LANES] = rx_ref[block]
+        tail = rx_ref[block, extra, :].astype(F32)
+        weight, first, second = (
+            tail[at : at + 1] + tail[at + 1 : at + 2] + tail[at + 2 : at + 3] for at in (0, 3, 6)
+        )
+        grad = rx_ref[block, 0:WIDTH, :].astype(F32) + rx_ref[block, WIDTH : 2 * WIDTH, :].astype(F32)
+        along = twice * (drag * first + lift * second)
+        grad = (along * grad).astype(BF16).astype(F32)
+        xs_ref[:, block * LANES : (block + 1) * LANES] = (weight * grad).astype(BF16)
     for pair in range(devices // 2):
         cut = slice(pair * 2 * LANES, (pair + 1) * 2 * LANES)
-        same_ref = (same_a, same_b)[pair % 2]
-        equal_cells(col_ref, cell_ref, same_ref, pair)
-        grad = mm(xs_ref[...], same_ref[...]) * slope_ref[:, cut]
+        grad = mm(xs_ref[...], same_ref[:, cut]) * slope_ref[:, cut]
         zpos = two_rows(zr_ref, pair)
         pg_ref[:, cut] = jnp.where(zpos >= 0, grad, 0.0).astype(BF16)
         spread_depth(grad, zpos, rp_ref, pair)
     slab_rows(lp_ref, rp_ref, msg_ref)
-    skip = mm_nt(lat_ref[...], pg_ref[...])
-    upper, lower = fold_rows(jnp.concatenate([skip, outp_ref[...]], axis=0))
+    upper, lower = fold_rows(mm_nt(lat_ref[...], pg_ref[...]))
     blocks = upper.shape[0] // 8
     for dest in range(devices):
         if dest < blocks:
@@ -524,7 +536,7 @@
         msg_ref[dest, 2 * own_rows : 2 * own_rows + 16, :] = rows
 
 
-def final_kernel(rx_ref, spec_ref, skip_ref, out_ref):
+def final_kernel(rx_ref, spec_ref, skip_ref):
     devices = rx_ref.shape[0]
     own_rows = (rx_ref.shape[1] - 16) // 2
     for source in range(devices):
@@ -540,25 +552,23 @@
                 spec_ref[which * MODES + 2 * source + low] = mm_tn(
                     left.astype(BF16), right.astype(BF16)
                 )
-    for source in range(WIDTH // 8 + 1):
+    for source in range(WIDTH // 8):
         rows = rx_ref[source, 2 * own_rows : 2 * own_rows + 16, :].astype(F32)
         value = (rows[0:8] + swap_halves(rows[0:8]) + rows[8:16])[:, 0:WIDTH]
-        if source < WIDTH // 8:
-            skip_ref[8 * source : 8 * source + 8, :] = value
-        else:
-            out_ref[...] = value
-
-
-def run(kernel, outs, ins, flops, scratch=(), smem=0):
+        skip_ref[8 * source : 8 * source + 8, :] = value
+
+
+def run(kernel, outs, ins, flops, scratch=(), smem=0, hbm=False, grant=16):
     vmem = pl.BlockSpec(memory_space=pltpu.VMEM)
+    rest = pl.BlockSpec(memory_space=pltpu.HBM) if hbm else vmem
     moved = sum(math.prod(a.shape) * a.dtype.itemsize for a in list(ins) + list(outs))
     return pl.pallas_call(
         kernel,
         out_shape=tuple(outs),
-        in_specs=[pl.BlockSpec(memory_space=pltpu.SMEM)] * smem + [vmem] * (len(ins) - smem),
+        in_specs=[pl.BlockSpec(memory_space=pltpu.SMEM)] * smem + [rest] * (len(ins) - smem),
         out_specs=tuple([vmem] * len(outs)),
         scratch_shapes=list(scratch),
-        compiler_params=pltpu.CompilerParams(vmem_limit_bytes=48 * 1024 * 1024),
+        compiler_params=pltpu.CompilerParams(vmem_limit_bytes=grant * 1024 * 1024),
         cost_estimate=pl.CostEstimate(flops=flops, bytes_accessed=moved, transcendentals=0),
     )(*ins)
 
@@ -613,28 +623,37 @@
         [shape((n, 2 * WIDTH, LANES), BF16), shape((n, LANES), F32)],
         [group, counts, point_rows, kernel[0], area_row, point_feats.T, spec_weight],
         2 * 80 * points * slots,
-        smem=2,
+        scratch=[
+            pltpu.VMEM((1, n), jnp.int32),
+            pltpu.VMEM((n, LANES), jnp.int32),
+            pltpu.VMEM((n, LANES), F32),
+            pltpu.VMEM((1, points), F32),
+            pltpu.VMEM((WIDTH, points), BF16),
+            pltpu.VMEM((MODES, WIDTH, WIDTH), BF16),
+            pltpu.SemaphoreType.DMA((6,)),
+        ],
+        smem=1,
+        hbm=True,
     )
     rx = exchange(msg)
-    col, lp, zr = run(
+    columns_scratch = pltpu.VMEM((slots, LANES), F32)
+    same, lp, zr = run(
         functools.partial(place_kernel, depth),
-        [shape((slots, LANES), F32), shape((rows, slots), BF16), shape((n, LANES), jnp.int32)],
+        [shape((slots, slots), BF16), shape((rows, slots), BF16), shape((n, LANES), jnp.int32)],
         [cells, by_rows],
         2 * rows * LANES * slots,
+        scratch=[columns_scratch],
     )
     other = lax.ppermute(rx[:, WIDTH : 2 * WIDTH, :], "groups", [(0, 1), (1, 0)])
-    sum_scratch = [
-        pltpu.VMEM((slots, 2 * LANES), BF16),
-        pltpu.VMEM((slots, 2 * LANES), BF16),
-        pltpu.VMEM((depth * WIDTH, slots), BF16),
-    ]
+    pair_rows = pltpu.VMEM((WIDTH, slots), BF16)
+    deep_rows = pltpu.VMEM((depth * WIDTH, slots), BF16)
     big = 2 * WIDTH * slots * slots + 2 * rows * slots * depth * WIDTH
     msg, lat = run(
         cell_kernel,
         [shape((n, main, LANES), BF16), shape((WIDTH, slots), BF16)],
-        [rx, cells, zr, col, lp],
+        [rx, same, zr, lp],
         big,
-        scratch=[pltpu.VMEM((WIDTH, slots), BF16)] + sum_scratch,
+        scratch=[pair_rows, deep_rows],
     )
     columns = exchange(msg)
     msg, spec = run(
@@ -656,35 +675,28 @@
     returned = exchange(msg)
     (slope,) = run(slope_kernel, [shape(pre.shape, F32)], [pre], 100 * WIDTH * slots)
     out_col = out_weight.reshape(WIDTH, 1)
-    pressure, part, head_pre = run(
+    pressure, msg = run(
         head_kernel,
-        [shape((1, points), F32), shape((n, 1, LANES), F32), shape((WIDTH, points), F32)],
+        [shape((1, points), F32), shape((n, 2 * WIDTH + 16, LANES), BF16)],
         [returned, point_rows, pw, head_weight, head_bias.reshape(WIDTH, 1), out_col, area_row, normals],
         2 * 3 * WIDTH * points * slots,
         scratch=[pltpu.VMEM((3 * WIDTH, slots), BF16), pltpu.VMEM((points, slots), BF16)],
     )
-    parts = exchange(part)
-    up, na, head = run(
-        pair_kernel,
-        [shape((WIDTH, slots), F32), shape((2, n, LANES), F32), shape((WIDTH, points), F32)],
-        [head_pre, point_rows, head_weight, out_col, area_row, normals],
-        2 * 208 * points * slots,
+    grads = exchange(msg)
+    (same,) = run(
+        same_kernel,
+        [shape((slots, slots), BF16)],
+        [cells, pressure],
+        2 * slots * slots,
+        scratch=[columns_scratch],
     )
     scale = 1.0 / math.sqrt(points * n)
-    msg, forces, outp = run(
-        functools.partial(grad_kernel, scale),
-        [shape((n, WIDTH, LANES), BF16), shape((1, LANES), F32), shape((8, WIDTH), F32)],
-        [targets, parts, up, na, pw, head, area_row, normals],
-        10 * WIDTH * slots,
-        smem=1,
-    )
-    grads = exchange(msg)
-    (msg,) = run(
-        back_kernel,
-        [shape((n, main + 16, LANES), BF16)],
-        [grads, cells, zr, col, lp, lat, slope, outp],
+    msg, forces, out_grad = run(
+        functools.partial(back_kernel, scale),
+        [shape((n, main + 16, LANES), BF16), shape((1, 2), F32), shape((1, WIDTH), F32)],
+        [grads, targets.reshape(1, 2), same, zr, lp, lat, slope],
         big,
-        scratch=[pltpu.VMEM((WIDTH, slots), BF16)] * 2 + sum_scratch,
+        scratch=[pair_rows, pair_rows, deep_rows],
     )
     grad_columns = exchange(msg)
     (msg,) = run(
@@ -695,17 +707,13 @@
         scratch=[pltpu.VMEM((MODES * low * levels, LANES), F32)],
     )
     finals = exchange(msg)
-    spec_grad, skip_grad, out_grad = run(
+    spec_grad, skip_grad = run(
         final_kernel,
-        [
-            shape((spec_weight.shape[0], WIDTH, WIDTH), F32),
-            shape((WIDTH, WIDTH), F32),
-            shape((8, WIDTH), F32),
-        ],
+        [shape((spec_weight.shape[0], WIDTH, WIDTH), F32), shape((WIDTH, WIDTH), F32)],
         [finals],
         2 * NMODE * WIDTH * WIDTH * depth // n,
     )
-    return (pressure.reshape(points), forces[0, 0:2], spec_grad, skip_grad, out_grad[0])
+    return (pressure.reshape(points), forces.reshape(2), spec_grad, skip_grad, out_grad.reshape(WIDTH))
 
 
 def solution(mesh):

time: 164 us -> 159 us (0.970)
  waiting for transfers between devices: 74.8 us -> 53.3 us
  blocking collectives: 20 us -> 35.3 us
  local copies, waits for them, and re-layouts: 10.8 us -> 20.7 us
  starting transfers between devices: 32.2 us -> 25 us
    all_to_all x7 -> x5, waiting for transfers between devices: 67.6 us -> 46.1 us  [exchange(): lax.all_to_all(message, 'gx', split_axis=0, concat_axis=0, tiled=True)]
    all_to_all x1 -> x2, blocking collectives: 20 us -> 35.3 us  [exchange(): lax.all_to_all(message, 'gx', split_axis=0, concat_axis=0, tiled=True)]
    unnamed x46 -> x50, local copies, waits for them, and re-layouts: 9.48 us -> 20.4 us
    all_to_all x7 -> x5, starting transfers between devices: 30.7 us -> 23.5 us  [exchange(): lax.all_to_all(message, 'gx', split_axis=0, concat_axis=0, tiled=True)]
    pallas_call x12 -> x11, Pallas kernels: 24.5 us -> 23 us  [run(): pl.pallas_call(kernel, out_shape=tuple(outs), in_specs=[pl.BlockSpec(memo...]
  transfers between devices with their start and end apart: 8 -> 6, of which waited for: 8 -> 6; matrix products, arithmetic and copies ran while one was open for 1% -> 0% of each run, Pallas kernels for 1% -> 3%
where the time goes in v2:
time: 159 us; the launch traced here: 158 us
  waiting for transfers between devices  53.3 us (34%)
  blocking collectives  35.3 us (22%)
  starting transfers between devices  25 us (16%)
  Pallas kernels  23 us (14%)
  local copies, waits for them, and re-layouts  20.7 us (13%)
    all_to_all x5, waiting for transfers between devices, exchange(): lax.all_to_all(message, 'gx', split_axis=0, concat_axis=0, tiled=True)  46.1 us
    all_to_all x2, blocking collectives, exchange(): lax.all_to_all(message, 'gx', split_axis=0, concat_axis=0, tiled=True)  35.3 us
    all_to_all x5, starting transfers between devices, exchange(): lax.all_to_all(message, 'gx', split_axis=0, concat_axis=0, tiled=True)  23.5 us
    pallas_call x11, Pallas kernels, run(): pl.pallas_call(kernel, out_shape=tuple(outs), in_specs=[pl.BlockSpec(memo...  23 us
    unnamed x50, local copies, waits for them, and re-layouts  20.4 us
    ppermute x1, waiting for transfers between devices, slab_step(): other = lax.ppermute(rx[:, WIDTH:2 * WIDTH, :], 'groups', [(0, 1), (1, 0)])  7.16 us
  transfers between devices with their start and end apart: 6, of which 6 were waited for; matrix products, arithmetic and copies ran while one was open for 0% of the time, Pallas kernels for 3%

profile of v2, /device:TPU:0, one launch (start us, length us, event | category | flops | bytes accessed | tf_op | source)
XLA Modules:
  0.0 158.1 jit_solution(9703853717882754776)
XLA Ops:
  0.7 1.2 copy-done.4
  1.9 0.8 copy-done.6
  2.7 0.7 copy-done.8
  3.4 0.7 copy-done.9
  5.5 1.7 %shard_map.200 = (bf16[16,128,128]{2,1,0:T(8,128)(2,1)}, f32[16,128]{1,0:T(8,128)S(1)}) custom-call(s32[1]{0:T(128)} %bitcast.group_ref, s32[1,16]{1,0:T(1,128)S(1)} %copy-done.16, s32[16,128]{1,0:T(8,128)S(1)} %bitcast.15, f32[16,128]{1,0:T(8,128)S(1)} %bitcast.14, f32[1,512]{1,0:T(1,128)S(1)} %bitcast.20, bf16[64,512]{1,0:T(8,128)(2,1)S(1)} %bitcast.13, ...), custom_call_target="tpu_custom_call" | custom-call | flops 167772160 | bytes 1140804 | tf_op jit(solution)/shard_map/pallas_call | solution.py:565
  7.1 7.4 %all-to-all-start = ((bf16[16,128,128]{2,1,0:T(8,128)(2,1)}), bf16[16,128,128]{2,1,0:T(8,128)(2,1)S(1)}, u32[]{:S(2)}, u32[]{:S(2)}) async-start(bf16[16,128,128]{2,1,0:T(8,128)(2,1)} %get-tuple-element.23), calls=%async_computation | async-start | bytes 1048576 | tf_op jit(solution)/shard_map/all_to_all | solution.py:615
  15.2 0.8 copy-done.21
  16.1 2.9 %shard_map.201 = (bf16[2048,2048]{1,0:T(8,128)(2,1)S(1)}, bf16[256,2048]{1,0:T(8,128)(2,1)S(1)}, s32[16,128]{1,0:T(8,128)S(1)}) custom-call(s32[16,128]{1,0:T(8,128)S(1)} %bitcast.17, bf16[256,128]{1,0:T(8,128)(2,1)S(1)} %copy-done.21), custom_call_target="tpu_custom_call" | custom-call | flops 134217728 | bytes 9519104 | tf_op jit(solution)/shard_map/pallas_call | solution.py:565
  19.0 3.3 %copy-done.2 = bf16[2048,2048]{1,0:T(8,128)(2,1)} copy-done((bf16[2048,2048]{1,0:T(8,128)(2,1)}, bf16[2048,2048]{1,0:T(8,128)(2,1)S(1)}, u32[]{:S(2)}) %copy-start.2) | copy-done | bytes 8388632
  22.3 6.7 %all-to-all-done.rx_ref.own_ref = bf16[16,128,128]{2,1,0:T(8,128)(2,1)S(1)} async-done(((bf16[16,128,128]{2,1,0:T(8,128)(2,1)}), bf16[16,128,128]{2,1,0:T(8,128)(2,1)S(1)}, u32[]{:S(2)}, u32[]{:S(2)}) %all-to-all-start) | async-done | bytes 524320 | tf_op jit(solution)/shard_map/all_to_all | solution.py:615
  29.0 3.4 %copy-done.3 = bf16[2048,2048]{1,0:T(8,128)(2,1)S(1)} copy-done((bf16[2048,2048]{1,0:T(8,128)(2,1)S(1)}, bf16[2048,2048]{1,0:T(8,128)(2,1)}, u32[]{:S(2)}) %copy-start.3) | copy-done | bytes 8388632
  32.4 3.5 %shard_map.202 = (bf16[16,128,128]{2,1,0:T(8,128)(2,1)}, bf16[64,2048]{1,0:T(8,128)(2,1)S(1)}) custom-call(bf16[16,128,128]{2,1,0:T(8,128)(2,1)S(1)} %all-to-all-done.rx_ref.own_ref, bf16[2048,2048]{1,0:T(8,128)(2,1)S(1)} %copy-done.3, s32[16,128]{1,0:T(8,128)S(1)} %get-tuple-element.25.zr_ref, bf16[256,2048]{1,0:T(8,128)(2,1)S(1)} %get-tuple-element.26.lp_ref), custom_call_target="tpu_custom_call" | custom-call | flops 1610612736 | bytes 10756096 | tf_op jit(solution)/shard_map/pallas_call | solution.py:565
  36.0 4.1 %all-to-all-start.1 = ((bf16[16,128,128]{2,1,0:T(8,128)(2,1)}), bf16[16,128,128]{2,1,0:T(8,128)(2,1)S(1)}, u32[]{:S(2)}, u32[]{:S(2)}) async-start(bf16[16,128,128]{2,1,0:T(8,128)(2,1)} %get-tuple-element.27), calls=%async_computation.1 | async-start | bytes 1048576 | tf_op jit(solution)/shard_map/all_to_all | solution.py:615
  40.1 1.5 collective-permute-start
  41.6 7.2 %collective-permute-done.other_ref = bf16[16,64,128]{2,1,0:T(8,128)(2,1)S(1)} collective-permute-done((bf16[16,64,128]{2,1,0:T(8,128)(2,1)S(1)}, bf16[16,64,128]{2,1,0:T(8,128)(2,1)S(1)}, u32[]{:S(2)}, u32[]{:S(2)}) %collective-permute-start) | collective-permute-done | bytes 262176 | tf_op jit(solution)/shard_map/ppermute | solution.py:647
  48.8 5.7 %all-to-all-done.1.rx_ref = bf16[16,128,128]{2,1,0:T(8,128)(2,1)S(1)} async-done(((bf16[16,128,128]{2,1,0:T(8,128)(2,1)}), bf16[16,128,128]{2,1,0:T(8,128)(2,1)S(1)}, u32[]{:S(2)}, u32[]{:S(2)}) %all-to-all-start.1) | async-done | bytes 524320 | tf_op jit(solution)/shard_map/all_to_all | solution.py:615
  54.5 1.7 %shard_map.203 = (bf16[16,128,128]{2,1,0:T(8,128)(2,1)}, bf16[16,32,128]{2,1,0:T(8,128)(2,1)S(1)}) custom-call(s32[1]{0:T(128)} %bitcast.group_ref, bf16[16,128,128]{2,1,0:T(8,128)(2,1)S(1)} %all-to-all-done.1.rx_ref, bf16[16,128,128]{2,1,0:T(8,128)(2,1)S(1)} %all-to-all-done.rx_ref.own_ref, bf16[16,64,128]{2,1,0:T(8,128)(2,1)S(1)} %collective-permute-done.other_ref, ...), custom_call_target="tpu_custom_call" | custom-call | flops 67108864 | bytes 2031620 | tf_op jit(solution)/shard_map/pallas_call | solution.py:565
  56.2 4.1 %all-to-all-start.2 = ((bf16[16,128,128]{2,1,0:T(8,128)(2,1)}), bf16[16,128,128]{2,1,0:T(8,128)(2,1)S(1)}, u32[]{:S(2)}, u32[]{:S(2)}) async-start(bf16[16,128,128]{2,1,0:T(8,128)(2,1)} %get-tuple-element.28), calls=%async_computation.2 | async-start | bytes 1048576 | tf_op jit(solution)/shard_map/all_to_all | solution.py:615
  60.5 14.3 %all-to-all-done.2.rx_ref = bf16[16,128,128]{2,1,0:T(8,128)(2,1)S(1)} async-done(((bf16[16,128,128]{2,1,0:T(8,128)(2,1)}), bf16[16,128,128]{2,1,0:T(8,128)(2,1)S(1)}, u32[]{:S(2)}, u32[]{:S(2)}) %all-to-all-start.2) | async-done | bytes 524320 | tf_op jit(solution)/shard_map/all_to_all | solution.py:615
  74.8 2.2 %shard_map.204 = (bf16[16,64,128]{2,1,0:T(8,128)(2,1)}, f32[64,2048]{1,0:T(8,128)S(1)}) custom-call(bf16[16,128,128]{2,1,0:T(8,128)(2,1)S(1)} %all-to-all-done.2.rx_ref, bf16[256,2048]{1,0:T(8,128)(2,1)S(1)} %get-tuple-element.26.lp_ref, bf16[64,2048]{1,0:T(8,128)(2,1)S(1)} %get-tuple-element.29.lat_ref, s32[16,128]{1,0:T(8,128)S(1)} %bitcast.18, ...), custom_call_target="tpu_custom_call" | custom-call | flops 1073741824 | bytes 2638080 | tf_op jit(solution)/shard_map/pallas_call | solution.py:565
  77.0 4.1 %all-to-all-start.3 = ((bf16[16,64,128]{2,1,0:T(8,128)(2,1)}), bf16[16,64,128]{2,1,0:T(8,128)(2,1)S(1)}, u32[]{:S(2)}, u32[]{:S(2)}) async-start(bf16[16,64,128]{2,1,0:T(8,128)(2,1)} %get-tuple-element.30), calls=%async_computation.3 | async-start | bytes 524288 | tf_op jit(solution)/shard_map/all_to_all | solution.py:615
  81.3 9.8 %all-to-all-done.3.rx_ref = bf16[16,64,128]{2,1,0:T(8,128)(2,1)S(1)} async-done(((bf16[16,64,128]{2,1,0:T(8,128)(2,1)}), bf16[16,64,128]{2,1,0:T(8,128)(2,1)S(1)}, u32[]{:S(2)}, u32[]{:S(2)}) %all-to-all-start.3) | async-done | bytes 262176 | tf_op jit(solution)/shard_map/all_to_all | solution.py:615
  91.2 3.4 %shard_map.205 = (f32[1,512]{1,0:T(1,128)}, bf16[16,144,128]{2,1,0:T(8,128)(2,1)}) custom-call(bf16[16,64,128]{2,1,0:T(8,128)(2,1)S(1)} %all-to-all-done.3.rx_ref, s32[16,128]{1,0:T(8,128)S(1)} %bitcast.16, f32[16,128]{1,0:T(8,128)S(1)} %get-tuple-element.31.pw_ref, bf16[64,64]{1,0:T(8,128)(2,1)S(1)} %copy-done.19, f32[64,1]{1,0:T(8,128)S(1)} %copy.23.bias_ref, ...), custom_call_target="tpu_custom_call" | custom-call | flops 402653184 | bytes 885248 | tf_op jit(solution)/shard_map/pallas_call | solution.py:565
  94.6 3.8 %all-to-all-start.4 = ((bf16[16,144,128]{2,1,0:T(8,128)(2,1)}), bf16[16,144,128]{2,1,0:T(8,128)(2,1)S(1)}, u32[]{:S(2)}, u32[]{:S(2)}) async-start(bf16[16,144,128]{2,1,0:T(8,128)(2,1)} %get-tuple-element.33), calls=%async_computation.4 | async-start | bytes 1179648 | tf_op jit(solution)/shard_map/all_to_all | solution.py:615
  99.2 1.7 %shard_map.206.same_ref = bf16[2048,2048]{1,0:T(8,128)(2,1)S(1)} custom-call(s32[16,128]{1,0:T(8,128)S(1)} %bitcast.19, f32[1,512]{1,0:T(1,128)S(1)} %copy-done.15), custom_call_target="tpu_custom_call" | custom-call | flops 8388608 | bytes 8398848 | tf_op jit(solution)/shard_map/pallas_call | solution.py:565
  100.9 3.3 %copy-done = bf16[2048,2048]{1,0:T(8,128)(2,1)} copy-done((bf16[2048,2048]{1,0:T(8,128)(2,1)}, bf16[2048,2048]{1,0:T(8,128)(2,1)S(1)}, u32[]{:S(2)}) %copy-start) | copy-done | bytes 8388632
  104.2 9.5 %all-to-all-done.4.rx_ref = bf16[16,144,128]{2,1,0:T(8,128)(2,1)S(1)} async-done(((bf16[16,144,128]{2,1,0:T(8,128)(2,1)}), bf16[16,144,128]{2,1,0:T(8,128)(2,1)S(1)}, u32[]{:S(2)}, u32[]{:S(2)}) %all-to-all-start.4) | async-done | bytes 589856 | tf_op jit(solution)/shard_map/all_to_all | solution.py:615
  113.7 3.4 %copy-done.1 = bf16[2048,2048]{1,0:T(8,128)(2,1)S(1)} copy-done((bf16[2048,2048]{1,0:T(8,128)(2,1)S(1)}, bf16[2048,2048]{1,0:T(8,128)(2,1)}, u32[]{:S(2)}) %copy-start.1) | copy-done | bytes 8388632
  117.0 3.5 %shard_map.208 = (bf16[16,144,128]{2,1,0:T(8,128)(2,1)S(1)}, f32[1,2]{1,0:T(1,128)}, f32[1,64]{1,0:T(1,128)}) custom-call(bf16[16,144,128]{2,1,0:T(8,128)(2,1)S(1)} %all-to-all-done.4.rx_ref, f32[1,2]{1,0:T(1,128)S(1)} %bitcast.23, bf16[2048,2048]{1,0:T(8,128)(2,1)S(1)} %copy-done.1, s32[16,128]{1,0:T(8,128)S(1)} %get-tuple-element.25.zr_ref, ...), custom_call_target="tpu_custom_call" | custom-call | flops 1610612736 | bytes 11411728 | tf_op jit(solution)/shard_map/pallas_call | solution.py:565
  120.5 21.4 %all_to_all.35.rx_ref = bf16[16,144,128]{2,1,0:T(8,128)(2,1)S(1)} all-to-all(bf16[16,144,128]{2,1,0:T(8,128)(2,1)S(1)} %get-tuple-element.36), channel_id=1, replica_groups=mesh['groups'=2,'gx'=16] {'gx'}, dimensions={0} | all-to-all | bytes 1179648 | tf_op jit(solution)/shard_map/all_to_all | solution.py:615
  142.1 13.9 %all_to_all.36.rx_ref = bf16[16,80,128]{2,1,0:T(8,128)(2,1)S(1)} all-to-all(bf16[16,80,128]{2,1,0:T(8,128)(2,1)S(1)} %shard_map.209), channel_id=1, replica_groups=mesh['groups'=2,'gx'=16] {'gx'}, dimensions={0} | all-to-all | bytes 655360 | tf_op jit(solution)/shard_map/all_to_all | solution.py:615
  156.0 2.0 %shard_map.210 = (f32[64,64,64]{2,1,0:T(8,128)}, f32[64,64]{1,0:T(8,128)}) custom-call(bf16[16,80,128]{2,1,0:T(8,128)(2,1)S(1)} %all_to_all.36.rx_ref), custom_call_target="tpu_custom_call" | custom-call | flops 8388608 | bytes 1392640 | tf_op jit(solution)/shard_map/pallas_call | solution.py:565
  (47 shorter events, 3.5 us)
Async XLA Ops:
  0.6 74.2 %copy-start.12 = (s32[16,1,128]{2,1,0:T(1,128)S(1)}, s32[16,1,128]{2,1,0:T(1,128)}, u32[]{:S(2)}) copy-start(s32[16,1,128]{2,1,0:T(1,128)} %param.19) | copy-start | bytes 24580
  0.6 59.7 %copy-start.22 = (f32[64]{0:T(128)S(1)}, f32[64]{0:T(128)}, u32[]{:S(2)}) copy-start(f32[64]{0:T(128)} %param.27) | copy-start | bytes 772
  0.7 1.2 copy-start.4
  1.9 0.8 copy-start.6
  2.7 0.7 copy-start.8
  3.4 0.7 copy-start.9
  4.1 0.7 copy-start.13
  4.8 0.7 copy-start.16
  5.5 49.1 %copy-start.5 = (bf16[64,256]{1,0:T(8,128)(2,1)S(1)}, bf16[64,256]{1,0:T(8,128)(2,1)}, u32[]{:S(2)}) copy-start(bf16[64,256]{1,0:T(8,128)(2,1)} %constant.14.clone.table_ref) | copy-start | bytes 98308
  5.5 49.1 %copy-start.7 = (bf16[256,64]{1,0:T(8,128)(2,1)S(1)}, bf16[256,64]{1,0:T(8,128)(2,1)}, u32[]{:S(2)}) copy-start(bf16[256,64]{1,0:T(8,128)(2,1)} %constant.13.clone.back_ref) | copy-start | bytes 98308
  5.5 69.3 %copy-start.18 = (bf16[64,64]{1,0:T(8,128)(2,1)S(1)}, bf16[64,64]{1,0:T(8,128)(2,1)}, u32[]{:S(2)}) copy-start(bf16[64,64]{1,0:T(8,128)(2,1)} %skip_ref.1) | copy-start | bytes 24580
  7.1 21.9 %all-to-all-start = ((bf16[16,128,128]{2,1,0:T(8,128)(2,1)}), bf16[16,128,128]{2,1,0:T(8,128)(2,1)S(1)}, u32[]{:S(2)}, u32[]{:S(2)}) async-start(bf16[16,128,128]{2,1,0:T(8,128)(2,1)} %get-tuple-element.23), calls=%async_computation | async-start | bytes 1048576 | tf_op jit(solution)/shard_map/all_to_all | solution.py:615
  14.5 0.7 copy-start.11
  15.2 0.8 copy-start.21
  19.0 3.3 %copy-start.2 = (bf16[2048,2048]{1,0:T(8,128)(2,1)}, bf16[2048,2048]{1,0:T(8,128)(2,1)S(1)}, u32[]{:S(2)}) copy-start(bf16[2048,2048]{1,0:T(8,128)(2,1)S(1)} %get-tuple-element.24.same_ref) | copy-start | bytes 25165828
  29.0 3.4 %copy-start.3 = (bf16[2048,2048]{1,0:T(8,128)(2,1)S(1)}, bf16[2048,2048]{1,0:T(8,128)(2,1)}, u32[]{:S(2)}) copy-start(bf16[2048,2048]{1,0:T(8,128)(2,1)} %copy-done.2) | copy-start | bytes 25165828
  32.4 48.7 %copy-start.23 = (f32[64]{0:T(128)S(1)}, f32[64]{0:T(128)}, u32[]{:S(2)}) copy-start(f32[64]{0:T(128)} %param.29) | copy-start | bytes 772
  32.4 48.8 %copy-start.24 = (f32[64]{0:T(128)S(1)}, f32[64]{0:T(128)}, u32[]{:S(2)}) copy-start(f32[64]{0:T(128)} %param.30) | copy-start | bytes 772
  32.4 58.8 %copy-start.10 = (s32[1,16,128]{2,1,0:T(8,128)S(1)}, s32[1,16,128]{2,1,0:T(8,128)}, u32[]{:S(2)}) copy-start(s32[1,16,128]{2,1,0:T(8,128)} %param.18) | copy-start | bytes 24580
  32.4 58.8 %copy-start.14 = (f32[512]{0:T(512)S(1)}, f32[512]{0:T(512)}, u32[]{:S(2)}) copy-start(f32[512]{0:T(512)} %param.22) | copy-start | bytes 6148
  32.4 58.8 %copy-start.19 = (bf16[64,64]{1,0:T(8,128)(2,1)S(1)}, bf16[64,64]{1,0:T(8,128)(2,1)}, u32[]{:S(2)}) copy-start(bf16[64,64]{1,0:T(8,128)(2,1)} %head_ref.1) | copy-start | bytes 24580
  32.4 58.8 %copy-start.20 = (f32[2,512]{1,0:T(2,128)S(1)}, f32[2,512]{1,0:T(2,128)}, u32[]{:S(2)}) copy-start(f32[2,512]{1,0:T(2,128)} %normal_ref.1) | copy-start | bytes 12292
  36.0 18.6 %all-to-all-start.1 = ((bf16[16,128,128]{2,1,0:T(8,128)(2,1)}), bf16[16,128,128]{2,1,0:T(8,128)(2,1)S(1)}, u32[]{:S(2)}, u32[]{:S(2)}) async-start(bf16[16,128,128]{2,1,0:T(8,128)(2,1)} %get-tuple-element.27), calls=%async_computation.1 | async-start | bytes 1048576 | tf_op jit(solution)/shard_map/all_to_all | solution.py:615
  40.1 8.7 %collective-permute-start = (bf16[16,64,128]{2,1,0:T(8,128)(2,1)S(1)}, bf16[16,64,128]{2,1,0:T(8,128)(2,1)S(1)}, u32[]{:S(2)}, u32[]{:S(2)}) collective-permute-start(bf16[16,64,128]{2,1,0:T(8,128)(2,1)S(1)} %slice.4), channel_id=1, source_target_pairs={{0,16},{16,0},{1,17},{17,1},{2,18},{18,2},{3,19},{19,3},{4,20},{20... | collective-permute-start | bytes 786440 | tf_op jit(solution)/shard_map/ppermute | solution.py:647
  56.2 18.6 %all-to-all-start.2 = ((bf16[16,128,128]{2,1,0:T(8,128)(2,1)}), bf16[16,128,128]{2,1,0:T(8,128)(2,1)S(1)}, u32[]{:S(2)}, u32[]{:S(2)}) async-start(bf16[16,128,128]{2,1,0:T(8,128)(2,1)} %get-tuple-element.28), calls=%async_computation.2 | async-start | bytes 1048576 | tf_op jit(solution)/shard_map/all_to_all | solution.py:615
  60.3 53.3 %copy-start.17 = (f32[2]{0:T(128)S(1)}, f32[2]{0:T(128)}, u32[]{:S(2)}) copy-start(f32[2]{0:T(128)} %param.24) | copy-start | bytes 28
  77.0 14.2 %all-to-all-start.3 = ((bf16[16,64,128]{2,1,0:T(8,128)(2,1)}), bf16[16,64,128]{2,1,0:T(8,128)(2,1)S(1)}, u32[]{:S(2)}, u32[]{:S(2)}) async-start(bf16[16,64,128]{2,1,0:T(8,128)(2,1)} %get-tuple-element.30), calls=%async_computation.3 | async-start | bytes 524288 | tf_op jit(solution)/shard_map/all_to_all | solution.py:615
  94.6 19.1 %all-to-all-start.4 = ((bf16[16,144,128]{2,1,0:T(8,128)(2,1)}), bf16[16,144,128]{2,1,0:T(8,128)(2,1)S(1)}, u32[]{:S(2)}, u32[]{:S(2)}) async-start(bf16[16,144,128]{2,1,0:T(8,128)(2,1)} %get-tuple-element.33), calls=%async_computation.4 | async-start | bytes 1179648 | tf_op jit(solution)/shard_map/all_to_all | solution.py:615
  98.5 0.7 copy-start.15
  100.9 3.3 %copy-start = (bf16[2048,2048]{1,0:T(8,128)(2,1)}, bf16[2048,2048]{1,0:T(8,128)(2,1)S(1)}, u32[]{:S(2)}) copy-start(bf16[2048,2048]{1,0:T(8,128)(2,1)S(1)} %shard_map.206.same_ref) | copy-start | bytes 25165828
  113.7 3.4 %copy-start.1 = (bf16[2048,2048]{1,0:T(8,128)(2,1)S(1)}, bf16[2048,2048]{1,0:T(8,128)(2,1)}, u32[]{:S(2)}) copy-start(bf16[2048,2048]{1,0:T(8,128)(2,1)} %copy-done) | copy-start | bytes 25165828

commit v3 on v2

--- a/solution.py
+++ b/solution.py
@@ -251,7 +251,7 @@
         )
 
 
-def place_kernel(depth, cell_ref, by_ref, same_ref, lp_ref, zr_ref, col_ref):
+def place_kernel(depth, cell_ref, by_ref, same_hbm, lp_ref, zr_ref, same_ref, col_ref, sems):
     devices = cell_ref.shape[0]
     zbits = depth.bit_length() - 1
     rows = by_ref.shape[0]
@@ -281,23 +281,27 @@
         zr_ref[block : block + 1, :] = jnp.where(
             seen > 0.0, -1, jnp.bitwise_and(cells, depth - 1)
         )
-    equal_cells(cell_ref, col_ref, same_ref)
-
-
-def equal_cells(cell_ref, col_ref, same_ref):
-    for block in range(cell_ref.shape[0]):
-        row = cell_ref[block : block + 1, :].astype(F32)
-        same_ref[:, block * LANES : (block + 1) * LANES] = jnp.where(
-            col_ref[...] == row, 1.0, 0.0
-        ).astype(BF16)
-
-
-def same_kernel(cell_ref, after_ref, same_ref, col_ref):
-    for block in range(cell_ref.shape[0]):
-        row = cell_ref[block : block + 1, :].astype(F32)
-        cut = slice(block * LANES, (block + 1) * LANES)
-        col_ref[cut, :] = jnp.broadcast_to(row, (LANES, LANES)).T
-    equal_cells(cell_ref, col_ref, same_ref)
+    copies = []
+    for pair in range(devices // 2):
+        for half in range(2):
+            row = cell_ref[2 * pair + half : 2 * pair + half + 1, :].astype(F32)
+            same_ref[pair, :, half * LANES : (half + 1) * LANES] = jnp.where(
+                col_ref[...] == row, 1.0, 0.0
+            ).astype(BF16)
+        copies.append(pltpu.make_async_copy(same_ref.at[pair], same_hbm.at[pair], sems.at[pair]))
+        copies[-1].start()
+    for copy in copies:
+        copy.wait()
+
+
+def fetch_blocks(source, place, sems):
+    copies = [
+        pltpu.make_async_copy(source.at[block], place.at[block], sems.at[block])
+        for block in range(source.shape[0])
+    ]
+    for copy in copies:
+        copy.start()
+    return copies
 
 
 def spread_depth(values, zpos, rp_ref, pair):
@@ -321,25 +325,27 @@
                 ]
 
 
-def cell_kernel(rx_ref, same_ref, zr_ref, lp_ref, msg_ref, lat_ref, xs_ref, rp_ref):
+def cell_kernel(same_hbm, rx_ref, zr_ref, lp_ref, msg_ref, lat_ref, same_ref, sems, xs_ref, rp_ref):
     devices = rx_ref.shape[0]
+    copies = fetch_blocks(same_hbm, same_ref, sems)
     for block in range(devices):
         xs_ref[:, block * LANES : (block + 1) * LANES] = rx_ref[block, 0:WIDTH, :]
     for pair in range(devices // 2):
         cut = slice(pair * 2 * LANES, (pair + 1) * 2 * LANES)
-        latent = mm(xs_ref[...], same_ref[:, cut])
+        copies[pair].wait()
+        latent = mm(xs_ref[...], same_ref[pair])
         lat_ref[:, cut] = latent.astype(BF16)
         spread_depth(latent, two_rows(zr_ref, pair), rp_ref, pair)
     slab_rows(lp_ref, rp_ref, msg_ref)
 
 
-def to_modes(rx_ref, table_ref, sp_ref):
-    levels = sp_ref.shape[0] // table_ref.shape[0]
-    step = table_ref.shape[1] // rx_ref.shape[0]
+def to_modes(rx_ref, table, sp_ref):
+    levels = sp_ref.shape[0] // table.shape[0]
+    step = table.shape[1] // rx_ref.shape[0]
     for level in range(levels):
-        block = rx_ref[:, level * step : (level + 1) * step, :].reshape(table_ref.shape[1], LANES)
-        coeffs = mm(table_ref[...], block).astype(BF16).astype(F32)
-        sp_ref[pl.ds(level, table_ref.shape[0], stride=levels), :] = coeffs
+        block = rx_ref[:, level * step : (level + 1) * step, :].reshape(table.shape[1], LANES)
+        coeffs = mm(table, block).astype(BF16).astype(F32)
+        sp_ref[pl.ds(level, table.shape[0], stride=levels), :] = coeffs
 
 
 def swap_halves(values):
@@ -352,7 +358,7 @@
     modes = table_ref.shape[0]
     levels = sp_ref.shape[0] // modes
     step = back_ref.shape[0] // devices
-    to_modes(rx_ref, table_ref, sp_ref)
+    to_modes(rx_ref, table_ref[...], sp_ref)
     for dest in range(devices):
         spec_ref[dest] = sp_ref[dest * own_rows : (dest + 1) * own_rows, :].astype(BF16)
     left = lax.broadcasted_iota(jnp.int32, (levels, LANES), 1) < WIDTH
@@ -473,9 +479,10 @@
     return upper, lower
 
 
-def back_kernel(scale, rx_ref, target_ref, same_ref, zr_ref, lp_ref, lat_ref, slope_ref, msg_ref, force_ref, outg_ref, xs_ref, pg_ref, rp_ref):
+def back_kernel(scale, same_hbm, rx_ref, target_ref, zr_ref, lp_ref, lat_ref, slope_ref, msg_ref, force_ref, outg_ref, same_ref, sems, xs_ref, pg_ref, rp_ref):
     devices = rx_ref.shape[0]
-    main = lp_ref.shape[0] // devices * (rp_ref.shape[0] // LANES)
+    main = msg_ref.shape[1] - 16
+    copies = fetch_blocks(same_hbm, same_ref, sems)
     extra = slice(2 * WIDTH, 2 * WIDTH + 16)
     total = rx_ref[0, extra, :].astype(F32)
     for block in range(1, devices):
@@ -498,29 +505,27 @@
         xs_ref[:, block * LANES : (block + 1) * LANES] = (weight * grad).astype(BF16)
     for pair in range(devices // 2):
         cut = slice(pair * 2 * LANES, (pair + 1) * 2 * LANES)
-        grad = mm(xs_ref[...], same_ref[:, cut]) * slope_ref[:, cut]
+        copies[pair].wait()
+        grad = mm(xs_ref[...], same_ref[pair]) * slope_ref[:, cut]
         zpos = two_rows(zr_ref, pair)
         pg_ref[:, cut] = jnp.where(zpos >= 0, grad, 0.0).astype(BF16)
         spread_depth(grad, zpos, rp_ref, pair)
     slab_rows(lp_ref, rp_ref, msg_ref)
     upper, lower = fold_rows(mm_nt(lat_ref[...], pg_ref[...]))
-    blocks = upper.shape[0] // 8
-    for dest in range(devices):
-        if dest < blocks:
-            cut = slice(8 * dest, 8 * dest + 8)
-            rows = jnp.concatenate([upper[cut], lower[cut]], axis=0)
-        else:
-            rows = jnp.zeros((16, LANES), F32)
+    for dest in range(msg_ref.shape[0]):
+        cut = slice(8 * dest, 8 * dest + 8)
+        rows = jnp.concatenate([upper[cut], lower[cut]], axis=0)
         msg_ref[dest, main : main + 16, :] = rows.astype(BF16)
 
 
-def spec_kernel(rx_ref, table_ref, spec_ref, msg_ref, sp_ref):
-    devices = rx_ref.shape[0]
-    own_rows = spec_ref.shape[1]
+def spec_kernel(half_ref, rx_ref, table_ref, spec_ref, msg_ref, sp_ref):
+    peers = rx_ref.shape[0]
+    devices, own_rows = spec_ref.shape[0], spec_ref.shape[1]
+    part_rows = sp_ref.shape[0] // devices
     main = rx_ref.shape[1] - 16
-    to_modes(rx_ref, table_ref, sp_ref)
+    to_modes(rx_ref, table_ref[half_ref[0]], sp_ref)
     total = rx_ref[0, main : main + 16, :].astype(F32)
-    for source in range(1, devices):
+    for source in range(1, peers):
         total += rx_ref[source, main : main + 16, :].astype(F32)
     upper, lower = total[0:8], total[8:16]
     left = lax.broadcasted_iota(jnp.int32, (8, LANES), 1) < WIDTH
@@ -530,43 +535,60 @@
     rows = jnp.concatenate([upper, third.astype(F32)], axis=0).astype(BF16)
     for dest in range(devices):
         msg_ref[dest, 0:own_rows, :] = spec_ref[dest]
-        msg_ref[dest, own_rows : 2 * own_rows, :] = sp_ref[
-            dest * own_rows : (dest + 1) * own_rows, :
+        msg_ref[dest, own_rows : own_rows + part_rows, :] = sp_ref[
+            dest * part_rows : (dest + 1) * part_rows, :
         ].astype(BF16)
-        msg_ref[dest, 2 * own_rows : 2 * own_rows + 16, :] = rows
-
-
-def final_kernel(rx_ref, spec_ref, skip_ref):
+        msg_ref[dest, own_rows + part_rows : own_rows + part_rows + 16, :] = rows
+
+
+def both_halves(values):
+    return jnp.concatenate([values, swap_halves(values)], axis=0)[:, 0:WIDTH]
+
+
+def final_kernel(peers, rx_ref, spec_ref, skip_ref):
     devices = rx_ref.shape[0]
-    own_rows = (rx_ref.shape[1] - 16) // 2
+    low = MODES // devices
+    high = MODES // peers
+    owned = spec_ref.shape[0] // MODES
+    part_rows = owned * high * 8
+    own_rows = rx_ref.shape[1] - 16 - part_rows
     for source in range(devices):
-        for which in range(own_rows // 16):
-            at = which * 16
-            coeffs = rx_ref[source, at : at + 16, :].astype(F32)
-            grads = rx_ref[source, own_rows + at : own_rows + at + 16, :].astype(F32)
-            for low in range(2):
-                cut = slice(8 * low, 8 * low + 8)
-                left, right = coeffs[cut], grads[cut]
-                left = jnp.concatenate([left, swap_halves(left)], axis=0)[:, 0:WIDTH]
-                right = jnp.concatenate([right, swap_halves(right)], axis=0)[:, 0:WIDTH]
-                spec_ref[which * MODES + 2 * source + low] = mm_tn(
+        for which in range(owned):
+            at = which * 8 * low
+            coeffs = rx_ref[source, at : at + 8 * low, :].astype(F32)
+            peer, inner = divmod(low * source, high)
+            at = own_rows + (which * high + inner) * 8
+            grads = [
+                rx_ref[peer + shift, at : at + 8 * low, :].astype(F32)
+                for shift in range(0, devices, peers)
+            ]
+            for index in range(low):
+                cut = slice(8 * index, 8 * index + 8)
+                left = both_halves(coeffs[cut])
+                left = jnp.concatenate([left] * len(grads), axis=0)
+                right = jnp.concatenate([both_halves(part[cut]) for part in grads], axis=0)
+                spec_ref[which * MODES + low * source + index] = mm_tn(
                     left.astype(BF16), right.astype(BF16)
                 )
-    for source in range(WIDTH // 8):
-        rows = rx_ref[source, 2 * own_rows : 2 * own_rows + 16, :].astype(F32)
+    at = own_rows + part_rows
+    for peer in range(peers):
+        rows = rx_ref[peer, at : at + 16, :].astype(F32)
+        for shift in range(peers, devices, peers):
+            rows += rx_ref[peer + shift, at : at + 16, :].astype(F32)
         value = (rows[0:8] + swap_halves(rows[0:8]) + rows[8:16])[:, 0:WIDTH]
-        skip_ref[8 * source : 8 * source + 8, :] = value
-
-
-def run(kernel, outs, ins, flops, scratch=(), smem=0, hbm=False, grant=16):
+        skip_ref[8 * peer : 8 * peer + 8, :] = value
+
+
+def run(kernel, outs, ins, flops, scratch=(), smem=0, hbm=0, hbm_outs=0, grant=16):
     vmem = pl.BlockSpec(memory_space=pltpu.VMEM)
-    rest = pl.BlockSpec(memory_space=pltpu.HBM) if hbm else vmem
+    far = pl.BlockSpec(memory_space=pltpu.HBM)
+    scalar = pl.BlockSpec(memory_space=pltpu.SMEM)
     moved = sum(math.prod(a.shape) * a.dtype.itemsize for a in list(ins) + list(outs))
     return pl.pallas_call(
         kernel,
         out_shape=tuple(outs),
-        in_specs=[pl.BlockSpec(memory_space=pltpu.SMEM)] * smem + [rest] * (len(ins) - smem),
-        out_specs=tuple([vmem] * len(outs)),
+        in_specs=[scalar] * smem + [far] * hbm + [vmem] * (len(ins) - smem - hbm),
+        out_specs=tuple([far] * hbm_outs + [vmem] * (len(outs) - hbm_outs)),
         scratch_shapes=list(scratch),
         compiler_params=pltpu.CompilerParams(vmem_limit_bytes=grant * 1024 * 1024),
         cost_estimate=pl.CostEstimate(flops=flops, bytes_accessed=moved, transcendentals=0),
@@ -610,6 +632,17 @@
     table = table.reshape(MODES * low, rows)
     back = jnp.asarray(np.ascontiguousarray(table.T))
     table = jnp.asarray(table)
+    peers = 8
+    halves = n // peers
+    high = MODES // peers
+    part_table = np.zeros((halves, MODES, high, peers, high, slab), ml_dtypes.bfloat16)
+    for index in range(high):
+        part_table[:, :, index, :, index, :] = np.moveaxis(
+            bx.reshape(MODES, halves, peers, slab), 1, 0
+        )
+    part_table = jnp.asarray(part_table.reshape(halves, MODES * high, rows))
+    near = [[half * peers + peer for peer in range(peers)] for half in range(halves)]
+    half = (lax.axis_index("gx") // peers).astype(jnp.int32).reshape(1)
 
     def exchange(message):
         return lax.all_to_all(message, "gx", split_axis=0, concat_axis=0, tiled=True)
@@ -633,16 +666,24 @@
             pltpu.SemaphoreType.DMA((6,)),
         ],
         smem=1,
-        hbm=True,
+        hbm=6,
+        grant=60,
     )
     rx = exchange(msg)
-    columns_scratch = pltpu.VMEM((slots, LANES), F32)
+    same_shape = (n // 2, slots, 2 * LANES)
+    same_scratch = [pltpu.VMEM(same_shape, BF16), pltpu.SemaphoreType.DMA((n // 2,))]
     same, lp, zr = run(
         functools.partial(place_kernel, depth),
-        [shape((slots, slots), BF16), shape((rows, slots), BF16), shape((n, LANES), jnp.int32)],
+        [shape(same_shape, BF16), shape((rows, slots), BF16), shape((n, LANES), jnp.int32)],
         [cells, by_rows],
         2 * rows * LANES * slots,
-        scratch=[columns_scratch],
+        scratch=[
+            pltpu.VMEM(same_shape, BF16),
+            pltpu.VMEM((slots, LANES), F32),
+            pltpu.SemaphoreType.DMA((n // 2,)),
+        ],
+        hbm_outs=1,
+        grant=24,
     )
     other = lax.ppermute(rx[:, WIDTH : 2 * WIDTH, :], "groups", [(0, 1), (1, 0)])
     pair_rows = pltpu.VMEM((WIDTH, slots), BF16)
@@ -651,9 +692,11 @@
     msg, lat = run(
         cell_kernel,
         [shape((n, main, LANES), BF16), shape((WIDTH, slots), BF16)],
-        [rx, same, zr, lp],
+        [same, rx, zr, lp],
         big,
-        scratch=[pair_rows, deep_rows],
+        scratch=same_scratch + [pair_rows, deep_rows],
+        hbm=1,
+        grant=56,
     )
     columns = exchange(msg)
     msg, spec = run(
@@ -683,32 +726,35 @@
         scratch=[pltpu.VMEM((3 * WIDTH, slots), BF16), pltpu.VMEM((points, slots), BF16)],
     )
     grads = exchange(msg)
-    (same,) = run(
-        same_kernel,
-        [shape((slots, slots), BF16)],
-        [cells, pressure],
-        2 * slots * slots,
-        scratch=[columns_scratch],
-    )
     scale = 1.0 / math.sqrt(points * n)
     msg, forces, out_grad = run(
         functools.partial(back_kernel, scale),
-        [shape((n, main + 16, LANES), BF16), shape((1, 2), F32), shape((1, WIDTH), F32)],
-        [grads, targets.reshape(1, 2), same, zr, lp, lat, slope],
+        [
+            shape((peers, halves * main + 16, LANES), BF16),
+            shape((1, 2), F32),
+            shape((1, WIDTH), F32),
+        ],
+        [same, grads, targets.reshape(1, 2), zr, lp, lat, slope],
         big,
-        scratch=[pair_rows, pair_rows, deep_rows],
-    )
-    grad_columns = exchange(msg)
+        scratch=same_scratch + [pair_rows, pair_rows, deep_rows],
+        hbm=1,
+        grant=56,
+    )
+    grad_columns = lax.all_to_all(
+        msg, "gx", split_axis=0, concat_axis=0, tiled=True, axis_index_groups=near
+    )
+    part_rows = MODES * high * levels // n
     (msg,) = run(
         spec_kernel,
-        [shape((n, 2 * own_rows + 16, LANES), BF16)],
-        [grad_columns, table, spec],
-        2 * MODES * low * rows * depth * WIDTH,
-        scratch=[pltpu.VMEM((MODES * low * levels, LANES), F32)],
+        [shape((n, own_rows + part_rows + 16, LANES), BF16)],
+        [half, grad_columns, part_table, spec],
+        2 * MODES * high * rows * depth * WIDTH,
+        scratch=[pltpu.VMEM((MODES * high * levels, LANES), F32)],
+        smem=1,
     )
     finals = exchange(msg)
     spec_grad, skip_grad = run(
-        final_kernel,
+        functools.partial(final_kernel, peers),
         [shape((spec_weight.shape[0], WIDTH, WIDTH), F32), shape((WIDTH, WIDTH), F32)],
         [finals],
         2 * NMODE * WIDTH * WIDTH * depth // n,

time: 159 us -> 157 us (0.987)
  blocking collectives: 35.3 us -> 17.9 us
  waiting for transfers between devices: 53.3 us -> 64.1 us
  Pallas kernels: 23 us -> 32.8 us
  local copies, waits for them, and re-layouts: 20.7 us -> 12.2 us
  starting transfers between devices: 25 us -> 28.5 us
    all_to_all x2 -> x1, blocking collectives: 35.3 us -> 17.9 us  [exchange(): lax.all_to_all(message, 'gx', split_axis=0, concat_axis=0, tiled=True)]
    pallas_call x11 -> x10, Pallas kernels: 23 us -> 32.8 us  [run(): pl.pallas_call(kernel, out_shape=tuple(outs), in_specs=[scalar] * smem +...]
    unnamed x50 -> x48, local copies, waits for them, and re-layouts: 20.4 us -> 10.9 us
    all_to_all x0 -> x1, waiting for transfers between devices: none -> 9.1 us  [slab_step(): lax.all_to_all(msg, 'gx', split_axis=0, concat_axis=0, tiled=True, axis_i...]
    all_to_all x0 -> x1, starting transfers between devices: none -> 3.55 us  [slab_step(): lax.all_to_all(msg, 'gx', split_axis=0, concat_axis=0, tiled=True, axis_i...]
    all_to_all x5, waiting for transfers between devices: 46.1 us -> 47.8 us  [exchange(): lax.all_to_all(message, 'gx', split_axis=0, concat_axis=0, tiled=True)]
  transfers between devices with their start and end apart: 6 -> 7, of which waited for: 6 -> 7; matrix products, arithmetic and copies ran while one was open for 0% -> 1% of each run, Pallas kernels for 3% -> 2%
where the time goes in v3:
time: 157 us; the launch traced here: 156 us
  waiting for transfers between devices  64.1 us (41%)
  Pallas kernels  32.8 us (21%)
  starting transfers between devices  28.5 us (18%)
  blocking collectives  17.9 us (11%)
  local copies, waits for them, and re-layouts  12.2 us (8%)
    all_to_all x5, waiting for transfers between devices, exchange(): lax.all_to_all(message, 'gx', split_axis=0, concat_axis=0, tiled=True)  47.8 us
    pallas_call x10, Pallas kernels, run(): pl.pallas_call(kernel, out_shape=tuple(outs), in_specs=[scalar] * smem +...  32.8 us
    all_to_all x5, starting transfers between devices, exchange(): lax.all_to_all(message, 'gx', split_axis=0, concat_axis=0, tiled=True)  23.4 us
    all_to_all x1, blocking collectives, exchange(): lax.all_to_all(message, 'gx', split_axis=0, concat_axis=0, tiled=True)  17.9 us
    unnamed x48, local copies, waits for them, and re-layouts  10.9 us
    all_to_all x1, waiting for transfers between devices, slab_step(): lax.all_to_all(msg, 'gx', split_axis=0, concat_axis=0, tiled=True, axis_i...  9.1 us
    ppermute x1, waiting for transfers between devices, slab_step(): other = lax.ppermute(rx[:, WIDTH:2 * WIDTH, :], 'groups', [(0, 1), (1, 0)])  7.14 us
    all_to_all x1, starting transfers between devices, slab_step(): lax.all_to_all(msg, 'gx', split_axis=0, concat_axis=0, tiled=True, axis_i...  3.55 us
  transfers between devices with their start and end apart: 7, of which 7 were waited for; matrix products, arithmetic and copies ran while one was open for 1% of the time, Pallas kernels for 2%

profile of v3, /device:TPU:0, one launch (start us, length us, event | category | flops | bytes accessed | tf_op | source)
XLA Modules:
  0.0 156.4 jit_solution(6464403734655143352)
XLA Ops:
  0.7 2.5 %shard_map.210 = (bf16[16,128,128]{2,1,0:T(8,128)(2,1)}, f32[16,128]{1,0:T(8,128)}) custom-call(s32[1]{0:T(128)} %bitcast.group_ref, s32[1,16]{1,0:T(1,128)} %count_hbm.1, s32[16,128]{1,0:T(8,128)} %bitcast.14, f32[16,128]{1,0:T(8,128)} %bitcast.21, f32[1,512]{1,0:T(1,128)} %bitcast.16, bf16[64,512]{1,0:T(8,128)(2,1)} %bitcast.20, bf16[64,64,64]{2,1,0:T(8,128)(2,1)} %weight_hbm.1), custom_call_target="tpu_custom_call" | custom-call | flops 167772160 | bytes 1140804 | tf_op jit(solution)/shard_map/pallas_call | solution.py:587
  3.2 7.4 %all-to-all-start = ((bf16[16,128,128]{2,1,0:T(8,128)(2,1)}), bf16[16,128,128]{2,1,0:T(8,128)(2,1)S(1)}, u32[]{:S(2)}, u32[]{:S(2)}) async-start(bf16[16,128,128]{2,1,0:T(8,128)(2,1)} %get-tuple-element.24), calls=%async_computation | async-start | bytes 1048576 | tf_op jit(solution)/shard_map/all_to_all | solution.py:648
  11.3 0.8 copy-done.19
  12.1 3.7 %shard_map.209 = (bf16[8,2048,256]{2,1,0:T(8,128)(2,1)S(1)}, bf16[256,2048]{1,0:T(8,128)(2,1)S(1)}, s32[16,128]{1,0:T(8,128)S(1)}) custom-call(s32[16,128]{1,0:T(8,128)S(1)} %bitcast.18, bf16[256,128]{1,0:T(8,128)(2,1)S(1)} %copy-done.19), custom_call_target="tpu_custom_call" | custom-call | flops 134217728 | bytes 9519104 | tf_op jit(solution)/shard_map/pallas_call | solution.py:587
  15.8 3.3 %copy-done = bf16[8,2048,256]{2,1,0:T(8,128)(2,1)} copy-done((bf16[8,2048,256]{2,1,0:T(8,128)(2,1)}, bf16[8,2048,256]{2,1,0:T(8,128)(2,1)S(1)}, u32[]{:S(2)}) %copy-start) | copy-done | bytes 8388632
  19.1 1.0 copy-done.3
  20.7 4.4 %all-to-all-done.rx_ref.own_ref = bf16[16,128,128]{2,1,0:T(8,128)(2,1)S(1)} async-done(((bf16[16,128,128]{2,1,0:T(8,128)(2,1)}), bf16[16,128,128]{2,1,0:T(8,128)(2,1)S(1)}, u32[]{:S(2)}, u32[]{:S(2)}) %all-to-all-start) | async-done | bytes 524320 | tf_op jit(solution)/shard_map/all_to_all | solution.py:648
  25.0 0.8 copy-done.1
  25.9 8.2 %shard_map.211 = (bf16[16,128,128]{2,1,0:T(8,128)(2,1)}, bf16[64,2048]{1,0:T(8,128)(2,1)}) custom-call(bf16[8,2048,256]{2,1,0:T(8,128)(2,1)} %copy-done, bf16[16,128,128]{2,1,0:T(8,128)(2,1)} %copy-done.1, s32[16,128]{1,0:T(8,128)} %copy-done.10, bf16[256,2048]{1,0:T(8,128)(2,1)} %copy-done.3), custom_call_target="tpu_custom_call" | custom-call | flops 1610612736 | bytes 10756096 | tf_op jit(solution)/shard_map/pallas_call | solution.py:587
  34.1 4.1 %all-to-all-start.1 = ((bf16[16,128,128]{2,1,0:T(8,128)(2,1)}), bf16[16,128,128]{2,1,0:T(8,128)(2,1)S(1)}, u32[]{:S(2)}, u32[]{:S(2)}) async-start(bf16[16,128,128]{2,1,0:T(8,128)(2,1)} %get-tuple-element.27), calls=%async_computation.1 | async-start | bytes 1048576 | tf_op jit(solution)/shard_map/all_to_all | solution.py:648
  38.3 1.0 slice.4
  39.2 1.6 collective-permute-start
  40.8 7.1 %collective-permute-done.other_ref = bf16[16,64,128]{2,1,0:T(8,128)(2,1)S(1)} collective-permute-done((bf16[16,64,128]{2,1,0:T(8,128)(2,1)S(1)}, bf16[16,64,128]{2,1,0:T(8,128)(2,1)S(1)}, u32[]{:S(2)}, u32[]{:S(2)}) %collective-permute-start) | collective-permute-done | bytes 262176 | tf_op jit(solution)/shard_map/ppermute | solution.py:688
  47.9 4.8 %all-to-all-done.1.rx_ref = bf16[16,128,128]{2,1,0:T(8,128)(2,1)S(1)} async-done(((bf16[16,128,128]{2,1,0:T(8,128)(2,1)}), bf16[16,128,128]{2,1,0:T(8,128)(2,1)S(1)}, u32[]{:S(2)}, u32[]{:S(2)}) %all-to-all-start.1) | async-done | bytes 524320 | tf_op jit(solution)/shard_map/all_to_all | solution.py:648
  52.7 1.0 copy-done.2
  53.8 1.7 %shard_map.212 = (bf16[16,128,128]{2,1,0:T(8,128)(2,1)}, bf16[16,32,128]{2,1,0:T(8,128)(2,1)S(1)}) custom-call(s32[1]{0:T(128)} %bitcast.group_ref, bf16[16,128,128]{2,1,0:T(8,128)(2,1)S(1)} %all-to-all-done.1.rx_ref, bf16[16,128,128]{2,1,0:T(8,128)(2,1)S(1)} %copy-done.2, bf16[16,64,128]{2,1,0:T(8,128)(2,1)S(1)} %collective-permute-done.other_ref, ...), custom_call_target="tpu_custom_call" | custom-call | flops 67108864 | bytes 2031620 | tf_op jit(solution)/shard_map/pallas_call | solution.py:587
  55.5 4.1 %all-to-all-start.2 = ((bf16[16,128,128]{2,1,0:T(8,128)(2,1)}), bf16[16,128,128]{2,1,0:T(8,128)(2,1)S(1)}, u32[]{:S(2)}, u32[]{:S(2)}) async-start(bf16[16,128,128]{2,1,0:T(8,128)(2,1)} %get-tuple-element.28), calls=%async_computation.2 | async-start | bytes 1048576 | tf_op jit(solution)/shard_map/all_to_all | solution.py:648
  59.7 14.4 %all-to-all-done.2.rx_ref = bf16[16,128,128]{2,1,0:T(8,128)(2,1)S(1)} async-done(((bf16[16,128,128]{2,1,0:T(8,128)(2,1)}), bf16[16,128,128]{2,1,0:T(8,128)(2,1)S(1)}, u32[]{:S(2)}, u32[]{:S(2)}) %all-to-all-start.2) | async-done | bytes 524320 | tf_op jit(solution)/shard_map/all_to_all | solution.py:648
  74.1 0.9 copy-done.6
  75.0 2.2 %shard_map.213 = (bf16[16,64,128]{2,1,0:T(8,128)(2,1)}, f32[64,2048]{1,0:T(8,128)S(1)}) custom-call(bf16[16,128,128]{2,1,0:T(8,128)(2,1)S(1)} %all-to-all-done.2.rx_ref, bf16[256,2048]{1,0:T(8,128)(2,1)S(1)} %copy-done.4, bf16[64,2048]{1,0:T(8,128)(2,1)S(1)} %copy-done.6, s32[16,128]{1,0:T(8,128)S(1)} %bitcast.19, bf16[64,64]{1,0:T(8,128)(2,1)S(1)} %copy-done.13, ...), custom_call_target="tpu_custom_call" | custom-call | flops 1073741824 | bytes 2638080 | tf_op jit(solution)/shard_map/pallas_call | solution.py:587
  77.3 4.2 %all-to-all-start.3 = ((bf16[16,64,128]{2,1,0:T(8,128)(2,1)}), bf16[16,64,128]{2,1,0:T(8,128)(2,1)S(1)}, u32[]{:S(2)}, u32[]{:S(2)}) async-start(bf16[16,64,128]{2,1,0:T(8,128)(2,1)} %get-tuple-element.30), calls=%async_computation.3 | async-start | bytes 524288 | tf_op jit(solution)/shard_map/all_to_all | solution.py:648
  81.7 9.8 %all-to-all-done.3.rx_ref = bf16[16,64,128]{2,1,0:T(8,128)(2,1)S(1)} async-done(((bf16[16,64,128]{2,1,0:T(8,128)(2,1)}), bf16[16,64,128]{2,1,0:T(8,128)(2,1)S(1)}, u32[]{:S(2)}, u32[]{:S(2)}) %all-to-all-start.3) | async-done | bytes 262176 | tf_op jit(solution)/shard_map/all_to_all | solution.py:648
  91.6 3.4 %shard_map.214 = (f32[1,512]{1,0:T(1,128)}, bf16[16,144,128]{2,1,0:T(8,128)(2,1)}) custom-call(bf16[16,64,128]{2,1,0:T(8,128)(2,1)S(1)} %all-to-all-done.3.rx_ref, s32[16,128]{1,0:T(8,128)S(1)} %bitcast.15, f32[16,128]{1,0:T(8,128)S(1)} %copy-done.17, bf16[64,64]{1,0:T(8,128)(2,1)S(1)} %copy-done.14, f32[64,1]{1,0:T(8,128)S(1)} %copy.24.bias_ref, ...), custom_call_target="tpu_custom_call" | custom-call | flops 402653184 | bytes 885248 | tf_op jit(solution)/shard_map/pallas_call | solution.py:587
  95.0 3.6 %all-to-all-start.4 = ((bf16[16,144,128]{2,1,0:T(8,128)(2,1)}), bf16[16,144,128]{2,1,0:T(8,128)(2,1)S(1)}, u32[]{:S(2)}, u32[]{:S(2)}) async-start(bf16[16,144,128]{2,1,0:T(8,128)(2,1)} %get-tuple-element.33), calls=%async_computation.4 | async-start | bytes 1179648 | tf_op jit(solution)/shard_map/all_to_all | solution.py:648
  98.8 0.8 copy-done.5
  99.6 14.5 %all-to-all-done.4.rx_ref = bf16[16,144,128]{2,1,0:T(8,128)(2,1)S(1)} async-done(((bf16[16,144,128]{2,1,0:T(8,128)(2,1)}), bf16[16,144,128]{2,1,0:T(8,128)(2,1)S(1)}, u32[]{:S(2)}, u32[]{:S(2)}) %all-to-all-start.4) | async-done | bytes 589856 | tf_op jit(solution)/shard_map/all_to_all | solution.py:648
  114.1 0.8 copy-done.20
  114.9 8.5 %shard_map.216 = (bf16[8,272,128]{2,1,0:T(8,128)(2,1)}, f32[1,2]{1,0:T(1,128)}, f32[1,64]{1,0:T(1,128)}) custom-call(bf16[8,2048,256]{2,1,0:T(8,128)(2,1)} %copy-done, bf16[16,144,128]{2,1,0:T(8,128)(2,1)} %copy-done.20, f32[1,2]{1,0:T(1,128)} %bitcast.25, s32[16,128]{1,0:T(8,128)} %copy-done.10, bf16[256,2048]{1,0:T(8,128)(2,1)} %copy-done.3, ...), custom_call_target="tpu_custom_call" | custom-call | flops 1610612736 | bytes 11378960 | tf_op jit(solution)/shard_map/pallas_call | solution.py:587
  123.4 3.5 %all-to-all-start.5 = ((bf16[8,272,128]{2,1,0:T(8,128)(2,1)}), bf16[8,272,128]{2,1,0:T(8,128)(2,1)S(1)}, u32[]{:S(2)}, u32[]{:S(2)}) async-start(bf16[8,272,128]{2,1,0:T(8,128)(2,1)} %get-tuple-element.36), calls=%async_computation.5 | async-start | bytes 1114112 | tf_op jit(solution)/shard_map/all_to_all | solution.py:743
  127.0 9.1 %all-to-all-done.5.rx_ref = bf16[8,272,128]{2,1,0:T(8,128)(2,1)S(1)} async-done(((bf16[8,272,128]{2,1,0:T(8,128)(2,1)}), bf16[8,272,128]{2,1,0:T(8,128)(2,1)S(1)}, u32[]{:S(2)}, u32[]{:S(2)}) %all-to-all-start.5) | async-done | bytes 557088 | tf_op jit(solution)/shard_map/all_to_all | solution.py:743
  136.4 17.9 %all_to_all.35.rx_ref = bf16[16,112,128]{2,1,0:T(8,128)(2,1)S(1)} all-to-all(bf16[16,112,128]{2,1,0:T(8,128)(2,1)S(1)} %shard_map.217), channel_id=1, replica_groups=mesh['groups'=2,'gx'=16] {'gx'}, dimensions={0} | all-to-all | bytes 917504 | tf_op jit(solution)/shard_map/all_to_all | solution.py:648
  154.3 2.1 %shard_map.218 = (f32[64,64,64]{2,1,0:T(8,128)}, f32[64,64]{1,0:T(8,128)}) custom-call(bf16[16,112,128]{2,1,0:T(8,128)(2,1)S(1)} %all_to_all.35.rx_ref), custom_call_target="tpu_custom_call" | custom-call | flops 8388608 | bytes 1523712 | tf_op jit(solution)/shard_map/pallas_call | solution.py:587
  (45 shorter events, 2.2 us)
Async XLA Ops:
  0.6 52.1 %copy-start.8 = (bf16[256,64]{1,0:T(8,128)(2,1)S(1)}, bf16[256,64]{1,0:T(8,128)(2,1)}, u32[]{:S(2)}) copy-start(bf16[256,64]{1,0:T(8,128)(2,1)} %constant.34.clone.back_ref) | copy-start | bytes 98308
  0.6 52.1 %copy-start.9 = (bf16[64,256]{1,0:T(8,128)(2,1)S(1)}, bf16[64,256]{1,0:T(8,128)(2,1)}, u32[]{:S(2)}) copy-start(bf16[64,256]{1,0:T(8,128)(2,1)} %constant.35.clone.table_ref) | copy-start | bytes 98308
  0.7 73.4 %copy-start.16 = (s32[16,1,128]{2,1,0:T(1,128)S(1)}, s32[16,1,128]{2,1,0:T(1,128)}, u32[]{:S(2)}) copy-start(s32[16,1,128]{2,1,0:T(1,128)} %param.20) | copy-start | bytes 24580
  0.7 58.9 %copy-start.21 = (f32[64]{0:T(128)S(1)}, f32[64]{0:T(128)}, u32[]{:S(2)}) copy-start(f32[64]{0:T(128)} %param.28) | copy-start | bytes 772
  0.7 73.4 %copy-start.13 = (bf16[64,64]{1,0:T(8,128)(2,1)S(1)}, bf16[64,64]{1,0:T(8,128)(2,1)}, u32[]{:S(2)}) copy-start(bf16[64,64]{1,0:T(8,128)(2,1)} %skip_ref.1) | copy-start | bytes 24580
  3.2 21.9 %all-to-all-start = ((bf16[16,128,128]{2,1,0:T(8,128)(2,1)}), bf16[16,128,128]{2,1,0:T(8,128)(2,1)S(1)}, u32[]{:S(2)}, u32[]{:S(2)}) async-start(bf16[16,128,128]{2,1,0:T(8,128)(2,1)} %get-tuple-element.24), calls=%async_computation | async-start | bytes 1048576 | tf_op jit(solution)/shard_map/all_to_all | solution.py:648
  10.6 0.7 copy-start.15
  11.3 0.8 copy-start.19
  15.8 3.3 %copy-start = (bf16[8,2048,256]{2,1,0:T(8,128)(2,1)}, bf16[8,2048,256]{2,1,0:T(8,128)(2,1)S(1)}, u32[]{:S(2)}) copy-start(bf16[8,2048,256]{2,1,0:T(8,128)(2,1)S(1)} %get-tuple-element.23.same_hbm) | copy-start | bytes 25165828
  19.1 1.0 copy-start.3
  20.1 0.6 copy-start.10
  25.0 0.8 copy-start.1
  25.0 49.0 %copy-start.4 = (bf16[256,2048]{1,0:T(8,128)(2,1)S(1)}, bf16[256,2048]{1,0:T(8,128)(2,1)}, u32[]{:S(2)}) copy-start(bf16[256,2048]{1,0:T(8,128)(2,1)} %copy-done.3) | copy-start | bytes 3145732
  25.9 55.6 %copy-start.22 = (f32[64]{0:T(128)S(1)}, f32[64]{0:T(128)}, u32[]{:S(2)}) copy-start(f32[64]{0:T(128)} %param.30) | copy-start | bytes 772
  25.9 55.7 %copy-start.23 = (f32[64]{0:T(128)S(1)}, f32[64]{0:T(128)}, u32[]{:S(2)}) copy-start(f32[64]{0:T(128)} %param.31) | copy-start | bytes 772
  25.9 65.7 %copy-start.11 = (s32[1,16,128]{2,1,0:T(8,128)S(1)}, s32[1,16,128]{2,1,0:T(8,128)}, u32[]{:S(2)}) copy-start(s32[1,16,128]{2,1,0:T(8,128)} %param.19) | copy-start | bytes 24580
  25.9 65.7 %copy-start.12 = (f32[512]{0:T(512)S(1)}, f32[512]{0:T(512)}, u32[]{:S(2)}) copy-start(f32[512]{0:T(512)} %param.23) | copy-start | bytes 6148
  25.9 65.7 %copy-start.14 = (bf16[64,64]{1,0:T(8,128)(2,1)S(1)}, bf16[64,64]{1,0:T(8,128)(2,1)}, u32[]{:S(2)}) copy-start(bf16[64,64]{1,0:T(8,128)(2,1)} %head_ref.1) | copy-start | bytes 24580
  25.9 65.7 %copy-start.17 = (f32[16,128]{1,0:T(8,128)S(1)}, f32[16,128]{1,0:T(8,128)}, u32[]{:S(2)}) copy-start(f32[16,128]{1,0:T(8,128)} %get-tuple-element.31.pw_ref) | copy-start | bytes 24580
  25.9 65.7 %copy-start.18 = (f32[2,512]{1,0:T(2,128)S(1)}, f32[2,512]{1,0:T(2,128)}, u32[]{:S(2)}) copy-start(f32[2,512]{1,0:T(2,128)} %normal_ref.1) | copy-start | bytes 12292
  34.1 18.6 %all-to-all-start.1 = ((bf16[16,128,128]{2,1,0:T(8,128)(2,1)}), bf16[16,128,128]{2,1,0:T(8,128)(2,1)S(1)}, u32[]{:S(2)}, u32[]{:S(2)}) async-start(bf16[16,128,128]{2,1,0:T(8,128)(2,1)} %get-tuple-element.27), calls=%async_computation.1 | async-start | bytes 1048576 | tf_op jit(solution)/shard_map/all_to_all | solution.py:648
  39.2 8.7 %collective-permute-start = (bf16[16,64,128]{2,1,0:T(8,128)(2,1)S(1)}, bf16[16,64,128]{2,1,0:T(8,128)(2,1)S(1)}, u32[]{:S(2)}, u32[]{:S(2)}) collective-permute-start(bf16[16,64,128]{2,1,0:T(8,128)(2,1)S(1)} %slice.4), channel_id=1, source_target_pairs={{0,16},{16,0},{1,17},{17,1},{2,18},{18,2},{3,19},{19,3},{4,20},{20... | collective-permute-start | bytes 786440 | tf_op jit(solution)/shard_map/ppermute | solution.py:688
  52.7 1.0 copy-start.2
  55.5 18.6 %all-to-all-start.2 = ((bf16[16,128,128]{2,1,0:T(8,128)(2,1)}), bf16[16,128,128]{2,1,0:T(8,128)(2,1)S(1)}, u32[]{:S(2)}, u32[]{:S(2)}) async-start(bf16[16,128,128]{2,1,0:T(8,128)(2,1)} %get-tuple-element.28), calls=%async_computation.2 | async-start | bytes 1048576 | tf_op jit(solution)/shard_map/all_to_all | solution.py:648
  74.1 1.0 copy-start.6
  77.3 58.8 %copy-start.7 = (bf16[2,128,256]{2,1,0:T(8,128)(2,1)S(1)}, bf16[2,128,256]{2,1,0:T(8,128)(2,1)}, u32[]{:S(2)}) copy-start(bf16[2,128,256]{2,1,0:T(8,128)(2,1)} %constant.36.clone.table_ref) | copy-start | bytes 393220
  77.3 14.3 %all-to-all-start.3 = ((bf16[16,64,128]{2,1,0:T(8,128)(2,1)}), bf16[16,64,128]{2,1,0:T(8,128)(2,1)S(1)}, u32[]{:S(2)}, u32[]{:S(2)}) async-start(bf16[16,64,128]{2,1,0:T(8,128)(2,1)} %get-tuple-element.30), calls=%async_computation.3 | async-start | bytes 524288 | tf_op jit(solution)/shard_map/all_to_all | solution.py:648
  95.0 19.1 %all-to-all-start.4 = ((bf16[16,144,128]{2,1,0:T(8,128)(2,1)}), bf16[16,144,128]{2,1,0:T(8,128)(2,1)S(1)}, u32[]{:S(2)}, u32[]{:S(2)}) async-start(bf16[16,144,128]{2,1,0:T(8,128)(2,1)} %get-tuple-element.33), calls=%async_computation.4 | async-start | bytes 1179648 | tf_op jit(solution)/shard_map/all_to_all | solution.py:648
  98.8 0.8 copy-start.5
  114.1 0.8 copy-start.20
  123.4 12.7 %all-to-all-start.5 = ((bf16[8,272,128]{2,1,0:T(8,128)(2,1)}), bf16[8,272,128]{2,1,0:T(8,128)(2,1)S(1)}, u32[]{:S(2)}, u32[]{:S(2)}) async-start(bf16[8,272,128]{2,1,0:T(8,128)(2,1)} %get-tuple-element.36), calls=%async_computation.5 | async-start | bytes 1114112 | tf_op jit(solution)/shard_map/all_to_all | solution.py:743

commit v4 on v3

--- a/solution.py
+++ b/solution.py
@@ -251,57 +251,102 @@
         )
 
 
-def place_kernel(depth, cell_ref, by_ref, same_hbm, lp_ref, zr_ref, same_ref, col_ref, sems):
+def columns_of(row):
+    return jnp.broadcast_to(row, (LANES, LANES)).T
+
+
+def pick_rows(rank_ref, pick_ref):
+    rows = lax.broadcasted_iota(jnp.int32, (pick_ref.shape[0], LANES), 0)
+    for block in range(rank_ref.shape[0]):
+        pick_ref[:, block * LANES : (block + 1) * LANES] = jnp.where(
+            rows == rank_ref[block : block + 1, :], 1.0, 0.0
+        ).astype(BF16)
+
+
+def place_kernel(depth, cell_ref, by_ref, lp_ref, zr_ref, rank_ref, same_ref, col_ref, flag_ref, pick_ref, part_ref):
     devices = cell_ref.shape[0]
+    shared = same_ref.shape[0]
     zbits = depth.bit_length() - 1
     rows = by_ref.shape[0]
     slab = rows // MODES
     yrow = lax.broadcasted_iota(jnp.int32, (GY, LANES), 0)
     xrow = jnp.bitwise_and(lax.broadcasted_iota(jnp.int32, (rows, LANES), 0), slab - 1)
-    up = lax.broadcasted_iota(jnp.int32, (LANES, LANES), 0) < lax.broadcasted_iota(
-        jnp.int32, (LANES, LANES), 1
-    )
+    down = lax.broadcasted_iota(jnp.int32, (LANES, LANES), 0)
+    along = lax.broadcasted_iota(jnp.int32, (LANES, LANES), 1)
+    place = lax.broadcasted_iota(jnp.int32, (16, LANES), 0)
     for block in range(devices):
         cells = cell_ref[block : block + 1, :]
         cut = slice(block * LANES, (block + 1) * LANES)
-        col_ref[cut, :] = jnp.broadcast_to(cells.astype(F32), (LANES, LANES)).T
+        col_ref[cut, :] = columns_of(cells.astype(F32))
         ypos = jnp.bitwise_and(jnp.right_shift(cells, zbits), GY - 1)
         xpos = jnp.right_shift(cells, zbits + GY.bit_length() - 1)
         hot = jnp.where(yrow == ypos, 1.0, 0.0).astype(BF16)
         lp_ref[:, cut] = jnp.where(xrow == xpos, mm(by_ref[...], hot), 0.0).astype(BF16)
+        high = jnp.right_shift(cells, 7).astype(F32)
+        low = jnp.bitwise_and(cells, 127).astype(F32)
+        part_ref[:, cut] = jnp.where(place == 0, high, jnp.where(place == 1, low, 0.0)).astype(BF16)
     for block in range(devices):
         cells = cell_ref[block : block + 1, :]
         row = cells.astype(F32)
         cut = slice(block * LANES, (block + 1) * LANES)
-        same = jnp.where(jnp.logical_and(col_ref[cut, :] == row, up), 1.0, 0.0)
-        seen = jnp.max(same, axis=0, keepdims=True)
+        same = jnp.where(col_ref[cut, :] == row, 1.0, 0.0)
+        before = jnp.sum(jnp.where(down < along, same, 0.0), axis=0, keepdims=True)
+        count = jnp.sum(same, axis=0, keepdims=True)
         if block:
-            before = jnp.where(col_ref[0 : block * LANES, :] == row, 1.0, 0.0)
-            seen = jnp.maximum(seen, jnp.max(before, axis=0, keepdims=True))
+            early = jnp.where(col_ref[0 : block * LANES, :] == row, 1.0, 0.0)
+            early = jnp.sum(early, axis=0, keepdims=True)
+            before += early
+            count += early
+        if block < devices - 1:
+            late = jnp.where(col_ref[(block + 1) * LANES :, :] == row, 1.0, 0.0)
+            count += jnp.sum(late, axis=0, keepdims=True)
         zr_ref[block : block + 1, :] = jnp.where(
-            seen > 0.0, -1, jnp.bitwise_and(cells, depth - 1)
+            before > 0.0, -1, jnp.bitwise_and(cells, depth - 1)
         )
-    copies = []
-    for pair in range(devices // 2):
-        for half in range(2):
-            row = cell_ref[2 * pair + half : 2 * pair + half + 1, :].astype(F32)
-            same_ref[pair, :, half * LANES : (half + 1) * LANES] = jnp.where(
-                col_ref[...] == row, 1.0, 0.0
-            ).astype(BF16)
-        copies.append(pltpu.make_async_copy(same_ref.at[pair], same_hbm.at[pair], sems.at[pair]))
-        copies[-1].start()
-    for copy in copies:
-        copy.wait()
-
-
-def fetch_blocks(source, place, sems):
-    copies = [
-        pltpu.make_async_copy(source.at[block], place.at[block], sems.at[block])
-        for block in range(source.shape[0])
-    ]
-    for copy in copies:
-        copy.start()
-    return copies
+        flag_ref[block : block + 1, :] = jnp.where(count > 1.0, 1.0, 0.0)
+    flags = flag_ref[...]
+    marks = flags.astype(BF16)
+    inside = mm(marks, jnp.where(down <= along, 1.0, 0.0).astype(BF16))
+    above = jnp.where(down < along, 1.0, 0.0)[:, 0:devices][0:devices]
+    ahead = jnp.sum(mm_tn(above.astype(BF16), marks), axis=1, keepdims=True)
+    rank_ref[...] = jnp.where(flags > 0.0, (inside + ahead - flags).astype(jnp.int32), -1)
+    pick_rows(rank_ref, pick_ref)
+    found = mm_nt(part_ref[...], pick_ref[...])
+    found = found[0:1] * 128.0 + found[1:2]
+    for block in range(shared // LANES):
+        column = columns_of(found[:, block * LANES : (block + 1) * LANES])
+        same_ref[block * LANES : (block + 1) * LANES, :] = jnp.where(
+            jnp.concatenate([column] * (shared // LANES), axis=1) == found, 1.0, 0.0
+        ).astype(BF16)
+
+
+def sum_cells(xs_ref, cell_ref, rank_ref, same_ref, sums_ref, pick_ref, full_ref, col_ref):
+    devices = cell_ref.shape[0]
+    shared = same_ref.shape[0]
+    few = jnp.max(rank_ref[...]) < shared
+
+    @pl.when(few)
+    def _():
+        pick_rows(rank_ref, pick_ref)
+        picked = mm_nt(xs_ref[...], pick_ref[...]).astype(BF16)
+        parts = jnp.concatenate(three_parts(mm(picked, same_ref[...])), axis=0)
+        for pair in range(devices // 2):
+            span = slice(pair * 2 * LANES, (pair + 1) * 2 * LANES)
+            got = mm(parts, pick_ref[:, span])
+            got = got[0:WIDTH] + got[WIDTH : 2 * WIDTH] + got[2 * WIDTH : 3 * WIDTH]
+            alone = two_rows(rank_ref, pair) < 0
+            sums_ref[:, span] = jnp.where(alone, xs_ref[:, span].astype(F32), got)
+
+    @pl.when(jnp.logical_not(few))
+    def _():
+        for block in range(devices):
+            col_ref[block * LANES : (block + 1) * LANES, :] = columns_of(
+                cell_ref[block : block + 1, :].astype(F32)
+            )
+        for block in range(devices):
+            row = cell_ref[block : block + 1, :].astype(F32)
+            full_ref[...] = jnp.where(col_ref[...] == row, 1.0, 0.0).astype(BF16)
+            sums_ref[:, block * LANES : (block + 1) * LANES] = mm(xs_ref[...], full_ref[...])
 
 
 def spread_depth(values, zpos, rp_ref, pair):
@@ -325,15 +370,14 @@
                 ]
 
 
-def cell_kernel(same_hbm, rx_ref, zr_ref, lp_ref, msg_ref, lat_ref, same_ref, sems, xs_ref, rp_ref):
+def cell_kernel(rx_ref, cell_ref, rank_ref, same_ref, zr_ref, lp_ref, msg_ref, lat_ref, sums_ref, pick_ref, full_ref, col_ref, xs_ref, rp_ref):
     devices = rx_ref.shape[0]
-    copies = fetch_blocks(same_hbm, same_ref, sems)
     for block in range(devices):
         xs_ref[:, block * LANES : (block + 1) * LANES] = rx_ref[block, 0:WIDTH, :]
+    sum_cells(xs_ref, cell_ref, rank_ref, same_ref, sums_ref, pick_ref, full_ref, col_ref)
     for pair in range(devices // 2):
         cut = slice(pair * 2 * LANES, (pair + 1) * 2 * LANES)
-        copies[pair].wait()
-        latent = mm(xs_ref[...], same_ref[pair])
+        latent = sums_ref[:, cut]
         lat_ref[:, cut] = latent.astype(BF16)
         spread_depth(latent, two_rows(zr_ref, pair), rp_ref, pair)
     slab_rows(lp_ref, rp_ref, msg_ref)
@@ -367,7 +411,7 @@
         mine = jnp.full((WIDTH, LANES), group_ref[0], jnp.int32) == which
         weight = jnp.where(
             mine,
-            own_ref[source, WIDTH : 2 * WIDTH, :].astype(F32),
+            own_ref[source].astype(F32),
             other_ref[source].astype(F32),
         ).astype(BF16)
         at = order * 2 * levels
@@ -479,10 +523,9 @@
     return upper, lower
 
 
-def back_kernel(scale, same_hbm, rx_ref, target_ref, zr_ref, lp_ref, lat_ref, slope_ref, msg_ref, force_ref, outg_ref, same_ref, sems, xs_ref, pg_ref, rp_ref):
+def back_kernel(scale, rx_ref, target_ref, cell_ref, rank_ref, same_ref, zr_ref, lp_ref, lat_ref, slope_ref, msg_ref, force_ref, outg_ref, sums_ref, pick_ref, full_ref, col_ref, xs_ref, pg_ref, rp_ref):
     devices = rx_ref.shape[0]
     main = msg_ref.shape[1] - 16
-    copies = fetch_blocks(same_hbm, same_ref, sems)
     extra = slice(2 * WIDTH, 2 * WIDTH + 16)
     total = rx_ref[0, extra, :].astype(F32)
     for block in range(1, devices):
@@ -503,10 +546,10 @@
         along = twice * (drag * first + lift * second)
         grad = (along * grad).astype(BF16).astype(F32)
         xs_ref[:, block * LANES : (block + 1) * LANES] = (weight * grad).astype(BF16)
+    sum_cells(xs_ref, cell_ref, rank_ref, same_ref, sums_ref, pick_ref, full_ref, col_ref)
     for pair in range(devices // 2):
         cut = slice(pair * 2 * LANES, (pair + 1) * 2 * LANES)
-        copies[pair].wait()
-        grad = mm(xs_ref[...], same_ref[pair]) * slope_ref[:, cut]
+        grad = sums_ref[:, cut] * slope_ref[:, cut]
         zpos = two_rows(zr_ref, pair)
         pg_ref[:, cut] = jnp.where(zpos >= 0, grad, 0.0).astype(BF16)
         spread_depth(grad, zpos, rp_ref, pair)
@@ -545,15 +588,16 @@
     return jnp.concatenate([values, swap_halves(values)], axis=0)[:, 0:WIDTH]
 
 
-def final_kernel(peers, rx_ref, spec_ref, skip_ref):
+def final_kernel(peers, rx_ref, spec_hbm, skip_ref, spec_ref, sems):
     devices = rx_ref.shape[0]
     low = MODES // devices
     high = MODES // peers
     owned = spec_ref.shape[0] // MODES
     part_rows = owned * high * 8
     own_rows = rx_ref.shape[1] - 16 - part_rows
-    for source in range(devices):
-        for which in range(owned):
+    copies = []
+    for which in range(owned):
+        for source in range(devices):
             at = which * 8 * low
             coeffs = rx_ref[source, at : at + 8 * low, :].astype(F32)
             peer, inner = divmod(low * source, high)
@@ -570,6 +614,15 @@
                 spec_ref[which * MODES + low * source + index] = mm_tn(
                     left.astype(BF16), right.astype(BF16)
                 )
+            done = which * MODES + low * (source + 1)
+            if done % 16 == 0:
+                span = pl.ds(done - 16, 16)
+                copies.append(
+                    pltpu.make_async_copy(
+                        spec_ref.at[span], spec_hbm.at[span], sems.at[done // 16 - 1]
+                    )
+                )
+                copies[-1].start()
     at = own_rows + part_rows
     for peer in range(peers):
         rows = rx_ref[peer, at : at + 16, :].astype(F32)
@@ -577,6 +630,8 @@
             rows += rx_ref[peer + shift, at : at + 16, :].astype(F32)
         value = (rows[0:8] + swap_halves(rows[0:8]) + rows[8:16])[:, 0:WIDTH]
         skip_ref[8 * peer : 8 * peer + 8, :] = value
+    for copy in copies:
+        copy.wait()
 
 
 def run(kernel, outs, ins, flops, scratch=(), smem=0, hbm=0, hbm_outs=0, grant=16):
@@ -670,39 +725,48 @@
         grant=60,
     )
     rx = exchange(msg)
-    same_shape = (n // 2, slots, 2 * LANES)
-    same_scratch = [pltpu.VMEM(same_shape, BF16), pltpu.SemaphoreType.DMA((n // 2,))]
-    same, lp, zr = run(
+    shared = 512
+    lp, zr, rank, same = run(
         functools.partial(place_kernel, depth),
-        [shape(same_shape, BF16), shape((rows, slots), BF16), shape((n, LANES), jnp.int32)],
+        [
+            shape((rows, slots), BF16),
+            shape((n, LANES), jnp.int32),
+            shape((n, LANES), jnp.int32),
+            shape((shared, shared), BF16),
+        ],
         [cells, by_rows],
         2 * rows * LANES * slots,
         scratch=[
-            pltpu.VMEM(same_shape, BF16),
             pltpu.VMEM((slots, LANES), F32),
-            pltpu.SemaphoreType.DMA((n // 2,)),
+            pltpu.VMEM((n, LANES), F32),
+            pltpu.VMEM((shared, slots), BF16),
+            pltpu.VMEM((16, slots), BF16),
         ],
-        hbm_outs=1,
-        grant=24,
-    )
-    other = lax.ppermute(rx[:, WIDTH : 2 * WIDTH, :], "groups", [(0, 1), (1, 0)])
+    )
+    sum_scratch = [
+        pltpu.VMEM((WIDTH, slots), F32),
+        pltpu.VMEM((shared, slots), BF16),
+        pltpu.VMEM((slots, LANES), BF16),
+        pltpu.VMEM((slots, LANES), F32),
+    ]
+    own = rx[:, WIDTH : 2 * WIDTH, :]
+    other = lax.ppermute(own, "groups", [(0, 1), (1, 0)])
     pair_rows = pltpu.VMEM((WIDTH, slots), BF16)
     deep_rows = pltpu.VMEM((depth * WIDTH, slots), BF16)
     big = 2 * WIDTH * slots * slots + 2 * rows * slots * depth * WIDTH
     msg, lat = run(
         cell_kernel,
         [shape((n, main, LANES), BF16), shape((WIDTH, slots), BF16)],
-        [same, rx, zr, lp],
+        [rx, cells, rank, same, zr, lp],
         big,
-        scratch=same_scratch + [pair_rows, deep_rows],
-        hbm=1,
-        grant=56,
+        scratch=sum_scratch + [pair_rows, deep_rows],
+        grant=20,
     )
     columns = exchange(msg)
     msg, spec = run(
         mode_kernel,
         [shape((n, main, LANES), BF16), shape((n, own_rows, LANES), BF16)],
-        [group, columns, rx, other, table, back],
+        [group, columns, own, other, table, back],
         4 * MODES * low * rows * depth * WIDTH,
         scratch=[pltpu.VMEM((MODES * low * levels, LANES), F32)] * 2,
         smem=1,
@@ -734,11 +798,10 @@
             shape((1, 2), F32),
             shape((1, WIDTH), F32),
         ],
-        [same, grads, targets.reshape(1, 2), zr, lp, lat, slope],
+        [grads, targets.reshape(1, 2), cells, rank, same, zr, lp, lat, slope],
         big,
-        scratch=same_scratch + [pair_rows, pair_rows, deep_rows],
-        hbm=1,
-        grant=56,
+        scratch=sum_scratch + [pair_rows, pair_rows, deep_rows],
+        grant=20,
     )
     grad_columns = lax.all_to_all(
         msg, "gx", split_axis=0, concat_axis=0, tiled=True, axis_index_groups=near
@@ -758,6 +821,11 @@
         [shape((spec_weight.shape[0], WIDTH, WIDTH), F32), shape((WIDTH, WIDTH), F32)],
         [finals],
         2 * NMODE * WIDTH * WIDTH * depth // n,
+        scratch=[
+            pltpu.VMEM((spec_weight.shape[0], WIDTH, WIDTH), F32),
+            pltpu.SemaphoreType.DMA((spec_weight.shape[0] // 16,)),
+        ],
+        hbm_outs=1,
     )
     return (pressure.reshape(points), forces.reshape(2), spec_grad, skip_grad, out_grad.reshape(WIDTH))
 

time: 157 us -> 148 us (0.943)
  local copies, waits for them, and re-layouts: 12.2 us -> 2.97 us
  Pallas kernels: 32.8 us -> 23.8 us
  waiting for transfers between devices: 64.1 us -> 72.7 us
    pallas_call x10, Pallas kernels: 32.8 us -> 23.8 us  [run(): pl.pallas_call(kernel, out_shape=tuple(outs), in_specs=[scalar] * smem +...]
    all_to_all x5, waiting for transfers between devices: 47.8 us -> 56.4 us  [exchange(): lax.all_to_all(message, 'gx', split_axis=0, concat_axis=0, tiled=True)]
    unnamed x48 -> x36, local copies, waits for them, and re-layouts: 10.9 us -> 2.66 us
  transfers between devices with their start and end apart: 7 -> 7, of which waited for: 7 -> 7; matrix products, arithmetic and copies ran while one was open for 1% -> 0% of each run, Pallas kernels for 2% -> 2%
where the time goes in v4:
time: 148 us; the launch traced here: 147 us
  waiting for transfers between devices  72.7 us (49%)
  starting transfers between devices  28.5 us (19%)
  Pallas kernels  23.8 us (16%)
  blocking collectives  17.9 us (12%)
  local copies, waits for them, and re-layouts  2.97 us (2%)
    all_to_all x5, waiting for transfers between devices, exchange(): lax.all_to_all(message, 'gx', split_axis=0, concat_axis=0, tiled=True)  56.4 us
    pallas_call x10, Pallas kernels, run(): pl.pallas_call(kernel, out_shape=tuple(outs), in_specs=[scalar] * smem +...  23.8 us
    all_to_all x5, starting transfers between devices, exchange(): lax.all_to_all(message, 'gx', split_axis=0, concat_axis=0, tiled=True)  23.4 us
    all_to_all x1, blocking collectives, exchange(): lax.all_to_all(message, 'gx', split_axis=0, concat_axis=0, tiled=True)  17.9 us
    all_to_all x1, waiting for transfers between devices, slab_step(): lax.all_to_all(msg, 'gx', split_axis=0, concat_axis=0, tiled=True, axis_i...  9.1 us
    ppermute x1, waiting for transfers between devices, slab_step(): other = lax.ppermute(own, 'groups', [(0, 1), (1, 0)])  7.15 us
    all_to_all x1, starting transfers between devices, slab_step(): lax.all_to_all(msg, 'gx', split_axis=0, concat_axis=0, tiled=True, axis_i...  3.54 us
  transfers between devices with their start and end apart: 7, of which 7 were waited for; matrix products, arithmetic and copies ran while one was open for 0% of the time, Pallas kernels for 2%

profile of v4, /device:TPU:0, one launch (start us, length us, event | category | flops | bytes accessed | tf_op | source)
XLA Modules:
  0.0 146.9 jit_solution(1237686944061831965)
XLA Ops:
  0.6 0.0 copy-start.11
  0.7 2.4 %shard_map.209 = (bf16[16,128,128]{2,1,0:T(8,128)(2,1)}, f32[16,128]{1,0:T(8,128)}) custom-call(s32[1]{0:T(128)} %bitcast.group_ref, s32[1,16]{1,0:T(1,128)} %count_hbm.1, s32[16,128]{1,0:T(8,128)} %bitcast.14, f32[16,128]{1,0:T(8,128)} %bitcast.24, f32[1,512]{1,0:T(1,128)} %bitcast.16, bf16[64,512]{1,0:T(8,128)(2,1)} %bitcast.23, bf16[64,64,64]{2,1,0:T(8,128)(2,1)} %weight_hbm.1), custom_call_target="tpu_custom_call" | custom-call | flops 167772160 | bytes 1140804 | tf_op jit(solution)/shard_map/pallas_call | solution.py:642
  3.1 7.4 %all-to-all-start = ((bf16[16,128,128]{2,1,0:T(8,128)(2,1)}), bf16[16,128,128]{2,1,0:T(8,128)(2,1)S(1)}, u32[]{:S(2)}, u32[]{:S(2)}) async-start(bf16[16,128,128]{2,1,0:T(8,128)(2,1)} %get-tuple-element.24), calls=%async_computation | async-start | bytes 1048576 | tf_op jit(solution)/shard_map/all_to_all | solution.py:703
  10.5 3.2 %shard_map.210 = (bf16[256,2048]{1,0:T(8,128)(2,1)S(1)}, s32[16,128]{1,0:T(8,128)S(1)}, s32[16,128]{1,0:T(8,128)S(1)}, bf16[512,512]{1,0:T(8,128)(2,1)S(1)}) custom-call(s32[16,128]{1,0:T(8,128)S(1)} %bitcast.18, bf16[256,128]{1,0:T(8,128)(2,1)S(1)} %copy-done.11), custom_call_target="tpu_custom_call" | custom-call | flops 134217728 | bytes 1662976 | tf_op jit(solution)/shard_map/pallas_call | solution.py:642
  13.8 11.2 %all-to-all-done.rx_ref = bf16[16,128,128]{2,1,0:T(8,128)(2,1)S(1)} async-done(((bf16[16,128,128]{2,1,0:T(8,128)(2,1)}), bf16[16,128,128]{2,1,0:T(8,128)(2,1)S(1)}, u32[]{:S(2)}, u32[]{:S(2)}) %all-to-all-start) | async-done | bytes 524320 | tf_op jit(solution)/shard_map/all_to_all | solution.py:703
  25.0 3.8 %shard_map.211 = (bf16[16,128,128]{2,1,0:T(8,128)(2,1)}, bf16[64,2048]{1,0:T(8,128)(2,1)S(1)}) custom-call(bf16[16,128,128]{2,1,0:T(8,128)(2,1)S(1)} %all-to-all-done.rx_ref, s32[16,128]{1,0:T(8,128)S(1)} %bitcast.19, s32[16,128]{1,0:T(8,128)S(1)} %get-tuple-element.25.rank_ref, bf16[512,512]{1,0:T(8,128)(2,1)S(1)} %get-tuple-element.26.same_ref, ...), custom_call_target="tpu_custom_call" | custom-call | flops 1610612736 | bytes 2908160 | tf_op jit(solution)/shard_map/pallas_call | solution.py:642
  28.8 0.7 copy-done.12
  29.5 4.1 %all-to-all-start.1 = ((bf16[16,128,128]{2,1,0:T(8,128)(2,1)}), bf16[16,128,128]{2,1,0:T(8,128)(2,1)S(1)}, u32[]{:S(2)}, u32[]{:S(2)}) async-start(bf16[16,128,128]{2,1,0:T(8,128)(2,1)} %get-tuple-element.29), calls=%async_computation.1 | async-start | bytes 1048576 | tf_op jit(solution)/shard_map/all_to_all | solution.py:703
  33.7 1.6 %collective-permute-start = (bf16[16,64,128]{2,1,0:T(8,128)(2,1)S(1)}, bf16[16,64,128]{2,1,0:T(8,128)(2,1)S(1)}, u32[]{:S(2)}, u32[]{:S(2)}) collective-permute-start(bf16[16,64,128]{2,1,0:T(8,128)(2,1)S(1)} %slice.4.own_ref), channel_id=1, source_target_pairs={{0,16},{16,0},{1,17},{17,1},{2,18},{18,2},{3,19},{19,3},{4,20},{20... | collective-permute-start | bytes 786440 | tf_op jit(solution)/shard_map/ppermute | solution.py:753
  35.2 7.2 %collective-permute-done.other_ref = bf16[16,64,128]{2,1,0:T(8,128)(2,1)S(1)} collective-permute-done((bf16[16,64,128]{2,1,0:T(8,128)(2,1)S(1)}, bf16[16,64,128]{2,1,0:T(8,128)(2,1)S(1)}, u32[]{:S(2)}, u32[]{:S(2)}) %collective-permute-start) | collective-permute-done | bytes 262176 | tf_op jit(solution)/shard_map/ppermute | solution.py:753
  42.4 5.7 %all-to-all-done.1.rx_ref = bf16[16,128,128]{2,1,0:T(8,128)(2,1)S(1)} async-done(((bf16[16,128,128]{2,1,0:T(8,128)(2,1)}), bf16[16,128,128]{2,1,0:T(8,128)(2,1)S(1)}, u32[]{:S(2)}, u32[]{:S(2)}) %all-to-all-start.1) | async-done | bytes 524320 | tf_op jit(solution)/shard_map/all_to_all | solution.py:703
  48.1 1.7 %shard_map.212 = (bf16[16,128,128]{2,1,0:T(8,128)(2,1)}, bf16[16,32,128]{2,1,0:T(8,128)(2,1)S(1)}) custom-call(s32[1]{0:T(128)} %bitcast.group_ref, bf16[16,128,128]{2,1,0:T(8,128)(2,1)S(1)} %all-to-all-done.1.rx_ref, bf16[16,64,128]{2,1,0:T(8,128)(2,1)S(1)} %slice.4.own_ref, bf16[16,64,128]{2,1,0:T(8,128)(2,1)S(1)} %collective-permute-done.other_ref, ...), custom_call_target="tpu_custom_call" | custom-call | flops 67108864 | bytes 1769476 | tf_op jit(solution)/shard_map/pallas_call | solution.py:642
  49.8 4.1 %all-to-all-start.2 = ((bf16[16,128,128]{2,1,0:T(8,128)(2,1)}), bf16[16,128,128]{2,1,0:T(8,128)(2,1)S(1)}, u32[]{:S(2)}, u32[]{:S(2)}) async-start(bf16[16,128,128]{2,1,0:T(8,128)(2,1)} %get-tuple-element.30), calls=%async_computation.2 | async-start | bytes 1048576 | tf_op jit(solution)/shard_map/all_to_all | solution.py:703
  53.9 0.1 copy.23.bias_ref
  54.0 14.4 %all-to-all-done.2.rx_ref = bf16[16,128,128]{2,1,0:T(8,128)(2,1)S(1)} async-done(((bf16[16,128,128]{2,1,0:T(8,128)(2,1)}), bf16[16,128,128]{2,1,0:T(8,128)(2,1)S(1)}, u32[]{:S(2)}, u32[]{:S(2)}) %all-to-all-start.2) | async-done | bytes 524320 | tf_op jit(solution)/shard_map/all_to_all | solution.py:703
  68.4 0.9 copy-done.13
  69.4 2.2 %shard_map.213 = (bf16[16,64,128]{2,1,0:T(8,128)(2,1)}, f32[64,2048]{1,0:T(8,128)S(1)}) custom-call(bf16[16,128,128]{2,1,0:T(8,128)(2,1)S(1)} %all-to-all-done.2.rx_ref, bf16[256,2048]{1,0:T(8,128)(2,1)S(1)} %get-tuple-element.28.lp_ref, bf16[64,2048]{1,0:T(8,128)(2,1)S(1)} %copy-done.13, s32[16,128]{1,0:T(8,128)S(1)} %bitcast.20, ...), custom_call_target="tpu_custom_call" | custom-call | flops 1073741824 | bytes 2638080 | tf_op jit(solution)/shard_map/pallas_call | solution.py:642
  71.6 4.2 %all-to-all-start.3 = ((bf16[16,64,128]{2,1,0:T(8,128)(2,1)}), bf16[16,64,128]{2,1,0:T(8,128)(2,1)S(1)}, u32[]{:S(2)}, u32[]{:S(2)}) async-start(bf16[16,64,128]{2,1,0:T(8,128)(2,1)} %get-tuple-element.32), calls=%async_computation.3 | async-start | bytes 524288 | tf_op jit(solution)/shard_map/all_to_all | solution.py:703
  75.8 0.1 copy.24.bias_ref
  75.9 0.1 copy.25.out_ref
  76.0 9.8 %all-to-all-done.3.rx_ref = bf16[16,64,128]{2,1,0:T(8,128)(2,1)S(1)} async-done(((bf16[16,64,128]{2,1,0:T(8,128)(2,1)}), bf16[16,64,128]{2,1,0:T(8,128)(2,1)S(1)}, u32[]{:S(2)}, u32[]{:S(2)}) %all-to-all-start.3) | async-done | bytes 262176 | tf_op jit(solution)/shard_map/all_to_all | solution.py:703
  85.9 3.4 %shard_map.214 = (f32[1,512]{1,0:T(1,128)}, bf16[16,144,128]{2,1,0:T(8,128)(2,1)}) custom-call(bf16[16,64,128]{2,1,0:T(8,128)(2,1)S(1)} %all-to-all-done.3.rx_ref, s32[16,128]{1,0:T(8,128)S(1)} %bitcast.15, f32[16,128]{1,0:T(8,128)S(1)} %copy-done.8, bf16[64,64]{1,0:T(8,128)(2,1)S(1)} %copy-done.6, f32[64,1]{1,0:T(8,128)S(1)} %copy.24.bias_ref, ...), custom_call_target="tpu_custom_call" | custom-call | flops 402653184 | bytes 885248 | tf_op jit(solution)/shard_map/pallas_call | solution.py:642
  89.3 3.6 %all-to-all-start.4 = ((bf16[16,144,128]{2,1,0:T(8,128)(2,1)}), bf16[16,144,128]{2,1,0:T(8,128)(2,1)S(1)}, u32[]{:S(2)}, u32[]{:S(2)}) async-start(bf16[16,144,128]{2,1,0:T(8,128)(2,1)} %get-tuple-element.35), calls=%async_computation.4 | async-start | bytes 1179648 | tf_op jit(solution)/shard_map/all_to_all | solution.py:703
  92.9 0.2 shard_map.215.slope_ref
  93.1 15.3 %all-to-all-done.4.rx_ref = bf16[16,144,128]{2,1,0:T(8,128)(2,1)S(1)} async-done(((bf16[16,144,128]{2,1,0:T(8,128)(2,1)}), bf16[16,144,128]{2,1,0:T(8,128)(2,1)S(1)}, u32[]{:S(2)}, u32[]{:S(2)}) %all-to-all-start.4) | async-done | bytes 589856 | tf_op jit(solution)/shard_map/all_to_all | solution.py:703
  108.4 0.9 copy-done.14
  109.3 4.1 %shard_map.216 = (bf16[8,272,128]{2,1,0:T(8,128)(2,1)}, f32[1,2]{1,0:T(1,128)}, f32[1,64]{1,0:T(1,128)}) custom-call(bf16[16,144,128]{2,1,0:T(8,128)(2,1)S(1)} %all-to-all-done.4.rx_ref, f32[1,2]{1,0:T(1,128)S(1)} %bitcast.22, s32[16,128]{1,0:T(8,128)S(1)} %bitcast.21, s32[16,128]{1,0:T(8,128)S(1)} %get-tuple-element.25.rank_ref, ...), custom_call_target="tpu_custom_call" | custom-call | flops 1610612736 | bytes 3531024 | tf_op jit(solution)/shard_map/pallas_call | solution.py:642
  113.4 3.5 %all-to-all-start.5 = ((bf16[8,272,128]{2,1,0:T(8,128)(2,1)}), bf16[8,272,128]{2,1,0:T(8,128)(2,1)S(1)}, u32[]{:S(2)}, u32[]{:S(2)}) async-start(bf16[8,272,128]{2,1,0:T(8,128)(2,1)} %get-tuple-element.38), calls=%async_computation.5 | async-start | bytes 1114112 | tf_op jit(solution)/shard_map/all_to_all | solution.py:806
  117.0 9.1 %all-to-all-done.5.rx_ref = bf16[8,272,128]{2,1,0:T(8,128)(2,1)S(1)} async-done(((bf16[8,272,128]{2,1,0:T(8,128)(2,1)}), bf16[8,272,128]{2,1,0:T(8,128)(2,1)S(1)}, u32[]{:S(2)}, u32[]{:S(2)}) %all-to-all-start.5) | async-done | bytes 557088 | tf_op jit(solution)/shard_map/all_to_all | solution.py:806
  126.1 0.3 shard_map.217
  126.4 17.9 %all_to_all.35.rx_ref = bf16[16,112,128]{2,1,0:T(8,128)(2,1)S(1)} all-to-all(bf16[16,112,128]{2,1,0:T(8,128)(2,1)S(1)} %shard_map.217), channel_id=1, replica_groups=mesh['groups'=2,'gx'=16] {'gx'}, dimensions={0} | all-to-all | bytes 917504 | tf_op jit(solution)/shard_map/all_to_all | solution.py:703
  144.3 2.4 %shard_map.218 = (f32[64,64,64]{2,1,0:T(8,128)}, f32[64,64]{1,0:T(8,128)}) custom-call(bf16[16,112,128]{2,1,0:T(8,128)(2,1)S(1)} %all_to_all.35.rx_ref), custom_call_target="tpu_custom_call" | custom-call | flops 8388608 | bytes 1523712 | tf_op jit(solution)/shard_map/pallas_call | solution.py:642
  (33 shorter events, 0.1 us)
Async XLA Ops:
  0.6 9.9 %copy-start.11 = (bf16[256,128]{1,0:T(8,128)(2,1)S(1)}, bf16[256,128]{1,0:T(8,128)(2,1)}, u32[]{:S(2)}) copy-start(bf16[256,128]{1,0:T(8,128)(2,1)} %constant.33.clone.by_ref) | copy-start | bytes 196612
  0.6 9.9 %copy-start.7 = (s32[16,1,128]{2,1,0:T(1,128)S(1)}, s32[16,1,128]{2,1,0:T(1,128)}, u32[]{:S(2)}) copy-start(s32[16,1,128]{2,1,0:T(1,128)} %param.20) | copy-start | bytes 24580
  3.1 21.9 %all-to-all-start = ((bf16[16,128,128]{2,1,0:T(8,128)(2,1)}), bf16[16,128,128]{2,1,0:T(8,128)(2,1)S(1)}, u32[]{:S(2)}, u32[]{:S(2)}) async-start(bf16[16,128,128]{2,1,0:T(8,128)(2,1)} %get-tuple-element.24), calls=%async_computation | async-start | bytes 1048576 | tf_op jit(solution)/shard_map/all_to_all | solution.py:703
  25.0 23.1 %copy-start.1 = (bf16[256,64]{1,0:T(8,128)(2,1)S(1)}, bf16[256,64]{1,0:T(8,128)(2,1)}, u32[]{:S(2)}) copy-start(bf16[256,64]{1,0:T(8,128)(2,1)} %constant.34.clone.back_ref) | copy-start | bytes 98308
  25.0 23.1 %copy-start.2 = (bf16[64,256]{1,0:T(8,128)(2,1)S(1)}, bf16[64,256]{1,0:T(8,128)(2,1)}, u32[]{:S(2)}) copy-start(bf16[64,256]{1,0:T(8,128)(2,1)} %constant.35.clone.table_ref) | copy-start | bytes 98308
  28.8 0.7 copy-start.12
  28.8 25.1 %copy-start.15 = (f32[64]{0:T(128)S(1)}, f32[64]{0:T(128)}, u32[]{:S(2)}) copy-start(f32[64]{0:T(128)} %param.28) | copy-start | bytes 772
  28.8 39.5 %copy-start.5 = (bf16[64,64]{1,0:T(8,128)(2,1)S(1)}, bf16[64,64]{1,0:T(8,128)(2,1)}, u32[]{:S(2)}) copy-start(bf16[64,64]{1,0:T(8,128)(2,1)} %skip_ref.1) | copy-start | bytes 24580
  29.5 18.6 %all-to-all-start.1 = ((bf16[16,128,128]{2,1,0:T(8,128)(2,1)}), bf16[16,128,128]{2,1,0:T(8,128)(2,1)S(1)}, u32[]{:S(2)}, u32[]{:S(2)}) async-start(bf16[16,128,128]{2,1,0:T(8,128)(2,1)} %get-tuple-element.29), calls=%async_computation.1 | async-start | bytes 1048576 | tf_op jit(solution)/shard_map/all_to_all | solution.py:703
  33.7 8.7 %collective-permute-start = (bf16[16,64,128]{2,1,0:T(8,128)(2,1)S(1)}, bf16[16,64,128]{2,1,0:T(8,128)(2,1)S(1)}, u32[]{:S(2)}, u32[]{:S(2)}) collective-permute-start(bf16[16,64,128]{2,1,0:T(8,128)(2,1)S(1)} %slice.4.own_ref), channel_id=1, source_target_pairs={{0,16},{16,0},{1,17},{17,1},{2,18},{18,2},{3,19},{19,3},{4,20},{20... | collective-permute-start | bytes 786440 | tf_op jit(solution)/shard_map/ppermute | solution.py:753
  49.8 18.6 %all-to-all-start.2 = ((bf16[16,128,128]{2,1,0:T(8,128)(2,1)}), bf16[16,128,128]{2,1,0:T(8,128)(2,1)S(1)}, u32[]{:S(2)}, u32[]{:S(2)}) async-start(bf16[16,128,128]{2,1,0:T(8,128)(2,1)} %get-tuple-element.30), calls=%async_computation.2 | async-start | bytes 1048576 | tf_op jit(solution)/shard_map/all_to_all | solution.py:703
  68.4 1.0 copy-start.13
  69.3 6.5 %copy-start.16 = (f32[64]{0:T(128)S(1)}, f32[64]{0:T(128)}, u32[]{:S(2)}) copy-start(f32[64]{0:T(128)} %param.30) | copy-start | bytes 772
  69.3 6.6 %copy-start.17 = (f32[64]{0:T(128)S(1)}, f32[64]{0:T(128)}, u32[]{:S(2)}) copy-start(f32[64]{0:T(128)} %param.31) | copy-start | bytes 772
  69.3 16.5 %copy-start.3 = (s32[1,16,128]{2,1,0:T(8,128)S(1)}, s32[1,16,128]{2,1,0:T(8,128)}, u32[]{:S(2)}) copy-start(s32[1,16,128]{2,1,0:T(8,128)} %param.19) | copy-start | bytes 24580
  69.3 16.5 %copy-start.4 = (f32[512]{0:T(512)S(1)}, f32[512]{0:T(512)}, u32[]{:S(2)}) copy-start(f32[512]{0:T(512)} %param.23) | copy-start | bytes 6148
  69.3 16.5 %copy-start.6 = (bf16[64,64]{1,0:T(8,128)(2,1)S(1)}, bf16[64,64]{1,0:T(8,128)(2,1)}, u32[]{:S(2)}) copy-start(bf16[64,64]{1,0:T(8,128)(2,1)} %head_ref.1) | copy-start | bytes 24580
  69.3 16.5 %copy-start.8 = (f32[16,128]{1,0:T(8,128)S(1)}, f32[16,128]{1,0:T(8,128)}, u32[]{:S(2)}) copy-start(f32[16,128]{1,0:T(8,128)} %get-tuple-element.33.pw_ref) | copy-start | bytes 24580
  69.4 16.5 %copy-start.9 = (f32[2,512]{1,0:T(2,128)S(1)}, f32[2,512]{1,0:T(2,128)}, u32[]{:S(2)}) copy-start(f32[2,512]{1,0:T(2,128)} %normal_ref.1) | copy-start | bytes 12292
  71.6 36.8 %copy-start.10 = (f32[2]{0:T(128)S(1)}, f32[2]{0:T(128)}, u32[]{:S(2)}) copy-start(f32[2]{0:T(128)} %param.25) | copy-start | bytes 28
  71.6 14.3 %all-to-all-start.3 = ((bf16[16,64,128]{2,1,0:T(8,128)(2,1)}), bf16[16,64,128]{2,1,0:T(8,128)(2,1)S(1)}, u32[]{:S(2)}, u32[]{:S(2)}) async-start(bf16[16,64,128]{2,1,0:T(8,128)(2,1)} %get-tuple-element.32), calls=%async_computation.3 | async-start | bytes 524288 | tf_op jit(solution)/shard_map/all_to_all | solution.py:703
  89.3 19.1 %all-to-all-start.4 = ((bf16[16,144,128]{2,1,0:T(8,128)(2,1)}), bf16[16,144,128]{2,1,0:T(8,128)(2,1)S(1)}, u32[]{:S(2)}, u32[]{:S(2)}) async-start(bf16[16,144,128]{2,1,0:T(8,128)(2,1)} %get-tuple-element.35), calls=%async_computation.4 | async-start | bytes 1179648 | tf_op jit(solution)/shard_map/all_to_all | solution.py:703
  108.4 1.0 copy-start.14
  109.3 16.8 %copy-start = (bf16[2,128,256]{2,1,0:T(8,128)(2,1)S(1)}, bf16[2,128,256]{2,1,0:T(8,128)(2,1)}, u32[]{:S(2)}) copy-start(bf16[2,128,256]{2,1,0:T(8,128)(2,1)} %constant.36.clone.table_ref) | copy-start | bytes 393220
  113.4 12.7 %all-to-all-start.5 = ((bf16[8,272,128]{2,1,0:T(8,128)(2,1)}), bf16[8,272,128]{2,1,0:T(8,128)(2,1)S(1)}, u32[]{:S(2)}, u32[]{:S(2)}) async-start(bf16[8,272,128]{2,1,0:T(8,128)(2,1)} %get-tuple-element.38), calls=%async_computation.5 | async-start | bytes 1114112 | tf_op jit(solution)/shard_map/all_to_all | solution.py:806

commit v5 on v4

--- a/solution.py
+++ b/solution.py
@@ -263,14 +263,26 @@
         ).astype(BF16)
 
 
-def place_kernel(depth, cell_ref, by_ref, lp_ref, zr_ref, rank_ref, same_ref, col_ref, flag_ref, pick_ref, part_ref):
-    devices = cell_ref.shape[0]
-    shared = same_ref.shape[0]
+def basis_rows(depth, cell_ref, by_ref, lp_ref):
     zbits = depth.bit_length() - 1
     rows = by_ref.shape[0]
     slab = rows // MODES
-    yrow = lax.broadcasted_iota(jnp.int32, (GY, LANES), 0)
-    xrow = jnp.bitwise_and(lax.broadcasted_iota(jnp.int32, (rows, LANES), 0), slab - 1)
+    wide = 2 * LANES
+    yrow = lax.broadcasted_iota(jnp.int32, (GY, wide), 0)
+    xrow = jnp.bitwise_and(lax.broadcasted_iota(jnp.int32, (rows, wide), 0), slab - 1)
+    for pair in range(cell_ref.shape[0] // 2):
+        cells = two_rows(cell_ref, pair)
+        ypos = jnp.bitwise_and(jnp.right_shift(cells, zbits), GY - 1)
+        xpos = jnp.right_shift(cells, zbits + GY.bit_length() - 1)
+        hot = jnp.where(yrow == ypos, 1.0, 0.0).astype(BF16)
+        lp_ref[:, pair * wide : (pair + 1) * wide] = jnp.where(
+            xrow == xpos, mm(by_ref[...], hot), 0.0
+        ).astype(BF16)
+
+
+def place_kernel(depth, cell_ref, zr_ref, rank_ref, same_ref, col_ref, flag_ref, pick_ref, part_ref):
+    devices = cell_ref.shape[0]
+    shared = same_ref.shape[0]
     down = lax.broadcasted_iota(jnp.int32, (LANES, LANES), 0)
     along = lax.broadcasted_iota(jnp.int32, (LANES, LANES), 1)
     place = lax.broadcasted_iota(jnp.int32, (16, LANES), 0)
@@ -278,10 +290,6 @@
         cells = cell_ref[block : block + 1, :]
         cut = slice(block * LANES, (block + 1) * LANES)
         col_ref[cut, :] = columns_of(cells.astype(F32))
-        ypos = jnp.bitwise_and(jnp.right_shift(cells, zbits), GY - 1)
-        xpos = jnp.right_shift(cells, zbits + GY.bit_length() - 1)
-        hot = jnp.where(yrow == ypos, 1.0, 0.0).astype(BF16)
-        lp_ref[:, cut] = jnp.where(xrow == xpos, mm(by_ref[...], hot), 0.0).astype(BF16)
         high = jnp.right_shift(cells, 7).astype(F32)
         low = jnp.bitwise_and(cells, 127).astype(F32)
         part_ref[:, cut] = jnp.where(place == 0, high, jnp.where(place == 1, low, 0.0)).astype(BF16)
@@ -320,7 +328,14 @@
         ).astype(BF16)
 
 
-def sum_cells(xs_ref, cell_ref, rank_ref, same_ref, sums_ref, pick_ref, full_ref, col_ref):
+def fold_parts(values):
+    total = values[0:WIDTH]
+    for at in range(WIDTH, values.shape[0], WIDTH):
+        total = total + values[at : at + WIDTH]
+    return total
+
+
+def sum_cells(terms, xs_ref, cell_ref, rank_ref, same_ref, sums_ref, pick_ref, full_ref, col_ref):
     devices = cell_ref.shape[0]
     shared = same_ref.shape[0]
     few = jnp.max(rank_ref[...]) < shared
@@ -329,13 +344,12 @@
     def _():
         pick_rows(rank_ref, pick_ref)
         picked = mm_nt(xs_ref[...], pick_ref[...]).astype(BF16)
-        parts = jnp.concatenate(three_parts(mm(picked, same_ref[...])), axis=0)
+        total = fold_parts(mm(picked, same_ref[...]))
+        parts = jnp.concatenate(three_parts(total)[0 : xs_ref.shape[0] // WIDTH], axis=0)
         for pair in range(devices // 2):
             span = slice(pair * 2 * LANES, (pair + 1) * 2 * LANES)
-            got = mm(parts, pick_ref[:, span])
-            got = got[0:WIDTH] + got[WIDTH : 2 * WIDTH] + got[2 * WIDTH : 3 * WIDTH]
-            alone = two_rows(rank_ref, pair) < 0
-            sums_ref[:, span] = jnp.where(alone, xs_ref[:, span].astype(F32), got)
+            got = fold_parts(mm(parts, pick_ref[:, span]))
+            sums_ref[:, span] = jnp.where(two_rows(rank_ref, pair) < 0, terms(span), got)
 
     @pl.when(jnp.logical_not(few))
     def _():
@@ -346,7 +360,9 @@
         for block in range(devices):
             row = cell_ref[block : block + 1, :].astype(F32)
             full_ref[...] = jnp.where(col_ref[...] == row, 1.0, 0.0).astype(BF16)
-            sums_ref[:, block * LANES : (block + 1) * LANES] = mm(xs_ref[...], full_ref[...])
+            sums_ref[:, block * LANES : (block + 1) * LANES] = fold_parts(
+                mm(xs_ref[...], full_ref[...])
+            )
 
 
 def spread_depth(values, zpos, rp_ref, pair):
@@ -370,11 +386,15 @@
                 ]
 
 
-def cell_kernel(rx_ref, cell_ref, rank_ref, same_ref, zr_ref, lp_ref, msg_ref, lat_ref, sums_ref, pick_ref, full_ref, col_ref, xs_ref, rp_ref):
+def cell_kernel(depth, rx_ref, cell_ref, rank_ref, same_ref, zr_ref, by_ref, msg_ref, lat_ref, sums_ref, pick_ref, full_ref, col_ref, xs_ref, rp_ref, lp_ref):
     devices = rx_ref.shape[0]
     for block in range(devices):
         xs_ref[:, block * LANES : (block + 1) * LANES] = rx_ref[block, 0:WIDTH, :]
-    sum_cells(xs_ref, cell_ref, rank_ref, same_ref, sums_ref, pick_ref, full_ref, col_ref)
+    sum_cells(
+        lambda span: xs_ref[:, span].astype(F32),
+        xs_ref, cell_ref, rank_ref, same_ref, sums_ref, pick_ref, full_ref, col_ref,
+    )
+    basis_rows(depth, cell_ref, by_ref, lp_ref)
     for pair in range(devices // 2):
         cut = slice(pair * 2 * LANES, (pair + 1) * 2 * LANES)
         latent = sums_ref[:, cut]
@@ -432,8 +452,9 @@
             msg_ref[dest, level * step : (level + 1) * step, :] = out[dest * step : (dest + 1) * step]
 
 
-def pre_kernel(depth, rx_ref, lp_ref, lat_ref, cell_ref, skip_ref, bias_ref, msg_ref, pre_ref, rt_ref):
+def pre_kernel(depth, rx_ref, by_ref, lat_ref, cell_ref, skip_ref, bias_ref, msg_ref, pre_ref, rt_ref, lp_ref):
     devices = rx_ref.shape[0]
+    basis_rows(depth, cell_ref, by_ref, lp_ref)
     rows = lp_ref.shape[0]
     step = rows // devices
     for level in range(rt_ref.shape[0] // LANES):
@@ -483,9 +504,7 @@
     for which in range(2):
         for index, part in enumerate(three_parts(along[which])):
             extra = jnp.where(place == 3 + 3 * which + index, part.astype(F32), extra)
-    upper = grad.astype(BF16)
-    lower = (grad - upper.astype(F32)).astype(BF16)
-    table = jnp.concatenate([upper, lower, extra.astype(BF16)], axis=0)
+    table = jnp.concatenate([grad.astype(BF16), extra.astype(BF16)], axis=0)
     lane = lax.broadcasted_iota(jnp.int32, (1, LANES), 1)
     partial = []
     for which in range(2):
@@ -506,14 +525,16 @@
         common = jnp.where(place == 9 + index, part.astype(F32), common)
     for index, part in enumerate(three_parts(force_row)):
         common = jnp.where(place == 12 + index, part.astype(F32), common)
-    for block in range(devices):
-        cut = slice(block * LANES, (block + 1) * LANES)
-        got = mm(table, hot_ref[:, cut])
-        msg_ref[block, 0 : 2 * WIDTH, :] = got[0 : 2 * WIDTH].astype(BF16)
-        tail = got[2 * WIDTH : 2 * WIDTH + 16] + common
-        for index, part in enumerate(three_parts(pw_ref[block : block + 1, :])):
-            tail = jnp.where(place == index, part.astype(F32), tail)
-        msg_ref[block, 2 * WIDTH : 2 * WIDTH + 16, :] = tail.astype(BF16)
+    for pair in range(devices // 2):
+        got = mm(table, hot_ref[:, pair * 2 * LANES : (pair + 1) * 2 * LANES])
+        for half in range(2):
+            block = 2 * pair + half
+            cut = slice(half * LANES, (half + 1) * LANES)
+            msg_ref[block, 0:WIDTH, :] = got[0:WIDTH, cut].astype(BF16)
+            tail = got[WIDTH : WIDTH + 16, cut] + common
+            for index, part in enumerate(three_parts(pw_ref[block : block + 1, :])):
+                tail = jnp.where(place == index, part.astype(F32), tail)
+            msg_ref[block, WIDTH : WIDTH + 16, :] = tail.astype(BF16)
 
 
 def fold_rows(values):
@@ -523,10 +544,10 @@
     return upper, lower
 
 
-def back_kernel(scale, rx_ref, target_ref, cell_ref, rank_ref, same_ref, zr_ref, lp_ref, lat_ref, slope_ref, msg_ref, force_ref, outg_ref, sums_ref, pick_ref, full_ref, col_ref, xs_ref, pg_ref, rp_ref):
+def back_kernel(depth, scale, rx_ref, target_ref, cell_ref, rank_ref, same_ref, zr_ref, by_ref, lat_ref, slope_ref, msg_ref, force_ref, outg_ref, sums_ref, pick_ref, full_ref, col_ref, xs_ref, pg_ref, rp_ref, lp_ref, gp_ref):
     devices = rx_ref.shape[0]
     main = msg_ref.shape[1] - 16
-    extra = slice(2 * WIDTH, 2 * WIDTH + 16)
+    extra = slice(WIDTH, WIDTH + 16)
     total = rx_ref[0, extra, :].astype(F32)
     for block in range(1, devices):
         total += rx_ref[block, extra, :].astype(F32)
@@ -542,11 +563,18 @@
         weight, first, second = (
             tail[at : at + 1] + tail[at + 1 : at + 2] + tail[at + 2 : at + 3] for at in (0, 3, 6)
         )
-        grad = rx_ref[block, 0:WIDTH, :].astype(F32) + rx_ref[block, WIDTH : 2 * WIDTH, :].astype(F32)
-        along = twice * (drag * first + lift * second)
-        grad = (along * grad).astype(BF16).astype(F32)
-        xs_ref[:, block * LANES : (block + 1) * LANES] = (weight * grad).astype(BF16)
-    sum_cells(xs_ref, cell_ref, rank_ref, same_ref, sums_ref, pick_ref, full_ref, col_ref)
+        factor = weight * (twice * (drag * first + lift * second))
+        grad = factor * rx_ref[block, 0:WIDTH, :].astype(F32)
+        cut = slice(block * LANES, (block + 1) * LANES)
+        gp_ref[:, cut] = grad
+        upper = grad.astype(BF16)
+        xs_ref[0:WIDTH, cut] = upper
+        xs_ref[WIDTH : 2 * WIDTH, cut] = (grad - upper.astype(F32)).astype(BF16)
+    sum_cells(
+        lambda span: gp_ref[:, span],
+        xs_ref, cell_ref, rank_ref, same_ref, sums_ref, pick_ref, full_ref, col_ref,
+    )
+    basis_rows(depth, cell_ref, by_ref, lp_ref)
     for pair in range(devices // 2):
         cut = slice(pair * 2 * LANES, (pair + 1) * 2 * LANES)
         grad = sums_ref[:, cut] * slope_ref[:, cut]
@@ -588,14 +616,13 @@
     return jnp.concatenate([values, swap_halves(values)], axis=0)[:, 0:WIDTH]
 
 
-def final_kernel(peers, rx_ref, spec_hbm, skip_ref, spec_ref, sems):
+def final_kernel(peers, rx_ref, spec_ref, skip_ref):
     devices = rx_ref.shape[0]
     low = MODES // devices
     high = MODES // peers
     owned = spec_ref.shape[0] // MODES
     part_rows = owned * high * 8
     own_rows = rx_ref.shape[1] - 16 - part_rows
-    copies = []
     for which in range(owned):
         for source in range(devices):
             at = which * 8 * low
@@ -614,15 +641,6 @@
                 spec_ref[which * MODES + low * source + index] = mm_tn(
                     left.astype(BF16), right.astype(BF16)
                 )
-            done = which * MODES + low * (source + 1)
-            if done % 16 == 0:
-                span = pl.ds(done - 16, 16)
-                copies.append(
-                    pltpu.make_async_copy(
-                        spec_ref.at[span], spec_hbm.at[span], sems.at[done // 16 - 1]
-                    )
-                )
-                copies[-1].start()
     at = own_rows + part_rows
     for peer in range(peers):
         rows = rx_ref[peer, at : at + 16, :].astype(F32)
@@ -630,8 +648,6 @@
             rows += rx_ref[peer + shift, at : at + 16, :].astype(F32)
         value = (rows[0:8] + swap_halves(rows[0:8]) + rows[8:16])[:, 0:WIDTH]
         skip_ref[8 * peer : 8 * peer + 8, :] = value
-    for copy in copies:
-        copy.wait()
 
 
 def run(kernel, outs, ins, flops, scratch=(), smem=0, hbm=0, hbm_outs=0, grant=16):
@@ -725,16 +741,15 @@
         grant=60,
     )
     rx = exchange(msg)
-    shared = 512
-    lp, zr, rank, same = run(
+    shared = 384
+    zr, rank, same = run(
         functools.partial(place_kernel, depth),
         [
-            shape((rows, slots), BF16),
             shape((n, LANES), jnp.int32),
             shape((n, LANES), jnp.int32),
             shape((shared, shared), BF16),
         ],
-        [cells, by_rows],
+        [cells],
         2 * rows * LANES * slots,
         scratch=[
             pltpu.VMEM((slots, LANES), F32),
@@ -752,14 +767,15 @@
     own = rx[:, WIDTH : 2 * WIDTH, :]
     other = lax.ppermute(own, "groups", [(0, 1), (1, 0)])
     pair_rows = pltpu.VMEM((WIDTH, slots), BF16)
+    basis = pltpu.VMEM((rows, slots), BF16)
     deep_rows = pltpu.VMEM((depth * WIDTH, slots), BF16)
     big = 2 * WIDTH * slots * slots + 2 * rows * slots * depth * WIDTH
     msg, lat = run(
-        cell_kernel,
+        functools.partial(cell_kernel, depth),
         [shape((n, main, LANES), BF16), shape((WIDTH, slots), BF16)],
-        [rx, cells, rank, same, zr, lp],
+        [rx, cells, rank, same, zr, by_rows],
         big,
-        scratch=sum_scratch + [pair_rows, deep_rows],
+        scratch=sum_scratch + [pair_rows, deep_rows, basis],
         grant=20,
     )
     columns = exchange(msg)
@@ -775,16 +791,16 @@
     msg, pre = run(
         functools.partial(pre_kernel, depth),
         [shape((n, WIDTH, LANES), BF16), shape((WIDTH, slots), F32)],
-        [slabs, lp, lat, cells, skip_weight, skip_bias.reshape(WIDTH, 1)],
+        [slabs, by_rows, lat, cells, skip_weight, skip_bias.reshape(WIDTH, 1)],
         2 * rows * slots * depth * WIDTH,
-        scratch=[pltpu.VMEM((depth * WIDTH, rows), BF16)],
+        scratch=[pltpu.VMEM((depth * WIDTH, rows), BF16), basis],
     )
     returned = exchange(msg)
     (slope,) = run(slope_kernel, [shape(pre.shape, F32)], [pre], 100 * WIDTH * slots)
     out_col = out_weight.reshape(WIDTH, 1)
     pressure, msg = run(
         head_kernel,
-        [shape((1, points), F32), shape((n, 2 * WIDTH + 16, LANES), BF16)],
+        [shape((1, points), F32), shape((n, WIDTH + 16, LANES), BF16)],
         [returned, point_rows, pw, head_weight, head_bias.reshape(WIDTH, 1), out_col, area_row, normals],
         2 * 3 * WIDTH * points * slots,
         scratch=[pltpu.VMEM((3 * WIDTH, slots), BF16), pltpu.VMEM((points, slots), BF16)],
@@ -792,15 +808,17 @@
     grads = exchange(msg)
     scale = 1.0 / math.sqrt(points * n)
     msg, forces, out_grad = run(
-        functools.partial(back_kernel, scale),
+        functools.partial(back_kernel, depth, scale),
         [
             shape((peers, halves * main + 16, LANES), BF16),
             shape((1, 2), F32),
             shape((1, WIDTH), F32),
         ],
-        [grads, targets.reshape(1, 2), cells, rank, same, zr, lp, lat, slope],
+        [grads, targets.reshape(1, 2), cells, rank, same, zr, by_rows, lat, slope],
         big,
-        scratch=sum_scratch + [pair_rows, pair_rows, deep_rows],
+        scratch=sum_scratch
+        + [pltpu.VMEM((2 * WIDTH, slots), BF16), pair_rows, deep_rows, basis]
+        + [pltpu.VMEM((WIDTH, slots), F32)],
         grant=20,
     )
     grad_columns = lax.all_to_all(
@@ -821,11 +839,6 @@
         [shape((spec_weight.shape[0], WIDTH, WIDTH), F32), shape((WIDTH, WIDTH), F32)],
         [finals],
         2 * NMODE * WIDTH * WIDTH * depth // n,
-        scratch=[
-            pltpu.VMEM((spec_weight.shape[0], WIDTH, WIDTH), F32),
-            pltpu.SemaphoreType.DMA((spec_weight.shape[0] // 16,)),
-        ],
-        hbm_outs=1,
     )
     return (pressure.reshape(points), forces.reshape(2), spec_grad, skip_grad, out_grad.reshape(WIDTH))
 

time: 148 us -> 139 us (0.939)
  waiting for transfers between devices: 72.7 us -> 68.7 us
  local copies, waits for them, and re-layouts: 2.97 us -> 0.38 us
    all_to_all x5, waiting for transfers between devices: 56.4 us -> 52.4 us  [exchange(): lax.all_to_all(message, 'gx', split_axis=0, concat_axis=0, tiled=True)]
    unnamed x36 -> x30, local copies, waits for them, and re-layouts: 2.66 us -> 0.07 us
where the time goes in v5:
time: 139 us; the launch traced here: 138 us
  waiting for transfers between devices  68.7 us (49%)
  starting transfers between devices  28.6 us (21%)
  Pallas kernels  23.1 us (17%)
  blocking collectives  16.7 us (12%)
    all_to_all x5, waiting for transfers between devices, exchange(): lax.all_to_all(message, 'gx', split_axis=0, concat_axis=0, tiled=True)  52.4 us
    all_to_all x5, starting transfers between devices, exchange(): lax.all_to_all(message, 'gx', split_axis=0, concat_axis=0, tiled=True)  23.5 us
    pallas_call x10, Pallas kernels, run(): pl.pallas_call(kernel, out_shape=tuple(outs), in_specs=[scalar] * smem +...  23.1 us
    all_to_all x1, blocking collectives, exchange(): lax.all_to_all(message, 'gx', split_axis=0, concat_axis=0, tiled=True)  16.7 us
    all_to_all x1, waiting for transfers between devices, slab_step(): lax.all_to_all(msg, 'gx', split_axis=0, concat_axis=0, tiled=True, axis_i...  9.1 us
    ppermute x1, waiting for transfers between devices, slab_step(): other = lax.ppermute(own, 'groups', [(0, 1), (1, 0)])  7.15 us
    all_to_all x1, starting transfers between devices, slab_step(): lax.all_to_all(msg, 'gx', split_axis=0, concat_axis=0, tiled=True, axis_i...  3.54 us
  transfers between devices with their start and end apart: 7, of which 7 were waited for; matrix products, arithmetic and copies ran while one was open for 0% of the time, Pallas kernels for 2%

profile of v5, /device:TPU:0, one launch (start us, length us, event | category | flops | bytes accessed | tf_op | source)
XLA Modules:
  0.0 138.4 jit_solution(4163440752611324426)
XLA Ops:
  0.6 0.0 copy-start.11
  0.7 2.4 %shard_map.209 = (bf16[16,128,128]{2,1,0:T(8,128)(2,1)}, f32[16,128]{1,0:T(8,128)}) custom-call(s32[1]{0:T(128)} %bitcast.group_ref, s32[1,16]{1,0:T(1,128)} %count_hbm.1, s32[16,128]{1,0:T(8,128)} %bitcast.14, f32[16,128]{1,0:T(8,128)} %bitcast.24, f32[1,512]{1,0:T(1,128)} %bitcast.16, bf16[64,512]{1,0:T(8,128)(2,1)} %bitcast.23, bf16[64,64,64]{2,1,0:T(8,128)(2,1)} %weight_hbm.1), custom_call_target="tpu_custom_call" | custom-call | flops 167772160 | bytes 1140804 | tf_op jit(solution)/shard_map/pallas_call | solution.py:658
  3.1 7.4 %all-to-all-start = ((bf16[16,128,128]{2,1,0:T(8,128)(2,1)}), bf16[16,128,128]{2,1,0:T(8,128)(2,1)S(1)}, u32[]{:S(2)}, u32[]{:S(2)}) async-start(bf16[16,128,128]{2,1,0:T(8,128)(2,1)} %get-tuple-element.23), calls=%async_computation | async-start | bytes 1048576 | tf_op jit(solution)/shard_map/all_to_all | solution.py:719
  10.5 2.8 %shard_map.210 = (s32[16,128]{1,0:T(8,128)S(1)}, s32[16,128]{1,0:T(8,128)S(1)}, bf16[384,384]{1,0:T(8,128)(2,1)S(1)}) custom-call(s32[16,128]{1,0:T(8,128)S(1)} %bitcast.18), custom_call_target="tpu_custom_call" | custom-call | flops 134217728 | bytes 319488 | tf_op jit(solution)/shard_map/pallas_call | solution.py:658
  13.3 11.6 %all-to-all-done.rx_ref = bf16[16,128,128]{2,1,0:T(8,128)(2,1)S(1)} async-done(((bf16[16,128,128]{2,1,0:T(8,128)(2,1)}), bf16[16,128,128]{2,1,0:T(8,128)(2,1)S(1)}, u32[]{:S(2)}, u32[]{:S(2)}) %all-to-all-start) | async-done | bytes 524320 | tf_op jit(solution)/shard_map/all_to_all | solution.py:719
  25.0 3.9 %shard_map.211 = (bf16[16,128,128]{2,1,0:T(8,128)(2,1)}, bf16[64,2048]{1,0:T(8,128)(2,1)S(1)}) custom-call(bf16[16,128,128]{2,1,0:T(8,128)(2,1)S(1)} %all-to-all-done.rx_ref, s32[16,128]{1,0:T(8,128)S(1)} %bitcast.19, s32[16,128]{1,0:T(8,128)S(1)} %get-tuple-element.24.rank_ref, bf16[384,384]{1,0:T(8,128)(2,1)S(1)} %get-tuple-element.25.same_ref, ...), custom_call_target="tpu_custom_call" | custom-call | flops 1610612736 | bytes 1695744 | tf_op jit(solution)/shard_map/pallas_call | solution.py:658
  28.9 4.2 %all-to-all-start.1 = ((bf16[16,128,128]{2,1,0:T(8,128)(2,1)}), bf16[16,128,128]{2,1,0:T(8,128)(2,1)S(1)}, u32[]{:S(2)}, u32[]{:S(2)}) async-start(bf16[16,128,128]{2,1,0:T(8,128)(2,1)} %get-tuple-element.27), calls=%async_computation.1 | async-start | bytes 1048576 | tf_op jit(solution)/shard_map/all_to_all | solution.py:719
  33.1 1.6 %collective-permute-start = (bf16[16,64,128]{2,1,0:T(8,128)(2,1)S(1)}, bf16[16,64,128]{2,1,0:T(8,128)(2,1)S(1)}, u32[]{:S(2)}, u32[]{:S(2)}) collective-permute-start(bf16[16,64,128]{2,1,0:T(8,128)(2,1)S(1)} %slice.4.own_ref), channel_id=1, source_target_pairs={{0,16},{16,0},{1,17},{17,1},{2,18},{18,2},{3,19},{19,3},{4,20},{20... | collective-permute-start | bytes 786440 | tf_op jit(solution)/shard_map/ppermute | solution.py:768
  34.7 7.2 %collective-permute-done.other_ref = bf16[16,64,128]{2,1,0:T(8,128)(2,1)S(1)} collective-permute-done((bf16[16,64,128]{2,1,0:T(8,128)(2,1)S(1)}, bf16[16,64,128]{2,1,0:T(8,128)(2,1)S(1)}, u32[]{:S(2)}, u32[]{:S(2)}) %collective-permute-start) | collective-permute-done | bytes 262176 | tf_op jit(solution)/shard_map/ppermute | solution.py:768
  41.9 5.7 %all-to-all-done.1.rx_ref = bf16[16,128,128]{2,1,0:T(8,128)(2,1)S(1)} async-done(((bf16[16,128,128]{2,1,0:T(8,128)(2,1)}), bf16[16,128,128]{2,1,0:T(8,128)(2,1)S(1)}, u32[]{:S(2)}, u32[]{:S(2)}) %all-to-all-start.1) | async-done | bytes 524320 | tf_op jit(solution)/shard_map/all_to_all | solution.py:719
  47.6 1.7 %shard_map.212 = (bf16[16,128,128]{2,1,0:T(8,128)(2,1)}, bf16[16,32,128]{2,1,0:T(8,128)(2,1)S(1)}) custom-call(s32[1]{0:T(128)} %bitcast.group_ref, bf16[16,128,128]{2,1,0:T(8,128)(2,1)S(1)} %all-to-all-done.1.rx_ref, bf16[16,64,128]{2,1,0:T(8,128)(2,1)S(1)} %slice.4.own_ref, bf16[16,64,128]{2,1,0:T(8,128)(2,1)S(1)} %collective-permute-done.other_ref, ...), custom_call_target="tpu_custom_call" | custom-call | flops 67108864 | bytes 1769476 | tf_op jit(solution)/shard_map/pallas_call | solution.py:658
  49.3 4.1 %all-to-all-start.2 = ((bf16[16,128,128]{2,1,0:T(8,128)(2,1)}), bf16[16,128,128]{2,1,0:T(8,128)(2,1)S(1)}, u32[]{:S(2)}, u32[]{:S(2)}) async-start(bf16[16,128,128]{2,1,0:T(8,128)(2,1)} %get-tuple-element.28), calls=%async_computation.2 | async-start | bytes 1048576 | tf_op jit(solution)/shard_map/all_to_all | solution.py:719
  53.4 0.1 copy.23.bias_ref
  53.5 14.4 %all-to-all-done.2.rx_ref = bf16[16,128,128]{2,1,0:T(8,128)(2,1)S(1)} async-done(((bf16[16,128,128]{2,1,0:T(8,128)(2,1)}), bf16[16,128,128]{2,1,0:T(8,128)(2,1)S(1)}, u32[]{:S(2)}, u32[]{:S(2)}) %all-to-all-start.2) | async-done | bytes 524320 | tf_op jit(solution)/shard_map/all_to_all | solution.py:719
  67.9 0.0 copy-start.4
  67.9 0.0 copy-start.6
  67.9 0.0 copy-start.9
  67.9 2.5 %shard_map.213 = (bf16[16,64,128]{2,1,0:T(8,128)(2,1)}, f32[64,2048]{1,0:T(8,128)S(1)}) custom-call(bf16[16,128,128]{2,1,0:T(8,128)(2,1)S(1)} %all-to-all-done.2.rx_ref, bf16[256,128]{1,0:T(8,128)(2,1)S(1)} %copy-done.11, bf16[64,2048]{1,0:T(8,128)(2,1)S(1)} %get-tuple-element.29.lat_ref, s32[16,128]{1,0:T(8,128)S(1)} %bitcast.20, ...), custom_call_target="tpu_custom_call" | custom-call | flops 1073741824 | bytes 1655040 | tf_op jit(solution)/shard_map/pallas_call | solution.py:658
  70.4 4.2 %all-to-all-start.3 = ((bf16[16,64,128]{2,1,0:T(8,128)(2,1)}), bf16[16,64,128]{2,1,0:T(8,128)(2,1)S(1)}, u32[]{:S(2)}, u32[]{:S(2)}) async-start(bf16[16,64,128]{2,1,0:T(8,128)(2,1)} %get-tuple-element.30), calls=%async_computation.3 | async-start | bytes 524288 | tf_op jit(solution)/shard_map/all_to_all | solution.py:719
  74.6 0.1 copy.24.bias_ref
  74.7 0.1 copy.25.out_ref
  74.8 9.8 %all-to-all-done.3.rx_ref = bf16[16,64,128]{2,1,0:T(8,128)(2,1)S(1)} async-done(((bf16[16,64,128]{2,1,0:T(8,128)(2,1)}), bf16[16,64,128]{2,1,0:T(8,128)(2,1)S(1)}, u32[]{:S(2)}, u32[]{:S(2)}) %all-to-all-start.3) | async-done | bytes 262176 | tf_op jit(solution)/shard_map/all_to_all | solution.py:719
  84.7 2.9 %shard_map.214 = (f32[1,512]{1,0:T(1,128)}, bf16[16,80,128]{2,1,0:T(8,128)(2,1)}) custom-call(bf16[16,64,128]{2,1,0:T(8,128)(2,1)S(1)} %all-to-all-done.3.rx_ref, s32[16,128]{1,0:T(8,128)S(1)} %bitcast.15, f32[16,128]{1,0:T(8,128)S(1)} %copy-done.8, bf16[64,64]{1,0:T(8,128)(2,1)S(1)} %copy-done.6, f32[64,1]{1,0:T(8,128)S(1)} %copy.24.bias_ref, ...), custom_call_target="tpu_custom_call" | custom-call | flops 402653184 | bytes 623104 | tf_op jit(solution)/shard_map/pallas_call | solution.py:658
  87.6 3.5 %all-to-all-start.4 = ((bf16[16,80,128]{2,1,0:T(8,128)(2,1)}), bf16[16,80,128]{2,1,0:T(8,128)(2,1)S(1)}, u32[]{:S(2)}, u32[]{:S(2)}) async-start(bf16[16,80,128]{2,1,0:T(8,128)(2,1)} %get-tuple-element.33), calls=%async_computation.4 | async-start | bytes 655360 | tf_op jit(solution)/shard_map/all_to_all | solution.py:719
  91.2 0.2 shard_map.215.slope_ref
  91.4 10.9 %all-to-all-done.4.rx_ref = bf16[16,80,128]{2,1,0:T(8,128)(2,1)S(1)} async-done(((bf16[16,80,128]{2,1,0:T(8,128)(2,1)}), bf16[16,80,128]{2,1,0:T(8,128)(2,1)S(1)}, u32[]{:S(2)}, u32[]{:S(2)}) %all-to-all-start.4) | async-done | bytes 327712 | tf_op jit(solution)/shard_map/all_to_all | solution.py:719
  102.3 4.3 %shard_map.216 = (bf16[8,272,128]{2,1,0:T(8,128)(2,1)}, f32[1,2]{1,0:T(1,128)}, f32[1,64]{1,0:T(1,128)}) custom-call(bf16[16,80,128]{2,1,0:T(8,128)(2,1)S(1)} %all-to-all-done.4.rx_ref, f32[1,2]{1,0:T(1,128)S(1)} %bitcast.22, s32[16,128]{1,0:T(8,128)S(1)} %bitcast.21, s32[16,128]{1,0:T(8,128)S(1)} %get-tuple-element.24.rank_ref, ...), custom_call_target="tpu_custom_call" | custom-call | flops 1610612736 | bytes 2056464 | tf_op jit(solution)/shard_map/pallas_call | solution.py:658
  106.6 3.5 %all-to-all-start.5 = ((bf16[8,272,128]{2,1,0:T(8,128)(2,1)}), bf16[8,272,128]{2,1,0:T(8,128)(2,1)S(1)}, u32[]{:S(2)}, u32[]{:S(2)}) async-start(bf16[8,272,128]{2,1,0:T(8,128)(2,1)} %get-tuple-element.36), calls=%async_computation.5 | async-start | bytes 1114112 | tf_op jit(solution)/shard_map/all_to_all | solution.py:824
  110.1 9.1 %all-to-all-done.5.rx_ref = bf16[8,272,128]{2,1,0:T(8,128)(2,1)S(1)} async-done(((bf16[8,272,128]{2,1,0:T(8,128)(2,1)}), bf16[8,272,128]{2,1,0:T(8,128)(2,1)S(1)}, u32[]{:S(2)}, u32[]{:S(2)}) %all-to-all-start.5) | async-done | bytes 557088 | tf_op jit(solution)/shard_map/all_to_all | solution.py:824
  119.2 0.3 shard_map.217
  119.5 16.7 %all_to_all.35.rx_ref = bf16[16,112,128]{2,1,0:T(8,128)(2,1)S(1)} all-to-all(bf16[16,112,128]{2,1,0:T(8,128)(2,1)S(1)} %shard_map.217), channel_id=1, replica_groups=mesh['groups'=2,'gx'=16] {'gx'}, dimensions={0} | all-to-all | bytes 917504 | tf_op jit(solution)/shard_map/all_to_all | solution.py:719
  136.3 2.1 %shard_map.218 = (f32[64,64,64]{2,1,0:T(8,128)}, f32[64,64]{1,0:T(8,128)}) custom-call(bf16[16,112,128]{2,1,0:T(8,128)(2,1)S(1)} %all_to_all.35.rx_ref), custom_call_target="tpu_custom_call" | custom-call | flops 8388608 | bytes 1523712 | tf_op jit(solution)/shard_map/pallas_call | solution.py:658
  (27 shorter events, 0.1 us)
Async XLA Ops:
  0.6 24.4 %copy-start.11 = (bf16[256,128]{1,0:T(8,128)(2,1)S(1)}, bf16[256,128]{1,0:T(8,128)(2,1)}, u32[]{:S(2)}) copy-start(bf16[256,128]{1,0:T(8,128)(2,1)} %constant.33.clone.by_ref) | copy-start | bytes 196612
  0.6 9.9 %copy-start.7 = (s32[16,1,128]{2,1,0:T(1,128)S(1)}, s32[16,1,128]{2,1,0:T(1,128)}, u32[]{:S(2)}) copy-start(s32[16,1,128]{2,1,0:T(1,128)} %param.20) | copy-start | bytes 24580
  3.1 21.9 %all-to-all-start = ((bf16[16,128,128]{2,1,0:T(8,128)(2,1)}), bf16[16,128,128]{2,1,0:T(8,128)(2,1)S(1)}, u32[]{:S(2)}, u32[]{:S(2)}) async-start(bf16[16,128,128]{2,1,0:T(8,128)(2,1)} %get-tuple-element.23), calls=%async_computation | async-start | bytes 1048576 | tf_op jit(solution)/shard_map/all_to_all | solution.py:719
  25.0 22.6 %copy-start.1 = (bf16[256,64]{1,0:T(8,128)(2,1)S(1)}, bf16[256,64]{1,0:T(8,128)(2,1)}, u32[]{:S(2)}) copy-start(bf16[256,64]{1,0:T(8,128)(2,1)} %constant.34.clone.back_ref) | copy-start | bytes 98308
  25.0 22.6 %copy-start.2 = (bf16[64,256]{1,0:T(8,128)(2,1)S(1)}, bf16[64,256]{1,0:T(8,128)(2,1)}, u32[]{:S(2)}) copy-start(bf16[64,256]{1,0:T(8,128)(2,1)} %constant.35.clone.table_ref) | copy-start | bytes 98308
  28.9 24.5 %copy-start.12 = (f32[64]{0:T(128)S(1)}, f32[64]{0:T(128)}, u32[]{:S(2)}) copy-start(f32[64]{0:T(128)} %param.28) | copy-start | bytes 772
  28.9 39.0 %copy-start.5 = (bf16[64,64]{1,0:T(8,128)(2,1)S(1)}, bf16[64,64]{1,0:T(8,128)(2,1)}, u32[]{:S(2)}) copy-start(bf16[64,64]{1,0:T(8,128)(2,1)} %skip_ref.1) | copy-start | bytes 24580
  28.9 18.7 %all-to-all-start.1 = ((bf16[16,128,128]{2,1,0:T(8,128)(2,1)}), bf16[16,128,128]{2,1,0:T(8,128)(2,1)S(1)}, u32[]{:S(2)}, u32[]{:S(2)}) async-start(bf16[16,128,128]{2,1,0:T(8,128)(2,1)} %get-tuple-element.27), calls=%async_computation.1 | async-start | bytes 1048576 | tf_op jit(solution)/shard_map/all_to_all | solution.py:719
  33.1 8.7 %collective-permute-start = (bf16[16,64,128]{2,1,0:T(8,128)(2,1)S(1)}, bf16[16,64,128]{2,1,0:T(8,128)(2,1)S(1)}, u32[]{:S(2)}, u32[]{:S(2)}) collective-permute-start(bf16[16,64,128]{2,1,0:T(8,128)(2,1)S(1)} %slice.4.own_ref), channel_id=1, source_target_pairs={{0,16},{16,0},{1,17},{17,1},{2,18},{18,2},{3,19},{19,3},{4,20},{20... | collective-permute-start | bytes 786440 | tf_op jit(solution)/shard_map/ppermute | solution.py:768
  49.3 18.6 %all-to-all-start.2 = ((bf16[16,128,128]{2,1,0:T(8,128)(2,1)}), bf16[16,128,128]{2,1,0:T(8,128)(2,1)S(1)}, u32[]{:S(2)}, u32[]{:S(2)}) async-start(bf16[16,128,128]{2,1,0:T(8,128)(2,1)} %get-tuple-element.28), calls=%async_computation.2 | async-start | bytes 1048576 | tf_op jit(solution)/shard_map/all_to_all | solution.py:719
  67.9 6.8 %copy-start.13 = (f32[64]{0:T(128)S(1)}, f32[64]{0:T(128)}, u32[]{:S(2)}) copy-start(f32[64]{0:T(128)} %param.30) | copy-start | bytes 772
  67.9 6.9 %copy-start.14 = (f32[64]{0:T(128)S(1)}, f32[64]{0:T(128)}, u32[]{:S(2)}) copy-start(f32[64]{0:T(128)} %param.31) | copy-start | bytes 772
  67.9 16.8 %copy-start.3 = (s32[1,16,128]{2,1,0:T(8,128)S(1)}, s32[1,16,128]{2,1,0:T(8,128)}, u32[]{:S(2)}) copy-start(s32[1,16,128]{2,1,0:T(8,128)} %param.19) | copy-start | bytes 24580
  67.9 16.8 %copy-start.4 = (f32[512]{0:T(512)S(1)}, f32[512]{0:T(512)}, u32[]{:S(2)}) copy-start(f32[512]{0:T(512)} %param.23) | copy-start | bytes 6148
  67.9 16.8 %copy-start.6 = (bf16[64,64]{1,0:T(8,128)(2,1)S(1)}, bf16[64,64]{1,0:T(8,128)(2,1)}, u32[]{:S(2)}) copy-start(bf16[64,64]{1,0:T(8,128)(2,1)} %head_ref.1) | copy-start | bytes 24580
  67.9 16.8 %copy-start.8 = (f32[16,128]{1,0:T(8,128)S(1)}, f32[16,128]{1,0:T(8,128)}, u32[]{:S(2)}) copy-start(f32[16,128]{1,0:T(8,128)} %get-tuple-element.31.pw_ref) | copy-start | bytes 24580
  67.9 16.8 %copy-start.9 = (f32[2,512]{1,0:T(2,128)S(1)}, f32[2,512]{1,0:T(2,128)}, u32[]{:S(2)}) copy-start(f32[2,512]{1,0:T(2,128)} %normal_ref.1) | copy-start | bytes 12292
  70.4 31.9 %copy-start.10 = (f32[2]{0:T(128)S(1)}, f32[2]{0:T(128)}, u32[]{:S(2)}) copy-start(f32[2]{0:T(128)} %param.25) | copy-start | bytes 28
  70.4 14.3 %all-to-all-start.3 = ((bf16[16,64,128]{2,1,0:T(8,128)(2,1)}), bf16[16,64,128]{2,1,0:T(8,128)(2,1)S(1)}, u32[]{:S(2)}, u32[]{:S(2)}) async-start(bf16[16,64,128]{2,1,0:T(8,128)(2,1)} %get-tuple-element.30), calls=%async_computation.3 | async-start | bytes 524288 | tf_op jit(solution)/shard_map/all_to_all | solution.py:719
  87.6 14.6 %all-to-all-start.4 = ((bf16[16,80,128]{2,1,0:T(8,128)(2,1)}), bf16[16,80,128]{2,1,0:T(8,128)(2,1)S(1)}, u32[]{:S(2)}, u32[]{:S(2)}) async-start(bf16[16,80,128]{2,1,0:T(8,128)(2,1)} %get-tuple-element.33), calls=%async_computation.4 | async-start | bytes 655360 | tf_op jit(solution)/shard_map/all_to_all | solution.py:719
  102.3 17.0 %copy-start = (bf16[2,128,256]{2,1,0:T(8,128)(2,1)S(1)}, bf16[2,128,256]{2,1,0:T(8,128)(2,1)}, u32[]{:S(2)}) copy-start(bf16[2,128,256]{2,1,0:T(8,128)(2,1)} %constant.36.clone.table_ref) | copy-start | bytes 393220
  106.6 12.7 %all-to-all-start.5 = ((bf16[8,272,128]{2,1,0:T(8,128)(2,1)}), bf16[8,272,128]{2,1,0:T(8,128)(2,1)S(1)}, u32[]{:S(2)}, u32[]{:S(2)}) async-start(bf16[8,272,128]{2,1,0:T(8,128)(2,1)} %get-tuple-element.36), calls=%async_computation.5 | async-start | bytes 1114112 | tf_op jit(solution)/shard_map/all_to_all | solution.py:824

commit v6 on v5

--- a/solution.py
+++ b/solution.py
@@ -280,8 +280,13 @@
         ).astype(BF16)
 
 
-def place_kernel(depth, cell_ref, zr_ref, rank_ref, same_ref, col_ref, flag_ref, pick_ref, part_ref):
+def basis_kernel(depth, cell_ref, by_ref, after_ref, lp_ref):
+    basis_rows(depth, cell_ref, by_ref, lp_ref)
+
+
+def place_kernel(depth, cell_ref, by_ref, zr_ref, rank_ref, same_ref, lp_ref, col_ref, flag_ref, pick_ref, part_ref):
     devices = cell_ref.shape[0]
+    basis_rows(depth, cell_ref, by_ref, lp_ref)
     shared = same_ref.shape[0]
     down = lax.broadcasted_iota(jnp.int32, (LANES, LANES), 0)
     along = lax.broadcasted_iota(jnp.int32, (LANES, LANES), 1)
@@ -343,9 +348,10 @@
     @pl.when(few)
     def _():
         pick_rows(rank_ref, pick_ref)
-        picked = mm_nt(xs_ref[...], pick_ref[...]).astype(BF16)
-        total = fold_parts(mm(picked, same_ref[...]))
-        parts = jnp.concatenate(three_parts(total)[0 : xs_ref.shape[0] // WIDTH], axis=0)
+        picked = mm_nt(pick_ref[...], xs_ref[...]).astype(BF16)
+        total = mm(same_ref[...], picked).T
+        parts = three_parts(fold_parts(total))[0 : xs_ref.shape[0] // WIDTH]
+        parts = jnp.concatenate(parts, axis=0)
         for pair in range(devices // 2):
             span = slice(pair * 2 * LANES, (pair + 1) * 2 * LANES)
             got = fold_parts(mm(parts, pick_ref[:, span]))
@@ -386,7 +392,7 @@
                 ]
 
 
-def cell_kernel(depth, rx_ref, cell_ref, rank_ref, same_ref, zr_ref, by_ref, msg_ref, lat_ref, sums_ref, pick_ref, full_ref, col_ref, xs_ref, rp_ref, lp_ref):
+def cell_kernel(rx_ref, cell_ref, rank_ref, same_ref, zr_ref, lp_ref, msg_ref, lat_ref, sums_ref, pick_ref, full_ref, col_ref, xs_ref, rp_ref):
     devices = rx_ref.shape[0]
     for block in range(devices):
         xs_ref[:, block * LANES : (block + 1) * LANES] = rx_ref[block, 0:WIDTH, :]
@@ -394,7 +400,6 @@
         lambda span: xs_ref[:, span].astype(F32),
         xs_ref, cell_ref, rank_ref, same_ref, sums_ref, pick_ref, full_ref, col_ref,
     )
-    basis_rows(depth, cell_ref, by_ref, lp_ref)
     for pair in range(devices // 2):
         cut = slice(pair * 2 * LANES, (pair + 1) * 2 * LANES)
         latent = sums_ref[:, cut]
@@ -416,7 +421,16 @@
     return pltpu.roll(values, WIDTH, 1)
 
 
-def mode_kernel(group_ref, rx_ref, own_ref, other_ref, table_ref, back_ref, msg_ref, spec_ref, sp_ref, mx_ref):
+def weight_kernel(group_ref, own_ref, other_ref, weight_ref):
+    for order in range(MODES):
+        source, which = order // 2, order % 2
+        mine = jnp.full((WIDTH, LANES), group_ref[0], jnp.int32) == which
+        weight_ref[order] = jnp.where(
+            mine, own_ref[source].astype(F32), other_ref[source].astype(F32)
+        ).astype(BF16)
+
+
+def mode_kernel(rx_ref, weight_ref, table_ref, back_ref, msg_ref, spec_ref, sp_ref, mx_ref):
     devices = rx_ref.shape[0]
     own_rows = spec_ref.shape[1]
     modes = table_ref.shape[0]
@@ -427,18 +441,11 @@
         spec_ref[dest] = sp_ref[dest * own_rows : (dest + 1) * own_rows, :].astype(BF16)
     left = lax.broadcasted_iota(jnp.int32, (levels, LANES), 1) < WIDTH
     for order in range(MODES):
-        source, which = order // 2, order % 2
-        mine = jnp.full((WIDTH, LANES), group_ref[0], jnp.int32) == which
-        weight = jnp.where(
-            mine,
-            own_ref[source].astype(F32),
-            other_ref[source].astype(F32),
-        ).astype(BF16)
         at = order * 2 * levels
         even = sp_ref[at : at + levels, :]
         odd = sp_ref[at + levels : at + 2 * levels, :]
         rows = jnp.concatenate([even, swap_halves(even), odd, swap_halves(odd)], axis=0)
-        out = mm(rows[:, 0:WIDTH].astype(BF16), weight)
+        out = mm(rows[:, 0:WIDTH].astype(BF16), weight_ref[order])
         mx_ref[at : at + levels, :] = jnp.where(
             left, out[0:levels], swap_halves(out[levels : 2 * levels])
         )
@@ -452,9 +459,13 @@
             msg_ref[dest, level * step : (level + 1) * step, :] = out[dest * step : (dest + 1) * step]
 
 
-def pre_kernel(depth, rx_ref, by_ref, lat_ref, cell_ref, skip_ref, bias_ref, msg_ref, pre_ref, rt_ref, lp_ref):
+def skip_kernel(depth, cell_ref, by_ref, after_ref, lat_ref, skip_ref, bias_ref, lp_ref, term_ref):
+    basis_rows(depth, cell_ref, by_ref, lp_ref)
+    term_ref[...] = mm_tn(skip_ref[...], lat_ref[...]) + bias_ref[...]
+
+
+def pre_kernel(depth, rx_ref, lp_ref, term_ref, cell_ref, spec_ref, msg_ref, pre_ref, rt_ref):
     devices = rx_ref.shape[0]
-    basis_rows(depth, cell_ref, by_ref, lp_ref)
     rows = lp_ref.shape[0]
     step = rows // devices
     for level in range(rt_ref.shape[0] // LANES):
@@ -467,24 +478,26 @@
         total = jnp.where(zpos == 0, field[0:WIDTH], 0.0)
         for level in range(1, depth):
             total += jnp.where(zpos == level, field[level * WIDTH : (level + 1) * WIDTH], 0.0)
-        pre = total + mm_tn(skip_ref[...], lat_ref[:, cut]) + bias_ref[...]
+        pre = total + term_ref[:, cut]
         pre_ref[:, cut] = pre
         feats = gelu_value(pre).astype(BF16)
         for half in range(2):
-            msg_ref[2 * pair + half] = feats[:, half * LANES : (half + 1) * LANES]
+            dest = 2 * pair + half
+            msg_ref[dest, 0:WIDTH, :] = feats[:, half * LANES : (half + 1) * LANES]
+            msg_ref[dest, WIDTH:, :] = spec_ref[dest]
 
 
 def slope_kernel(pre_ref, slope_ref):
     slope_ref[...] = gelu_slope(pre_ref[...])
 
 
-def head_kernel(rx_ref, point_ref, pw_ref, head_ref, bias_ref, out_ref, area_ref, normal_ref, pres_ref, msg_ref, value_ref, hot_ref):
+def head_kernel(rx_ref, point_ref, pw_ref, head_ref, bias_ref, out_ref, area_ref, normal_ref, pres_ref, msg_ref, spec_ref, value_ref, hot_ref):
     devices = rx_ref.shape[0]
     points = area_ref.shape[1]
     rows = lax.broadcasted_iota(jnp.int32, (points, LANES), 0)
     for block in range(devices):
         cut = slice(block * LANES, (block + 1) * LANES)
-        parts = three_parts(pw_ref[block : block + 1, :] * rx_ref[block].astype(F32))
+        parts = three_parts(pw_ref[block : block + 1, :] * rx_ref[block, 0:WIDTH, :].astype(F32))
         for index, part in enumerate(parts):
             value_ref[index * WIDTH : (index + 1) * WIDTH, cut] = part
         hot_ref[:, cut] = jnp.where(rows == point_ref[block : block + 1, :], 1.0, 0.0).astype(BF16)
@@ -535,6 +548,7 @@
             for index, part in enumerate(three_parts(pw_ref[block : block + 1, :])):
                 tail = jnp.where(place == index, part.astype(F32), tail)
             msg_ref[block, WIDTH : WIDTH + 16, :] = tail.astype(BF16)
+            spec_ref[block] = rx_ref[block, WIDTH:, :]
 
 
 def fold_rows(values):
@@ -544,7 +558,7 @@
     return upper, lower
 
 
-def back_kernel(depth, scale, rx_ref, target_ref, cell_ref, rank_ref, same_ref, zr_ref, by_ref, lat_ref, slope_ref, msg_ref, force_ref, outg_ref, sums_ref, pick_ref, full_ref, col_ref, xs_ref, pg_ref, rp_ref, lp_ref, gp_ref):
+def back_kernel(scale, rx_ref, target_ref, cell_ref, rank_ref, same_ref, zr_ref, lp_ref, lat_ref, slope_ref, msg_ref, force_ref, outg_ref, sums_ref, pick_ref, full_ref, col_ref, xs_ref, pg_ref, rp_ref, gp_ref):
     devices = rx_ref.shape[0]
     main = msg_ref.shape[1] - 16
     extra = slice(WIDTH, WIDTH + 16)
@@ -574,7 +588,6 @@
         lambda span: gp_ref[:, span],
         xs_ref, cell_ref, rank_ref, same_ref, sums_ref, pick_ref, full_ref, col_ref,
     )
-    basis_rows(depth, cell_ref, by_ref, lp_ref)
     for pair in range(devices // 2):
         cut = slice(pair * 2 * LANES, (pair + 1) * 2 * LANES)
         grad = sums_ref[:, cut] * slope_ref[:, cut]
@@ -589,9 +602,8 @@
         msg_ref[dest, main : main + 16, :] = rows.astype(BF16)
 
 
-def spec_kernel(half_ref, rx_ref, table_ref, spec_ref, msg_ref, sp_ref):
-    peers = rx_ref.shape[0]
-    devices, own_rows = spec_ref.shape[0], spec_ref.shape[1]
+def spec_kernel(half_ref, rx_ref, table_ref, msg_ref, sp_ref):
+    peers, devices = rx_ref.shape[0], msg_ref.shape[0]
     part_rows = sp_ref.shape[0] // devices
     main = rx_ref.shape[1] - 16
     to_modes(rx_ref, table_ref[half_ref[0]], sp_ref)
@@ -605,47 +617,44 @@
     upper = first.astype(F32) + swap_halves(second.astype(F32))
     rows = jnp.concatenate([upper, third.astype(F32)], axis=0).astype(BF16)
     for dest in range(devices):
-        msg_ref[dest, 0:own_rows, :] = spec_ref[dest]
-        msg_ref[dest, own_rows : own_rows + part_rows, :] = sp_ref[
-            dest * part_rows : (dest + 1) * part_rows, :
-        ].astype(BF16)
-        msg_ref[dest, own_rows + part_rows : own_rows + part_rows + 16, :] = rows
-
-
-def both_halves(values):
-    return jnp.concatenate([values, swap_halves(values)], axis=0)[:, 0:WIDTH]
-
-
-def final_kernel(peers, rx_ref, spec_ref, skip_ref):
+        msg_ref[dest, 0:part_rows, :] = sp_ref[dest * part_rows : (dest + 1) * part_rows, :].astype(BF16)
+        msg_ref[dest, part_rows : part_rows + 16, :] = rows
+
+
+def final_kernel(peers, rx_ref, own_ref, spec_ref, skip_ref):
     devices = rx_ref.shape[0]
     low = MODES // devices
     high = MODES // peers
     owned = spec_ref.shape[0] // MODES
-    part_rows = owned * high * 8
-    own_rows = rx_ref.shape[1] - 16 - part_rows
+    part_rows = rx_ref.shape[1] - 16
+    left = lax.broadcasted_iota(jnp.int32, (8, LANES), 1) < WIDTH
     for which in range(owned):
         for source in range(devices):
             at = which * 8 * low
-            coeffs = rx_ref[source, at : at + 8 * low, :].astype(F32)
+            coeffs = own_ref[source, at : at + 8 * low, :].astype(F32)
+            first, second = coeffs[0:8], coeffs[8:16]
+            block = [
+                jnp.where(left, first, 0.0),
+                jnp.where(left, swap_halves(first), 0.0),
+                jnp.where(left, 0.0, swap_halves(second)),
+                jnp.where(left, 0.0, second),
+            ]
             peer, inner = divmod(low * source, high)
-            at = own_rows + (which * high + inner) * 8
-            grads = [
-                rx_ref[peer + shift, at : at + 8 * low, :].astype(F32)
-                for shift in range(0, devices, peers)
-            ]
-            for index in range(low):
-                cut = slice(8 * index, 8 * index + 8)
-                left = both_halves(coeffs[cut])
-                left = jnp.concatenate([left] * len(grads), axis=0)
-                right = jnp.concatenate([both_halves(part[cut]) for part in grads], axis=0)
-                spec_ref[which * MODES + low * source + index] = mm_tn(
-                    left.astype(BF16), right.astype(BF16)
-                )
-    at = own_rows + part_rows
+            at = (which * high + inner) * 8
+            grads = []
+            for shift in range(0, devices, peers):
+                part = rx_ref[peer + shift, at : at + 8 * low, :].astype(F32)
+                grads += [part[0:8], swap_halves(part[0:8]), part[8:16], swap_halves(part[8:16])]
+            block = jnp.concatenate(block * (devices // peers), axis=0).astype(BF16)
+            grads = jnp.concatenate(grads, axis=0)[:, 0:WIDTH].astype(BF16)
+            found = mm_tn(block, grads)
+            mode = which * MODES + low * source
+            spec_ref[mode] = found[0:WIDTH]
+            spec_ref[mode + 1] = found[WIDTH : 2 * WIDTH]
     for peer in range(peers):
-        rows = rx_ref[peer, at : at + 16, :].astype(F32)
+        rows = rx_ref[peer, part_rows : part_rows + 16, :].astype(F32)
         for shift in range(peers, devices, peers):
-            rows += rx_ref[peer + shift, at : at + 16, :].astype(F32)
+            rows += rx_ref[peer + shift, part_rows : part_rows + 16, :].astype(F32)
         value = (rows[0:8] + swap_halves(rows[0:8]) + rows[8:16])[:, 0:WIDTH]
         skip_ref[8 * peer : 8 * peer + 8, :] = value
 
@@ -742,14 +751,15 @@
     )
     rx = exchange(msg)
     shared = 384
-    zr, rank, same = run(
+    zr, rank, same, lp = run(
         functools.partial(place_kernel, depth),
         [
             shape((n, LANES), jnp.int32),
             shape((n, LANES), jnp.int32),
             shape((shared, shared), BF16),
+            shape((rows, slots), BF16),
         ],
-        [cells],
+        [cells, by_rows],
         2 * rows * LANES * slots,
         scratch=[
             pltpu.VMEM((slots, LANES), F32),
@@ -767,57 +777,79 @@
     own = rx[:, WIDTH : 2 * WIDTH, :]
     other = lax.ppermute(own, "groups", [(0, 1), (1, 0)])
     pair_rows = pltpu.VMEM((WIDTH, slots), BF16)
-    basis = pltpu.VMEM((rows, slots), BF16)
+    basis = shape((rows, slots), BF16)
     deep_rows = pltpu.VMEM((depth * WIDTH, slots), BF16)
     big = 2 * WIDTH * slots * slots + 2 * rows * slots * depth * WIDTH
     msg, lat = run(
-        functools.partial(cell_kernel, depth),
+        cell_kernel,
         [shape((n, main, LANES), BF16), shape((WIDTH, slots), BF16)],
-        [rx, cells, rank, same, zr, by_rows],
+        [rx, cells, rank, same, zr, lp],
         big,
-        scratch=sum_scratch + [pair_rows, deep_rows, basis],
+        scratch=sum_scratch + [pair_rows, deep_rows],
         grant=20,
     )
     columns = exchange(msg)
+    (weights,) = run(
+        weight_kernel,
+        [shape((MODES, WIDTH, LANES), BF16)],
+        [group, own, other],
+        MODES * WIDTH * LANES,
+        smem=1,
+    )
     msg, spec = run(
         mode_kernel,
         [shape((n, main, LANES), BF16), shape((n, own_rows, LANES), BF16)],
-        [group, columns, own, other, table, back],
+        [columns, weights, table, back],
         4 * MODES * low * rows * depth * WIDTH,
         scratch=[pltpu.VMEM((MODES * low * levels, LANES), F32)] * 2,
-        smem=1,
     )
     slabs = exchange(msg)
+    lp, term = run(
+        functools.partial(skip_kernel, depth),
+        [basis, shape((WIDTH, slots), F32)],
+        [cells, by_rows, spec, lat, skip_weight, skip_bias.reshape(WIDTH, 1)],
+        2 * rows * LANES * slots,
+    )
     msg, pre = run(
         functools.partial(pre_kernel, depth),
-        [shape((n, WIDTH, LANES), BF16), shape((WIDTH, slots), F32)],
-        [slabs, by_rows, lat, cells, skip_weight, skip_bias.reshape(WIDTH, 1)],
+        [shape((n, WIDTH + own_rows, LANES), BF16), shape((WIDTH, slots), F32)],
+        [slabs, lp, term, cells, spec],
         2 * rows * slots * depth * WIDTH,
-        scratch=[pltpu.VMEM((depth * WIDTH, rows), BF16), basis],
+        scratch=[pltpu.VMEM((depth * WIDTH, rows), BF16)],
     )
     returned = exchange(msg)
     (slope,) = run(slope_kernel, [shape(pre.shape, F32)], [pre], 100 * WIDTH * slots)
     out_col = out_weight.reshape(WIDTH, 1)
-    pressure, msg = run(
+    pressure, msg, own_spec = run(
         head_kernel,
-        [shape((1, points), F32), shape((n, WIDTH + 16, LANES), BF16)],
+        [
+            shape((1, points), F32),
+            shape((n, WIDTH + 16, LANES), BF16),
+            shape((n, own_rows, LANES), BF16),
+        ],
         [returned, point_rows, pw, head_weight, head_bias.reshape(WIDTH, 1), out_col, area_row, normals],
         2 * 3 * WIDTH * points * slots,
         scratch=[pltpu.VMEM((3 * WIDTH, slots), BF16), pltpu.VMEM((points, slots), BF16)],
     )
     grads = exchange(msg)
+    (lp,) = run(
+        functools.partial(basis_kernel, depth),
+        [basis],
+        [cells, by_rows, pressure],
+        2 * rows * LANES * slots,
+    )
     scale = 1.0 / math.sqrt(points * n)
     msg, forces, out_grad = run(
-        functools.partial(back_kernel, depth, scale),
+        functools.partial(back_kernel, scale),
         [
             shape((peers, halves * main + 16, LANES), BF16),
             shape((1, 2), F32),
             shape((1, WIDTH), F32),
         ],
-        [grads, targets.reshape(1, 2), cells, rank, same, zr, by_rows, lat, slope],
+        [grads, targets.reshape(1, 2), cells, rank, same, zr, lp, lat, slope],
         big,
         scratch=sum_scratch
-        + [pltpu.VMEM((2 * WIDTH, slots), BF16), pair_rows, deep_rows, basis]
+        + [pltpu.VMEM((2 * WIDTH, slots), BF16), pair_rows, deep_rows]
         + [pltpu.VMEM((WIDTH, slots), F32)],
         grant=20,
     )
@@ -827,8 +859,8 @@
     part_rows = MODES * high * levels // n
     (msg,) = run(
         spec_kernel,
-        [shape((n, own_rows + part_rows + 16, LANES), BF16)],
-        [half, grad_columns, part_table, spec],
+        [shape((n, part_rows + 16, LANES), BF16)],
+        [half, grad_columns, part_table],
         2 * MODES * high * rows * depth * WIDTH,
         scratch=[pltpu.VMEM((MODES * high * levels, LANES), F32)],
         smem=1,
@@ -837,7 +869,7 @@
     spec_grad, skip_grad = run(
         functools.partial(final_kernel, peers),
         [shape((spec_weight.shape[0], WIDTH, WIDTH), F32), shape((WIDTH, WIDTH), F32)],
-        [finals],
+        [finals, own_spec],
         2 * NMODE * WIDTH * WIDTH * depth // n,
     )
     return (pressure.reshape(points), forces.reshape(2), spec_grad, skip_grad, out_grad.reshape(WIDTH))

time: 139 us -> 139 us (level)
  blocking collectives: 16.7 us -> 14.6 us
    all_to_all x1, blocking collectives: 16.7 us -> 14.6 us  [exchange(): lax.all_to_all(message, 'gx', split_axis=0, concat_axis=0, tiled=True)]
    pallas_call x10 -> x13, Pallas kernels: 23.1 us -> 24.1 us  [run(): pl.pallas_call(kernel, out_shape=tuple(outs), in_specs=[scalar] * smem +...]
  transfers between devices with their start and end apart: 7 -> 7, of which waited for: 7 -> 7; matrix products, arithmetic and copies ran while one was open for 0% -> 0% of each run, Pallas kernels for 2% -> 3%
where the time goes in v6:
time: 139 us; the launch traced here: 138 us
  waiting for transfers between devices  68.8 us (49%)
  starting transfers between devices  28.5 us (21%)
  Pallas kernels  24.1 us (17%)
  blocking collectives  14.6 us (11%)
    all_to_all x5, waiting for transfers between devices, exchange(): lax.all_to_all(message, 'gx', split_axis=0, concat_axis=0, tiled=True)  52.6 us
    pallas_call x13, Pallas kernels, run(): pl.pallas_call(kernel, out_shape=tuple(outs), in_specs=[scalar] * smem +...  24.1 us
    all_to_all x5, starting transfers between devices, exchange(): lax.all_to_all(message, 'gx', split_axis=0, concat_axis=0, tiled=True)  23.4 us
    all_to_all x1, blocking collectives, exchange(): lax.all_to_all(message, 'gx', split_axis=0, concat_axis=0, tiled=True)  14.6 us
    all_to_all x1, waiting for transfers between devices, slab_step(): lax.all_to_all(msg, 'gx', split_axis=0, concat_axis=0, tiled=True, axis_i...  9.1 us
    ppermute x1, waiting for transfers between devices, slab_step(): other = lax.ppermute(own, 'groups', [(0, 1), (1, 0)])  7.15 us
    all_to_all x1, starting transfers between devices, slab_step(): lax.all_to_all(msg, 'gx', split_axis=0, concat_axis=0, tiled=True, axis_i...  3.54 us
  transfers between devices with their start and end apart: 7, of which 7 were waited for; matrix products, arithmetic and copies ran while one was open for 0% of the time, Pallas kernels for 3%

profile of v6, /device:TPU:0, one launch (start us, length us, event | category | flops | bytes accessed | tf_op | source)
XLA Modules:
  0.0 138.0 jit_solution(16414548229200741570)
XLA Ops:
  0.7 2.4 %shard_map.209 = (bf16[16,128,128]{2,1,0:T(8,128)(2,1)}, f32[16,128]{1,0:T(8,128)}) custom-call(s32[1]{0:T(128)} %bitcast.group_ref, s32[1,16]{1,0:T(1,128)} %count_hbm.1, s32[16,128]{1,0:T(8,128)} %bitcast.20, f32[16,128]{1,0:T(8,128)} %bitcast.27, f32[1,512]{1,0:T(1,128)} %bitcast.22, bf16[64,512]{1,0:T(8,128)(2,1)} %bitcast.26, bf16[64,64,64]{2,1,0:T(8,128)(2,1)} %weight_hbm.1), custom_call_target="tpu_custom_call" | custom-call | flops 167772160 | bytes 1140804 | tf_op jit(solution)/shard_map/pallas_call | solution.py:667
  3.1 7.4 %all-to-all-start = ((bf16[16,128,128]{2,1,0:T(8,128)(2,1)}), bf16[16,128,128]{2,1,0:T(8,128)(2,1)S(1)}, u32[]{:S(2)}, u32[]{:S(2)}) async-start(bf16[16,128,128]{2,1,0:T(8,128)(2,1)} %get-tuple-element.27), calls=%async_computation | async-start | bytes 1048576 | tf_op jit(solution)/shard_map/all_to_all | solution.py:728
  10.5 3.1 %shard_map.210 = (s32[16,128]{1,0:T(8,128)S(1)}, s32[16,128]{1,0:T(8,128)S(1)}, bf16[384,384]{1,0:T(8,128)(2,1)S(1)}, bf16[256,2048]{1,0:T(8,128)(2,1)S(1)}) custom-call(s32[16,128]{1,0:T(8,128)S(1)} %bitcast.14, bf16[256,128]{1,0:T(8,128)(2,1)S(1)} %copy-done), custom_call_target="tpu_custom_call" | custom-call | flops 134217728 | bytes 1433600 | tf_op jit(solution)/shard_map/pallas_call | solution.py:667
  13.7 11.3 %all-to-all-done.rx_ref = bf16[16,128,128]{2,1,0:T(8,128)(2,1)S(1)} async-done(((bf16[16,128,128]{2,1,0:T(8,128)(2,1)}), bf16[16,128,128]{2,1,0:T(8,128)(2,1)S(1)}, u32[]{:S(2)}, u32[]{:S(2)}) %all-to-all-start) | async-done | bytes 524320 | tf_op jit(solution)/shard_map/all_to_all | solution.py:728
  25.0 3.9 %shard_map.211 = (bf16[16,128,128]{2,1,0:T(8,128)(2,1)}, bf16[64,2048]{1,0:T(8,128)(2,1)S(1)}) custom-call(bf16[16,128,128]{2,1,0:T(8,128)(2,1)S(1)} %all-to-all-done.rx_ref, s32[16,128]{1,0:T(8,128)S(1)} %bitcast.15, s32[16,128]{1,0:T(8,128)S(1)} %get-tuple-element.28.rank_ref, bf16[384,384]{1,0:T(8,128)(2,1)S(1)} %get-tuple-element.29.same_ref, ...), custom_call_target="tpu_custom_call" | custom-call | flops 1610612736 | bytes 2678784 | tf_op jit(solution)/shard_map/pallas_call | solution.py:667
  28.9 4.2 %all-to-all-start.1 = ((bf16[16,128,128]{2,1,0:T(8,128)(2,1)}), bf16[16,128,128]{2,1,0:T(8,128)(2,1)S(1)}, u32[]{:S(2)}, u32[]{:S(2)}) async-start(bf16[16,128,128]{2,1,0:T(8,128)(2,1)} %get-tuple-element.32), calls=%async_computation.1 | async-start | bytes 1048576 | tf_op jit(solution)/shard_map/all_to_all | solution.py:728
  33.2 1.6 %collective-permute-start = (bf16[16,64,128]{2,1,0:T(8,128)(2,1)S(1)}, bf16[16,64,128]{2,1,0:T(8,128)(2,1)S(1)}, u32[]{:S(2)}, u32[]{:S(2)}) collective-permute-start(bf16[16,64,128]{2,1,0:T(8,128)(2,1)S(1)} %slice.4.own_ref), channel_id=1, source_target_pairs={{0,16},{16,0},{1,17},{17,1},{2,18},{18,2},{3,19},{19,3},{4,20},{20... | collective-permute-start | bytes 786440 | tf_op jit(solution)/shard_map/ppermute | solution.py:778
  34.8 7.2 %collective-permute-done.other_ref = bf16[16,64,128]{2,1,0:T(8,128)(2,1)S(1)} collective-permute-done((bf16[16,64,128]{2,1,0:T(8,128)(2,1)S(1)}, bf16[16,64,128]{2,1,0:T(8,128)(2,1)S(1)}, u32[]{:S(2)}, u32[]{:S(2)}) %collective-permute-start) | collective-permute-done | bytes 262176 | tf_op jit(solution)/shard_map/ppermute | solution.py:778
  41.9 0.1 shard_map.212.weight_ref
  42.0 5.6 %all-to-all-done.1.rx_ref = bf16[16,128,128]{2,1,0:T(8,128)(2,1)S(1)} async-done(((bf16[16,128,128]{2,1,0:T(8,128)(2,1)}), bf16[16,128,128]{2,1,0:T(8,128)(2,1)S(1)}, u32[]{:S(2)}, u32[]{:S(2)}) %all-to-all-start.1) | async-done | bytes 524320 | tf_op jit(solution)/shard_map/all_to_all | solution.py:728
  47.7 1.7 %shard_map.213 = (bf16[16,128,128]{2,1,0:T(8,128)(2,1)}, bf16[16,32,128]{2,1,0:T(8,128)(2,1)S(1)}) custom-call(bf16[16,128,128]{2,1,0:T(8,128)(2,1)S(1)} %all-to-all-done.1.rx_ref, bf16[32,64,128]{2,1,0:T(8,128)(2,1)S(1)} %shard_map.212.weight_ref, bf16[64,256]{1,0:T(8,128)(2,1)S(1)} %copy-done.4, bf16[256,64]{1,0:T(8,128)(2,1)S(1)} %copy-done.2), custom_call_target="tpu_custom_call" | custom-call | flops 67108864 | bytes 1769472 | tf_op jit(solution)/shard_map/pallas_call | solution.py:667
  49.3 4.1 %all-to-all-start.2 = ((bf16[16,128,128]{2,1,0:T(8,128)(2,1)}), bf16[16,128,128]{2,1,0:T(8,128)(2,1)S(1)}, u32[]{:S(2)}, u32[]{:S(2)}) async-start(bf16[16,128,128]{2,1,0:T(8,128)(2,1)} %get-tuple-element.33), calls=%async_computation.2 | async-start | bytes 1048576 | tf_op jit(solution)/shard_map/all_to_all | solution.py:728
  53.5 0.1 copy.23.bias_ref
  53.6 0.5 shard_map.214
  54.1 13.9 %all-to-all-done.2.rx_ref = bf16[16,128,128]{2,1,0:T(8,128)(2,1)S(1)} async-done(((bf16[16,128,128]{2,1,0:T(8,128)(2,1)}), bf16[16,128,128]{2,1,0:T(8,128)(2,1)S(1)}, u32[]{:S(2)}, u32[]{:S(2)}) %all-to-all-start.2) | async-done | bytes 524320 | tf_op jit(solution)/shard_map/all_to_all | solution.py:728
  68.0 2.1 %shard_map.215 = (bf16[16,96,128]{2,1,0:T(8,128)(2,1)}, f32[64,2048]{1,0:T(8,128)S(1)}) custom-call(bf16[16,128,128]{2,1,0:T(8,128)(2,1)S(1)} %all-to-all-done.2.rx_ref, bf16[256,2048]{1,0:T(8,128)(2,1)S(1)} %get-tuple-element.36.lp_ref, f32[64,2048]{1,0:T(8,128)S(1)} %get-tuple-element.37.term_ref, s32[16,128]{1,0:T(8,128)S(1)} %bitcast.17, ...), custom_call_target="tpu_custom_call" | custom-call | flops 1073741824 | bytes 3153920 | tf_op jit(solution)/shard_map/pallas_call | solution.py:667
  70.1 4.1 %all-to-all-start.3 = ((bf16[16,96,128]{2,1,0:T(8,128)(2,1)}), bf16[16,96,128]{2,1,0:T(8,128)(2,1)S(1)}, u32[]{:S(2)}, u32[]{:S(2)}) async-start(bf16[16,96,128]{2,1,0:T(8,128)(2,1)} %get-tuple-element.38), calls=%async_computation.3 | async-start | bytes 786432 | tf_op jit(solution)/shard_map/all_to_all | solution.py:728
  74.2 0.1 copy.24.bias_ref
  74.3 0.1 copy.25.out_ref
  74.4 12.0 %all-to-all-done.3.rx_ref = bf16[16,96,128]{2,1,0:T(8,128)(2,1)S(1)} async-done(((bf16[16,96,128]{2,1,0:T(8,128)(2,1)}), bf16[16,96,128]{2,1,0:T(8,128)(2,1)S(1)}, u32[]{:S(2)}, u32[]{:S(2)}) %all-to-all-start.3) | async-done | bytes 393248 | tf_op jit(solution)/shard_map/all_to_all | solution.py:728
  86.4 2.9 %shard_map.216 = (f32[1,512]{1,0:T(1,128)}, bf16[16,80,128]{2,1,0:T(8,128)(2,1)}, bf16[16,32,128]{2,1,0:T(8,128)(2,1)S(1)}) custom-call(bf16[16,96,128]{2,1,0:T(8,128)(2,1)S(1)} %all-to-all-done.3.rx_ref, s32[16,128]{1,0:T(8,128)S(1)} %bitcast.21, f32[16,128]{1,0:T(8,128)S(1)} %copy-done.10, bf16[64,64]{1,0:T(8,128)(2,1)S(1)} %copy-done.9, ...), custom_call_target="tpu_custom_call" | custom-call | flops 402653184 | bytes 885248 | tf_op jit(solution)/shard_map/pallas_call | solution.py:667
  89.3 3.5 %all-to-all-start.4 = ((bf16[16,80,128]{2,1,0:T(8,128)(2,1)}), bf16[16,80,128]{2,1,0:T(8,128)(2,1)S(1)}, u32[]{:S(2)}, u32[]{:S(2)}) async-start(bf16[16,80,128]{2,1,0:T(8,128)(2,1)} %get-tuple-element.41), calls=%async_computation.4 | async-start | bytes 655360 | tf_op jit(solution)/shard_map/all_to_all | solution.py:728
  92.9 0.2 shard_map.218.slope_ref
  93.1 0.7 copy-done.8
  93.8 0.4 shard_map.217.lp_ref
  94.2 9.8 %all-to-all-done.4.rx_ref = bf16[16,80,128]{2,1,0:T(8,128)(2,1)S(1)} async-done(((bf16[16,80,128]{2,1,0:T(8,128)(2,1)}), bf16[16,80,128]{2,1,0:T(8,128)(2,1)S(1)}, u32[]{:S(2)}, u32[]{:S(2)}) %all-to-all-start.4) | async-done | bytes 327712 | tf_op jit(solution)/shard_map/all_to_all | solution.py:728
  104.0 4.5 %shard_map.219 = (bf16[8,272,128]{2,1,0:T(8,128)(2,1)}, f32[1,2]{1,0:T(1,128)}, f32[1,64]{1,0:T(1,128)}) custom-call(bf16[16,80,128]{2,1,0:T(8,128)(2,1)S(1)} %all-to-all-done.4.rx_ref, f32[1,2]{1,0:T(1,128)S(1)} %bitcast.25, s32[16,128]{1,0:T(8,128)S(1)} %bitcast.19, s32[16,128]{1,0:T(8,128)S(1)} %get-tuple-element.28.rank_ref, ...), custom_call_target="tpu_custom_call" | custom-call | flops 1610612736 | bytes 3039504 | tf_op jit(solution)/shard_map/pallas_call | solution.py:667
  108.4 3.5 %all-to-all-start.5 = ((bf16[8,272,128]{2,1,0:T(8,128)(2,1)}), bf16[8,272,128]{2,1,0:T(8,128)(2,1)S(1)}, u32[]{:S(2)}, u32[]{:S(2)}) async-start(bf16[8,272,128]{2,1,0:T(8,128)(2,1)} %get-tuple-element.44), calls=%async_computation.5 | async-start | bytes 1114112 | tf_op jit(solution)/shard_map/all_to_all | solution.py:856
  112.0 9.1 %all-to-all-done.5.rx_ref = bf16[8,272,128]{2,1,0:T(8,128)(2,1)S(1)} async-done(((bf16[8,272,128]{2,1,0:T(8,128)(2,1)}), bf16[8,272,128]{2,1,0:T(8,128)(2,1)S(1)}, u32[]{:S(2)}, u32[]{:S(2)}) %all-to-all-start.5) | async-done | bytes 557088 | tf_op jit(solution)/shard_map/all_to_all | solution.py:856
  121.1 0.3 shard_map.220
  121.4 14.6 %all_to_all.35.rx_ref = bf16[16,80,128]{2,1,0:T(8,128)(2,1)S(1)} all-to-all(bf16[16,80,128]{2,1,0:T(8,128)(2,1)S(1)} %shard_map.220), channel_id=1, replica_groups=mesh['groups'=2,'gx'=16] {'gx'}, dimensions={0} | all-to-all | bytes 655360 | tf_op jit(solution)/shard_map/all_to_all | solution.py:728
  136.0 2.0 %shard_map.221 = (f32[64,64,64]{2,1,0:T(8,128)}, f32[64,64]{1,0:T(8,128)}) custom-call(bf16[16,80,128]{2,1,0:T(8,128)(2,1)S(1)} %all_to_all.35.rx_ref, bf16[16,32,128]{2,1,0:T(8,128)(2,1)S(1)} %get-tuple-element.45.own_ref), custom_call_target="tpu_custom_call" | custom-call | flops 8388608 | bytes 1523712 | tf_op jit(solution)/shard_map/pallas_call | solution.py:667
  (36 shorter events, 0.1 us)
Async XLA Ops:
  0.6 9.9 %copy-start = (bf16[256,128]{1,0:T(8,128)(2,1)S(1)}, bf16[256,128]{1,0:T(8,128)(2,1)}, u32[]{:S(2)}) copy-start(bf16[256,128]{1,0:T(8,128)(2,1)} %constant.33.clone.by_ref) | copy-start | bytes 196612
  0.6 9.9 %copy-start.3 = (s32[16,1,128]{2,1,0:T(1,128)S(1)}, s32[16,1,128]{2,1,0:T(1,128)}, u32[]{:S(2)}) copy-start(s32[16,1,128]{2,1,0:T(1,128)} %param.20) | copy-start | bytes 24580
  3.1 21.9 %all-to-all-start = ((bf16[16,128,128]{2,1,0:T(8,128)(2,1)}), bf16[16,128,128]{2,1,0:T(8,128)(2,1)S(1)}, u32[]{:S(2)}, u32[]{:S(2)}) async-start(bf16[16,128,128]{2,1,0:T(8,128)(2,1)} %get-tuple-element.27), calls=%async_computation | async-start | bytes 1048576 | tf_op jit(solution)/shard_map/all_to_all | solution.py:728
  13.6 15.3 %copy-start.13 = (bf16[384,384]{1,0:T(8,128)(2,1)}, bf16[384,384]{1,0:T(8,128)(2,1)S(1)}, u32[]{:S(2)}) copy-start(bf16[384,384]{1,0:T(8,128)(2,1)S(1)} %get-tuple-element.29.same_ref) | copy-start | bytes 884740
  28.9 18.7 %copy-start.2 = (bf16[256,64]{1,0:T(8,128)(2,1)S(1)}, bf16[256,64]{1,0:T(8,128)(2,1)}, u32[]{:S(2)}) copy-start(bf16[256,64]{1,0:T(8,128)(2,1)} %constant.34.clone.back_ref) | copy-start | bytes 98308
  28.9 18.7 %copy-start.4 = (bf16[64,256]{1,0:T(8,128)(2,1)S(1)}, bf16[64,256]{1,0:T(8,128)(2,1)}, u32[]{:S(2)}) copy-start(bf16[64,256]{1,0:T(8,128)(2,1)} %constant.35.clone.table_ref) | copy-start | bytes 98308
  28.9 18.7 %all-to-all-start.1 = ((bf16[16,128,128]{2,1,0:T(8,128)(2,1)}), bf16[16,128,128]{2,1,0:T(8,128)(2,1)S(1)}, u32[]{:S(2)}, u32[]{:S(2)}) async-start(bf16[16,128,128]{2,1,0:T(8,128)(2,1)} %get-tuple-element.32), calls=%async_computation.1 | async-start | bytes 1048576 | tf_op jit(solution)/shard_map/all_to_all | solution.py:728
  33.2 20.3 %copy-start.15 = (f32[64]{0:T(128)S(1)}, f32[64]{0:T(128)}, u32[]{:S(2)}) copy-start(f32[64]{0:T(128)} %param.28) | copy-start | bytes 772
  33.2 20.4 %copy-start.5 = (bf16[64,64]{1,0:T(8,128)(2,1)S(1)}, bf16[64,64]{1,0:T(8,128)(2,1)}, u32[]{:S(2)}) copy-start(bf16[64,64]{1,0:T(8,128)(2,1)} %skip_ref.1) | copy-start | bytes 24580
  33.2 8.7 %collective-permute-start = (bf16[16,64,128]{2,1,0:T(8,128)(2,1)S(1)}, bf16[16,64,128]{2,1,0:T(8,128)(2,1)S(1)}, u32[]{:S(2)}, u32[]{:S(2)}) collective-permute-start(bf16[16,64,128]{2,1,0:T(8,128)(2,1)S(1)} %slice.4.own_ref), channel_id=1, source_target_pairs={{0,16},{16,0},{1,17},{17,1},{2,18},{18,2},{3,19},{19,3},{4,20},{20... | collective-permute-start | bytes 786440 | tf_op jit(solution)/shard_map/ppermute | solution.py:778
  49.3 18.6 %all-to-all-start.2 = ((bf16[16,128,128]{2,1,0:T(8,128)(2,1)}), bf16[16,128,128]{2,1,0:T(8,128)(2,1)S(1)}, u32[]{:S(2)}, u32[]{:S(2)}) async-start(bf16[16,128,128]{2,1,0:T(8,128)(2,1)} %get-tuple-element.33), calls=%async_computation.2 | async-start | bytes 1048576 | tf_op jit(solution)/shard_map/all_to_all | solution.py:728
  67.9 6.2 %copy-start.16 = (f32[64]{0:T(128)S(1)}, f32[64]{0:T(128)}, u32[]{:S(2)}) copy-start(f32[64]{0:T(128)} %param.30) | copy-start | bytes 772
  67.9 6.3 %copy-start.17 = (f32[64]{0:T(128)S(1)}, f32[64]{0:T(128)}, u32[]{:S(2)}) copy-start(f32[64]{0:T(128)} %param.31) | copy-start | bytes 772
  67.9 18.4 %copy-start.6 = (s32[1,16,128]{2,1,0:T(8,128)S(1)}, s32[1,16,128]{2,1,0:T(8,128)}, u32[]{:S(2)}) copy-start(s32[1,16,128]{2,1,0:T(8,128)} %param.19) | copy-start | bytes 24580
  67.9 18.4 %copy-start.7 = (f32[512]{0:T(512)S(1)}, f32[512]{0:T(512)}, u32[]{:S(2)}) copy-start(f32[512]{0:T(512)} %param.23) | copy-start | bytes 6148
  67.9 18.4 %copy-start.9 = (bf16[64,64]{1,0:T(8,128)(2,1)S(1)}, bf16[64,64]{1,0:T(8,128)(2,1)}, u32[]{:S(2)}) copy-start(bf16[64,64]{1,0:T(8,128)(2,1)} %head_ref.1) | copy-start | bytes 24580
  67.9 18.4 %copy-start.10 = (f32[16,128]{1,0:T(8,128)S(1)}, f32[16,128]{1,0:T(8,128)}, u32[]{:S(2)}) copy-start(f32[16,128]{1,0:T(8,128)} %get-tuple-element.39.pw_ref) | copy-start | bytes 24580
  68.0 18.4 %copy-start.11 = (f32[2,512]{1,0:T(2,128)S(1)}, f32[2,512]{1,0:T(2,128)}, u32[]{:S(2)}) copy-start(f32[2,512]{1,0:T(2,128)} %normal_ref.1) | copy-start | bytes 12292
  70.1 16.3 %all-to-all-start.3 = ((bf16[16,96,128]{2,1,0:T(8,128)(2,1)}), bf16[16,96,128]{2,1,0:T(8,128)(2,1)S(1)}, u32[]{:S(2)}, u32[]{:S(2)}) async-start(bf16[16,96,128]{2,1,0:T(8,128)(2,1)} %get-tuple-element.38), calls=%async_computation.3 | async-start | bytes 786432 | tf_op jit(solution)/shard_map/all_to_all | solution.py:728
  86.4 17.6 %copy-start.12 = (f32[2]{0:T(128)S(1)}, f32[2]{0:T(128)}, u32[]{:S(2)}) copy-start(f32[2]{0:T(128)} %param.25) | copy-start | bytes 28
  86.4 17.6 %copy-start.14 = (bf16[384,384]{1,0:T(8,128)(2,1)S(1)}, bf16[384,384]{1,0:T(8,128)(2,1)}, u32[]{:S(2)}) copy-start(bf16[384,384]{1,0:T(8,128)(2,1)} %copy-done.13) | copy-start | bytes 884740
  89.3 14.6 %all-to-all-start.4 = ((bf16[16,80,128]{2,1,0:T(8,128)(2,1)}), bf16[16,80,128]{2,1,0:T(8,128)(2,1)S(1)}, u32[]{:S(2)}, u32[]{:S(2)}) async-start(bf16[16,80,128]{2,1,0:T(8,128)(2,1)} %get-tuple-element.41), calls=%async_computation.4 | async-start | bytes 655360 | tf_op jit(solution)/shard_map/all_to_all | solution.py:728
  93.1 0.7 copy-start.8
  104.0 17.1 %copy-start.1 = (bf16[2,128,256]{2,1,0:T(8,128)(2,1)S(1)}, bf16[2,128,256]{2,1,0:T(8,128)(2,1)}, u32[]{:S(2)}) copy-start(bf16[2,128,256]{2,1,0:T(8,128)(2,1)} %constant.36.clone.table_ref) | copy-start | bytes 393220
  108.4 12.7 %all-to-all-start.5 = ((bf16[8,272,128]{2,1,0:T(8,128)(2,1)}), bf16[8,272,128]{2,1,0:T(8,128)(2,1)S(1)}, u32[]{:S(2)}, u32[]{:S(2)}) async-start(bf16[8,272,128]{2,1,0:T(8,128)(2,1)} %get-tuple-element.44), calls=%async_computation.5 | async-start | bytes 1114112 | tf_op jit(solution)/shard_map/all_to_all | solution.py:856

commit v7 on v6

--- a/solution.py
+++ b/solution.py
@@ -284,39 +284,29 @@
     basis_rows(depth, cell_ref, by_ref, lp_ref)
 
 
-def place_kernel(depth, cell_ref, by_ref, zr_ref, rank_ref, same_ref, lp_ref, col_ref, flag_ref, pick_ref, part_ref):
+def place_kernel(depth, cell_ref, by_ref, zr_ref, rank_ref, home_ref, lp_ref, col_ref, flag_ref, pick_ref, part_ref):
     devices = cell_ref.shape[0]
     basis_rows(depth, cell_ref, by_ref, lp_ref)
-    shared = same_ref.shape[0]
     down = lax.broadcasted_iota(jnp.int32, (LANES, LANES), 0)
     along = lax.broadcasted_iota(jnp.int32, (LANES, LANES), 1)
     place = lax.broadcasted_iota(jnp.int32, (16, LANES), 0)
     for block in range(devices):
         cells = cell_ref[block : block + 1, :]
+        row = cells.astype(F32)
         cut = slice(block * LANES, (block + 1) * LANES)
-        col_ref[cut, :] = columns_of(cells.astype(F32))
+        col_ref[cut, :] = columns_of(row)
         high = jnp.right_shift(cells, 7).astype(F32)
         low = jnp.bitwise_and(cells, 127).astype(F32)
         part_ref[:, cut] = jnp.where(place == 0, high, jnp.where(place == 1, low, 0.0)).astype(BF16)
-    for block in range(devices):
-        cells = cell_ref[block : block + 1, :]
-        row = cells.astype(F32)
-        cut = slice(block * LANES, (block + 1) * LANES)
-        same = jnp.where(col_ref[cut, :] == row, 1.0, 0.0)
-        before = jnp.sum(jnp.where(down < along, same, 0.0), axis=0, keepdims=True)
-        count = jnp.sum(same, axis=0, keepdims=True)
+        same = jnp.logical_and(col_ref[cut, :] == row, down < along)
+        before = jnp.max(jnp.where(same, 1.0, 0.0), axis=0, keepdims=True)
         if block:
             early = jnp.where(col_ref[0 : block * LANES, :] == row, 1.0, 0.0)
-            early = jnp.sum(early, axis=0, keepdims=True)
-            before += early
-            count += early
-        if block < devices - 1:
-            late = jnp.where(col_ref[(block + 1) * LANES :, :] == row, 1.0, 0.0)
-            count += jnp.sum(late, axis=0, keepdims=True)
+            before = jnp.maximum(before, jnp.max(early, axis=0, keepdims=True))
         zr_ref[block : block + 1, :] = jnp.where(
             before > 0.0, -1, jnp.bitwise_and(cells, depth - 1)
         )
-        flag_ref[block : block + 1, :] = jnp.where(count > 1.0, 1.0, 0.0)
+        flag_ref[block : block + 1, :] = before
     flags = flag_ref[...]
     marks = flags.astype(BF16)
     inside = mm(marks, jnp.where(down <= along, 1.0, 0.0).astype(BF16))
@@ -326,10 +316,17 @@
     pick_rows(rank_ref, pick_ref)
     found = mm_nt(part_ref[...], pick_ref[...])
     found = found[0:1] * 128.0 + found[1:2]
-    for block in range(shared // LANES):
-        column = columns_of(found[:, block * LANES : (block + 1) * LANES])
-        same_ref[block * LANES : (block + 1) * LANES, :] = jnp.where(
-            jnp.concatenate([column] * (shared // LANES), axis=1) == found, 1.0, 0.0
+    for block in range(home_ref.shape[0] // LANES):
+        cut = slice(block * LANES, (block + 1) * LANES)
+        home_ref[cut, :] = columns_of(found[:, cut])
+
+
+def first_rows(cell_ref, zr_ref, home_ref, first_ref):
+    for block in range(cell_ref.shape[0]):
+        here = slice(block, block + 1)
+        row = jnp.where(zr_ref[here, :] < 0, -1.0, cell_ref[here, :].astype(F32))
+        first_ref[:, block * LANES : (block + 1) * LANES] = jnp.where(
+            home_ref[...] == row, 1.0, 0.0
         ).astype(BF16)
 
 
@@ -340,22 +337,18 @@
     return total
 
 
-def sum_cells(terms, xs_ref, cell_ref, rank_ref, same_ref, sums_ref, pick_ref, full_ref, col_ref):
+def sum_cells(terms, xs_ref, cell_ref, rank_ref, zr_ref, home_ref, sums_ref, pick_ref, first_ref, full_ref, col_ref):
     devices = cell_ref.shape[0]
-    shared = same_ref.shape[0]
-    few = jnp.max(rank_ref[...]) < shared
+    few = jnp.max(rank_ref[...]) < home_ref.shape[0]
 
     @pl.when(few)
     def _():
         pick_rows(rank_ref, pick_ref)
-        picked = mm_nt(pick_ref[...], xs_ref[...]).astype(BF16)
-        total = mm(same_ref[...], picked).T
-        parts = three_parts(fold_parts(total))[0 : xs_ref.shape[0] // WIDTH]
-        parts = jnp.concatenate(parts, axis=0)
+        first_rows(cell_ref, zr_ref, home_ref, first_ref)
+        moved = mm_nt(xs_ref[...], pick_ref[...]).astype(BF16)
         for pair in range(devices // 2):
             span = slice(pair * 2 * LANES, (pair + 1) * 2 * LANES)
-            got = fold_parts(mm(parts, pick_ref[:, span]))
-            sums_ref[:, span] = jnp.where(two_rows(rank_ref, pair) < 0, terms(span), got)
+            sums_ref[:, span] = terms(span) + fold_parts(mm(moved, first_ref[:, span]))
 
     @pl.when(jnp.logical_not(few))
     def _():
@@ -392,13 +385,13 @@
                 ]
 
 
-def cell_kernel(rx_ref, cell_ref, rank_ref, same_ref, zr_ref, lp_ref, msg_ref, lat_ref, sums_ref, pick_ref, full_ref, col_ref, xs_ref, rp_ref):
+def cell_kernel(rx_ref, cell_ref, rank_ref, zr_ref, home_ref, lp_ref, msg_ref, lat_ref, sums_ref, pick_ref, first_ref, full_ref, col_ref, xs_ref, rp_ref):
     devices = rx_ref.shape[0]
     for block in range(devices):
         xs_ref[:, block * LANES : (block + 1) * LANES] = rx_ref[block, 0:WIDTH, :]
     sum_cells(
         lambda span: xs_ref[:, span].astype(F32),
-        xs_ref, cell_ref, rank_ref, same_ref, sums_ref, pick_ref, full_ref, col_ref,
+        xs_ref, cell_ref, rank_ref, zr_ref, home_ref, sums_ref, pick_ref, first_ref, full_ref, col_ref,
     )
     for pair in range(devices // 2):
         cut = slice(pair * 2 * LANES, (pair + 1) * 2 * LANES)
@@ -459,9 +452,17 @@
             msg_ref[dest, level * step : (level + 1) * step, :] = out[dest * step : (dest + 1) * step]
 
 
-def skip_kernel(depth, cell_ref, by_ref, after_ref, lat_ref, skip_ref, bias_ref, lp_ref, term_ref):
+def skip_kernel(depth, cell_ref, by_ref, after_ref, rank_ref, zr_ref, home_ref, lat_ref, skip_ref, bias_ref, lp_ref, term_ref, pick_ref, first_ref):
     basis_rows(depth, cell_ref, by_ref, lp_ref)
-    term_ref[...] = mm_tn(skip_ref[...], lat_ref[...]) + bias_ref[...]
+    few = jnp.max(rank_ref[...]) < home_ref.shape[0]
+    pick_rows(rank_ref, pick_ref)
+    first_rows(cell_ref, zr_ref, home_ref, first_ref)
+    shared = mm_nt(lat_ref[...], first_ref[...]).astype(BF16)
+    for pair in range(cell_ref.shape[0] // 2):
+        span = slice(pair * 2 * LANES, (pair + 1) * 2 * LANES)
+        later = jnp.logical_and(two_rows(rank_ref, pair) >= 0, few)
+        latent = jnp.where(later, mm(shared, pick_ref[:, span]), lat_ref[:, span].astype(F32))
+        term_ref[:, span] = mm_tn(skip_ref[...], latent.astype(BF16)) + bias_ref[...]
 
 
 def pre_kernel(depth, rx_ref, lp_ref, term_ref, cell_ref, spec_ref, msg_ref, pre_ref, rt_ref):
@@ -491,7 +492,7 @@
     slope_ref[...] = gelu_slope(pre_ref[...])
 
 
-def head_kernel(rx_ref, point_ref, pw_ref, head_ref, bias_ref, out_ref, area_ref, normal_ref, pres_ref, msg_ref, spec_ref, value_ref, hot_ref):
+def head_kernel(rx_ref, point_ref, pw_ref, head_ref, bias_ref, out_ref, area_ref, normal_ref, pres_ref, msg_ref, spec_ref, value_ref, hot_ref, na_ref):
     devices = rx_ref.shape[0]
     points = area_ref.shape[1]
     rows = lax.broadcasted_iota(jnp.int32, (points, LANES), 0)
@@ -516,14 +517,17 @@
     extra = jnp.zeros((16, points), F32)
     for which in range(2):
         for index, part in enumerate(three_parts(along[which])):
-            extra = jnp.where(place == 3 + 3 * which + index, part.astype(F32), extra)
+            extra = jnp.where(place == 3 * which + index, part.astype(F32), extra)
     table = jnp.concatenate([grad.astype(BF16), extra.astype(BF16)], axis=0)
     lane = lax.broadcasted_iota(jnp.int32, (1, LANES), 1)
     partial = []
     for which in range(2):
         force = jnp.sum(pressure * area_ref[...] * normal_ref[which : which + 1, :], axis=1, keepdims=True)
         partial.append(force)
-    force_row = jnp.where(lane == 0, partial[0], jnp.where(lane == 1, partial[1], 0.0))
+    force_row = jnp.zeros((1, LANES), F32)
+    for which in range(2):
+        for index, part in enumerate(three_parts(partial[which])):
+            force_row = jnp.where(lane == 3 * which + index, part.astype(F32), force_row)
     out_rows = lax.dot_general(
         jnp.concatenate([along[0], along[1], jnp.zeros((6, points), F32)], axis=0),
         head,
@@ -532,52 +536,55 @@
         preferred_element_type=F32,
     )
     out_row = jnp.concatenate([out_rows[0:1], out_rows[1:2]], axis=1)
-    place = lax.broadcasted_iota(jnp.int32, (16, LANES), 0)
-    common = jnp.zeros((16, LANES), F32)
-    for index, part in enumerate(three_parts(out_row)):
-        common = jnp.where(place == 9 + index, part.astype(F32), common)
-    for index, part in enumerate(three_parts(force_row)):
-        common = jnp.where(place == 12 + index, part.astype(F32), common)
+    place = lax.broadcasted_iota(jnp.int32, (8, LANES), 0)
+    out_parts = three_parts(out_row)
+    common = jnp.where(
+        place == 4,
+        out_parts[0].astype(F32),
+        jnp.where(place == 5, out_parts[1].astype(F32), jnp.where(place == 6, force_row, 0.0)),
+    )
     for pair in range(devices // 2):
         got = mm(table, hot_ref[:, pair * 2 * LANES : (pair + 1) * 2 * LANES])
         for half in range(2):
             block = 2 * pair + half
             cut = slice(half * LANES, (half + 1) * LANES)
             msg_ref[block, 0:WIDTH, :] = got[0:WIDTH, cut].astype(BF16)
-            tail = got[WIDTH : WIDTH + 16, cut] + common
-            for index, part in enumerate(three_parts(pw_ref[block : block + 1, :])):
-                tail = jnp.where(place == index, part.astype(F32), tail)
-            msg_ref[block, WIDTH : WIDTH + 16, :] = tail.astype(BF16)
             spec_ref[block] = rx_ref[block, WIDTH:, :]
-
-
-def fold_rows(values):
-    first, second, third = three_parts(values)
-    upper = jnp.concatenate([first.astype(F32), second.astype(F32)], axis=1)
-    lower = jnp.concatenate([third.astype(F32), jnp.zeros_like(values)], axis=1)
-    return upper, lower
-
-
-def back_kernel(scale, rx_ref, target_ref, cell_ref, rank_ref, same_ref, zr_ref, lp_ref, lat_ref, slope_ref, msg_ref, force_ref, outg_ref, sums_ref, pick_ref, full_ref, col_ref, xs_ref, pg_ref, rp_ref, gp_ref):
+            for which in range(2):
+                at = WIDTH + 3 * which
+                na_ref[which, block : block + 1, :] = (
+                    got[at : at + 1, cut] + got[at + 1 : at + 2, cut] + got[at + 2 : at + 3, cut]
+                )
+    scaled = [three_parts(pw_ref[...] * na_ref[which]) for which in range(2)]
+    rows = [scaled[which][index].astype(F32) for which in range(2) for index in range(2)]
+    for block in range(devices):
+        tail = common
+        for index, row in enumerate(rows):
+            tail = jnp.where(place == index, row[block : block + 1, :], tail)
+        msg_ref[block, WIDTH : WIDTH + 8, :] = tail.astype(BF16)
+
+
+def back_kernel(scale, rx_ref, target_ref, cell_ref, rank_ref, zr_ref, home_ref, lp_ref, lat_ref, slope_ref, msg_ref, skip_ref, force_ref, outg_ref, sums_ref, pick_ref, first_ref, full_ref, col_ref, xs_ref, pg_ref, rp_ref, gp_ref):
     devices = rx_ref.shape[0]
-    main = msg_ref.shape[1] - 16
-    extra = slice(WIDTH, WIDTH + 16)
+    extra = slice(WIDTH, WIDTH + 8)
     total = rx_ref[0, extra, :].astype(F32)
     for block in range(1, devices):
         total += rx_ref[block, extra, :].astype(F32)
-    forces = scale * (total[12:13] + total[13:14] + total[14:15])
-    force_ref[...] = forces[:, 0:2]
-    misfit = forces[:, 0:2] - target_ref[...]
+    force = total[6:7]
+    lane = lax.broadcasted_iota(jnp.int32, (1, 2), 1)
+    forces = scale * jnp.where(
+        lane == 0,
+        force[:, 0:1] + force[:, 1:2] + force[:, 2:3],
+        force[:, 3:4] + force[:, 4:5] + force[:, 5:6],
+    )
+    force_ref[...] = forces
+    misfit = (2.0 * scale) * (forces - target_ref[...])
     drag, lift = misfit[:, 0:1], misfit[:, 1:2]
-    twice = 2.0 * scale
-    out_row = total[9:10] + total[10:11] + total[11:12]
-    outg_ref[...] = twice * (drag * out_row[:, 0:WIDTH] + lift * out_row[:, WIDTH : 2 * WIDTH])
+    out_row = total[4:5] + total[5:6]
+    outg_ref[...] = drag * out_row[:, 0:WIDTH] + lift * out_row[:, WIDTH : 2 * WIDTH]
     for block in range(devices):
         tail = rx_ref[block, extra, :].astype(F32)
-        weight, first, second = (
-            tail[at : at + 1] + tail[at + 1 : at + 2] + tail[at + 2 : at + 3] for at in (0, 3, 6)
-        )
-        factor = weight * (twice * (drag * first + lift * second))
+        factor = drag * (tail[0:1] + tail[1:2]) + lift * (tail[2:3] + tail[3:4])
         grad = factor * rx_ref[block, 0:WIDTH, :].astype(F32)
         cut = slice(block * LANES, (block + 1) * LANES)
         gp_ref[:, cut] = grad
@@ -586,7 +593,7 @@
         xs_ref[WIDTH : 2 * WIDTH, cut] = (grad - upper.astype(F32)).astype(BF16)
     sum_cells(
         lambda span: gp_ref[:, span],
-        xs_ref, cell_ref, rank_ref, same_ref, sums_ref, pick_ref, full_ref, col_ref,
+        xs_ref, cell_ref, rank_ref, zr_ref, home_ref, sums_ref, pick_ref, first_ref, full_ref, col_ref,
     )
     for pair in range(devices // 2):
         cut = slice(pair * 2 * LANES, (pair + 1) * 2 * LANES)
@@ -595,38 +602,21 @@
         pg_ref[:, cut] = jnp.where(zpos >= 0, grad, 0.0).astype(BF16)
         spread_depth(grad, zpos, rp_ref, pair)
     slab_rows(lp_ref, rp_ref, msg_ref)
-    upper, lower = fold_rows(mm_nt(lat_ref[...], pg_ref[...]))
-    for dest in range(msg_ref.shape[0]):
-        cut = slice(8 * dest, 8 * dest + 8)
-        rows = jnp.concatenate([upper[cut], lower[cut]], axis=0)
-        msg_ref[dest, main : main + 16, :] = rows.astype(BF16)
+    skip_ref[...] = mm_nt(lat_ref[...], pg_ref[...])
 
 
 def spec_kernel(half_ref, rx_ref, table_ref, msg_ref, sp_ref):
-    peers, devices = rx_ref.shape[0], msg_ref.shape[0]
-    part_rows = sp_ref.shape[0] // devices
-    main = rx_ref.shape[1] - 16
+    devices, part_rows = msg_ref.shape[0], msg_ref.shape[1]
     to_modes(rx_ref, table_ref[half_ref[0]], sp_ref)
-    total = rx_ref[0, main : main + 16, :].astype(F32)
-    for source in range(1, peers):
-        total += rx_ref[source, main : main + 16, :].astype(F32)
-    upper, lower = total[0:8], total[8:16]
-    left = lax.broadcasted_iota(jnp.int32, (8, LANES), 1) < WIDTH
-    value = jnp.where(left, upper + swap_halves(upper) + lower, 0.0)
-    first, second, third = three_parts(value)
-    upper = first.astype(F32) + swap_halves(second.astype(F32))
-    rows = jnp.concatenate([upper, third.astype(F32)], axis=0).astype(BF16)
     for dest in range(devices):
-        msg_ref[dest, 0:part_rows, :] = sp_ref[dest * part_rows : (dest + 1) * part_rows, :].astype(BF16)
-        msg_ref[dest, part_rows : part_rows + 16, :] = rows
-
-
-def final_kernel(peers, rx_ref, own_ref, spec_ref, skip_ref):
+        msg_ref[dest] = sp_ref[dest * part_rows : (dest + 1) * part_rows, :].astype(BF16)
+
+
+def final_kernel(peers, rx_ref, own_ref, spec_ref):
     devices = rx_ref.shape[0]
     low = MODES // devices
     high = MODES // peers
     owned = spec_ref.shape[0] // MODES
-    part_rows = rx_ref.shape[1] - 16
     left = lax.broadcasted_iota(jnp.int32, (8, LANES), 1) < WIDTH
     for which in range(owned):
         for source in range(devices):
@@ -651,12 +641,6 @@
             mode = which * MODES + low * source
             spec_ref[mode] = found[0:WIDTH]
             spec_ref[mode + 1] = found[WIDTH : 2 * WIDTH]
-    for peer in range(peers):
-        rows = rx_ref[peer, part_rows : part_rows + 16, :].astype(F32)
-        for shift in range(peers, devices, peers):
-            rows += rx_ref[peer + shift, part_rows : part_rows + 16, :].astype(F32)
-        value = (rows[0:8] + swap_halves(rows[0:8]) + rows[8:16])[:, 0:WIDTH]
-        skip_ref[8 * peer : 8 * peer + 8, :] = value
 
 
 def run(kernel, outs, ins, flops, scratch=(), smem=0, hbm=0, hbm_outs=0, grant=16):
@@ -750,13 +734,13 @@
         grant=60,
     )
     rx = exchange(msg)
-    shared = 384
-    zr, rank, same, lp = run(
+    shared = 256
+    zr, rank, home, lp = run(
         functools.partial(place_kernel, depth),
         [
             shape((n, LANES), jnp.int32),
             shape((n, LANES), jnp.int32),
-            shape((shared, shared), BF16),
+            shape((shared, LANES), F32),
             shape((rows, slots), BF16),
         ],
         [cells, by_rows],
@@ -770,6 +754,7 @@
     )
     sum_scratch = [
         pltpu.VMEM((WIDTH, slots), F32),
+        pltpu.VMEM((shared, slots), BF16),
         pltpu.VMEM((shared, slots), BF16),
         pltpu.VMEM((slots, LANES), BF16),
         pltpu.VMEM((slots, LANES), F32),
@@ -783,7 +768,7 @@
     msg, lat = run(
         cell_kernel,
         [shape((n, main, LANES), BF16), shape((WIDTH, slots), BF16)],
-        [rx, cells, rank, same, zr, lp],
+        [rx, cells, rank, zr, home, lp],
         big,
         scratch=sum_scratch + [pair_rows, deep_rows],
         grant=20,
@@ -807,8 +792,9 @@
     lp, term = run(
         functools.partial(skip_kernel, depth),
         [basis, shape((WIDTH, slots), F32)],
-        [cells, by_rows, spec, lat, skip_weight, skip_bias.reshape(WIDTH, 1)],
+        [cells, by_rows, spec, rank, zr, home, lat, skip_weight, skip_bias.reshape(WIDTH, 1)],
         2 * rows * LANES * slots,
+        scratch=[pltpu.VMEM((shared, slots), BF16)] * 2,
     )
     msg, pre = run(
         functools.partial(pre_kernel, depth),
@@ -824,12 +810,16 @@
         head_kernel,
         [
             shape((1, points), F32),
-            shape((n, WIDTH + 16, LANES), BF16),
+            shape((n, WIDTH + 8, LANES), BF16),
             shape((n, own_rows, LANES), BF16),
         ],
         [returned, point_rows, pw, head_weight, head_bias.reshape(WIDTH, 1), out_col, area_row, normals],
         2 * 3 * WIDTH * points * slots,
-        scratch=[pltpu.VMEM((3 * WIDTH, slots), BF16), pltpu.VMEM((points, slots), BF16)],
+        scratch=[
+            pltpu.VMEM((3 * WIDTH, slots), BF16),
+            pltpu.VMEM((points, slots), BF16),
+            pltpu.VMEM((2, n, LANES), F32),
+        ],
     )
     grads = exchange(msg)
     (lp,) = run(
@@ -839,14 +829,15 @@
         2 * rows * LANES * slots,
     )
     scale = 1.0 / math.sqrt(points * n)
-    msg, forces, out_grad = run(
+    msg, skip_grad, forces, out_grad = run(
         functools.partial(back_kernel, scale),
         [
-            shape((peers, halves * main + 16, LANES), BF16),
+            shape((peers, halves * main, LANES), BF16),
+            shape((WIDTH, WIDTH), F32),
             shape((1, 2), F32),
             shape((1, WIDTH), F32),
         ],
-        [grads, targets.reshape(1, 2), cells, rank, same, zr, lp, lat, slope],
+        [grads, targets.reshape(1, 2), cells, rank, zr, home, lp, lat, slope],
         big,
         scratch=sum_scratch
         + [pltpu.VMEM((2 * WIDTH, slots), BF16), pair_rows, deep_rows]
@@ -856,19 +847,22 @@
     grad_columns = lax.all_to_all(
         msg, "gx", split_axis=0, concat_axis=0, tiled=True, axis_index_groups=near
     )
+    for bit in (1, 2, 4, 8):
+        partner = [(index, index ^ bit) for index in range(n)]
+        skip_grad = skip_grad + lax.ppermute(skip_grad, "gx", partner)
     part_rows = MODES * high * levels // n
     (msg,) = run(
         spec_kernel,
-        [shape((n, part_rows + 16, LANES), BF16)],
+        [shape((n, part_rows, LANES), BF16)],
         [half, grad_columns, part_table],
         2 * MODES * high * rows * depth * WIDTH,
         scratch=[pltpu.VMEM((MODES * high * levels, LANES), F32)],
         smem=1,
     )
     finals = exchange(msg)
-    spec_grad, skip_grad = run(
+    (spec_grad,) = run(
         functools.partial(final_kernel, peers),
-        [shape((spec_weight.shape[0], WIDTH, WIDTH), F32), shape((WIDTH, WIDTH), F32)],
+        [shape((spec_weight.shape[0], WIDTH, WIDTH), F32)],
         [finals, own_spec],
         2 * NMODE * WIDTH * WIDTH * depth // n,
     )

time: 139 us -> 144 us (1.036)
  blocking collectives: 14.6 us -> 0 us
  starting transfers between devices: 28.5 us -> 38.9 us
  local copies, waits for them, and re-layouts: 1.07 us -> 5.44 us
  waiting for transfers between devices: 68.8 us -> 72.5 us
    all_to_all x1 -> x0, blocking collectives: 14.6 us -> none  [exchange(): lax.all_to_all(message, 'gx', split_axis=0, concat_axis=0, tiled=True)]
    ppermute x0 -> x4, waiting for transfers between devices: none -> 7.51 us  [slab_step(): skip_grad = skip_grad + lax.ppermute(skip_grad, 'gx', partner)]
    ppermute x0 -> x4, starting transfers between devices: none -> 6.89 us  [slab_step(): skip_grad = skip_grad + lax.ppermute(skip_grad, 'gx', partner)]
    unnamed x36 -> x40, local copies, waits for them, and re-layouts: 0.76 us -> 5.13 us
    all_to_all x5 -> x6, starting transfers between devices: 23.4 us -> 26.9 us  [exchange(): lax.all_to_all(message, 'gx', split_axis=0, concat_axis=0, tiled=True)]
    all_to_all x5 -> x6, waiting for transfers between devices: 52.6 us -> 49.1 us  [exchange(): lax.all_to_all(message, 'gx', split_axis=0, concat_axis=0, tiled=True)]
  transfers between devices with their start and end apart: 7 -> 12, of which waited for: 7 -> 11; matrix products, arithmetic and copies ran while one was open for 0% -> 1% of each run, Pallas kernels for 3% -> 4%
where the time goes in v7:
time: 144 us; the launch traced here: 143 us
  waiting for transfers between devices  72.5 us (50%)
  starting transfers between devices  38.9 us (27%)
  Pallas kernels  24.3 us (17%)
  local copies, waits for them, and re-layouts  5.44 us (4%)
    all_to_all x6, waiting for transfers between devices, exchange(): lax.all_to_all(message, 'gx', split_axis=0, concat_axis=0, tiled=True)  49.1 us
    all_to_all x6, starting transfers between devices, exchange(): lax.all_to_all(message, 'gx', split_axis=0, concat_axis=0, tiled=True)  26.9 us
    pallas_call x13, Pallas kernels, run(): pl.pallas_call(kernel, out_shape=tuple(outs), in_specs=[scalar] * smem +...  24.3 us
    all_to_all x1, waiting for transfers between devices, slab_step(): lax.all_to_all(msg, 'gx', split_axis=0, concat_axis=0, tiled=True, axis_i...  8.75 us
    ppermute x4, waiting for transfers between devices, slab_step(): skip_grad = skip_grad + lax.ppermute(skip_grad, 'gx', partner)  7.51 us
    ppermute x1, waiting for transfers between devices, slab_step(): other = lax.ppermute(own, 'groups', [(0, 1), (1, 0)])  7.15 us
    ppermute x4, starting transfers between devices, slab_step(): skip_grad = skip_grad + lax.ppermute(skip_grad, 'gx', partner)  6.89 us
    unnamed x40, local copies, waits for them, and re-layouts  5.13 us
  transfers between devices with their start and end apart: 12, of which 11 were waited for; matrix products, arithmetic and copies ran while one was open for 1% of the time, Pallas kernels for 4%

profile of v7, /device:TPU:0, one launch (start us, length us, event | category | flops | bytes accessed | tf_op | source)
XLA Modules:
  0.0 142.7 jit_solution(10080718443428206798)
XLA Ops:
  0.7 2.5 %shard_map.209 = (bf16[16,128,128]{2,1,0:T(8,128)(2,1)}, f32[16,128]{1,0:T(8,128)}) custom-call(s32[1]{0:T(128)} %bitcast.group_ref, s32[1,16]{1,0:T(1,128)} %count_hbm.1, s32[16,128]{1,0:T(8,128)} %bitcast.20, f32[16,128]{1,0:T(8,128)} %bitcast.27, f32[1,512]{1,0:T(1,128)} %bitcast.22, bf16[64,512]{1,0:T(8,128)(2,1)} %bitcast.26, bf16[64,64,64]{2,1,0:T(8,128)(2,1)} %weight_hbm.1), custom_call_target="tpu_custom_call" | custom-call | flops 167772160 | bytes 1140804 | tf_op jit(solution)/shard_map/pallas_call | solution.py:651
  3.1 7.4 %all-to-all-start = ((bf16[16,128,128]{2,1,0:T(8,128)(2,1)}), bf16[16,128,128]{2,1,0:T(8,128)(2,1)S(1)}, u32[]{:S(2)}, u32[]{:S(2)}) async-start(bf16[16,128,128]{2,1,0:T(8,128)(2,1)} %get-tuple-element.26), calls=%async_computation | async-start | bytes 1048576 | tf_op jit(solution)/shard_map/all_to_all | solution.py:712
  10.5 2.2 %shard_map.210 = (s32[16,128]{1,0:T(8,128)S(1)}, s32[16,128]{1,0:T(8,128)S(1)}, f32[256,128]{1,0:T(8,128)S(1)}, bf16[256,2048]{1,0:T(8,128)(2,1)S(1)}) custom-call(s32[16,128]{1,0:T(8,128)S(1)} %bitcast.14, bf16[256,128]{1,0:T(8,128)(2,1)S(1)} %copy-done), custom_call_target="tpu_custom_call" | custom-call | flops 134217728 | bytes 1269760 | tf_op jit(solution)/shard_map/pallas_call | solution.py:651
  13.7 11.3 %all-to-all-done.rx_ref = bf16[16,128,128]{2,1,0:T(8,128)(2,1)S(1)} async-done(((bf16[16,128,128]{2,1,0:T(8,128)(2,1)}), bf16[16,128,128]{2,1,0:T(8,128)(2,1)S(1)}, u32[]{:S(2)}, u32[]{:S(2)}) %all-to-all-start) | async-done | bytes 524320 | tf_op jit(solution)/shard_map/all_to_all | solution.py:712
  25.0 1.2 copy-done.16
  26.2 3.3 %shard_map.211 = (bf16[16,128,128]{2,1,0:T(8,128)(2,1)}, bf16[64,2048]{1,0:T(8,128)(2,1)S(1)}) custom-call(bf16[16,128,128]{2,1,0:T(8,128)(2,1)S(1)} %all-to-all-done.rx_ref, s32[16,128]{1,0:T(8,128)S(1)} %bitcast.15, s32[16,128]{1,0:T(8,128)S(1)} %get-tuple-element.27.rank_ref, s32[16,128]{1,0:T(8,128)S(1)} %get-tuple-element.28.zr_ref, ...), custom_call_target="tpu_custom_call" | custom-call | flops 1610612736 | bytes 2514944 | tf_op jit(solution)/shard_map/pallas_call | solution.py:651
  29.5 4.2 %all-to-all-start.1 = ((bf16[16,128,128]{2,1,0:T(8,128)(2,1)}), bf16[16,128,128]{2,1,0:T(8,128)(2,1)S(1)}, u32[]{:S(2)}, u32[]{:S(2)}) async-start(bf16[16,128,128]{2,1,0:T(8,128)(2,1)} %get-tuple-element.31), calls=%async_computation.1 | async-start | bytes 1048576 | tf_op jit(solution)/shard_map/all_to_all | solution.py:712
  33.8 1.6 %collective-permute-start = (bf16[16,64,128]{2,1,0:T(8,128)(2,1)S(1)}, bf16[16,64,128]{2,1,0:T(8,128)(2,1)S(1)}, u32[]{:S(2)}, u32[]{:S(2)}) collective-permute-start(bf16[16,64,128]{2,1,0:T(8,128)(2,1)S(1)} %slice.4.own_ref), channel_id=1, source_target_pairs={{0,16},{16,0},{1,17},{17,1},{2,18},{18,2},{3,19},{19,3},{4,20},{20... | collective-permute-start | bytes 786440 | tf_op jit(solution)/shard_map/ppermute | solution.py:763
  35.4 7.2 %collective-permute-done.other_ref = bf16[16,64,128]{2,1,0:T(8,128)(2,1)S(1)} collective-permute-done((bf16[16,64,128]{2,1,0:T(8,128)(2,1)S(1)}, bf16[16,64,128]{2,1,0:T(8,128)(2,1)S(1)}, u32[]{:S(2)}, u32[]{:S(2)}) %collective-permute-start) | collective-permute-done | bytes 262176 | tf_op jit(solution)/shard_map/ppermute | solution.py:763
  42.6 5.6 %all-to-all-done.1.rx_ref = bf16[16,128,128]{2,1,0:T(8,128)(2,1)S(1)} async-done(((bf16[16,128,128]{2,1,0:T(8,128)(2,1)}), bf16[16,128,128]{2,1,0:T(8,128)(2,1)S(1)}, u32[]{:S(2)}, u32[]{:S(2)}) %all-to-all-start.1) | async-done | bytes 524320 | tf_op jit(solution)/shard_map/all_to_all | solution.py:712
  48.2 1.7 %shard_map.213 = (bf16[16,128,128]{2,1,0:T(8,128)(2,1)}, bf16[16,32,128]{2,1,0:T(8,128)(2,1)S(1)}) custom-call(bf16[16,128,128]{2,1,0:T(8,128)(2,1)S(1)} %all-to-all-done.1.rx_ref, bf16[32,64,128]{2,1,0:T(8,128)(2,1)S(1)} %shard_map.212.weight_ref, bf16[64,256]{1,0:T(8,128)(2,1)S(1)} %copy-done.3, bf16[256,64]{1,0:T(8,128)(2,1)S(1)} %copy-done.2), custom_call_target="tpu_custom_call" | custom-call | flops 67108864 | bytes 1769472 | tf_op jit(solution)/shard_map/pallas_call | solution.py:651
  49.9 4.1 %all-to-all-start.2 = ((bf16[16,128,128]{2,1,0:T(8,128)(2,1)}), bf16[16,128,128]{2,1,0:T(8,128)(2,1)S(1)}, u32[]{:S(2)}, u32[]{:S(2)}) async-start(bf16[16,128,128]{2,1,0:T(8,128)(2,1)} %get-tuple-element.32), calls=%async_computation.2 | async-start | bytes 1048576 | tf_op jit(solution)/shard_map/all_to_all | solution.py:712
  54.1 2.3 %shard_map.214 = (bf16[256,2048]{1,0:T(8,128)(2,1)S(1)}, f32[64,2048]{1,0:T(8,128)S(1)}) custom-call(s32[16,128]{1,0:T(8,128)S(1)} %bitcast.16, bf16[256,128]{1,0:T(8,128)(2,1)S(1)} %copy-done, bf16[16,32,128]{2,1,0:T(8,128)(2,1)S(1)} %get-tuple-element.33.after_ref.spec_ref, s32[16,128]{1,0:T(8,128)S(1)} %get-tuple-element.27.rank_ref, ...), custom_call_target="tpu_custom_call" | custom-call | flops 134217728 | bytes 2195712 | tf_op jit(solution)/shard_map/pallas_call | solution.py:651
  57.5 11.0 %all-to-all-done.2.rx_ref = bf16[16,128,128]{2,1,0:T(8,128)(2,1)S(1)} async-done(((bf16[16,128,128]{2,1,0:T(8,128)(2,1)}), bf16[16,128,128]{2,1,0:T(8,128)(2,1)S(1)}, u32[]{:S(2)}, u32[]{:S(2)}) %all-to-all-start.2) | async-done | bytes 524320 | tf_op jit(solution)/shard_map/all_to_all | solution.py:712
  68.5 1.2 copy-done.10
  69.8 2.1 %shard_map.215 = (bf16[16,96,128]{2,1,0:T(8,128)(2,1)}, f32[64,2048]{1,0:T(8,128)S(1)}) custom-call(bf16[16,128,128]{2,1,0:T(8,128)(2,1)S(1)} %all-to-all-done.2.rx_ref, bf16[256,2048]{1,0:T(8,128)(2,1)S(1)} %copy-done.10, f32[64,2048]{1,0:T(8,128)S(1)} %get-tuple-element.36.term_ref, s32[16,128]{1,0:T(8,128)S(1)} %bitcast.17, ...), custom_call_target="tpu_custom_call" | custom-call | flops 1073741824 | bytes 3153920 | tf_op jit(solution)/shard_map/pallas_call | solution.py:651
  71.9 4.1 %all-to-all-start.3 = ((bf16[16,96,128]{2,1,0:T(8,128)(2,1)}), bf16[16,96,128]{2,1,0:T(8,128)(2,1)S(1)}, u32[]{:S(2)}, u32[]{:S(2)}) async-start(bf16[16,96,128]{2,1,0:T(8,128)(2,1)} %get-tuple-element.37), calls=%async_computation.3 | async-start | bytes 786432 | tf_op jit(solution)/shard_map/all_to_all | solution.py:712
  76.2 12.0 %all-to-all-done.3.rx_ref = bf16[16,96,128]{2,1,0:T(8,128)(2,1)S(1)} async-done(((bf16[16,96,128]{2,1,0:T(8,128)(2,1)}), bf16[16,96,128]{2,1,0:T(8,128)(2,1)S(1)}, u32[]{:S(2)}, u32[]{:S(2)}) %all-to-all-start.3) | async-done | bytes 393248 | tf_op jit(solution)/shard_map/all_to_all | solution.py:712
  88.2 2.9 %shard_map.216 = (f32[1,512]{1,0:T(1,128)}, bf16[16,72,128]{2,1,0:T(8,128)(2,1)}, bf16[16,32,128]{2,1,0:T(8,128)(2,1)S(1)}) custom-call(bf16[16,96,128]{2,1,0:T(8,128)(2,1)S(1)} %all-to-all-done.3.rx_ref, s32[16,128]{1,0:T(8,128)S(1)} %bitcast.21, f32[16,128]{1,0:T(8,128)S(1)} %copy-done.12, bf16[64,64]{1,0:T(8,128)(2,1)S(1)} %copy-done.11, ...), custom_call_target="tpu_custom_call" | custom-call | flops 402653184 | bytes 852480 | tf_op jit(solution)/shard_map/pallas_call | solution.py:651
  91.1 3.5 %all-to-all-start.4 = ((bf16[16,72,128]{2,1,0:T(8,128)(2,1)}), bf16[16,72,128]{2,1,0:T(8,128)(2,1)S(1)}, u32[]{:S(2)}, u32[]{:S(2)}) async-start(bf16[16,72,128]{2,1,0:T(8,128)(2,1)} %get-tuple-element.40), calls=%async_computation.4 | async-start | bytes 589824 | tf_op jit(solution)/shard_map/all_to_all | solution.py:712
  96.0 9.2 %all-to-all-done.4.rx_ref = bf16[16,72,128]{2,1,0:T(8,128)(2,1)S(1)} async-done(((bf16[16,72,128]{2,1,0:T(8,128)(2,1)}), bf16[16,72,128]{2,1,0:T(8,128)(2,1)S(1)}, u32[]{:S(2)}, u32[]{:S(2)}) %all-to-all-start.4) | async-done | bytes 294944 | tf_op jit(solution)/shard_map/all_to_all | solution.py:712
  105.3 3.6 %shard_map.219 = (bf16[8,256,128]{2,1,0:T(8,128)(2,1)}, f32[64,64]{1,0:T(8,128)S(1)}, f32[1,2]{1,0:T(1,128)}, f32[1,64]{1,0:T(1,128)}) custom-call(bf16[16,72,128]{2,1,0:T(8,128)(2,1)S(1)} %all-to-all-done.4.rx_ref, f32[1,2]{1,0:T(1,128)S(1)} %bitcast.25, s32[16,128]{1,0:T(8,128)S(1)} %bitcast.19, s32[16,128]{1,0:T(8,128)S(1)} %get-tuple-element.27.rank_ref, ...), custom_call_target="tpu_custom_call" | custom-call | flops 1610612736 | bytes 2826512 | tf_op jit(solution)/shard_map/pallas_call | solution.py:651
  108.9 3.5 %all-to-all-start.5 = ((bf16[8,256,128]{2,1,0:T(8,128)(2,1)}), bf16[8,256,128]{2,1,0:T(8,128)(2,1)S(1)}, u32[]{:S(2)}, u32[]{:S(2)}) async-start(bf16[8,256,128]{2,1,0:T(8,128)(2,1)} %get-tuple-element.43), calls=%async_computation.5 | async-start | bytes 1048576 | tf_op jit(solution)/shard_map/all_to_all | solution.py:847
  112.4 8.7 %all-to-all-done.5.rx_ref = bf16[8,256,128]{2,1,0:T(8,128)(2,1)S(1)} async-done(((bf16[8,256,128]{2,1,0:T(8,128)(2,1)}), bf16[8,256,128]{2,1,0:T(8,128)(2,1)S(1)}, u32[]{:S(2)}, u32[]{:S(2)}) %all-to-all-start.5) | async-done | bytes 524320 | tf_op jit(solution)/shard_map/all_to_all | solution.py:847
  122.2 3.5 %all-to-all-start.6 = ((bf16[16,64,128]{2,1,0:T(8,128)(2,1)}), bf16[16,64,128]{2,1,0:T(8,128)(2,1)S(1)}, u32[]{:S(2)}, u32[]{:S(2)}) async-start(bf16[16,64,128]{2,1,0:T(8,128)(2,1)} %shard_map.220), calls=%async_computation.6 | async-start | bytes 524288 | tf_op jit(solution)/shard_map/all_to_all | solution.py:712
  127.0 1.9 %collective-permute-start.2 = (f32[64,64]{1,0:T(8,128)S(1)}, f32[64,64]{1,0:T(8,128)S(1)}, u32[]{:S(2)}, u32[]{:S(2)}) collective-permute-start(f32[64,64]{1,0:T(8,128)S(1)} %add.13), channel_id=1, source_target_pairs={{0,2},{1,3},{2,0},{3,1},{4,6},{5,7},{6,4},{7,5},{8,10},{9,11},{10,... | collective-permute-start | bytes 49160 | tf_op jit(solution)/shard_map/ppermute | solution.py:852
  128.8 2.4 %collective-permute-done.2 = f32[64,64]{1,0:T(8,128)S(1)} collective-permute-done((f32[64,64]{1,0:T(8,128)S(1)}, f32[64,64]{1,0:T(8,128)S(1)}, u32[]{:S(2)}, u32[]{:S(2)}) %collective-permute-start.2) | collective-permute-done | bytes 16416 | tf_op jit(solution)/shard_map/ppermute | solution.py:852
  131.3 2.0 %collective-permute-start.3 = (f32[64,64]{1,0:T(8,128)S(1)}, f32[64,64]{1,0:T(8,128)S(1)}, u32[]{:S(2)}, u32[]{:S(2)}) collective-permute-start(f32[64,64]{1,0:T(8,128)S(1)} %add.14), channel_id=1, source_target_pairs={{0,4},{1,5},{2,6},{3,7},{4,0},{5,1},{6,2},{7,3},{8,12},{9,13},{10,... | collective-permute-start | bytes 49160 | tf_op jit(solution)/shard_map/ppermute | solution.py:852
  133.2 2.1 %collective-permute-done.3 = f32[64,64]{1,0:T(8,128)S(1)} collective-permute-done((f32[64,64]{1,0:T(8,128)S(1)}, f32[64,64]{1,0:T(8,128)S(1)}, u32[]{:S(2)}, u32[]{:S(2)}) %collective-permute-start.3) | collective-permute-done | bytes 16416 | tf_op jit(solution)/shard_map/ppermute | solution.py:852
  135.3 2.7 %collective-permute-start.4 = (f32[64,64]{1,0:T(8,128)S(1)}, f32[64,64]{1,0:T(8,128)S(1)}, u32[]{:S(2)}, u32[]{:S(2)}) collective-permute-start(f32[64,64]{1,0:T(8,128)S(1)} %add.15), channel_id=1, source_target_pairs={{0,8},{1,9},{2,10},{3,11},{4,12},{5,13},{6,14},{7,15},{8,0},{9,1},... | collective-permute-start | bytes 49160 | tf_op jit(solution)/shard_map/ppermute | solution.py:852
  138.0 2.1 %collective-permute-done.4 = f32[64,64]{1,0:T(8,128)S(1)} collective-permute-done((f32[64,64]{1,0:T(8,128)S(1)}, f32[64,64]{1,0:T(8,128)S(1)}, u32[]{:S(2)}, u32[]{:S(2)}) %collective-permute-start.4) | collective-permute-done | bytes 16416 | tf_op jit(solution)/shard_map/ppermute | solution.py:852
  140.8 2.0 %shard_map.221 = f32[64,64,64]{2,1,0:T(8,128)} custom-call(bf16[16,64,128]{2,1,0:T(8,128)(2,1)S(1)} %all-to-all-done.6.rx_ref, bf16[16,32,128]{2,1,0:T(8,128)(2,1)S(1)} %get-tuple-element.44.own_ref), custom_call_target="tpu_custom_call" | custom-call | flops 8388608 | bytes 1441792 | tf_op jit(solution)/shard_map/pallas_call | solution.py:651
  (53 shorter events, 6.6 us)
Async XLA Ops:
  0.6 9.9 %copy-start = (bf16[256,128]{1,0:T(8,128)(2,1)S(1)}, bf16[256,128]{1,0:T(8,128)(2,1)}, u32[]{:S(2)}) copy-start(bf16[256,128]{1,0:T(8,128)(2,1)} %constant.33.clone.by_ref) | copy-start | bytes 196612
  0.6 9.9 %copy-start.4 = (s32[16,1,128]{2,1,0:T(1,128)S(1)}, s32[16,1,128]{2,1,0:T(1,128)}, u32[]{:S(2)}) copy-start(s32[16,1,128]{2,1,0:T(1,128)} %param.20) | copy-start | bytes 24580
  3.1 21.9 %all-to-all-start = ((bf16[16,128,128]{2,1,0:T(8,128)(2,1)}), bf16[16,128,128]{2,1,0:T(8,128)(2,1)S(1)}, u32[]{:S(2)}, u32[]{:S(2)}) async-start(bf16[16,128,128]{2,1,0:T(8,128)(2,1)} %get-tuple-element.26), calls=%async_computation | async-start | bytes 1048576 | tf_op jit(solution)/shard_map/all_to_all | solution.py:712
  12.8 1.0 copy-start.15
  25.0 1.2 copy-start.16
  29.5 18.7 %copy-start.2 = (bf16[256,64]{1,0:T(8,128)(2,1)S(1)}, bf16[256,64]{1,0:T(8,128)(2,1)}, u32[]{:S(2)}) copy-start(bf16[256,64]{1,0:T(8,128)(2,1)} %constant.34.clone.back_ref) | copy-start | bytes 98308
  29.5 18.7 %copy-start.3 = (bf16[64,256]{1,0:T(8,128)(2,1)S(1)}, bf16[64,256]{1,0:T(8,128)(2,1)}, u32[]{:S(2)}) copy-start(bf16[64,256]{1,0:T(8,128)(2,1)} %constant.35.clone.table_ref) | copy-start | bytes 98308
  29.5 18.7 %all-to-all-start.1 = ((bf16[16,128,128]{2,1,0:T(8,128)(2,1)}), bf16[16,128,128]{2,1,0:T(8,128)(2,1)S(1)}, u32[]{:S(2)}, u32[]{:S(2)}) async-start(bf16[16,128,128]{2,1,0:T(8,128)(2,1)} %get-tuple-element.31), calls=%async_computation.1 | async-start | bytes 1048576 | tf_op jit(solution)/shard_map/all_to_all | solution.py:712
  33.8 20.3 %copy-start.17 = (f32[64]{0:T(128)S(1)}, f32[64]{0:T(128)}, u32[]{:S(2)}) copy-start(f32[64]{0:T(128)} %param.28) | copy-start | bytes 772
  33.8 20.4 %copy-start.5 = (bf16[64,64]{1,0:T(8,128)(2,1)S(1)}, bf16[64,64]{1,0:T(8,128)(2,1)}, u32[]{:S(2)}) copy-start(bf16[64,64]{1,0:T(8,128)(2,1)} %skip_ref.1) | copy-start | bytes 24580
  33.8 8.7 %collective-permute-start = (bf16[16,64,128]{2,1,0:T(8,128)(2,1)S(1)}, bf16[16,64,128]{2,1,0:T(8,128)(2,1)S(1)}, u32[]{:S(2)}, u32[]{:S(2)}) collective-permute-start(bf16[16,64,128]{2,1,0:T(8,128)(2,1)S(1)} %slice.4.own_ref), channel_id=1, source_target_pairs={{0,16},{16,0},{1,17},{17,1},{2,18},{18,2},{3,19},{19,3},{4,20},{20... | collective-permute-start | bytes 786440 | tf_op jit(solution)/shard_map/ppermute | solution.py:763
  49.9 18.6 %all-to-all-start.2 = ((bf16[16,128,128]{2,1,0:T(8,128)(2,1)}), bf16[16,128,128]{2,1,0:T(8,128)(2,1)S(1)}, u32[]{:S(2)}, u32[]{:S(2)}) async-start(bf16[16,128,128]{2,1,0:T(8,128)(2,1)} %get-tuple-element.32), calls=%async_computation.2 | async-start | bytes 1048576 | tf_op jit(solution)/shard_map/all_to_all | solution.py:712
  56.5 1.0 copy-start.9
  68.5 1.2 copy-start.10
  69.7 6.2 %copy-start.18 = (f32[64]{0:T(128)S(1)}, f32[64]{0:T(128)}, u32[]{:S(2)}) copy-start(f32[64]{0:T(128)} %param.30) | copy-start | bytes 772
  69.7 6.3 %copy-start.19 = (f32[64]{0:T(128)S(1)}, f32[64]{0:T(128)}, u32[]{:S(2)}) copy-start(f32[64]{0:T(128)} %param.31) | copy-start | bytes 772
  69.7 18.4 %copy-start.6 = (s32[1,16,128]{2,1,0:T(8,128)S(1)}, s32[1,16,128]{2,1,0:T(8,128)}, u32[]{:S(2)}) copy-start(s32[1,16,128]{2,1,0:T(8,128)} %param.19) | copy-start | bytes 24580
  69.7 18.4 %copy-start.7 = (f32[512]{0:T(512)S(1)}, f32[512]{0:T(512)}, u32[]{:S(2)}) copy-start(f32[512]{0:T(512)} %param.23) | copy-start | bytes 6148
  69.7 18.4 %copy-start.11 = (bf16[64,64]{1,0:T(8,128)(2,1)S(1)}, bf16[64,64]{1,0:T(8,128)(2,1)}, u32[]{:S(2)}) copy-start(bf16[64,64]{1,0:T(8,128)(2,1)} %head_ref.1) | copy-start | bytes 24580
  69.8 18.4 %copy-start.12 = (f32[16,128]{1,0:T(8,128)S(1)}, f32[16,128]{1,0:T(8,128)}, u32[]{:S(2)}) copy-start(f32[16,128]{1,0:T(8,128)} %get-tuple-element.38.pw_ref) | copy-start | bytes 24580
  69.8 18.4 %copy-start.13 = (f32[2,512]{1,0:T(2,128)S(1)}, f32[2,512]{1,0:T(2,128)}, u32[]{:S(2)}) copy-start(f32[2,512]{1,0:T(2,128)} %normal_ref.1) | copy-start | bytes 12292
  71.9 16.3 %all-to-all-start.3 = ((bf16[16,96,128]{2,1,0:T(8,128)(2,1)}), bf16[16,96,128]{2,1,0:T(8,128)(2,1)S(1)}, u32[]{:S(2)}, u32[]{:S(2)}) async-start(bf16[16,96,128]{2,1,0:T(8,128)(2,1)} %get-tuple-element.37), calls=%async_computation.3 | async-start | bytes 786432 | tf_op jit(solution)/shard_map/all_to_all | solution.py:712
  88.2 17.1 %copy-start.14 = (f32[2]{0:T(128)S(1)}, f32[2]{0:T(128)}, u32[]{:S(2)}) copy-start(f32[2]{0:T(128)} %param.25) | copy-start | bytes 28
  91.1 14.1 %all-to-all-start.4 = ((bf16[16,72,128]{2,1,0:T(8,128)(2,1)}), bf16[16,72,128]{2,1,0:T(8,128)(2,1)S(1)}, u32[]{:S(2)}, u32[]{:S(2)}) async-start(bf16[16,72,128]{2,1,0:T(8,128)(2,1)} %get-tuple-element.40), calls=%async_computation.4 | async-start | bytes 589824 | tf_op jit(solution)/shard_map/all_to_all | solution.py:712
  94.9 0.7 copy-start.8
  105.3 15.9 %copy-start.1 = (bf16[2,128,256]{2,1,0:T(8,128)(2,1)S(1)}, bf16[2,128,256]{2,1,0:T(8,128)(2,1)}, u32[]{:S(2)}) copy-start(bf16[2,128,256]{2,1,0:T(8,128)(2,1)} %constant.36.clone.table_ref) | copy-start | bytes 393220
  108.9 12.3 %all-to-all-start.5 = ((bf16[8,256,128]{2,1,0:T(8,128)(2,1)}), bf16[8,256,128]{2,1,0:T(8,128)(2,1)S(1)}, u32[]{:S(2)}, u32[]{:S(2)}) async-start(bf16[8,256,128]{2,1,0:T(8,128)(2,1)} %get-tuple-element.43), calls=%async_computation.5 | async-start | bytes 1048576 | tf_op jit(solution)/shard_map/all_to_all | solution.py:847
  122.2 18.6 %all-to-all-start.6 = ((bf16[16,64,128]{2,1,0:T(8,128)(2,1)}), bf16[16,64,128]{2,1,0:T(8,128)(2,1)S(1)}, u32[]{:S(2)}, u32[]{:S(2)}) async-start(bf16[16,64,128]{2,1,0:T(8,128)(2,1)} %shard_map.220), calls=%async_computation.6 | async-start | bytes 524288 | tf_op jit(solution)/shard_map/all_to_all | solution.py:712
  125.7 1.3 collective-permute-start.1
  127.0 4.3 %collective-permute-start.2 = (f32[64,64]{1,0:T(8,128)S(1)}, f32[64,64]{1,0:T(8,128)S(1)}, u32[]{:S(2)}, u32[]{:S(2)}) collective-permute-start(f32[64,64]{1,0:T(8,128)S(1)} %add.13), channel_id=1, source_target_pairs={{0,2},{1,3},{2,0},{3,1},{4,6},{5,7},{6,4},{7,5},{8,10},{9,11},{10,... | collective-permute-start | bytes 49160 | tf_op jit(solution)/shard_map/ppermute | solution.py:852
  131.3 4.1 %collective-permute-start.3 = (f32[64,64]{1,0:T(8,128)S(1)}, f32[64,64]{1,0:T(8,128)S(1)}, u32[]{:S(2)}, u32[]{:S(2)}) collective-permute-start(f32[64,64]{1,0:T(8,128)S(1)} %add.14), channel_id=1, source_target_pairs={{0,4},{1,5},{2,6},{3,7},{4,0},{5,1},{6,2},{7,3},{8,12},{9,13},{10,... | collective-permute-start | bytes 49160 | tf_op jit(solution)/shard_map/ppermute | solution.py:852
  135.3 4.8 %collective-permute-start.4 = (f32[64,64]{1,0:T(8,128)S(1)}, f32[64,64]{1,0:T(8,128)S(1)}, u32[]{:S(2)}, u32[]{:S(2)}) collective-permute-start(f32[64,64]{1,0:T(8,128)S(1)} %add.15), channel_id=1, source_target_pairs={{0,8},{1,9},{2,10},{3,11},{4,12},{5,13},{6,14},{7,15},{8,0},{9,1},... | collective-permute-start | bytes 49160 | tf_op jit(solution)/shard_map/ppermute | solution.py:852

commit v8 on v7

--- a/solution.py
+++ b/solution.py
@@ -269,24 +269,20 @@
     slab = rows // MODES
     wide = 2 * LANES
     yrow = lax.broadcasted_iota(jnp.int32, (GY, wide), 0)
-    xrow = jnp.bitwise_and(lax.broadcasted_iota(jnp.int32, (rows, wide), 0), slab - 1)
+    xrow = jnp.bitwise_and(lax.broadcasted_iota(jnp.int32, (16, wide), 0), slab - 1)
     for pair in range(cell_ref.shape[0] // 2):
         cells = two_rows(cell_ref, pair)
         ypos = jnp.bitwise_and(jnp.right_shift(cells, zbits), GY - 1)
         xpos = jnp.right_shift(cells, zbits + GY.bit_length() - 1)
         hot = jnp.where(yrow == ypos, 1.0, 0.0).astype(BF16)
-        lp_ref[:, pair * wide : (pair + 1) * wide] = jnp.where(
-            xrow == xpos, mm(by_ref[...], hot), 0.0
-        ).astype(BF16)
-
-
-def basis_kernel(depth, cell_ref, by_ref, after_ref, lp_ref):
-    basis_rows(depth, cell_ref, by_ref, lp_ref)
-
-
-def place_kernel(depth, cell_ref, by_ref, zr_ref, rank_ref, home_ref, lp_ref, col_ref, flag_ref, pick_ref, part_ref):
+        mask = jnp.where(xrow == xpos, 1.0, 0.0).astype(BF16)
+        found = mm(by_ref[...], hot).astype(BF16)
+        for at in range(0, rows, 16):
+            lp_ref[at : at + 16, pair * wide : (pair + 1) * wide] = found[at : at + 16] * mask
+
+
+def place_kernel(depth, cell_ref, zr_ref, rank_ref, home_ref, col_ref, flag_ref, pick_ref, part_ref):
     devices = cell_ref.shape[0]
-    basis_rows(depth, cell_ref, by_ref, lp_ref)
     down = lax.broadcasted_iota(jnp.int32, (LANES, LANES), 0)
     along = lax.broadcasted_iota(jnp.int32, (LANES, LANES), 1)
     place = lax.broadcasted_iota(jnp.int32, (16, LANES), 0)
@@ -385,7 +381,7 @@
                 ]
 
 
-def cell_kernel(rx_ref, cell_ref, rank_ref, zr_ref, home_ref, lp_ref, msg_ref, lat_ref, sums_ref, pick_ref, first_ref, full_ref, col_ref, xs_ref, rp_ref):
+def cell_kernel(depth, rx_ref, cell_ref, rank_ref, zr_ref, home_ref, by_ref, msg_ref, lat_ref, sums_ref, pick_ref, first_ref, full_ref, col_ref, xs_ref, rp_ref, lp_ref):
     devices = rx_ref.shape[0]
     for block in range(devices):
         xs_ref[:, block * LANES : (block + 1) * LANES] = rx_ref[block, 0:WIDTH, :]
@@ -393,6 +389,7 @@
         lambda span: xs_ref[:, span].astype(F32),
         xs_ref, cell_ref, rank_ref, zr_ref, home_ref, sums_ref, pick_ref, first_ref, full_ref, col_ref,
     )
+    basis_rows(depth, cell_ref, by_ref, lp_ref)
     for pair in range(devices // 2):
         cut = slice(pair * 2 * LANES, (pair + 1) * 2 * LANES)
         latent = sums_ref[:, cut]
@@ -452,8 +449,7 @@
             msg_ref[dest, level * step : (level + 1) * step, :] = out[dest * step : (dest + 1) * step]
 
 
-def skip_kernel(depth, cell_ref, by_ref, after_ref, rank_ref, zr_ref, home_ref, lat_ref, skip_ref, bias_ref, lp_ref, term_ref, pick_ref, first_ref):
-    basis_rows(depth, cell_ref, by_ref, lp_ref)
+def skip_kernel(cell_ref, rank_ref, zr_ref, home_ref, lat_ref, skip_ref, bias_ref, term_ref, pick_ref, first_ref):
     few = jnp.max(rank_ref[...]) < home_ref.shape[0]
     pick_rows(rank_ref, pick_ref)
     first_rows(cell_ref, zr_ref, home_ref, first_ref)
@@ -465,8 +461,9 @@
         term_ref[:, span] = mm_tn(skip_ref[...], latent.astype(BF16)) + bias_ref[...]
 
 
-def pre_kernel(depth, rx_ref, lp_ref, term_ref, cell_ref, spec_ref, msg_ref, pre_ref, rt_ref):
+def pre_kernel(depth, rx_ref, by_ref, term_ref, cell_ref, spec_ref, msg_ref, pre_ref, rt_ref, lp_ref):
     devices = rx_ref.shape[0]
+    basis_rows(depth, cell_ref, by_ref, lp_ref)
     rows = lp_ref.shape[0]
     step = rows // devices
     for level in range(rt_ref.shape[0] // LANES):
@@ -486,10 +483,6 @@
             dest = 2 * pair + half
             msg_ref[dest, 0:WIDTH, :] = feats[:, half * LANES : (half + 1) * LANES]
             msg_ref[dest, WIDTH:, :] = spec_ref[dest]
-
-
-def slope_kernel(pre_ref, slope_ref):
-    slope_ref[...] = gelu_slope(pre_ref[...])
 
 
 def head_kernel(rx_ref, point_ref, pw_ref, head_ref, bias_ref, out_ref, area_ref, normal_ref, pres_ref, msg_ref, spec_ref, value_ref, hot_ref, na_ref):
@@ -564,8 +557,10 @@
         msg_ref[block, WIDTH : WIDTH + 8, :] = tail.astype(BF16)
 
 
-def back_kernel(scale, rx_ref, target_ref, cell_ref, rank_ref, zr_ref, home_ref, lp_ref, lat_ref, slope_ref, msg_ref, skip_ref, force_ref, outg_ref, sums_ref, pick_ref, first_ref, full_ref, col_ref, xs_ref, pg_ref, rp_ref, gp_ref):
+def back_kernel(depth, scale, rx_ref, target_ref, cell_ref, rank_ref, zr_ref, home_ref, by_ref, lat_ref, pre_ref, msg_ref, force_ref, outg_ref, sums_ref, pick_ref, first_ref, full_ref, col_ref, xs_ref, pg_ref, rp_ref, gp_ref, lp_ref):
     devices = rx_ref.shape[0]
+    main = msg_ref.shape[1] - 8
+    basis_rows(depth, cell_ref, by_ref, lp_ref)
     extra = slice(WIDTH, WIDTH + 8)
     total = rx_ref[0, extra, :].astype(F32)
     for block in range(1, devices):
@@ -597,22 +592,36 @@
     )
     for pair in range(devices // 2):
         cut = slice(pair * 2 * LANES, (pair + 1) * 2 * LANES)
-        grad = sums_ref[:, cut] * slope_ref[:, cut]
+        grad = sums_ref[:, cut] * gelu_slope(pre_ref[:, cut])
         zpos = two_rows(zr_ref, pair)
         pg_ref[:, cut] = jnp.where(zpos >= 0, grad, 0.0).astype(BF16)
         spread_depth(grad, zpos, rp_ref, pair)
     slab_rows(lp_ref, rp_ref, msg_ref)
-    skip_ref[...] = mm_nt(lat_ref[...], pg_ref[...])
+    skip = mm_nt(lat_ref[...], pg_ref[...])
+    for dest in range(msg_ref.shape[0]):
+        msg_ref[dest, main : main + 8, :] = two_parts(skip[8 * dest : 8 * dest + 8]).astype(BF16)
+
+
+def two_parts(values):
+    first, second, _ = three_parts(values)
+    return jnp.concatenate([first.astype(F32), second.astype(F32)], axis=1)
 
 
 def spec_kernel(half_ref, rx_ref, table_ref, msg_ref, sp_ref):
-    devices, part_rows = msg_ref.shape[0], msg_ref.shape[1]
+    peers, devices = rx_ref.shape[0], msg_ref.shape[0]
+    part_rows = sp_ref.shape[0] // devices
+    main = rx_ref.shape[1] - 8
     to_modes(rx_ref, table_ref[half_ref[0]], sp_ref)
+    total = rx_ref[0, main : main + 8, :].astype(F32)
+    for source in range(1, peers):
+        total += rx_ref[source, main : main + 8, :].astype(F32)
+    total = two_parts((total + swap_halves(total))[:, 0:WIDTH]).astype(BF16)
     for dest in range(devices):
-        msg_ref[dest] = sp_ref[dest * part_rows : (dest + 1) * part_rows, :].astype(BF16)
-
-
-def final_kernel(peers, rx_ref, own_ref, spec_ref):
+        msg_ref[dest, 0:part_rows, :] = sp_ref[dest * part_rows : (dest + 1) * part_rows, :].astype(BF16)
+        msg_ref[dest, part_rows : part_rows + 8, :] = total
+
+
+def final_kernel(peers, rx_ref, own_ref, spec_ref, skip_ref):
     devices = rx_ref.shape[0]
     low = MODES // devices
     high = MODES // peers
@@ -641,6 +650,12 @@
             mode = which * MODES + low * source
             spec_ref[mode] = found[0:WIDTH]
             spec_ref[mode + 1] = found[WIDTH : 2 * WIDTH]
+    main = rx_ref.shape[1] - 8
+    for peer in range(peers):
+        rows = rx_ref[peer, main : main + 8, :].astype(F32)
+        for shift in range(peers, devices, peers):
+            rows += rx_ref[peer + shift, main : main + 8, :].astype(F32)
+        skip_ref[8 * peer : 8 * peer + 8, :] = (rows + swap_halves(rows))[:, 0:WIDTH]
 
 
 def run(kernel, outs, ins, flops, scratch=(), smem=0, hbm=0, hbm_outs=0, grant=16):
@@ -711,6 +726,9 @@
     def exchange(message):
         return lax.all_to_all(message, "gx", split_axis=0, concat_axis=0, tiled=True)
 
+    def exchange_alone(message, *others):
+        return lax.optimization_barrier((exchange(message),) + others)
+
     group = lax.axis_index("groups").astype(jnp.int32).reshape(1)
     point_rows = pair_point[0]
     cells = pair_cell[:, 0, :]
@@ -735,15 +753,14 @@
     )
     rx = exchange(msg)
     shared = 256
-    zr, rank, home, lp = run(
+    zr, rank, home = run(
         functools.partial(place_kernel, depth),
         [
             shape((n, LANES), jnp.int32),
             shape((n, LANES), jnp.int32),
             shape((shared, LANES), F32),
-            shape((rows, slots), BF16),
         ],
-        [cells, by_rows],
+        [cells],
         2 * rows * LANES * slots,
         scratch=[
             pltpu.VMEM((slots, LANES), F32),
@@ -762,18 +779,25 @@
     own = rx[:, WIDTH : 2 * WIDTH, :]
     other = lax.ppermute(own, "groups", [(0, 1), (1, 0)])
     pair_rows = pltpu.VMEM((WIDTH, slots), BF16)
-    basis = shape((rows, slots), BF16)
+    basis = pltpu.VMEM((rows, slots), BF16)
     deep_rows = pltpu.VMEM((depth * WIDTH, slots), BF16)
     big = 2 * WIDTH * slots * slots + 2 * rows * slots * depth * WIDTH
     msg, lat = run(
-        cell_kernel,
+        functools.partial(cell_kernel, depth),
         [shape((n, main, LANES), BF16), shape((WIDTH, slots), BF16)],
-        [rx, cells, rank, zr, home, lp],
+        [rx, cells, rank, zr, home, by_rows],
         big,
-        scratch=sum_scratch + [pair_rows, deep_rows],
+        scratch=sum_scratch + [pair_rows, deep_rows, basis],
         grant=20,
     )
     columns = exchange(msg)
+    (term,) = run(
+        skip_kernel,
+        [shape((WIDTH, slots), F32)],
+        [cells, rank, zr, home, lat, skip_weight, skip_bias.reshape(WIDTH, 1)],
+        2 * shared * WIDTH * slots,
+        scratch=[pltpu.VMEM((shared, slots), BF16)] * 2,
+    )
     (weights,) = run(
         weight_kernel,
         [shape((MODES, WIDTH, LANES), BF16)],
@@ -788,23 +812,19 @@
         4 * MODES * low * rows * depth * WIDTH,
         scratch=[pltpu.VMEM((MODES * low * levels, LANES), F32)] * 2,
     )
-    slabs = exchange(msg)
-    lp, term = run(
-        functools.partial(skip_kernel, depth),
-        [basis, shape((WIDTH, slots), F32)],
-        [cells, by_rows, spec, rank, zr, home, lat, skip_weight, skip_bias.reshape(WIDTH, 1)],
-        2 * rows * LANES * slots,
-        scratch=[pltpu.VMEM((shared, slots), BF16)] * 2,
+    slabs, spec, lat, term, cells, zr, rank, home, pw = exchange_alone(
+        msg, spec, lat, term, cells, zr, rank, home, pw
     )
     msg, pre = run(
         functools.partial(pre_kernel, depth),
         [shape((n, WIDTH + own_rows, LANES), BF16), shape((WIDTH, slots), F32)],
-        [slabs, lp, term, cells, spec],
+        [slabs, by_rows, term, cells, spec],
         2 * rows * slots * depth * WIDTH,
-        scratch=[pltpu.VMEM((depth * WIDTH, rows), BF16)],
-    )
-    returned = exchange(msg)
-    (slope,) = run(slope_kernel, [shape(pre.shape, F32)], [pre], 100 * WIDTH * slots)
+        scratch=[pltpu.VMEM((depth * WIDTH, rows), BF16), basis],
+    )
+    returned, pre, lat, cells, zr, rank, home, pw = exchange_alone(
+        msg, pre, lat, cells, zr, rank, home, pw
+    )
     out_col = out_weight.reshape(WIDTH, 1)
     pressure, msg, own_spec = run(
         head_kernel,
@@ -821,48 +841,47 @@
             pltpu.VMEM((2, n, LANES), F32),
         ],
     )
-    grads = exchange(msg)
-    (lp,) = run(
-        functools.partial(basis_kernel, depth),
-        [basis],
-        [cells, by_rows, pressure],
-        2 * rows * LANES * slots,
+    grads, pressure, own_spec, pre, lat, cells, zr, rank, home = exchange_alone(
+        msg, pressure, own_spec, pre, lat, cells, zr, rank, home
     )
     scale = 1.0 / math.sqrt(points * n)
-    msg, skip_grad, forces, out_grad = run(
-        functools.partial(back_kernel, scale),
+    msg, forces, out_grad = run(
+        functools.partial(back_kernel, depth, scale),
         [
-            shape((peers, halves * main, LANES), BF16),
-            shape((WIDTH, WIDTH), F32),
+            shape((peers, halves * main + 8, LANES), BF16),
             shape((1, 2), F32),
             shape((1, WIDTH), F32),
         ],
-        [grads, targets.reshape(1, 2), cells, rank, zr, home, lp, lat, slope],
+        [grads, targets.reshape(1, 2), cells, rank, zr, home, by_rows, lat, pre],
         big,
         scratch=sum_scratch
         + [pltpu.VMEM((2 * WIDTH, slots), BF16), pair_rows, deep_rows]
-        + [pltpu.VMEM((WIDTH, slots), F32)],
+        + [pltpu.VMEM((WIDTH, slots), F32), basis],
         grant=20,
     )
-    grad_columns = lax.all_to_all(
-        msg, "gx", split_axis=0, concat_axis=0, tiled=True, axis_index_groups=near
-    )
-    for bit in (1, 2, 4, 8):
-        partner = [(index, index ^ bit) for index in range(n)]
-        skip_grad = skip_grad + lax.ppermute(skip_grad, "gx", partner)
+    grad_columns, forces, out_grad, own_spec = lax.optimization_barrier(
+        (
+            lax.all_to_all(
+                msg, "gx", split_axis=0, concat_axis=0, tiled=True, axis_index_groups=near
+            ),
+            forces,
+            out_grad,
+            own_spec,
+        )
+    )
     part_rows = MODES * high * levels // n
     (msg,) = run(
         spec_kernel,
-        [shape((n, part_rows, LANES), BF16)],
+        [shape((n, part_rows + 8, LANES), BF16)],
         [half, grad_columns, part_table],
         2 * MODES * high * rows * depth * WIDTH,
         scratch=[pltpu.VMEM((MODES * high * levels, LANES), F32)],
         smem=1,
     )
-    finals = exchange(msg)
-    (spec_grad,) = run(
+    finals, own_spec, forces, out_grad = exchange_alone(msg, own_spec, forces, out_grad)
+    spec_grad, skip_grad = run(
         functools.partial(final_kernel, peers),
-        [shape((spec_weight.shape[0], WIDTH, WIDTH), F32)],
+        [shape((spec_weight.shape[0], WIDTH, WIDTH), F32), shape((WIDTH, WIDTH), F32)],
         [finals, own_spec],
         2 * NMODE * WIDTH * WIDTH * depth // n,
     )

time: 144 us -> 136 us (0.944)
  blocking collectives: 0 us -> 27.8 us
  waiting for transfers between devices: 72.5 us -> 58.6 us
  starting transfers between devices: 38.9 us -> 25.1 us
  local copies, waits for them, and re-layouts: 5.44 us -> 0.38 us
  Pallas kernels: 24.3 us -> 22.3 us
    all_to_all x0 -> x2, blocking collectives: none -> 27.8 us  [exchange(): lax.all_to_all(message, 'gx', split_axis=0, concat_axis=0, tiled=True)]
    ppermute x4 -> x0, waiting for transfers between devices: 7.51 us -> none  [slab_step(): skip_grad = skip_grad + lax.ppermute(skip_grad, 'gx', partner)]
    all_to_all x6 -> x4, starting transfers between devices: 26.9 us -> 20 us  [exchange(): lax.all_to_all(message, 'gx', split_axis=0, concat_axis=0, tiled=True)]
    ppermute x4 -> x0, starting transfers between devices: 6.89 us -> none  [slab_step(): skip_grad = skip_grad + lax.ppermute(skip_grad, 'gx', partner)]
    all_to_all x6 -> x4, waiting for transfers between devices: 49.1 us -> 42.5 us  [exchange(): lax.all_to_all(message, 'gx', split_axis=0, concat_axis=0, tiled=True)]
    unnamed x40 -> x30, local copies, waits for them, and re-layouts: 5.13 us -> 0.07 us
    pallas_call x13 -> x11, Pallas kernels: 24.3 us -> 22.3 us  [run(): pl.pallas_call(kernel, out_shape=tuple(outs), in_specs=[scalar] * smem +...]
  transfers between devices with their start and end apart: 12 -> 6, of which waited for: 11 -> 6; matrix products, arithmetic and copies ran while one was open for 1% -> 0% of each run, Pallas kernels for 4% -> 3%
where the time goes in v8:
time: 136 us; the launch traced here: 135 us
  waiting for transfers between devices  58.6 us (43%)
  blocking collectives  27.8 us (20%)
  starting transfers between devices  25.1 us (18%)
  Pallas kernels  22.3 us (16%)
    all_to_all x4, waiting for transfers between devices, exchange(): lax.all_to_all(message, 'gx', split_axis=0, concat_axis=0, tiled=True)  42.5 us
    all_to_all x2, blocking collectives, exchange(): lax.all_to_all(message, 'gx', split_axis=0, concat_axis=0, tiled=True)  27.8 us
    pallas_call x11, Pallas kernels, run(): pl.pallas_call(kernel, out_shape=tuple(outs), in_specs=[scalar] * smem +...  22.3 us
    all_to_all x4, starting transfers between devices, exchange(): lax.all_to_all(message, 'gx', split_axis=0, concat_axis=0, tiled=True)  20 us
    all_to_all x1, waiting for transfers between devices, slab_step(): lax.all_to_all(msg, 'gx', split_axis=0, concat_axis=0, tiled=True, axis_i...  8.92 us
    ppermute x1, waiting for transfers between devices, slab_step(): other = lax.ppermute(own, 'groups', [(0, 1), (1, 0)])  7.15 us
    all_to_all x1, starting transfers between devices, slab_step(): lax.all_to_all(msg, 'gx', split_axis=0, concat_axis=0, tiled=True, axis_i...  3.54 us
  transfers between devices with their start and end apart: 6, of which 6 were waited for; matrix products, arithmetic and copies ran while one was open for 0% of the time, Pallas kernels for 3%

profile of v8, /device:TPU:0, one launch (start us, length us, event | category | flops | bytes accessed | tf_op | source)
XLA Modules:
  0.0 135.0 jit_solution(3123621404334180370)
XLA Ops:
  0.6 0.0 copy-start.11
  0.7 2.4 %shard_map.209 = (bf16[16,128,128]{2,1,0:T(8,128)(2,1)}, f32[16,128]{1,0:T(8,128)}) custom-call(s32[1]{0:T(128)} %bitcast.group_ref, s32[1,16]{1,0:T(1,128)} %count_hbm.1, s32[16,128]{1,0:T(8,128)} %bitcast.14, f32[16,128]{1,0:T(8,128)} %bitcast.25, f32[1,512]{1,0:T(1,128)} %bitcast.21, bf16[64,512]{1,0:T(8,128)(2,1)} %bitcast.24, bf16[64,64,64]{2,1,0:T(8,128)(2,1)} %weight_hbm.1), custom_call_target="tpu_custom_call" | custom-call | flops 167772160 | bytes 1140804 | tf_op jit(solution)/shard_map/pallas_call | solution.py:666
  3.1 7.4 %all-to-all-start = ((bf16[16,128,128]{2,1,0:T(8,128)(2,1)}), bf16[16,128,128]{2,1,0:T(8,128)(2,1)S(1)}, u32[]{:S(2)}, u32[]{:S(2)}) async-start(bf16[16,128,128]{2,1,0:T(8,128)(2,1)} %get-tuple-element.58), calls=%async_computation | async-start | bytes 1048576 | tf_op jit(solution)/shard_map/all_to_all | solution.py:727
  10.5 1.8 %shard_map.210 = (s32[16,128]{1,0:T(8,128)S(1)}, s32[16,128]{1,0:T(8,128)S(1)}, f32[256,128]{1,0:T(8,128)S(1)}) custom-call(s32[16,128]{1,0:T(8,128)S(1)} %bitcast.16), custom_call_target="tpu_custom_call" | custom-call | flops 134217728 | bytes 155648 | tf_op jit(solution)/shard_map/pallas_call | solution.py:666
  12.3 12.7 %all-to-all-done.rx_ref = bf16[16,128,128]{2,1,0:T(8,128)(2,1)S(1)} async-done(((bf16[16,128,128]{2,1,0:T(8,128)(2,1)}), bf16[16,128,128]{2,1,0:T(8,128)(2,1)S(1)}, u32[]{:S(2)}, u32[]{:S(2)}) %all-to-all-start) | async-done | bytes 524320 | tf_op jit(solution)/shard_map/all_to_all | solution.py:727
  25.0 3.5 %shard_map.211 = (bf16[16,128,128]{2,1,0:T(8,128)(2,1)}, bf16[64,2048]{1,0:T(8,128)(2,1)S(1)}) custom-call(bf16[16,128,128]{2,1,0:T(8,128)(2,1)S(1)} %all-to-all-done.rx_ref, s32[16,128]{1,0:T(8,128)S(1)} %bitcast.17, s32[16,128]{1,0:T(8,128)S(1)} %get-tuple-element.92.rank_ref, s32[16,128]{1,0:T(8,128)S(1)} %get-tuple-element.93.zr_ref, ...), custom_call_target="tpu_custom_call" | custom-call | flops 1610612736 | bytes 1531904 | tf_op jit(solution)/shard_map/pallas_call | solution.py:666
  28.5 4.2 %all-to-all-start.1 = ((bf16[16,128,128]{2,1,0:T(8,128)(2,1)}), bf16[16,128,128]{2,1,0:T(8,128)(2,1)S(1)}, u32[]{:S(2)}, u32[]{:S(2)}) async-start(bf16[16,128,128]{2,1,0:T(8,128)(2,1)} %get-tuple-element.62), calls=%async_computation.1 | async-start | bytes 1048576 | tf_op jit(solution)/shard_map/all_to_all | solution.py:727
  32.8 0.0 copy-start.12
  32.8 0.0 copy-start.3
  32.8 1.6 %collective-permute-start = (bf16[16,64,128]{2,1,0:T(8,128)(2,1)S(1)}, bf16[16,64,128]{2,1,0:T(8,128)(2,1)S(1)}, u32[]{:S(2)}, u32[]{:S(2)}) collective-permute-start(bf16[16,64,128]{2,1,0:T(8,128)(2,1)S(1)} %slice.4.own_ref), channel_id=1, source_target_pairs={{0,16},{16,0},{1,17},{17,1},{2,18},{18,2},{3,19},{19,3},{4,20},{20... | collective-permute-start | bytes 786440 | tf_op jit(solution)/shard_map/ppermute | solution.py:780
  34.4 7.2 %collective-permute-done.other_ref = bf16[16,64,128]{2,1,0:T(8,128)(2,1)S(1)} collective-permute-done((bf16[16,64,128]{2,1,0:T(8,128)(2,1)S(1)}, bf16[16,64,128]{2,1,0:T(8,128)(2,1)S(1)}, u32[]{:S(2)}, u32[]{:S(2)}) %collective-permute-start) | collective-permute-done | bytes 262176 | tf_op jit(solution)/shard_map/ppermute | solution.py:780
  41.5 0.1 shard_map.212.weight_ref
  41.6 5.6 %all-to-all-done.1.rx_ref = bf16[16,128,128]{2,1,0:T(8,128)(2,1)S(1)} async-done(((bf16[16,128,128]{2,1,0:T(8,128)(2,1)}), bf16[16,128,128]{2,1,0:T(8,128)(2,1)S(1)}, u32[]{:S(2)}, u32[]{:S(2)}) %all-to-all-start.1) | async-done | bytes 524320 | tf_op jit(solution)/shard_map/all_to_all | solution.py:727
  47.2 1.7 %shard_map.213 = (bf16[16,128,128]{2,1,0:T(8,128)(2,1)}, bf16[16,32,128]{2,1,0:T(8,128)(2,1)S(1)}) custom-call(bf16[16,128,128]{2,1,0:T(8,128)(2,1)S(1)} %all-to-all-done.1.rx_ref, bf16[32,64,128]{2,1,0:T(8,128)(2,1)S(1)} %shard_map.212.weight_ref, bf16[64,256]{1,0:T(8,128)(2,1)S(1)} %copy-done.2, bf16[256,64]{1,0:T(8,128)(2,1)S(1)} %copy-done.1), custom_call_target="tpu_custom_call" | custom-call | flops 67108864 | bytes 1769472 | tf_op jit(solution)/shard_map/pallas_call | solution.py:666
  48.9 4.1 %all-to-all-start.2 = ((bf16[16,128,128]{2,1,0:T(8,128)(2,1)}), bf16[16,128,128]{2,1,0:T(8,128)(2,1)S(1)}, u32[]{:S(2)}, u32[]{:S(2)}) async-start(bf16[16,128,128]{2,1,0:T(8,128)(2,1)} %get-tuple-element.63), calls=%async_computation.2 | async-start | bytes 1048576 | tf_op jit(solution)/shard_map/all_to_all | solution.py:727
  53.0 0.1 copy.23.bias_ref
  53.1 2.1 %shard_map.214.term_ref = f32[64,2048]{1,0:T(8,128)S(1)} custom-call(s32[16,128]{1,0:T(8,128)S(1)} %bitcast.18, s32[16,128]{1,0:T(8,128)S(1)} %get-tuple-element.92.rank_ref, s32[16,128]{1,0:T(8,128)S(1)} %get-tuple-element.93.zr_ref, f32[256,128]{1,0:T(8,128)S(1)} %get-tuple-element.94.home_ref, bf16[64,2048]{1,0:T(8,128)(2,1)S(1)} %get-tuple-element.95.lat_ref, ...), custom_call_target="tpu_custom_call" | custom-call | flops 67108864 | bytes 950528 | tf_op jit(solution)/shard_map/pallas_call | solution.py:666
  55.2 12.2 %all-to-all-done.2.rx_ref = bf16[16,128,128]{2,1,0:T(8,128)(2,1)S(1)} async-done(((bf16[16,128,128]{2,1,0:T(8,128)(2,1)}), bf16[16,128,128]{2,1,0:T(8,128)(2,1)S(1)}, u32[]{:S(2)}, u32[]{:S(2)}) %all-to-all-start.2) | async-done | bytes 524320 | tf_op jit(solution)/shard_map/all_to_all | solution.py:727
  67.5 0.0 copy-start.7
  67.5 2.3 %shard_map.215 = (bf16[16,96,128]{2,1,0:T(8,128)(2,1)}, f32[64,2048]{1,0:T(8,128)S(1)}) custom-call(bf16[16,128,128]{2,1,0:T(8,128)(2,1)S(1)} %all-to-all-done.2.rx_ref, bf16[256,128]{1,0:T(8,128)(2,1)S(1)} %copy-done.11, f32[64,2048]{1,0:T(8,128)S(1)} %shard_map.214.term_ref, s32[16,128]{1,0:T(8,128)S(1)} %bitcast.19, ...), custom_call_target="tpu_custom_call" | custom-call | flops 1073741824 | bytes 2170880 | tf_op jit(solution)/shard_map/pallas_call | solution.py:666
  69.9 4.2 %all-to-all-start.3 = ((bf16[16,96,128]{2,1,0:T(8,128)(2,1)}), bf16[16,96,128]{2,1,0:T(8,128)(2,1)S(1)}, u32[]{:S(2)}, u32[]{:S(2)}) async-start(bf16[16,96,128]{2,1,0:T(8,128)(2,1)} %get-tuple-element.71), calls=%async_computation.3 | async-start | bytes 786432 | tf_op jit(solution)/shard_map/all_to_all | solution.py:727
  74.1 0.1 copy.24.bias_ref
  74.2 0.1 copy.25.out_ref
  74.3 12.0 %all-to-all-done.3.rx_ref = bf16[16,96,128]{2,1,0:T(8,128)(2,1)S(1)} async-done(((bf16[16,96,128]{2,1,0:T(8,128)(2,1)}), bf16[16,96,128]{2,1,0:T(8,128)(2,1)S(1)}, u32[]{:S(2)}, u32[]{:S(2)}) %all-to-all-start.3) | async-done | bytes 393248 | tf_op jit(solution)/shard_map/all_to_all | solution.py:727
  86.3 2.2 %shard_map.216 = (f32[1,512]{1,0:T(1,128)}, bf16[16,72,128]{2,1,0:T(8,128)(2,1)S(1)}, bf16[16,32,128]{2,1,0:T(8,128)(2,1)S(1)}) custom-call(bf16[16,96,128]{2,1,0:T(8,128)(2,1)S(1)} %all-to-all-done.3.rx_ref, s32[16,128]{1,0:T(8,128)S(1)} %bitcast.15, f32[16,128]{1,0:T(8,128)S(1)} %copy-done.8, bf16[64,64]{1,0:T(8,128)(2,1)S(1)} %copy-done.7, ...), custom_call_target="tpu_custom_call" | custom-call | flops 402653184 | bytes 852480 | tf_op jit(solution)/shard_map/pallas_call | solution.py:666
  88.6 13.9 %all_to_all.35.rx_ref = bf16[16,72,128]{2,1,0:T(8,128)(2,1)S(1)} all-to-all(bf16[16,72,128]{2,1,0:T(8,128)(2,1)S(1)} %get-tuple-element.80), channel_id=1, replica_groups=mesh['groups'=2,'gx'=16] {'gx'}, dimensions={0} | all-to-all | bytes 589824 | tf_op jit(solution)/shard_map/all_to_all | solution.py:727
  102.5 3.9 %shard_map.217 = (bf16[8,264,128]{2,1,0:T(8,128)(2,1)}, f32[1,2]{1,0:T(1,128)}, f32[1,64]{1,0:T(1,128)}) custom-call(bf16[16,72,128]{2,1,0:T(8,128)(2,1)S(1)} %all_to_all.35.rx_ref, f32[1,2]{1,0:T(1,128)S(1)} %bitcast.23, s32[16,128]{1,0:T(8,128)S(1)} %bitcast.20, s32[16,128]{1,0:T(8,128)S(1)} %get-tuple-element.92.rank_ref, ...), custom_call_target="tpu_custom_call" | custom-call | flops 1610612736 | bytes 1843472 | tf_op jit(solution)/shard_map/pallas_call | solution.py:666
  106.4 3.5 %all-to-all-start.5 = ((bf16[8,264,128]{2,1,0:T(8,128)(2,1)}), bf16[8,264,128]{2,1,0:T(8,128)(2,1)S(1)}, u32[]{:S(2)}, u32[]{:S(2)}) async-start(bf16[8,264,128]{2,1,0:T(8,128)(2,1)} %get-tuple-element.97), calls=%async_computation.5 | async-start | bytes 1081344 | tf_op jit(solution)/shard_map/all_to_all | solution.py:864
  109.9 8.9 %all-to-all-done.5.rx_ref = bf16[8,264,128]{2,1,0:T(8,128)(2,1)S(1)} async-done(((bf16[8,264,128]{2,1,0:T(8,128)(2,1)}), bf16[8,264,128]{2,1,0:T(8,128)(2,1)S(1)}, u32[]{:S(2)}, u32[]{:S(2)}) %all-to-all-start.5) | async-done | bytes 540704 | tf_op jit(solution)/shard_map/all_to_all | solution.py:864
  118.8 0.3 shard_map.218
  119.2 13.9 %all_to_all.36.rx_ref = bf16[16,72,128]{2,1,0:T(8,128)(2,1)S(1)} all-to-all(bf16[16,72,128]{2,1,0:T(8,128)(2,1)S(1)} %shard_map.218), channel_id=1, replica_groups=mesh['groups'=2,'gx'=16] {'gx'}, dimensions={0} | all-to-all | bytes 589824 | tf_op jit(solution)/shard_map/all_to_all | solution.py:727
  133.1 2.0 %shard_map.219 = (f32[64,64,64]{2,1,0:T(8,128)}, f32[64,64]{1,0:T(8,128)}) custom-call(bf16[16,72,128]{2,1,0:T(8,128)(2,1)S(1)} %all_to_all.36.rx_ref, bf16[16,32,128]{2,1,0:T(8,128)(2,1)S(1)} %get-tuple-element.107.own_ref), custom_call_target="tpu_custom_call" | custom-call | flops 8388608 | bytes 1490944 | tf_op jit(solution)/shard_map/pallas_call | solution.py:666
  (27 shorter events, 0.1 us)
Async XLA Ops:
  0.6 24.4 %copy-start.11 = (bf16[256,128]{1,0:T(8,128)(2,1)S(1)}, bf16[256,128]{1,0:T(8,128)(2,1)}, u32[]{:S(2)}) copy-start(bf16[256,128]{1,0:T(8,128)(2,1)} %constant.33.clone.by_ref) | copy-start | bytes 196612
  0.6 9.9 %copy-start.5 = (s32[16,1,128]{2,1,0:T(1,128)S(1)}, s32[16,1,128]{2,1,0:T(1,128)}, u32[]{:S(2)}) copy-start(s32[16,1,128]{2,1,0:T(1,128)} %param.20) | copy-start | bytes 24580
  3.1 21.9 %all-to-all-start = ((bf16[16,128,128]{2,1,0:T(8,128)(2,1)}), bf16[16,128,128]{2,1,0:T(8,128)(2,1)S(1)}, u32[]{:S(2)}, u32[]{:S(2)}) async-start(bf16[16,128,128]{2,1,0:T(8,128)(2,1)} %get-tuple-element.58), calls=%async_computation | async-start | bytes 1048576 | tf_op jit(solution)/shard_map/all_to_all | solution.py:727
  28.5 18.7 %copy-start.1 = (bf16[256,64]{1,0:T(8,128)(2,1)S(1)}, bf16[256,64]{1,0:T(8,128)(2,1)}, u32[]{:S(2)}) copy-start(bf16[256,64]{1,0:T(8,128)(2,1)} %constant.34.clone.back_ref) | copy-start | bytes 98308
  28.5 18.7 %copy-start.2 = (bf16[64,256]{1,0:T(8,128)(2,1)S(1)}, bf16[64,256]{1,0:T(8,128)(2,1)}, u32[]{:S(2)}) copy-start(bf16[64,256]{1,0:T(8,128)(2,1)} %constant.35.clone.table_ref) | copy-start | bytes 98308
  28.5 18.7 %all-to-all-start.1 = ((bf16[16,128,128]{2,1,0:T(8,128)(2,1)}), bf16[16,128,128]{2,1,0:T(8,128)(2,1)S(1)}, u32[]{:S(2)}, u32[]{:S(2)}) async-start(bf16[16,128,128]{2,1,0:T(8,128)(2,1)} %get-tuple-element.62), calls=%async_computation.1 | async-start | bytes 1048576 | tf_op jit(solution)/shard_map/all_to_all | solution.py:727
  32.8 20.3 %copy-start.12 = (f32[64]{0:T(128)S(1)}, f32[64]{0:T(128)}, u32[]{:S(2)}) copy-start(f32[64]{0:T(128)} %param.28) | copy-start | bytes 772
  32.8 20.4 %copy-start.3 = (bf16[64,64]{1,0:T(8,128)(2,1)S(1)}, bf16[64,64]{1,0:T(8,128)(2,1)}, u32[]{:S(2)}) copy-start(bf16[64,64]{1,0:T(8,128)(2,1)} %skip_ref.1) | copy-start | bytes 24580
  32.8 8.7 %collective-permute-start = (bf16[16,64,128]{2,1,0:T(8,128)(2,1)S(1)}, bf16[16,64,128]{2,1,0:T(8,128)(2,1)S(1)}, u32[]{:S(2)}, u32[]{:S(2)}) collective-permute-start(bf16[16,64,128]{2,1,0:T(8,128)(2,1)S(1)} %slice.4.own_ref), channel_id=1, source_target_pairs={{0,16},{16,0},{1,17},{17,1},{2,18},{18,2},{3,19},{19,3},{4,20},{20... | collective-permute-start | bytes 786440 | tf_op jit(solution)/shard_map/ppermute | solution.py:780
  48.9 18.6 %all-to-all-start.2 = ((bf16[16,128,128]{2,1,0:T(8,128)(2,1)}), bf16[16,128,128]{2,1,0:T(8,128)(2,1)S(1)}, u32[]{:S(2)}, u32[]{:S(2)}) async-start(bf16[16,128,128]{2,1,0:T(8,128)(2,1)} %get-tuple-element.63), calls=%async_computation.2 | async-start | bytes 1048576 | tf_op jit(solution)/shard_map/all_to_all | solution.py:727
  67.5 6.6 %copy-start.13 = (f32[64]{0:T(128)S(1)}, f32[64]{0:T(128)}, u32[]{:S(2)}) copy-start(f32[64]{0:T(128)} %param.30) | copy-start | bytes 772
  67.5 6.7 %copy-start.14 = (f32[64]{0:T(128)S(1)}, f32[64]{0:T(128)}, u32[]{:S(2)}) copy-start(f32[64]{0:T(128)} %param.31) | copy-start | bytes 772
  67.5 18.8 %copy-start.4 = (s32[1,16,128]{2,1,0:T(8,128)S(1)}, s32[1,16,128]{2,1,0:T(8,128)}, u32[]{:S(2)}) copy-start(s32[1,16,128]{2,1,0:T(8,128)} %param.19) | copy-start | bytes 24580
  67.5 18.8 %copy-start.6 = (f32[512]{0:T(512)S(1)}, f32[512]{0:T(512)}, u32[]{:S(2)}) copy-start(f32[512]{0:T(512)} %param.23) | copy-start | bytes 6148
  67.5 18.8 %copy-start.7 = (bf16[64,64]{1,0:T(8,128)(2,1)S(1)}, bf16[64,64]{1,0:T(8,128)(2,1)}, u32[]{:S(2)}) copy-start(bf16[64,64]{1,0:T(8,128)(2,1)} %head_ref.1) | copy-start | bytes 24580
  67.5 18.8 %copy-start.8 = (f32[16,128]{1,0:T(8,128)S(1)}, f32[16,128]{1,0:T(8,128)}, u32[]{:S(2)}) copy-start(f32[16,128]{1,0:T(8,128)} %get-tuple-element.79.pw_ref) | copy-start | bytes 24580
  67.5 18.8 %copy-start.9 = (f32[2,512]{1,0:T(2,128)S(1)}, f32[2,512]{1,0:T(2,128)}, u32[]{:S(2)}) copy-start(f32[2,512]{1,0:T(2,128)} %normal_ref.1) | copy-start | bytes 12292
  69.9 32.6 %copy-start.10 = (f32[2]{0:T(128)S(1)}, f32[2]{0:T(128)}, u32[]{:S(2)}) copy-start(f32[2]{0:T(128)} %param.25) | copy-start | bytes 28
  69.9 16.4 %all-to-all-start.3 = ((bf16[16,96,128]{2,1,0:T(8,128)(2,1)}), bf16[16,96,128]{2,1,0:T(8,128)(2,1)S(1)}, u32[]{:S(2)}, u32[]{:S(2)}) async-start(bf16[16,96,128]{2,1,0:T(8,128)(2,1)} %get-tuple-element.71), calls=%async_computation.3 | async-start | bytes 786432 | tf_op jit(solution)/shard_map/all_to_all | solution.py:727
  102.5 16.4 %copy-start = (bf16[2,128,256]{2,1,0:T(8,128)(2,1)S(1)}, bf16[2,128,256]{2,1,0:T(8,128)(2,1)}, u32[]{:S(2)}) copy-start(bf16[2,128,256]{2,1,0:T(8,128)(2,1)} %constant.36.clone.table_ref) | copy-start | bytes 393220
  106.4 12.5 %all-to-all-start.5 = ((bf16[8,264,128]{2,1,0:T(8,128)(2,1)}), bf16[8,264,128]{2,1,0:T(8,128)(2,1)S(1)}, u32[]{:S(2)}, u32[]{:S(2)}) async-start(bf16[8,264,128]{2,1,0:T(8,128)(2,1)} %get-tuple-element.97), calls=%async_computation.5 | async-start | bytes 1081344 | tf_op jit(solution)/shard_map/all_to_all | solution.py:864

commit v9 on v8

--- a/solution.py
+++ b/solution.py
@@ -204,7 +204,7 @@
     return jnp.concatenate([ref[2 * pair : 2 * pair + 1, :], ref[2 * pair + 1 : 2 * pair + 2, :]], axis=1)
 
 
-def source_kernel(group_ref, count_hbm, point_hbm, kern_hbm, area_hbm, feat_hbm, weight_hbm, msg_ref, pw_ref, count_ref, point_ref, kern_ref, area_ref, feat_ref, weight_ref, sems):
+def source_kernel(group_ref, half_ref, count_hbm, point_hbm, kern_hbm, area_hbm, feat_hbm, weight_hbm, msg_ref, pw_ref, count_ref, point_ref, kern_ref, area_ref, feat_ref, weight_ref, sems):
     devices, points = point_ref.shape[0], feat_ref.shape[1]
     low = MODES // devices
     pieces = (
@@ -255,6 +255,12 @@
     return jnp.broadcast_to(row, (LANES, LANES)).T
 
 
+def column_of(row):
+    down = lax.broadcasted_iota(jnp.int32, (WIDTH, WIDTH), 0)
+    along = lax.broadcasted_iota(jnp.int32, (WIDTH, WIDTH), 1)
+    return jnp.sum(jnp.where(down == along, row, 0.0), axis=1, keepdims=True)
+
+
 def pick_rows(rank_ref, pick_ref):
     rows = lax.broadcasted_iota(jnp.int32, (pick_ref.shape[0], LANES), 0)
     for block in range(rank_ref.shape[0]):
@@ -420,7 +426,7 @@
         ).astype(BF16)
 
 
-def mode_kernel(rx_ref, weight_ref, table_ref, back_ref, msg_ref, spec_ref, sp_ref, mx_ref):
+def mode_kernel(rx_ref, weight_ref, table_ref, back_ref, term_ref, msg_ref, spec_ref, sp_ref, mx_ref):
     devices = rx_ref.shape[0]
     own_rows = spec_ref.shape[1]
     modes = table_ref.shape[0]
@@ -451,6 +457,7 @@
 
 def skip_kernel(cell_ref, rank_ref, zr_ref, home_ref, lat_ref, skip_ref, bias_ref, term_ref, pick_ref, first_ref):
     few = jnp.max(rank_ref[...]) < home_ref.shape[0]
+    bias = column_of(bias_ref[...])
     pick_rows(rank_ref, pick_ref)
     first_rows(cell_ref, zr_ref, home_ref, first_ref)
     shared = mm_nt(lat_ref[...], first_ref[...]).astype(BF16)
@@ -458,7 +465,7 @@
         span = slice(pair * 2 * LANES, (pair + 1) * 2 * LANES)
         later = jnp.logical_and(two_rows(rank_ref, pair) >= 0, few)
         latent = jnp.where(later, mm(shared, pick_ref[:, span]), lat_ref[:, span].astype(F32))
-        term_ref[:, span] = mm_tn(skip_ref[...], latent.astype(BF16)) + bias_ref[...]
+        term_ref[:, span] = mm_tn(skip_ref[...], latent.astype(BF16)) + bias
 
 
 def pre_kernel(depth, rx_ref, by_ref, term_ref, cell_ref, spec_ref, msg_ref, pre_ref, rt_ref, lp_ref):
@@ -499,12 +506,13 @@
     latent = sums[0:WIDTH] + sums[WIDTH : 2 * WIDTH] + sums[2 * WIDTH : 3 * WIDTH]
     first, second, third = three_parts(latent)
     weight = head_ref[...]
-    head_pre = mm_tn(weight, first) + mm_tn(weight, second) + mm_tn(weight, third) + bias_ref[...]
+    head_pre = mm_tn(weight, first) + mm_tn(weight, second) + mm_tn(weight, third) + column_of(bias_ref[...])
+    out_column = column_of(out_ref[...])
     head = gelu_value(head_pre)
-    pressure = jnp.sum(head * out_ref[...], axis=0, keepdims=True)
+    pressure = jnp.sum(head * out_column, axis=0, keepdims=True)
     pres_ref[...] = pressure
     along = [normal_ref[which : which + 1, :] * area_ref[...] for which in range(2)]
-    first, second, third = three_parts(out_ref[...] * gelu_slope(head_pre))
+    first, second, third = three_parts(out_column * gelu_slope(head_pre))
     grad = mm(weight, first) + mm(weight, second) + mm(weight, third)
     place = lax.broadcasted_iota(jnp.int32, (16, points), 0)
     extra = jnp.zeros((16, points), F32)
@@ -721,7 +729,8 @@
         )
     part_table = jnp.asarray(part_table.reshape(halves, MODES * high, rows))
     near = [[half * peers + peer for peer in range(peers)] for half in range(halves)]
-    half = (lax.axis_index("gx") // peers).astype(jnp.int32).reshape(1)
+    half = lax.shift_right_logical(lax.axis_index("gx"), peers.bit_length() - 1)
+    half = half.astype(jnp.int32).reshape(1)
 
     def exchange(message):
         return lax.all_to_all(message, "gx", split_axis=0, concat_axis=0, tiled=True)
@@ -736,7 +745,7 @@
     msg, pw = run(
         source_kernel,
         [shape((n, 2 * WIDTH, LANES), BF16), shape((n, LANES), F32)],
-        [group, counts, point_rows, kernel[0], area_row, point_feats.T, spec_weight],
+        [group, half, counts, point_rows, kernel[0], area_row, point_feats.T, spec_weight],
         2 * 80 * points * slots,
         scratch=[
             pltpu.VMEM((1, n), jnp.int32),
@@ -747,7 +756,7 @@
             pltpu.VMEM((MODES, WIDTH, WIDTH), BF16),
             pltpu.SemaphoreType.DMA((6,)),
         ],
-        smem=1,
+        smem=2,
         hbm=6,
         grant=60,
     )
@@ -794,7 +803,7 @@
     (term,) = run(
         skip_kernel,
         [shape((WIDTH, slots), F32)],
-        [cells, rank, zr, home, lat, skip_weight, skip_bias.reshape(WIDTH, 1)],
+        [cells, rank, zr, home, lat, skip_weight, skip_bias.reshape(1, WIDTH)],
         2 * shared * WIDTH * slots,
         scratch=[pltpu.VMEM((shared, slots), BF16)] * 2,
     )
@@ -808,7 +817,7 @@
     msg, spec = run(
         mode_kernel,
         [shape((n, main, LANES), BF16), shape((n, own_rows, LANES), BF16)],
-        [columns, weights, table, back],
+        [columns, weights, table, back, term],
         4 * MODES * low * rows * depth * WIDTH,
         scratch=[pltpu.VMEM((MODES * low * levels, LANES), F32)] * 2,
     )
@@ -825,7 +834,7 @@
     returned, pre, lat, cells, zr, rank, home, pw = exchange_alone(
         msg, pre, lat, cells, zr, rank, home, pw
     )
-    out_col = out_weight.reshape(WIDTH, 1)
+    out_row = out_weight.reshape(1, WIDTH)
     pressure, msg, own_spec = run(
         head_kernel,
         [
@@ -833,7 +842,7 @@
             shape((n, WIDTH + 8, LANES), BF16),
             shape((n, own_rows, LANES), BF16),
         ],
-        [returned, point_rows, pw, head_weight, head_bias.reshape(WIDTH, 1), out_col, area_row, normals],
+        [returned, point_rows, pw, head_weight, head_bias.reshape(1, WIDTH), out_row, area_row, normals],
         2 * 3 * WIDTH * points * slots,
         scratch=[
             pltpu.VMEM((3 * WIDTH, slots), BF16),

time: 136 us -> 132 us (0.971)
  blocking collectives: 27.8 us -> 73.9 us
  waiting for transfers between devices: 58.6 us -> 23.4 us
  starting transfers between devices: 25.1 us -> 13.2 us
  Pallas kernels: 22.3 us -> 20.3 us
    all_to_all x2 -> x4, blocking collectives: 27.8 us -> 61.5 us  [exchange(): lax.all_to_all(message, 'gx', split_axis=0, concat_axis=0, tiled=True)]
    all_to_all x4 -> x2, waiting for transfers between devices: 42.5 us -> 18.3 us  [exchange(): lax.all_to_all(message, 'gx', split_axis=0, concat_axis=0, tiled=True)]
    all_to_all x0 -> x1, blocking collectives: none -> 12.4 us  [slab_step(): lax.all_to_all(msg, 'gx', split_axis=0, concat_axis=0, tiled=True, axis_i...]
    all_to_all x1 -> x0, waiting for transfers between devices: 8.92 us -> none  [slab_step(): lax.all_to_all(msg, 'gx', split_axis=0, concat_axis=0, tiled=True, axis_i...]
    all_to_all x4 -> x2, starting transfers between devices: 20 us -> 11.6 us  [exchange(): lax.all_to_all(message, 'gx', split_axis=0, concat_axis=0, tiled=True)]
    all_to_all x1 -> x0, starting transfers between devices: 3.54 us -> none  [slab_step(): lax.all_to_all(msg, 'gx', split_axis=0, concat_axis=0, tiled=True, axis_i...]
    ppermute x1, waiting for transfers between devices: 7.15 us -> 5.03 us  [slab_step(): other = lax.ppermute(own, 'groups', [(0, 1), (1, 0)])]
    pallas_call x11, Pallas kernels: 22.3 us -> 20.3 us  [run(): pl.pallas_call(kernel, out_shape=tuple(outs), in_specs=[scalar] * smem +...]
  transfers between devices with their start and end apart: 6 -> 3, of which waited for: 6 -> 3; matrix products, arithmetic and copies ran while one was open for 0% -> 0% of each run, Pallas kernels for 3% -> 3%
where the time goes in v9:
time: 132 us
  blocking collectives  73.9 us (56%)
  waiting for transfers between devices  23.4 us (18%)
  Pallas kernels  20.3 us (15%)
  starting transfers between devices  13.2 us (10%)
    all_to_all x4, blocking collectives, exchange(): lax.all_to_all(message, 'gx', split_axis=0, concat_axis=0, tiled=True)  61.5 us
    pallas_call x11, Pallas kernels, run(): pl.pallas_call(kernel, out_shape=tuple(outs), in_specs=[scalar] * smem +...  20.3 us
    all_to_all x2, waiting for transfers between devices, exchange(): lax.all_to_all(message, 'gx', split_axis=0, concat_axis=0, tiled=True)  18.3 us
    all_to_all x1, blocking collectives, slab_step(): lax.all_to_all(msg, 'gx', split_axis=0, concat_axis=0, tiled=True, axis_i...  12.4 us
    all_to_all x2, starting transfers between devices, exchange(): lax.all_to_all(message, 'gx', split_axis=0, concat_axis=0, tiled=True)  11.6 us
    ppermute x1, waiting for transfers between devices, slab_step(): other = lax.ppermute(own, 'groups', [(0, 1), (1, 0)])  5.03 us
  transfers between devices with their start and end apart: 3, of which 3 were waited for; matrix products, arithmetic and copies ran while one was open for 0% of the time, Pallas kernels for 3%

profile of v9, /device:TPU:0, one launch (start us, length us, event | category | flops | bytes accessed | tf_op | source)
XLA Modules:
  0.0 131.7 jit_solution(13918796301672835530)
XLA Ops:
  0.6 0.0 copy-start.14
  0.6 0.0 copy-start.5
  0.7 2.4 %shard_map.209 = (bf16[16,128,128]{2,1,0:T(8,128)(2,1)}, f32[16,128]{1,0:T(8,128)}) custom-call(s32[1]{0:T(128)} %bitcast.group_ref, s32[1]{0:T(128)} %bitcast.1.half_ref, s32[1,16]{1,0:T(1,128)} %count_hbm.1, s32[16,128]{1,0:T(8,128)} %bitcast.14, f32[16,128]{1,0:T(8,128)} %bitcast.28, f32[1,512]{1,0:T(1,128)} %bitcast.21, bf16[64,512]{1,0:T(8,128)(2,1)} %bitcast.27, ...), custom_call_target="tpu_custom_call" | custom-call | flops 167772160 | bytes 1140808 | tf_op jit(solution)/shard_map/pallas_call | solution.py:674
  3.1 7.4 %all-to-all-start = ((bf16[16,128,128]{2,1,0:T(8,128)(2,1)}), bf16[16,128,128]{2,1,0:T(8,128)(2,1)S(1)}, u32[]{:S(2)}, u32[]{:S(2)}) async-start(bf16[16,128,128]{2,1,0:T(8,128)(2,1)} %get-tuple-element.58), calls=%async_computation | async-start | bytes 1048576 | tf_op jit(solution)/shard_map/all_to_all | solution.py:736
  10.5 0.0 copy-done.5
  10.5 1.8 %shard_map.210 = (s32[16,128]{1,0:T(8,128)S(1)}, s32[16,128]{1,0:T(8,128)S(1)}, f32[256,128]{1,0:T(8,128)S(1)}) custom-call(s32[16,128]{1,0:T(8,128)S(1)} %bitcast.16), custom_call_target="tpu_custom_call" | custom-call | flops 134217728 | bytes 155648 | tf_op jit(solution)/shard_map/pallas_call | solution.py:674
  12.3 12.7 %all-to-all-done.rx_ref = bf16[16,128,128]{2,1,0:T(8,128)(2,1)S(1)} async-done(((bf16[16,128,128]{2,1,0:T(8,128)(2,1)}), bf16[16,128,128]{2,1,0:T(8,128)(2,1)S(1)}, u32[]{:S(2)}, u32[]{:S(2)}) %all-to-all-start) | async-done | bytes 524320 | tf_op jit(solution)/shard_map/all_to_all | solution.py:736
  25.0 0.0 copy-done.14
  25.0 3.5 %shard_map.211 = (bf16[16,128,128]{2,1,0:T(8,128)(2,1)}, bf16[64,2048]{1,0:T(8,128)(2,1)S(1)}) custom-call(bf16[16,128,128]{2,1,0:T(8,128)(2,1)S(1)} %all-to-all-done.rx_ref, s32[16,128]{1,0:T(8,128)S(1)} %bitcast.17, s32[16,128]{1,0:T(8,128)S(1)} %get-tuple-element.92.rank_ref, s32[16,128]{1,0:T(8,128)S(1)} %get-tuple-element.93.zr_ref, ...), custom_call_target="tpu_custom_call" | custom-call | flops 1610612736 | bytes 1531904 | tf_op jit(solution)/shard_map/pallas_call | solution.py:674
  28.5 4.2 %all-to-all-start.1 = ((bf16[16,128,128]{2,1,0:T(8,128)(2,1)}), bf16[16,128,128]{2,1,0:T(8,128)(2,1)S(1)}, u32[]{:S(2)}, u32[]{:S(2)}) async-start(bf16[16,128,128]{2,1,0:T(8,128)(2,1)} %get-tuple-element.62), calls=%async_computation.1 | async-start | bytes 1048576 | tf_op jit(solution)/shard_map/all_to_all | solution.py:736
  32.8 1.6 %collective-permute-start = (bf16[16,64,128]{2,1,0:T(8,128)(2,1)S(1)}, bf16[16,64,128]{2,1,0:T(8,128)(2,1)S(1)}, u32[]{:S(2)}, u32[]{:S(2)}) collective-permute-start(bf16[16,64,128]{2,1,0:T(8,128)(2,1)S(1)} %slice.4.own_ref), channel_id=1, source_target_pairs={{0,16},{16,0},{1,17},{17,1},{2,18},{18,2},{3,19},{19,3},{4,20},{20... | collective-permute-start | bytes 786440 | tf_op jit(solution)/shard_map/ppermute | solution.py:789
  34.3 0.0 copy-done.7
  34.3 2.1 %shard_map.213.term_ref = f32[64,2048]{1,0:T(8,128)S(1)} custom-call(s32[16,128]{1,0:T(8,128)S(1)} %bitcast.18, s32[16,128]{1,0:T(8,128)S(1)} %get-tuple-element.92.rank_ref, s32[16,128]{1,0:T(8,128)S(1)} %get-tuple-element.93.zr_ref, f32[256,128]{1,0:T(8,128)S(1)} %get-tuple-element.94.home_ref, bf16[64,2048]{1,0:T(8,128)(2,1)S(1)} %get-tuple-element.95.lat_ref, ...), custom_call_target="tpu_custom_call" | custom-call | flops 67108864 | bytes 950528 | tf_op jit(solution)/shard_map/pallas_call | solution.py:674
  36.5 5.0 %collective-permute-done.other_ref = bf16[16,64,128]{2,1,0:T(8,128)(2,1)S(1)} collective-permute-done((bf16[16,64,128]{2,1,0:T(8,128)(2,1)S(1)}, bf16[16,64,128]{2,1,0:T(8,128)(2,1)S(1)}, u32[]{:S(2)}, u32[]{:S(2)}) %collective-permute-start) | collective-permute-done | bytes 262176 | tf_op jit(solution)/shard_map/ppermute | solution.py:789
  41.5 0.1 shard_map.212.weight_ref
  41.6 5.6 %all-to-all-done.1.rx_ref = bf16[16,128,128]{2,1,0:T(8,128)(2,1)S(1)} async-done(((bf16[16,128,128]{2,1,0:T(8,128)(2,1)}), bf16[16,128,128]{2,1,0:T(8,128)(2,1)S(1)}, u32[]{:S(2)}, u32[]{:S(2)}) %all-to-all-start.1) | async-done | bytes 524320 | tf_op jit(solution)/shard_map/all_to_all | solution.py:736
  47.2 0.9 shard_map.214
  48.1 18.4 %all_to_all.35.rx_ref = bf16[16,128,128]{2,1,0:T(8,128)(2,1)S(1)} all-to-all(bf16[16,128,128]{2,1,0:T(8,128)(2,1)S(1)} %get-tuple-element.64), channel_id=1, replica_groups=mesh['groups'=2,'gx'=16] {'gx'}, dimensions={0} | all-to-all | bytes 1048576 | tf_op jit(solution)/shard_map/all_to_all | solution.py:736
  66.5 0.0 copy-start.10
  66.5 0.0 copy-start.11
  66.5 0.0 copy-start.12
  66.5 1.6 %shard_map.215 = (bf16[16,96,128]{2,1,0:T(8,128)(2,1)S(1)}, f32[64,2048]{1,0:T(8,128)S(1)}) custom-call(bf16[16,128,128]{2,1,0:T(8,128)(2,1)S(1)} %all_to_all.35.rx_ref, bf16[256,128]{1,0:T(8,128)(2,1)S(1)} %copy-done.14, f32[64,2048]{1,0:T(8,128)S(1)} %shard_map.213.term_ref, s32[16,128]{1,0:T(8,128)S(1)} %bitcast.19, ...), custom_call_target="tpu_custom_call" | custom-call | flops 1073741824 | bytes 2170880 | tf_op jit(solution)/shard_map/pallas_call | solution.py:674
  68.1 0.0 copy-start.13
  68.1 16.1 %all_to_all.36.rx_ref = bf16[16,96,128]{2,1,0:T(8,128)(2,1)S(1)} all-to-all(bf16[16,96,128]{2,1,0:T(8,128)(2,1)S(1)} %get-tuple-element.71), channel_id=1, replica_groups=mesh['groups'=2,'gx'=16] {'gx'}, dimensions={0} | all-to-all | bytes 786432 | tf_op jit(solution)/shard_map/all_to_all | solution.py:736
  84.2 0.0 copy-done.6
  84.3 2.2 %shard_map.216 = (f32[1,512]{1,0:T(1,128)}, bf16[16,72,128]{2,1,0:T(8,128)(2,1)S(1)}, bf16[16,32,128]{2,1,0:T(8,128)(2,1)S(1)}) custom-call(bf16[16,96,128]{2,1,0:T(8,128)(2,1)S(1)} %all_to_all.36.rx_ref, s32[16,128]{1,0:T(8,128)S(1)} %bitcast.15, f32[16,128]{1,0:T(8,128)S(1)} %copy-done.9, bf16[64,64]{1,0:T(8,128)(2,1)S(1)} %copy-done.8, ...), custom_call_target="tpu_custom_call" | custom-call | flops 402653184 | bytes 852480 | tf_op jit(solution)/shard_map/pallas_call | solution.py:674
  86.5 13.9 %all_to_all.37.rx_ref = bf16[16,72,128]{2,1,0:T(8,128)(2,1)S(1)} all-to-all(bf16[16,72,128]{2,1,0:T(8,128)(2,1)S(1)} %get-tuple-element.80), channel_id=1, replica_groups=mesh['groups'=2,'gx'=16] {'gx'}, dimensions={0} | all-to-all | bytes 589824 | tf_op jit(solution)/shard_map/all_to_all | solution.py:736
  100.4 3.4 %shard_map.217 = (bf16[8,264,128]{2,1,0:T(8,128)(2,1)S(1)}, f32[1,2]{1,0:T(1,128)}, f32[1,64]{1,0:T(1,128)}) custom-call(bf16[16,72,128]{2,1,0:T(8,128)(2,1)S(1)} %all_to_all.37.rx_ref, f32[1,2]{1,0:T(1,128)S(1)} %bitcast.26, s32[16,128]{1,0:T(8,128)S(1)} %bitcast.20, s32[16,128]{1,0:T(8,128)S(1)} %get-tuple-element.92.rank_ref, ...), custom_call_target="tpu_custom_call" | custom-call | flops 1610612736 | bytes 1843472 | tf_op jit(solution)/shard_map/pallas_call | solution.py:674
  103.8 12.4 %all_to_all.38.rx_ref = bf16[8,264,128]{2,1,0:T(8,128)(2,1)S(1)} all-to-all(bf16[8,264,128]{2,1,0:T(8,128)(2,1)S(1)} %get-tuple-element.97), channel_id=1, replica_groups={{0,1,2,3,4,5,6,7},{8,9,10,11,12,13,14,15},{16,17,18,19,20,21,22,23},{24..., dimensions={0} | all-to-all | bytes 1081344 | tf_op jit(solution)/shard_map/all_to_all | solution.py:873
  116.2 0.3 shard_map.218
  116.5 13.2 %all_to_all.39.rx_ref = bf16[16,72,128]{2,1,0:T(8,128)(2,1)S(1)} all-to-all(bf16[16,72,128]{2,1,0:T(8,128)(2,1)S(1)} %shard_map.218), channel_id=1, replica_groups=mesh['groups'=2,'gx'=16] {'gx'}, dimensions={0} | all-to-all | bytes 589824 | tf_op jit(solution)/shard_map/all_to_all | solution.py:736
  129.7 2.0 %shard_map.219 = (f32[64,64,64]{2,1,0:T(8,128)}, f32[64,64]{1,0:T(8,128)}) custom-call(bf16[16,72,128]{2,1,0:T(8,128)(2,1)S(1)} %all_to_all.39.rx_ref, bf16[16,32,128]{2,1,0:T(8,128)(2,1)S(1)} %get-tuple-element.107.own_ref), custom_call_target="tpu_custom_call" | custom-call | flops 8388608 | bytes 1490944 | tf_op jit(solution)/shard_map/pallas_call | solution.py:674
  (21 shorter events, 0.1 us)
Async XLA Ops:
  0.6 24.4 %copy-start.14 = (bf16[256,128]{1,0:T(8,128)(2,1)S(1)}, bf16[256,128]{1,0:T(8,128)(2,1)}, u32[]{:S(2)}) copy-start(bf16[256,128]{1,0:T(8,128)(2,1)} %constant.19.clone.by_ref) | copy-start | bytes 196612
  0.6 9.9 %copy-start.5 = (s32[16,1,128]{2,1,0:T(1,128)S(1)}, s32[16,1,128]{2,1,0:T(1,128)}, u32[]{:S(2)}) copy-start(s32[16,1,128]{2,1,0:T(1,128)} %param.20) | copy-start | bytes 24580
  3.1 21.9 %all-to-all-start = ((bf16[16,128,128]{2,1,0:T(8,128)(2,1)}), bf16[16,128,128]{2,1,0:T(8,128)(2,1)S(1)}, u32[]{:S(2)}, u32[]{:S(2)}) async-start(bf16[16,128,128]{2,1,0:T(8,128)(2,1)} %get-tuple-element.58), calls=%async_computation | async-start | bytes 1048576 | tf_op jit(solution)/shard_map/all_to_all | solution.py:736
  25.0 9.3 %copy-start.3 = (bf16[64,64]{1,0:T(8,128)(2,1)S(1)}, bf16[64,64]{1,0:T(8,128)(2,1)}, u32[]{:S(2)}) copy-start(bf16[64,64]{1,0:T(8,128)(2,1)} %skip_ref.1) | copy-start | bytes 24580
  25.0 9.3 %copy-start.7 = (f32[64]{0:T(128)S(1)}, f32[64]{0:T(128)}, u32[]{:S(2)}) copy-start(f32[64]{0:T(128)} %param.28) | copy-start | bytes 772
  28.5 18.7 %copy-start.1 = (bf16[256,64]{1,0:T(8,128)(2,1)S(1)}, bf16[256,64]{1,0:T(8,128)(2,1)}, u32[]{:S(2)}) copy-start(bf16[256,64]{1,0:T(8,128)(2,1)} %constant.20.clone.back_ref) | copy-start | bytes 98308
  28.5 18.7 %copy-start.2 = (bf16[64,256]{1,0:T(8,128)(2,1)S(1)}, bf16[64,256]{1,0:T(8,128)(2,1)}, u32[]{:S(2)}) copy-start(bf16[64,256]{1,0:T(8,128)(2,1)} %constant.21.clone.table_ref) | copy-start | bytes 98308
  28.5 18.7 %all-to-all-start.1 = ((bf16[16,128,128]{2,1,0:T(8,128)(2,1)}), bf16[16,128,128]{2,1,0:T(8,128)(2,1)S(1)}, u32[]{:S(2)}, u32[]{:S(2)}) async-start(bf16[16,128,128]{2,1,0:T(8,128)(2,1)} %get-tuple-element.62), calls=%async_computation.1 | async-start | bytes 1048576 | tf_op jit(solution)/shard_map/all_to_all | solution.py:736
  32.8 8.7 %collective-permute-start = (bf16[16,64,128]{2,1,0:T(8,128)(2,1)S(1)}, bf16[16,64,128]{2,1,0:T(8,128)(2,1)S(1)}, u32[]{:S(2)}, u32[]{:S(2)}) collective-permute-start(bf16[16,64,128]{2,1,0:T(8,128)(2,1)S(1)} %slice.4.own_ref), channel_id=1, source_target_pairs={{0,16},{16,0},{1,17},{17,1},{2,18},{18,2},{3,19},{19,3},{4,20},{20... | collective-permute-start | bytes 786440 | tf_op jit(solution)/shard_map/ppermute | solution.py:789
  66.5 17.7 %copy-start.4 = (s32[1,16,128]{2,1,0:T(8,128)S(1)}, s32[1,16,128]{2,1,0:T(8,128)}, u32[]{:S(2)}) copy-start(s32[1,16,128]{2,1,0:T(8,128)} %param.19) | copy-start | bytes 24580
  66.5 17.7 %copy-start.6 = (f32[512]{0:T(512)S(1)}, f32[512]{0:T(512)}, u32[]{:S(2)}) copy-start(f32[512]{0:T(512)} %param.23) | copy-start | bytes 6148
  66.5 17.7 %copy-start.8 = (bf16[64,64]{1,0:T(8,128)(2,1)S(1)}, bf16[64,64]{1,0:T(8,128)(2,1)}, u32[]{:S(2)}) copy-start(bf16[64,64]{1,0:T(8,128)(2,1)} %head_ref.1) | copy-start | bytes 24580
  66.5 17.7 %copy-start.9 = (f32[16,128]{1,0:T(8,128)S(1)}, f32[16,128]{1,0:T(8,128)}, u32[]{:S(2)}) copy-start(f32[16,128]{1,0:T(8,128)} %get-tuple-element.79.pw_ref) | copy-start | bytes 24580
  66.5 17.7 %copy-start.10 = (f32[2,512]{1,0:T(2,128)S(1)}, f32[2,512]{1,0:T(2,128)}, u32[]{:S(2)}) copy-start(f32[2,512]{1,0:T(2,128)} %normal_ref.1) | copy-start | bytes 12292
  66.5 17.7 %copy-start.11 = (f32[64]{0:T(128)S(1)}, f32[64]{0:T(128)}, u32[]{:S(2)}) copy-start(f32[64]{0:T(128)} %param.30) | copy-start | bytes 772
  66.5 17.7 %copy-start.12 = (f32[64]{0:T(128)S(1)}, f32[64]{0:T(128)}, u32[]{:S(2)}) copy-start(f32[64]{0:T(128)} %param.31) | copy-start | bytes 772
  68.1 32.3 %copy-start.13 = (f32[2]{0:T(128)S(1)}, f32[2]{0:T(128)}, u32[]{:S(2)}) copy-start(f32[2]{0:T(128)} %param.25) | copy-start | bytes 28
  100.4 15.8 %copy-start = (bf16[2,128,256]{2,1,0:T(8,128)(2,1)S(1)}, bf16[2,128,256]{2,1,0:T(8,128)(2,1)}, u32[]{:S(2)}) copy-start(bf16[2,128,256]{2,1,0:T(8,128)(2,1)} %constant.22.clone.table_ref) | copy-start | bytes 393220

commit v10 on v9

--- a/solution.py
+++ b/solution.py
@@ -287,8 +287,9 @@
             lp_ref[at : at + 16, pair * wide : (pair + 1) * wide] = found[at : at + 16] * mask
 
 
-def place_kernel(depth, cell_ref, zr_ref, rank_ref, home_ref, col_ref, flag_ref, pick_ref, part_ref):
+def place_kernel(depth, cell_ref, by_ref, zr_ref, rank_ref, home_ref, lp_ref, col_ref, flag_ref, pick_ref, part_ref):
     devices = cell_ref.shape[0]
+    basis_rows(depth, cell_ref, by_ref, lp_ref)
     down = lax.broadcasted_iota(jnp.int32, (LANES, LANES), 0)
     along = lax.broadcasted_iota(jnp.int32, (LANES, LANES), 1)
     place = lax.broadcasted_iota(jnp.int32, (16, LANES), 0)
@@ -366,18 +367,18 @@
             )
 
 
-def spread_depth(values, zpos, rp_ref, pair):
-    cut = slice(pair * 2 * LANES, (pair + 1) * 2 * LANES)
-    for level in range(rp_ref.shape[0] // WIDTH):
-        rp_ref[level * WIDTH : (level + 1) * WIDTH, cut] = jnp.where(
-            zpos == level, values, 0.0
-        ).astype(BF16)
-
-
-def slab_rows(lp_ref, rp_ref, msg_ref):
+def slab_rows(value_ref, zr_ref, lp_ref, rp_ref, msg_ref):
     devices = msg_ref.shape[0]
     step = lp_ref.shape[0] // devices
     for quad in range(rp_ref.shape[0] // (4 * WIDTH)):
+        for pair in range(zr_ref.shape[0] // 2):
+            cut = slice(pair * 2 * LANES, (pair + 1) * 2 * LANES)
+            zpos = two_rows(zr_ref, pair)
+            values = value_ref[:, cut].astype(F32)
+            for level in range(4 * quad, 4 * quad + 4):
+                rp_ref[level * WIDTH : (level + 1) * WIDTH, cut] = jnp.where(
+                    zpos == level, values, 0.0
+                ).astype(BF16)
         out = mm_nt(lp_ref[...], rp_ref[quad * 4 * WIDTH : (quad + 1) * 4 * WIDTH, :]).astype(BF16)
         for half in range(2):
             level = 2 * quad + half
@@ -387,7 +388,7 @@
                 ]
 
 
-def cell_kernel(depth, rx_ref, cell_ref, rank_ref, zr_ref, home_ref, by_ref, msg_ref, lat_ref, sums_ref, pick_ref, first_ref, full_ref, col_ref, xs_ref, rp_ref, lp_ref):
+def cell_kernel(rx_ref, cell_ref, rank_ref, zr_ref, home_ref, lp_ref, msg_ref, lat_ref, sums_ref, pick_ref, first_ref, full_ref, col_ref, xs_ref, rp_ref):
     devices = rx_ref.shape[0]
     for block in range(devices):
         xs_ref[:, block * LANES : (block + 1) * LANES] = rx_ref[block, 0:WIDTH, :]
@@ -395,13 +396,11 @@
         lambda span: xs_ref[:, span].astype(F32),
         xs_ref, cell_ref, rank_ref, zr_ref, home_ref, sums_ref, pick_ref, first_ref, full_ref, col_ref,
     )
-    basis_rows(depth, cell_ref, by_ref, lp_ref)
     for pair in range(devices // 2):
         cut = slice(pair * 2 * LANES, (pair + 1) * 2 * LANES)
         latent = sums_ref[:, cut]
         lat_ref[:, cut] = latent.astype(BF16)
-        spread_depth(latent, two_rows(zr_ref, pair), rp_ref, pair)
-    slab_rows(lp_ref, rp_ref, msg_ref)
+    slab_rows(lat_ref, zr_ref, lp_ref, rp_ref, msg_ref)
 
 
 def to_modes(rx_ref, table, sp_ref):
@@ -468,9 +467,8 @@
         term_ref[:, span] = mm_tn(skip_ref[...], latent.astype(BF16)) + bias
 
 
-def pre_kernel(depth, rx_ref, by_ref, term_ref, cell_ref, spec_ref, msg_ref, pre_ref, rt_ref, lp_ref):
+def pre_kernel(depth, rx_ref, lp_ref, term_ref, cell_ref, spec_ref, msg_ref, pre_ref, rt_ref):
     devices = rx_ref.shape[0]
-    basis_rows(depth, cell_ref, by_ref, lp_ref)
     rows = lp_ref.shape[0]
     step = rows // devices
     for level in range(rt_ref.shape[0] // LANES):
@@ -565,10 +563,9 @@
         msg_ref[block, WIDTH : WIDTH + 8, :] = tail.astype(BF16)
 
 
-def back_kernel(depth, scale, rx_ref, target_ref, cell_ref, rank_ref, zr_ref, home_ref, by_ref, lat_ref, pre_ref, msg_ref, force_ref, outg_ref, sums_ref, pick_ref, first_ref, full_ref, col_ref, xs_ref, pg_ref, rp_ref, gp_ref, lp_ref):
+def back_kernel(depth, scale, rx_ref, target_ref, cell_ref, rank_ref, zr_ref, home_ref, lp_ref, lat_ref, pre_ref, msg_ref, force_ref, outg_ref, sums_ref, pick_ref, first_ref, full_ref, col_ref, xs_ref, pg_ref, rp_ref, gp_ref):
     devices = rx_ref.shape[0]
     main = msg_ref.shape[1] - 8
-    basis_rows(depth, cell_ref, by_ref, lp_ref)
     extra = slice(WIDTH, WIDTH + 8)
     total = rx_ref[0, extra, :].astype(F32)
     for block in range(1, devices):
@@ -603,8 +600,7 @@
         grad = sums_ref[:, cut] * gelu_slope(pre_ref[:, cut])
         zpos = two_rows(zr_ref, pair)
         pg_ref[:, cut] = jnp.where(zpos >= 0, grad, 0.0).astype(BF16)
-        spread_depth(grad, zpos, rp_ref, pair)
-    slab_rows(lp_ref, rp_ref, msg_ref)
+    slab_rows(pg_ref, zr_ref, lp_ref, rp_ref, msg_ref)
     skip = mm_nt(lat_ref[...], pg_ref[...])
     for dest in range(msg_ref.shape[0]):
         msg_ref[dest, main : main + 8, :] = two_parts(skip[8 * dest : 8 * dest + 8]).astype(BF16)
@@ -762,14 +758,15 @@
     )
     rx = exchange(msg)
     shared = 256
-    zr, rank, home = run(
+    zr, rank, home, lp = run(
         functools.partial(place_kernel, depth),
         [
             shape((n, LANES), jnp.int32),
             shape((n, LANES), jnp.int32),
             shape((shared, LANES), F32),
+            shape((rows, slots), BF16),
         ],
-        [cells],
+        [cells, by_rows],
         2 * rows * LANES * slots,
         scratch=[
             pltpu.VMEM((slots, LANES), F32),
@@ -792,11 +789,11 @@
     deep_rows = pltpu.VMEM((depth * WIDTH, slots), BF16)
     big = 2 * WIDTH * slots * slots + 2 * rows * slots * depth * WIDTH
     msg, lat = run(
-        functools.partial(cell_kernel, depth),
+        cell_kernel,
         [shape((n, main, LANES), BF16), shape((WIDTH, slots), BF16)],
-        [rx, cells, rank, zr, home, by_rows],
+        [rx, cells, rank, zr, home, lp],
         big,
-        scratch=sum_scratch + [pair_rows, deep_rows, basis],
+        scratch=sum_scratch + [pair_rows, deep_rows],
         grant=20,
     )
     columns = exchange(msg)
@@ -827,9 +824,9 @@
     msg, pre = run(
         functools.partial(pre_kernel, depth),
         [shape((n, WIDTH + own_rows, LANES), BF16), shape((WIDTH, slots), F32)],
-        [slabs, by_rows, term, cells, spec],
+        [slabs, lp, term, cells, spec],
         2 * rows * slots * depth * WIDTH,
-        scratch=[pltpu.VMEM((depth * WIDTH, rows), BF16), basis],
+        scratch=[pltpu.VMEM((depth * WIDTH, rows), BF16)],
     )
     returned, pre, lat, cells, zr, rank, home, pw = exchange_alone(
         msg, pre, lat, cells, zr, rank, home, pw
@@ -861,11 +858,11 @@
             shape((1, 2), F32),
             shape((1, WIDTH), F32),
         ],
-        [grads, targets.reshape(1, 2), cells, rank, zr, home, by_rows, lat, pre],
+        [grads, targets.reshape(1, 2), cells, rank, zr, home, lp, lat, pre],
         big,
         scratch=sum_scratch
         + [pltpu.VMEM((2 * WIDTH, slots), BF16), pair_rows, deep_rows]
-        + [pltpu.VMEM((WIDTH, slots), F32), basis],
+        + [pltpu.VMEM((WIDTH, slots), F32)],
         grant=20,
     )
     grad_columns, forces, out_grad, own_spec = lax.optimization_barrier(

time: 132 us -> 132 us (level)
  no operation moved by 1% of the time
where the time goes in v10:
time: 132 us; the launch traced here: 131 us
  blocking collectives  73.9 us (56%)
  waiting for transfers between devices  22.9 us (17%)
  Pallas kernels  20.1 us (15%)
  starting transfers between devices  13.2 us (10%)
    all_to_all x4, blocking collectives, exchange(): lax.all_to_all(message, 'gx', split_axis=0, concat_axis=0, tiled=True)  61.5 us
    pallas_call x11, Pallas kernels, run(): pl.pallas_call(kernel, out_shape=tuple(outs), in_specs=[scalar] * smem +...  20.1 us
    all_to_all x2, waiting for transfers between devices, exchange(): lax.all_to_all(message, 'gx', split_axis=0, concat_axis=0, tiled=True)  17.9 us
    all_to_all x1, blocking collectives, slab_step(): lax.all_to_all(msg, 'gx', split_axis=0, concat_axis=0, tiled=True, axis_i...  12.4 us
    all_to_all x2, starting transfers between devices, exchange(): lax.all_to_all(message, 'gx', split_axis=0, concat_axis=0, tiled=True)  11.6 us
    ppermute x1, waiting for transfers between devices, slab_step(): other = lax.ppermute(own, 'groups', [(0, 1), (1, 0)])  5.03 us
  transfers between devices with their start and end apart: 3, of which 3 were waited for; matrix products, arithmetic and copies ran while one was open for 0% of the time, Pallas kernels for 3%

profile of v10, /device:TPU:0, one launch (start us, length us, event | category | flops | bytes accessed | tf_op | source)
XLA Modules:
  0.0 131.1 jit_solution(9265791452832724040)
XLA Ops:
  0.6 0.0 copy-start.14
  0.6 0.0 copy-start.5
  0.7 2.4 %shard_map.209 = (bf16[16,128,128]{2,1,0:T(8,128)(2,1)}, f32[16,128]{1,0:T(8,128)}) custom-call(s32[1]{0:T(128)} %bitcast.group_ref, s32[1]{0:T(128)} %bitcast.1.half_ref, s32[1,16]{1,0:T(1,128)} %count_hbm.1, s32[16,128]{1,0:T(8,128)} %bitcast.14, f32[16,128]{1,0:T(8,128)} %bitcast.28, f32[1,512]{1,0:T(1,128)} %bitcast.21, bf16[64,512]{1,0:T(8,128)(2,1)} %bitcast.27, ...), custom_call_target="tpu_custom_call" | custom-call | flops 167772160 | bytes 1140808 | tf_op jit(solution)/shard_map/pallas_call | solution.py:670
  3.1 7.4 %all-to-all-start = ((bf16[16,128,128]{2,1,0:T(8,128)(2,1)}), bf16[16,128,128]{2,1,0:T(8,128)(2,1)S(1)}, u32[]{:S(2)}, u32[]{:S(2)}) async-start(bf16[16,128,128]{2,1,0:T(8,128)(2,1)} %get-tuple-element.59), calls=%async_computation | async-start | bytes 1048576 | tf_op jit(solution)/shard_map/all_to_all | solution.py:732
  10.5 0.0 copy-done.14
  10.5 0.0 copy-done.5
  10.5 2.2 %shard_map.210 = (s32[16,128]{1,0:T(8,128)S(1)}, s32[16,128]{1,0:T(8,128)S(1)}, f32[256,128]{1,0:T(8,128)S(1)}, bf16[256,2048]{1,0:T(8,128)(2,1)S(1)}) custom-call(s32[16,128]{1,0:T(8,128)S(1)} %bitcast.16, bf16[256,128]{1,0:T(8,128)(2,1)S(1)} %copy-done.14), custom_call_target="tpu_custom_call" | custom-call | flops 134217728 | bytes 1269760 | tf_op jit(solution)/shard_map/pallas_call | solution.py:670
  12.7 12.3 %all-to-all-done.rx_ref = bf16[16,128,128]{2,1,0:T(8,128)(2,1)S(1)} async-done(((bf16[16,128,128]{2,1,0:T(8,128)(2,1)}), bf16[16,128,128]{2,1,0:T(8,128)(2,1)S(1)}, u32[]{:S(2)}, u32[]{:S(2)}) %all-to-all-start) | async-done | bytes 524320 | tf_op jit(solution)/shard_map/all_to_all | solution.py:732
  25.0 3.3 %shard_map.211 = (bf16[16,128,128]{2,1,0:T(8,128)(2,1)}, bf16[64,2048]{1,0:T(8,128)(2,1)S(1)}) custom-call(bf16[16,128,128]{2,1,0:T(8,128)(2,1)S(1)} %all-to-all-done.rx_ref, s32[16,128]{1,0:T(8,128)S(1)} %bitcast.17, s32[16,128]{1,0:T(8,128)S(1)} %get-tuple-element.94.rank_ref, s32[16,128]{1,0:T(8,128)S(1)} %get-tuple-element.95.zr_ref, ...), custom_call_target="tpu_custom_call" | custom-call | flops 1610612736 | bytes 2514944 | tf_op jit(solution)/shard_map/pallas_call | solution.py:670
  28.3 4.2 %all-to-all-start.1 = ((bf16[16,128,128]{2,1,0:T(8,128)(2,1)}), bf16[16,128,128]{2,1,0:T(8,128)(2,1)S(1)}, u32[]{:S(2)}, u32[]{:S(2)}) async-start(bf16[16,128,128]{2,1,0:T(8,128)(2,1)} %get-tuple-element.64), calls=%async_computation.1 | async-start | bytes 1048576 | tf_op jit(solution)/shard_map/all_to_all | solution.py:732
  32.6 1.6 %collective-permute-start = (bf16[16,64,128]{2,1,0:T(8,128)(2,1)S(1)}, bf16[16,64,128]{2,1,0:T(8,128)(2,1)S(1)}, u32[]{:S(2)}, u32[]{:S(2)}) collective-permute-start(bf16[16,64,128]{2,1,0:T(8,128)(2,1)S(1)} %slice.4.own_ref), channel_id=1, source_target_pairs={{0,16},{16,0},{1,17},{17,1},{2,18},{18,2},{3,19},{19,3},{4,20},{20... | collective-permute-start | bytes 786440 | tf_op jit(solution)/shard_map/ppermute | solution.py:786
  34.1 0.0 copy-done.3
  34.1 0.0 copy-done.7
  34.1 2.1 %shard_map.213.term_ref = f32[64,2048]{1,0:T(8,128)S(1)} custom-call(s32[16,128]{1,0:T(8,128)S(1)} %bitcast.18, s32[16,128]{1,0:T(8,128)S(1)} %get-tuple-element.94.rank_ref, s32[16,128]{1,0:T(8,128)S(1)} %get-tuple-element.95.zr_ref, f32[256,128]{1,0:T(8,128)S(1)} %get-tuple-element.96.home_ref, bf16[64,2048]{1,0:T(8,128)(2,1)S(1)} %get-tuple-element.97.lat_ref, ...), custom_call_target="tpu_custom_call" | custom-call | flops 67108864 | bytes 950528 | tf_op jit(solution)/shard_map/pallas_call | solution.py:670
  36.2 5.0 %collective-permute-done.other_ref = bf16[16,64,128]{2,1,0:T(8,128)(2,1)S(1)} collective-permute-done((bf16[16,64,128]{2,1,0:T(8,128)(2,1)S(1)}, bf16[16,64,128]{2,1,0:T(8,128)(2,1)S(1)}, u32[]{:S(2)}, u32[]{:S(2)}) %collective-permute-start) | collective-permute-done | bytes 262176 | tf_op jit(solution)/shard_map/ppermute | solution.py:786
  41.3 0.1 shard_map.212.weight_ref
  41.3 5.6 %all-to-all-done.1.rx_ref = bf16[16,128,128]{2,1,0:T(8,128)(2,1)S(1)} async-done(((bf16[16,128,128]{2,1,0:T(8,128)(2,1)}), bf16[16,128,128]{2,1,0:T(8,128)(2,1)S(1)}, u32[]{:S(2)}, u32[]{:S(2)}) %all-to-all-start.1) | async-done | bytes 524320 | tf_op jit(solution)/shard_map/all_to_all | solution.py:732
  47.0 0.9 shard_map.214
  47.9 18.4 %all_to_all.35.rx_ref = bf16[16,128,128]{2,1,0:T(8,128)(2,1)S(1)} all-to-all(bf16[16,128,128]{2,1,0:T(8,128)(2,1)S(1)} %get-tuple-element.66), channel_id=1, replica_groups=mesh['groups'=2,'gx'=16] {'gx'}, dimensions={0} | all-to-all | bytes 1048576 | tf_op jit(solution)/shard_map/all_to_all | solution.py:732
  66.3 0.0 copy-start.10
  66.3 0.0 copy-start.11
  66.3 0.0 copy-start.12
  66.3 1.3 %shard_map.215 = (bf16[16,96,128]{2,1,0:T(8,128)(2,1)S(1)}, f32[64,2048]{1,0:T(8,128)S(1)}) custom-call(bf16[16,128,128]{2,1,0:T(8,128)(2,1)S(1)} %all_to_all.35.rx_ref, bf16[256,2048]{1,0:T(8,128)(2,1)S(1)} %get-tuple-element.63.lp_ref, f32[64,2048]{1,0:T(8,128)S(1)} %shard_map.213.term_ref, s32[16,128]{1,0:T(8,128)S(1)} %bitcast.19, ...), custom_call_target="tpu_custom_call" | custom-call | flops 1073741824 | bytes 3153920 | tf_op jit(solution)/shard_map/pallas_call | solution.py:670
  67.7 0.0 copy-start.13
  67.7 16.1 %all_to_all.36.rx_ref = bf16[16,96,128]{2,1,0:T(8,128)(2,1)S(1)} all-to-all(bf16[16,96,128]{2,1,0:T(8,128)(2,1)S(1)} %get-tuple-element.73), channel_id=1, replica_groups=mesh['groups'=2,'gx'=16] {'gx'}, dimensions={0} | all-to-all | bytes 786432 | tf_op jit(solution)/shard_map/all_to_all | solution.py:732
  83.8 2.2 %shard_map.216 = (f32[1,512]{1,0:T(1,128)}, bf16[16,72,128]{2,1,0:T(8,128)(2,1)S(1)}, bf16[16,32,128]{2,1,0:T(8,128)(2,1)S(1)}) custom-call(bf16[16,96,128]{2,1,0:T(8,128)(2,1)S(1)} %all_to_all.36.rx_ref, s32[16,128]{1,0:T(8,128)S(1)} %bitcast.15, f32[16,128]{1,0:T(8,128)S(1)} %copy-done.9, bf16[64,64]{1,0:T(8,128)(2,1)S(1)} %copy-done.8, ...), custom_call_target="tpu_custom_call" | custom-call | flops 402653184 | bytes 852480 | tf_op jit(solution)/shard_map/pallas_call | solution.py:670
  86.1 13.9 %all_to_all.37.rx_ref = bf16[16,72,128]{2,1,0:T(8,128)(2,1)S(1)} all-to-all(bf16[16,72,128]{2,1,0:T(8,128)(2,1)S(1)} %get-tuple-element.82), channel_id=1, replica_groups=mesh['groups'=2,'gx'=16] {'gx'}, dimensions={0} | all-to-all | bytes 589824 | tf_op jit(solution)/shard_map/all_to_all | solution.py:732
  100.0 3.3 %shard_map.217 = (bf16[8,264,128]{2,1,0:T(8,128)(2,1)S(1)}, f32[1,2]{1,0:T(1,128)}, f32[1,64]{1,0:T(1,128)}) custom-call(bf16[16,72,128]{2,1,0:T(8,128)(2,1)S(1)} %all_to_all.37.rx_ref, f32[1,2]{1,0:T(1,128)S(1)} %bitcast.26, s32[16,128]{1,0:T(8,128)S(1)} %bitcast.20, s32[16,128]{1,0:T(8,128)S(1)} %get-tuple-element.94.rank_ref, ...), custom_call_target="tpu_custom_call" | custom-call | flops 1610612736 | bytes 2826512 | tf_op jit(solution)/shard_map/pallas_call | solution.py:670
  103.2 12.4 %all_to_all.38.rx_ref = bf16[8,264,128]{2,1,0:T(8,128)(2,1)S(1)} all-to-all(bf16[8,264,128]{2,1,0:T(8,128)(2,1)S(1)} %get-tuple-element.99), channel_id=1, replica_groups={{0,1,2,3,4,5,6,7},{8,9,10,11,12,13,14,15},{16,17,18,19,20,21,22,23},{24..., dimensions={0} | all-to-all | bytes 1081344 | tf_op jit(solution)/shard_map/all_to_all | solution.py:870
  115.6 0.3 shard_map.218
  115.9 13.2 %all_to_all.39.rx_ref = bf16[16,72,128]{2,1,0:T(8,128)(2,1)S(1)} all-to-all(bf16[16,72,128]{2,1,0:T(8,128)(2,1)S(1)} %shard_map.218), channel_id=1, replica_groups=mesh['groups'=2,'gx'=16] {'gx'}, dimensions={0} | all-to-all | bytes 589824 | tf_op jit(solution)/shard_map/all_to_all | solution.py:732
  129.1 2.0 %shard_map.219 = (f32[64,64,64]{2,1,0:T(8,128)}, f32[64,64]{1,0:T(8,128)}) custom-call(bf16[16,72,128]{2,1,0:T(8,128)(2,1)S(1)} %all_to_all.39.rx_ref, bf16[16,32,128]{2,1,0:T(8,128)(2,1)S(1)} %get-tuple-element.109.own_ref), custom_call_target="tpu_custom_call" | custom-call | flops 8388608 | bytes 1490944 | tf_op jit(solution)/shard_map/pallas_call | solution.py:670
  (21 shorter events, 0.1 us)
Async XLA Ops:
  0.6 9.9 %copy-start.14 = (bf16[256,128]{1,0:T(8,128)(2,1)S(1)}, bf16[256,128]{1,0:T(8,128)(2,1)}, u32[]{:S(2)}) copy-start(bf16[256,128]{1,0:T(8,128)(2,1)} %constant.19.clone.by_ref) | copy-start | bytes 196612
  0.6 9.9 %copy-start.5 = (s32[16,1,128]{2,1,0:T(1,128)S(1)}, s32[16,1,128]{2,1,0:T(1,128)}, u32[]{:S(2)}) copy-start(s32[16,1,128]{2,1,0:T(1,128)} %param.20) | copy-start | bytes 24580
  3.1 21.9 %all-to-all-start = ((bf16[16,128,128]{2,1,0:T(8,128)(2,1)}), bf16[16,128,128]{2,1,0:T(8,128)(2,1)S(1)}, u32[]{:S(2)}, u32[]{:S(2)}) async-start(bf16[16,128,128]{2,1,0:T(8,128)(2,1)} %get-tuple-element.59), calls=%async_computation | async-start | bytes 1048576 | tf_op jit(solution)/shard_map/all_to_all | solution.py:732
  25.0 9.1 %copy-start.3 = (bf16[64,64]{1,0:T(8,128)(2,1)S(1)}, bf16[64,64]{1,0:T(8,128)(2,1)}, u32[]{:S(2)}) copy-start(bf16[64,64]{1,0:T(8,128)(2,1)} %skip_ref.1) | copy-start | bytes 24580
  25.0 9.1 %copy-start.7 = (f32[64]{0:T(128)S(1)}, f32[64]{0:T(128)}, u32[]{:S(2)}) copy-start(f32[64]{0:T(128)} %param.28) | copy-start | bytes 772
  28.3 18.7 %copy-start.1 = (bf16[256,64]{1,0:T(8,128)(2,1)S(1)}, bf16[256,64]{1,0:T(8,128)(2,1)}, u32[]{:S(2)}) copy-start(bf16[256,64]{1,0:T(8,128)(2,1)} %constant.20.clone.back_ref) | copy-start | bytes 98308
  28.3 18.7 %copy-start.2 = (bf16[64,256]{1,0:T(8,128)(2,1)S(1)}, bf16[64,256]{1,0:T(8,128)(2,1)}, u32[]{:S(2)}) copy-start(bf16[64,256]{1,0:T(8,128)(2,1)} %constant.21.clone.table_ref) | copy-start | bytes 98308
  28.3 18.7 %all-to-all-start.1 = ((bf16[16,128,128]{2,1,0:T(8,128)(2,1)}), bf16[16,128,128]{2,1,0:T(8,128)(2,1)S(1)}, u32[]{:S(2)}, u32[]{:S(2)}) async-start(bf16[16,128,128]{2,1,0:T(8,128)(2,1)} %get-tuple-element.64), calls=%async_computation.1 | async-start | bytes 1048576 | tf_op jit(solution)/shard_map/all_to_all | solution.py:732
  32.6 8.7 %collective-permute-start = (bf16[16,64,128]{2,1,0:T(8,128)(2,1)S(1)}, bf16[16,64,128]{2,1,0:T(8,128)(2,1)S(1)}, u32[]{:S(2)}, u32[]{:S(2)}) collective-permute-start(bf16[16,64,128]{2,1,0:T(8,128)(2,1)S(1)} %slice.4.own_ref), channel_id=1, source_target_pairs={{0,16},{16,0},{1,17},{17,1},{2,18},{18,2},{3,19},{19,3},{4,20},{20... | collective-permute-start | bytes 786440 | tf_op jit(solution)/shard_map/ppermute | solution.py:786
  66.3 17.5 %copy-start.4 = (s32[1,16,128]{2,1,0:T(8,128)S(1)}, s32[1,16,128]{2,1,0:T(8,128)}, u32[]{:S(2)}) copy-start(s32[1,16,128]{2,1,0:T(8,128)} %param.19) | copy-start | bytes 24580
  66.3 17.5 %copy-start.6 = (f32[512]{0:T(512)S(1)}, f32[512]{0:T(512)}, u32[]{:S(2)}) copy-start(f32[512]{0:T(512)} %param.23) | copy-start | bytes 6148
  66.3 17.5 %copy-start.8 = (bf16[64,64]{1,0:T(8,128)(2,1)S(1)}, bf16[64,64]{1,0:T(8,128)(2,1)}, u32[]{:S(2)}) copy-start(bf16[64,64]{1,0:T(8,128)(2,1)} %head_ref.1) | copy-start | bytes 24580
  66.3 17.5 %copy-start.9 = (f32[16,128]{1,0:T(8,128)S(1)}, f32[16,128]{1,0:T(8,128)}, u32[]{:S(2)}) copy-start(f32[16,128]{1,0:T(8,128)} %get-tuple-element.81.pw_ref) | copy-start | bytes 24580
  66.3 17.5 %copy-start.10 = (f32[2,512]{1,0:T(2,128)S(1)}, f32[2,512]{1,0:T(2,128)}, u32[]{:S(2)}) copy-start(f32[2,512]{1,0:T(2,128)} %normal_ref.1) | copy-start | bytes 12292
  66.3 17.5 %copy-start.11 = (f32[64]{0:T(128)S(1)}, f32[64]{0:T(128)}, u32[]{:S(2)}) copy-start(f32[64]{0:T(128)} %param.30) | copy-start | bytes 772
  66.3 17.5 %copy-start.12 = (f32[64]{0:T(128)S(1)}, f32[64]{0:T(128)}, u32[]{:S(2)}) copy-start(f32[64]{0:T(128)} %param.31) | copy-start | bytes 772
  67.7 32.3 %copy-start.13 = (f32[2]{0:T(128)S(1)}, f32[2]{0:T(128)}, u32[]{:S(2)}) copy-start(f32[2]{0:T(128)} %param.25) | copy-start | bytes 28
  100.0 15.6 %copy-start = (bf16[2,128,256]{2,1,0:T(8,128)(2,1)S(1)}, bf16[2,128,256]{2,1,0:T(8,128)(2,1)}, u32[]{:S(2)}) copy-start(bf16[2,128,256]{2,1,0:T(8,128)(2,1)} %constant.22.clone.table_ref) | copy-start | bytes 393220

commit v11 on v10

--- a/solution.py
+++ b/solution.py
@@ -200,6 +200,16 @@
     return lax.dot_general(left, right, (((0,), (0,)), ((), ())), preferred_element_type=F32)
 
 
+def short_rows(count):
+    return lax.broadcasted_iota(jnp.int32, (count, LANES), 0).astype(jnp.int16)
+
+
+def matches(rows, row):
+    short = jnp.broadcast_to(row, (16, LANES)).astype(jnp.int16)
+    tall = jnp.broadcast_to(short[None], (rows.shape[0] // 16, 16, LANES)).reshape(rows.shape)
+    return jnp.where(rows == tall, jnp.ones((), BF16), jnp.zeros((), BF16))
+
+
 def two_rows(ref, pair):
     return jnp.concatenate([ref[2 * pair : 2 * pair + 1, :], ref[2 * pair + 1 : 2 * pair + 2, :]], axis=1)
 
@@ -231,10 +241,12 @@
         jnp.where(place == 1, second.astype(F32), jnp.where(place == 2, third.astype(F32), 0.0)),
     ).astype(BF16)
     table = jnp.concatenate([feat_ref[...], extra], axis=0)
-    rows = lax.broadcasted_iota(jnp.int32, (points, 2 * LANES), 0)
+    rows = short_rows(points)
     lane = lax.broadcasted_iota(jnp.int32, (1, LANES), 1)
     for pair in range(devices // 2):
-        hot = jnp.where(rows == two_rows(point_ref, pair), 1.0, 0.0).astype(BF16)
+        hot = jnp.concatenate(
+            [matches(rows, point_ref[at : at + 1, :]) for at in (2 * pair, 2 * pair + 1)], axis=1
+        )
         got = mm(table, hot)
         spread = got[WIDTH : WIDTH + 1] + got[WIDTH + 1 : WIDTH + 2] + got[WIDTH + 2 : WIDTH + 3]
         for half in range(2):
@@ -262,11 +274,11 @@
 
 
 def pick_rows(rank_ref, pick_ref):
-    rows = lax.broadcasted_iota(jnp.int32, (pick_ref.shape[0], LANES), 0)
+    rows = short_rows(pick_ref.shape[0])
     for block in range(rank_ref.shape[0]):
-        pick_ref[:, block * LANES : (block + 1) * LANES] = jnp.where(
-            rows == rank_ref[block : block + 1, :], 1.0, 0.0
-        ).astype(BF16)
+        pick_ref[:, block * LANES : (block + 1) * LANES] = matches(
+            rows, rank_ref[block : block + 1, :]
+        )
 
 
 def basis_rows(depth, cell_ref, by_ref, lp_ref):
@@ -325,12 +337,11 @@
 
 
 def first_rows(cell_ref, zr_ref, home_ref, first_ref):
+    homes = home_ref[...].astype(jnp.int32).astype(jnp.int16)
     for block in range(cell_ref.shape[0]):
         here = slice(block, block + 1)
-        row = jnp.where(zr_ref[here, :] < 0, -1.0, cell_ref[here, :].astype(F32))
-        first_ref[:, block * LANES : (block + 1) * LANES] = jnp.where(
-            home_ref[...] == row, 1.0, 0.0
-        ).astype(BF16)
+        row = jnp.where(zr_ref[here, :] < 0, -1, cell_ref[here, :])
+        first_ref[:, block * LANES : (block + 1) * LANES] = matches(homes, row)
 
 
 def fold_parts(values):
@@ -367,13 +378,13 @@
             )
 
 
-def slab_rows(value_ref, zr_ref, lp_ref, rp_ref, msg_ref):
+def slab_rows(value_ref, zpos_of, lp_ref, rp_ref, msg_ref):
     devices = msg_ref.shape[0]
     step = lp_ref.shape[0] // devices
     for quad in range(rp_ref.shape[0] // (4 * WIDTH)):
-        for pair in range(zr_ref.shape[0] // 2):
+        for pair in range(value_ref.shape[1] // (2 * LANES)):
             cut = slice(pair * 2 * LANES, (pair + 1) * 2 * LANES)
-            zpos = two_rows(zr_ref, pair)
+            zpos = zpos_of(pair)
             values = value_ref[:, cut].astype(F32)
             for level in range(4 * quad, 4 * quad + 4):
                 rp_ref[level * WIDTH : (level + 1) * WIDTH, cut] = jnp.where(
@@ -400,7 +411,7 @@
         cut = slice(pair * 2 * LANES, (pair + 1) * 2 * LANES)
         latent = sums_ref[:, cut]
         lat_ref[:, cut] = latent.astype(BF16)
-    slab_rows(lat_ref, zr_ref, lp_ref, rp_ref, msg_ref)
+    slab_rows(lat_ref, lambda pair: two_rows(zr_ref, pair), lp_ref, rp_ref, msg_ref)
 
 
 def to_modes(rx_ref, table, sp_ref):
@@ -454,7 +465,7 @@
             msg_ref[dest, level * step : (level + 1) * step, :] = out[dest * step : (dest + 1) * step]
 
 
-def skip_kernel(cell_ref, rank_ref, zr_ref, home_ref, lat_ref, skip_ref, bias_ref, term_ref, pick_ref, first_ref):
+def skip_kernel(cell_ref, rank_ref, zr_ref, home_ref, lat_ref, skip_ref, bias_ref, term_ref, full_ref, pick_ref, first_ref):
     few = jnp.max(rank_ref[...]) < home_ref.shape[0]
     bias = column_of(bias_ref[...])
     pick_rows(rank_ref, pick_ref)
@@ -464,6 +475,7 @@
         span = slice(pair * 2 * LANES, (pair + 1) * 2 * LANES)
         later = jnp.logical_and(two_rows(rank_ref, pair) >= 0, few)
         latent = jnp.where(later, mm(shared, pick_ref[:, span]), lat_ref[:, span].astype(F32))
+        full_ref[:, span] = latent.astype(BF16)
         term_ref[:, span] = mm_tn(skip_ref[...], latent.astype(BF16)) + bias
 
 
@@ -493,15 +505,15 @@
 def head_kernel(rx_ref, point_ref, pw_ref, head_ref, bias_ref, out_ref, area_ref, normal_ref, pres_ref, msg_ref, spec_ref, value_ref, hot_ref, na_ref):
     devices = rx_ref.shape[0]
     points = area_ref.shape[1]
-    rows = lax.broadcasted_iota(jnp.int32, (points, LANES), 0)
+    rows = short_rows(points)
     for block in range(devices):
         cut = slice(block * LANES, (block + 1) * LANES)
-        parts = three_parts(pw_ref[block : block + 1, :] * rx_ref[block, 0:WIDTH, :].astype(F32))
+        parts = three_parts(pw_ref[block : block + 1, :] * rx_ref[block, 0:WIDTH, :].astype(F32))[0:2]
         for index, part in enumerate(parts):
             value_ref[index * WIDTH : (index + 1) * WIDTH, cut] = part
-        hot_ref[:, cut] = jnp.where(rows == point_ref[block : block + 1, :], 1.0, 0.0).astype(BF16)
+        hot_ref[:, cut] = matches(rows, point_ref[block : block + 1, :])
     sums = mm_nt(value_ref[...], hot_ref[...])
-    latent = sums[0:WIDTH] + sums[WIDTH : 2 * WIDTH] + sums[2 * WIDTH : 3 * WIDTH]
+    latent = sums[0:WIDTH] + sums[WIDTH : 2 * WIDTH]
     first, second, third = three_parts(latent)
     weight = head_ref[...]
     head_pre = mm_tn(weight, first) + mm_tn(weight, second) + mm_tn(weight, third) + column_of(bias_ref[...])
@@ -563,7 +575,7 @@
         msg_ref[block, WIDTH : WIDTH + 8, :] = tail.astype(BF16)
 
 
-def back_kernel(depth, scale, rx_ref, target_ref, cell_ref, rank_ref, zr_ref, home_ref, lp_ref, lat_ref, pre_ref, msg_ref, force_ref, outg_ref, sums_ref, pick_ref, first_ref, full_ref, col_ref, xs_ref, pg_ref, rp_ref, gp_ref):
+def back_kernel(depth, scale, rx_ref, target_ref, cell_ref, lp_ref, lat_ref, pre_ref, msg_ref, force_ref, outg_ref, pg_ref, rp_ref):
     devices = rx_ref.shape[0]
     main = msg_ref.shape[1] - 8
     extra = slice(WIDTH, WIDTH + 8)
@@ -585,22 +597,15 @@
     for block in range(devices):
         tail = rx_ref[block, extra, :].astype(F32)
         factor = drag * (tail[0:1] + tail[1:2]) + lift * (tail[2:3] + tail[3:4])
-        grad = factor * rx_ref[block, 0:WIDTH, :].astype(F32)
         cut = slice(block * LANES, (block + 1) * LANES)
-        gp_ref[:, cut] = grad
-        upper = grad.astype(BF16)
-        xs_ref[0:WIDTH, cut] = upper
-        xs_ref[WIDTH : 2 * WIDTH, cut] = (grad - upper.astype(F32)).astype(BF16)
-    sum_cells(
-        lambda span: gp_ref[:, span],
-        xs_ref, cell_ref, rank_ref, zr_ref, home_ref, sums_ref, pick_ref, first_ref, full_ref, col_ref,
-    )
-    for pair in range(devices // 2):
-        cut = slice(pair * 2 * LANES, (pair + 1) * 2 * LANES)
-        grad = sums_ref[:, cut] * gelu_slope(pre_ref[:, cut])
-        zpos = two_rows(zr_ref, pair)
-        pg_ref[:, cut] = jnp.where(zpos >= 0, grad, 0.0).astype(BF16)
-    slab_rows(pg_ref, zr_ref, lp_ref, rp_ref, msg_ref)
+        slope = gelu_slope(pre_ref[:, cut])
+        grad = factor * rx_ref[block, 0:WIDTH, :].astype(F32) * slope
+        pg_ref[:, cut] = grad.astype(BF16)
+    slab_rows(
+        pg_ref,
+        lambda pair: jnp.bitwise_and(two_rows(cell_ref, pair), depth - 1),
+        lp_ref, rp_ref, msg_ref,
+    )
     skip = mm_nt(lat_ref[...], pg_ref[...])
     for dest in range(msg_ref.shape[0]):
         msg_ref[dest, main : main + 8, :] = two_parts(skip[8 * dest : 8 * dest + 8]).astype(BF16)
@@ -797,9 +802,9 @@
         grant=20,
     )
     columns = exchange(msg)
-    (term,) = run(
+    term, lat = run(
         skip_kernel,
-        [shape((WIDTH, slots), F32)],
+        [shape((WIDTH, slots), F32), shape((WIDTH, slots), BF16)],
         [cells, rank, zr, home, lat, skip_weight, skip_bias.reshape(1, WIDTH)],
         2 * shared * WIDTH * slots,
         scratch=[pltpu.VMEM((shared, slots), BF16)] * 2,
@@ -818,8 +823,8 @@
         4 * MODES * low * rows * depth * WIDTH,
         scratch=[pltpu.VMEM((MODES * low * levels, LANES), F32)] * 2,
     )
-    slabs, spec, lat, term, cells, zr, rank, home, pw = exchange_alone(
-        msg, spec, lat, term, cells, zr, rank, home, pw
+    slabs, spec, lat, term, cells, pw = exchange_alone(
+        msg, spec, lat, term, cells, pw
     )
     msg, pre = run(
         functools.partial(pre_kernel, depth),
@@ -828,8 +833,8 @@
         2 * rows * slots * depth * WIDTH,
         scratch=[pltpu.VMEM((depth * WIDTH, rows), BF16)],
     )
-    returned, pre, lat, cells, zr, rank, home, pw = exchange_alone(
-        msg, pre, lat, cells, zr, rank, home, pw
+    returned, pre, lat, cells, pw = exchange_alone(
+        msg, pre, lat, cells, pw
     )
     out_row = out_weight.reshape(1, WIDTH)
     pressure, msg, own_spec = run(
@@ -842,13 +847,13 @@
         [returned, point_rows, pw, head_weight, head_bias.reshape(1, WIDTH), out_row, area_row, normals],
         2 * 3 * WIDTH * points * slots,
         scratch=[
-            pltpu.VMEM((3 * WIDTH, slots), BF16),
+            pltpu.VMEM((2 * WIDTH, slots), BF16),
             pltpu.VMEM((points, slots), BF16),
             pltpu.VMEM((2, n, LANES), F32),
         ],
     )
-    grads, pressure, own_spec, pre, lat, cells, zr, rank, home = exchange_alone(
-        msg, pressure, own_spec, pre, lat, cells, zr, rank, home
+    grads, pressure, own_spec, pre, lat, cells = exchange_alone(
+        msg, pressure, own_spec, pre, lat, cells
     )
     scale = 1.0 / math.sqrt(points * n)
     msg, forces, out_grad = run(
@@ -858,11 +863,9 @@
             shape((1, 2), F32),
             shape((1, WIDTH), F32),
         ],
-        [grads, targets.reshape(1, 2), cells, rank, zr, home, lp, lat, pre],
-        big,
-        scratch=sum_scratch
-        + [pltpu.VMEM((2 * WIDTH, slots), BF16), pair_rows, deep_rows]
-        + [pltpu.VMEM((WIDTH, slots), F32)],
+        [grads, targets.reshape(1, 2), cells, lp, lat, pre],
+        2 * rows * slots * depth * WIDTH,
+        scratch=[pair_rows, deep_rows],
         grant=20,
     )
     grad_columns, forces, out_grad, own_spec = lax.optimization_barrier(

time: 132 us -> 130 us (0.985)
  Pallas kernels: 20.1 us -> 18.5 us
    pallas_call x11, Pallas kernels: 20.1 us -> 18.5 us  [run(): pl.pallas_call(kernel, out_shape=tuple(outs), in_specs=[scalar] * smem +...]
where the time goes in v11:
time: 130 us; the launch traced here: 129 us
  blocking collectives  73.9 us (57%)
  waiting for transfers between devices  22.9 us (18%)
  Pallas kernels  18.5 us (14%)
  starting transfers between devices  13.2 us (10%)
    all_to_all x4, blocking collectives, exchange(): lax.all_to_all(message, 'gx', split_axis=0, concat_axis=0, tiled=True)  61.5 us
    pallas_call x11, Pallas kernels, run(): pl.pallas_call(kernel, out_shape=tuple(outs), in_specs=[scalar] * smem +...  18.5 us
    all_to_all x2, waiting for transfers between devices, exchange(): lax.all_to_all(message, 'gx', split_axis=0, concat_axis=0, tiled=True)  17.9 us
    all_to_all x1, blocking collectives, slab_step(): lax.all_to_all(msg, 'gx', split_axis=0, concat_axis=0, tiled=True, axis_i...  12.4 us
    all_to_all x2, starting transfers between devices, exchange(): lax.all_to_all(message, 'gx', split_axis=0, concat_axis=0, tiled=True)  11.6 us
    ppermute x1, waiting for transfers between devices, slab_step(): other = lax.ppermute(own, 'groups', [(0, 1), (1, 0)])  5.01 us
  transfers between devices with their start and end apart: 3, of which 3 were waited for; matrix products, arithmetic and copies ran while one was open for 0% of the time, Pallas kernels for 3%

profile of v11, /device:TPU:0, one launch (start us, length us, event | category | flops | bytes accessed | tf_op | source)
XLA Modules:
  0.0 129.4 jit_solution(1825920862797077774)
XLA Ops:
  0.6 0.0 copy-start.14
  0.6 0.0 copy-start.5
  0.7 2.4 %shard_map.209 = (bf16[16,128,128]{2,1,0:T(8,128)(2,1)}, f32[16,128]{1,0:T(8,128)}) custom-call(s32[1]{0:T(128)} %bitcast.group_ref, s32[1]{0:T(128)} %bitcast.1.half_ref, s32[1,16]{1,0:T(1,128)} %count_hbm.1, s32[16,128]{1,0:T(8,128)} %bitcast.14, f32[16,128]{1,0:T(8,128)} %bitcast.28, f32[1,512]{1,0:T(1,128)} %bitcast.21, bf16[64,512]{1,0:T(8,128)(2,1)} %bitcast.27, ...), custom_call_target="tpu_custom_call" | custom-call | flops 167772160 | bytes 1140808 | tf_op jit(solution)/shard_map/pallas_call | solution.py:675
  3.1 7.4 %all-to-all-start = ((bf16[16,128,128]{2,1,0:T(8,128)(2,1)}), bf16[16,128,128]{2,1,0:T(8,128)(2,1)S(1)}, u32[]{:S(2)}, u32[]{:S(2)}) async-start(bf16[16,128,128]{2,1,0:T(8,128)(2,1)} %get-tuple-element.52), calls=%async_computation | async-start | bytes 1048576 | tf_op jit(solution)/shard_map/all_to_all | solution.py:737
  10.5 0.0 copy-done.14
  10.5 0.0 copy-done.5
  10.5 2.2 %shard_map.210 = (s32[16,128]{1,0:T(8,128)S(1)}, s32[16,128]{1,0:T(8,128)S(1)}, f32[256,128]{1,0:T(8,128)S(1)}, bf16[256,2048]{1,0:T(8,128)(2,1)S(1)}) custom-call(s32[16,128]{1,0:T(8,128)S(1)} %bitcast.16, bf16[256,128]{1,0:T(8,128)(2,1)S(1)} %copy-done.14), custom_call_target="tpu_custom_call" | custom-call | flops 134217728 | bytes 1269760 | tf_op jit(solution)/shard_map/pallas_call | solution.py:675
  12.7 12.3 %all-to-all-done.rx_ref = bf16[16,128,128]{2,1,0:T(8,128)(2,1)S(1)} async-done(((bf16[16,128,128]{2,1,0:T(8,128)(2,1)}), bf16[16,128,128]{2,1,0:T(8,128)(2,1)S(1)}, u32[]{:S(2)}, u32[]{:S(2)}) %all-to-all-start) | async-done | bytes 524320 | tf_op jit(solution)/shard_map/all_to_all | solution.py:737
  24.9 3.3 %shard_map.211 = (bf16[16,128,128]{2,1,0:T(8,128)(2,1)}, bf16[64,2048]{1,0:T(8,128)(2,1)S(1)}) custom-call(bf16[16,128,128]{2,1,0:T(8,128)(2,1)S(1)} %all-to-all-done.rx_ref, s32[16,128]{1,0:T(8,128)S(1)} %bitcast.17, s32[16,128]{1,0:T(8,128)S(1)} %get-tuple-element.53.rank_ref, s32[16,128]{1,0:T(8,128)S(1)} %get-tuple-element.54.zr_ref, ...), custom_call_target="tpu_custom_call" | custom-call | flops 1610612736 | bytes 2514944 | tf_op jit(solution)/shard_map/pallas_call | solution.py:675
  28.2 4.2 %all-to-all-start.1 = ((bf16[16,128,128]{2,1,0:T(8,128)(2,1)}), bf16[16,128,128]{2,1,0:T(8,128)(2,1)S(1)}, u32[]{:S(2)}, u32[]{:S(2)}) async-start(bf16[16,128,128]{2,1,0:T(8,128)(2,1)} %get-tuple-element.57), calls=%async_computation.1 | async-start | bytes 1048576 | tf_op jit(solution)/shard_map/all_to_all | solution.py:737
  32.5 1.6 %collective-permute-start = (bf16[16,64,128]{2,1,0:T(8,128)(2,1)S(1)}, bf16[16,64,128]{2,1,0:T(8,128)(2,1)S(1)}, u32[]{:S(2)}, u32[]{:S(2)}) collective-permute-start(bf16[16,64,128]{2,1,0:T(8,128)(2,1)S(1)} %slice.4.own_ref), channel_id=1, source_target_pairs={{0,16},{16,0},{1,17},{17,1},{2,18},{18,2},{3,19},{19,3},{4,20},{20... | collective-permute-start | bytes 786440 | tf_op jit(solution)/shard_map/ppermute | solution.py:791
  34.1 0.0 copy-done.3
  34.1 0.0 copy-done.7
  34.1 2.1 %shard_map.213 = (f32[64,2048]{1,0:T(8,128)S(1)}, bf16[64,2048]{1,0:T(8,128)(2,1)S(1)}) custom-call(s32[16,128]{1,0:T(8,128)S(1)} %bitcast.18, s32[16,128]{1,0:T(8,128)S(1)} %get-tuple-element.53.rank_ref, s32[16,128]{1,0:T(8,128)S(1)} %get-tuple-element.54.zr_ref, f32[256,128]{1,0:T(8,128)S(1)} %get-tuple-element.55.home_ref, ...), custom_call_target="tpu_custom_call" | custom-call | flops 67108864 | bytes 1212672 | tf_op jit(solution)/shard_map/pallas_call | solution.py:675
  36.2 5.0 %collective-permute-done.other_ref = bf16[16,64,128]{2,1,0:T(8,128)(2,1)S(1)} collective-permute-done((bf16[16,64,128]{2,1,0:T(8,128)(2,1)S(1)}, bf16[16,64,128]{2,1,0:T(8,128)(2,1)S(1)}, u32[]{:S(2)}, u32[]{:S(2)}) %collective-permute-start) | collective-permute-done | bytes 262176 | tf_op jit(solution)/shard_map/ppermute | solution.py:791
  41.2 0.1 shard_map.212.weight_ref
  41.3 5.6 %all-to-all-done.1.rx_ref = bf16[16,128,128]{2,1,0:T(8,128)(2,1)S(1)} async-done(((bf16[16,128,128]{2,1,0:T(8,128)(2,1)}), bf16[16,128,128]{2,1,0:T(8,128)(2,1)S(1)}, u32[]{:S(2)}, u32[]{:S(2)}) %all-to-all-start.1) | async-done | bytes 524320 | tf_op jit(solution)/shard_map/all_to_all | solution.py:737
  46.9 0.9 shard_map.214
  47.8 18.4 %all_to_all.35.rx_ref = bf16[16,128,128]{2,1,0:T(8,128)(2,1)S(1)} all-to-all(bf16[16,128,128]{2,1,0:T(8,128)(2,1)S(1)} %get-tuple-element.60), channel_id=1, replica_groups=mesh['groups'=2,'gx'=16] {'gx'}, dimensions={0} | all-to-all | bytes 1048576 | tf_op jit(solution)/shard_map/all_to_all | solution.py:737
  66.2 0.0 copy-start.10
  66.2 0.0 copy-start.11
  66.3 0.0 copy-start.12
  66.3 1.3 %shard_map.215 = (bf16[16,96,128]{2,1,0:T(8,128)(2,1)S(1)}, f32[64,2048]{1,0:T(8,128)S(1)}) custom-call(bf16[16,128,128]{2,1,0:T(8,128)(2,1)S(1)} %all_to_all.35.rx_ref, bf16[256,2048]{1,0:T(8,128)(2,1)S(1)} %get-tuple-element.56.lp_ref, f32[64,2048]{1,0:T(8,128)S(1)} %get-tuple-element.65.term_ref, s32[16,128]{1,0:T(8,128)S(1)} %bitcast.19, ...), custom_call_target="tpu_custom_call" | custom-call | flops 1073741824 | bytes 3153920 | tf_op jit(solution)/shard_map/pallas_call | solution.py:675
  67.6 0.0 copy-start.13
  67.6 16.1 %all_to_all.36.rx_ref = bf16[16,96,128]{2,1,0:T(8,128)(2,1)S(1)} all-to-all(bf16[16,96,128]{2,1,0:T(8,128)(2,1)S(1)} %get-tuple-element.68), channel_id=1, replica_groups=mesh['groups'=2,'gx'=16] {'gx'}, dimensions={0} | all-to-all | bytes 786432 | tf_op jit(solution)/shard_map/all_to_all | solution.py:737
  83.8 1.9 %shard_map.216 = (f32[1,512]{1,0:T(1,128)}, bf16[16,72,128]{2,1,0:T(8,128)(2,1)S(1)}, bf16[16,32,128]{2,1,0:T(8,128)(2,1)S(1)}) custom-call(bf16[16,96,128]{2,1,0:T(8,128)(2,1)S(1)} %all_to_all.36.rx_ref, s32[16,128]{1,0:T(8,128)S(1)} %bitcast.15, f32[16,128]{1,0:T(8,128)S(1)} %copy-done.9, bf16[64,64]{1,0:T(8,128)(2,1)S(1)} %copy-done.8, ...), custom_call_target="tpu_custom_call" | custom-call | flops 402653184 | bytes 852480 | tf_op jit(solution)/shard_map/pallas_call | solution.py:675
  85.7 13.9 %all_to_all.37.rx_ref = bf16[16,72,128]{2,1,0:T(8,128)(2,1)S(1)} all-to-all(bf16[16,72,128]{2,1,0:T(8,128)(2,1)S(1)} %get-tuple-element.74), channel_id=1, replica_groups=mesh['groups'=2,'gx'=16] {'gx'}, dimensions={0} | all-to-all | bytes 589824 | tf_op jit(solution)/shard_map/all_to_all | solution.py:737
  99.5 2.0 %shard_map.217 = (bf16[8,264,128]{2,1,0:T(8,128)(2,1)S(1)}, f32[1,2]{1,0:T(1,128)}, f32[1,64]{1,0:T(1,128)}) custom-call(bf16[16,72,128]{2,1,0:T(8,128)(2,1)S(1)} %all_to_all.37.rx_ref, f32[1,2]{1,0:T(1,128)S(1)} %bitcast.26, s32[16,128]{1,0:T(8,128)S(1)} %bitcast.20, bf16[256,2048]{1,0:T(8,128)(2,1)S(1)} %get-tuple-element.56.lp_ref, ...), custom_call_target="tpu_custom_call" | custom-call | flops 1073741824 | bytes 2679056 | tf_op jit(solution)/shard_map/pallas_call | solution.py:675
  101.6 12.4 %all_to_all.38.rx_ref = bf16[8,264,128]{2,1,0:T(8,128)(2,1)S(1)} all-to-all(bf16[8,264,128]{2,1,0:T(8,128)(2,1)S(1)} %get-tuple-element.85), channel_id=1, replica_groups={{0,1,2,3,4,5,6,7},{8,9,10,11,12,13,14,15},{16,17,18,19,20,21,22,23},{24..., dimensions={0} | all-to-all | bytes 1081344 | tf_op jit(solution)/shard_map/all_to_all | solution.py:873
  113.9 0.3 shard_map.218
  114.3 13.2 %all_to_all.39.rx_ref = bf16[16,72,128]{2,1,0:T(8,128)(2,1)S(1)} all-to-all(bf16[16,72,128]{2,1,0:T(8,128)(2,1)S(1)} %shard_map.218), channel_id=1, replica_groups=mesh['groups'=2,'gx'=16] {'gx'}, dimensions={0} | all-to-all | bytes 589824 | tf_op jit(solution)/shard_map/all_to_all | solution.py:737
  127.4 2.0 %shard_map.219 = (f32[64,64,64]{2,1,0:T(8,128)}, f32[64,64]{1,0:T(8,128)}) custom-call(bf16[16,72,128]{2,1,0:T(8,128)(2,1)S(1)} %all_to_all.39.rx_ref, bf16[16,32,128]{2,1,0:T(8,128)(2,1)S(1)} %get-tuple-element.95.own_ref), custom_call_target="tpu_custom_call" | custom-call | flops 8388608 | bytes 1490944 | tf_op jit(solution)/shard_map/pallas_call | solution.py:675
  (21 shorter events, 0.1 us)
Async XLA Ops:
  0.6 9.8 %copy-start.14 = (bf16[256,128]{1,0:T(8,128)(2,1)S(1)}, bf16[256,128]{1,0:T(8,128)(2,1)}, u32[]{:S(2)}) copy-start(bf16[256,128]{1,0:T(8,128)(2,1)} %constant.19.clone.by_ref) | copy-start | bytes 196612
  0.6 9.8 %copy-start.5 = (s32[16,1,128]{2,1,0:T(1,128)S(1)}, s32[16,1,128]{2,1,0:T(1,128)}, u32[]{:S(2)}) copy-start(s32[16,1,128]{2,1,0:T(1,128)} %param.20) | copy-start | bytes 24580
  3.1 21.9 %all-to-all-start = ((bf16[16,128,128]{2,1,0:T(8,128)(2,1)}), bf16[16,128,128]{2,1,0:T(8,128)(2,1)S(1)}, u32[]{:S(2)}, u32[]{:S(2)}) async-start(bf16[16,128,128]{2,1,0:T(8,128)(2,1)} %get-tuple-element.52), calls=%async_computation | async-start | bytes 1048576 | tf_op jit(solution)/shard_map/all_to_all | solution.py:737
  24.9 9.1 %copy-start.3 = (bf16[64,64]{1,0:T(8,128)(2,1)S(1)}, bf16[64,64]{1,0:T(8,128)(2,1)}, u32[]{:S(2)}) copy-start(bf16[64,64]{1,0:T(8,128)(2,1)} %skip_ref.1) | copy-start | bytes 24580
  24.9 9.1 %copy-start.7 = (f32[64]{0:T(128)S(1)}, f32[64]{0:T(128)}, u32[]{:S(2)}) copy-start(f32[64]{0:T(128)} %param.28) | copy-start | bytes 772
  28.2 18.7 %copy-start.1 = (bf16[256,64]{1,0:T(8,128)(2,1)S(1)}, bf16[256,64]{1,0:T(8,128)(2,1)}, u32[]{:S(2)}) copy-start(bf16[256,64]{1,0:T(8,128)(2,1)} %constant.20.clone.back_ref) | copy-start | bytes 98308
  28.2 18.7 %copy-start.2 = (bf16[64,256]{1,0:T(8,128)(2,1)S(1)}, bf16[64,256]{1,0:T(8,128)(2,1)}, u32[]{:S(2)}) copy-start(bf16[64,256]{1,0:T(8,128)(2,1)} %constant.21.clone.table_ref) | copy-start | bytes 98308
  28.2 18.7 %all-to-all-start.1 = ((bf16[16,128,128]{2,1,0:T(8,128)(2,1)}), bf16[16,128,128]{2,1,0:T(8,128)(2,1)S(1)}, u32[]{:S(2)}, u32[]{:S(2)}) async-start(bf16[16,128,128]{2,1,0:T(8,128)(2,1)} %get-tuple-element.57), calls=%async_computation.1 | async-start | bytes 1048576 | tf_op jit(solution)/shard_map/all_to_all | solution.py:737
  32.5 8.7 %collective-permute-start = (bf16[16,64,128]{2,1,0:T(8,128)(2,1)S(1)}, bf16[16,64,128]{2,1,0:T(8,128)(2,1)S(1)}, u32[]{:S(2)}, u32[]{:S(2)}) collective-permute-start(bf16[16,64,128]{2,1,0:T(8,128)(2,1)S(1)} %slice.4.own_ref), channel_id=1, source_target_pairs={{0,16},{16,0},{1,17},{17,1},{2,18},{18,2},{3,19},{19,3},{4,20},{20... | collective-permute-start | bytes 786440 | tf_op jit(solution)/shard_map/ppermute | solution.py:791
  66.2 17.5 %copy-start.4 = (s32[1,16,128]{2,1,0:T(8,128)S(1)}, s32[1,16,128]{2,1,0:T(8,128)}, u32[]{:S(2)}) copy-start(s32[1,16,128]{2,1,0:T(8,128)} %param.19) | copy-start | bytes 24580
  66.2 17.5 %copy-start.6 = (f32[512]{0:T(512)S(1)}, f32[512]{0:T(512)}, u32[]{:S(2)}) copy-start(f32[512]{0:T(512)} %param.23) | copy-start | bytes 6148
  66.2 17.5 %copy-start.8 = (bf16[64,64]{1,0:T(8,128)(2,1)S(1)}, bf16[64,64]{1,0:T(8,128)(2,1)}, u32[]{:S(2)}) copy-start(bf16[64,64]{1,0:T(8,128)(2,1)} %head_ref.1) | copy-start | bytes 24580
  66.2 17.5 %copy-start.9 = (f32[16,128]{1,0:T(8,128)S(1)}, f32[16,128]{1,0:T(8,128)}, u32[]{:S(2)}) copy-start(f32[16,128]{1,0:T(8,128)} %get-tuple-element.73.pw_ref) | copy-start | bytes 24580
  66.2 17.5 %copy-start.10 = (f32[2,512]{1,0:T(2,128)S(1)}, f32[2,512]{1,0:T(2,128)}, u32[]{:S(2)}) copy-start(f32[2,512]{1,0:T(2,128)} %normal_ref.1) | copy-start | bytes 12292
  66.2 17.5 %copy-start.11 = (f32[64]{0:T(128)S(1)}, f32[64]{0:T(128)}, u32[]{:S(2)}) copy-start(f32[64]{0:T(128)} %param.30) | copy-start | bytes 772
  66.3 17.5 %copy-start.12 = (f32[64]{0:T(128)S(1)}, f32[64]{0:T(128)}, u32[]{:S(2)}) copy-start(f32[64]{0:T(128)} %param.31) | copy-start | bytes 772
  67.6 31.9 %copy-start.13 = (f32[2]{0:T(128)S(1)}, f32[2]{0:T(128)}, u32[]{:S(2)}) copy-start(f32[2]{0:T(128)} %param.25) | copy-start | bytes 28
  99.5 14.4 %copy-start = (bf16[2,128,256]{2,1,0:T(8,128)(2,1)S(1)}, bf16[2,128,256]{2,1,0:T(8,128)(2,1)}, u32[]{:S(2)}) copy-start(bf16[2,128,256]{2,1,0:T(8,128)(2,1)} %constant.22.clone.table_ref) | copy-start | bytes 393220

commit v12 on v11

--- a/solution.py
+++ b/solution.py
@@ -180,6 +180,12 @@
     return table.astype(ml_dtypes.bfloat16)
 
 
+def gelu_both(values):
+    half = 0.5 * (1.0 + lax.erf(values * (1.0 / math.sqrt(2.0))))
+    bell = jnp.exp(-0.5 * values * values) * (1.0 / math.sqrt(2.0 * math.pi))
+    return values * half, half + values * bell
+
+
 def three_parts(values):
     first = values.astype(BF16)
     rest = values - first.astype(F32)
@@ -243,6 +249,7 @@
     table = jnp.concatenate([feat_ref[...], extra], axis=0)
     rows = short_rows(points)
     lane = lax.broadcasted_iota(jnp.int32, (1, LANES), 1)
+    kept = []
     for pair in range(devices // 2):
         hot = jnp.concatenate(
             [matches(rows, point_ref[at : at + 1, :]) for at in (2 * pair, 2 * pair + 1)], axis=1
@@ -254,8 +261,9 @@
             cut = slice(half * LANES, (half + 1) * LANES)
             valid = lane < count_ref[0:1, dest : dest + 1]
             weight = jnp.where(valid, kern_ref[dest : dest + 1, :], 0.0)
-            pw_ref[dest : dest + 1, :] = weight
+            kept.append(weight)
             msg_ref[dest, 0:WIDTH, :] = ((weight * spread[:, cut]) * got[0:WIDTH, cut]).astype(BF16)
+    pw_ref[...] = jnp.concatenate(kept, axis=0)
     copies[-1].wait()
     for dest in range(devices):
         msg_ref[dest, WIDTH : 2 * WIDTH, :] = jnp.concatenate(
@@ -299,12 +307,13 @@
             lp_ref[at : at + 16, pair * wide : (pair + 1) * wide] = found[at : at + 16] * mask
 
 
-def place_kernel(depth, cell_ref, by_ref, zr_ref, rank_ref, home_ref, lp_ref, col_ref, flag_ref, pick_ref, part_ref):
+def place_kernel(depth, cell_ref, by_ref, zr_ref, rank_ref, home_ref, lp_ref, col_ref, pick_ref, part_ref):
     devices = cell_ref.shape[0]
     basis_rows(depth, cell_ref, by_ref, lp_ref)
     down = lax.broadcasted_iota(jnp.int32, (LANES, LANES), 0)
     along = lax.broadcasted_iota(jnp.int32, (LANES, LANES), 1)
     place = lax.broadcasted_iota(jnp.int32, (16, LANES), 0)
+    seen = []
     for block in range(devices):
         cells = cell_ref[block : block + 1, :]
         row = cells.astype(F32)
@@ -318,11 +327,9 @@
         if block:
             early = jnp.where(col_ref[0 : block * LANES, :] == row, 1.0, 0.0)
             before = jnp.maximum(before, jnp.max(early, axis=0, keepdims=True))
-        zr_ref[block : block + 1, :] = jnp.where(
-            before > 0.0, -1, jnp.bitwise_and(cells, depth - 1)
-        )
-        flag_ref[block : block + 1, :] = before
-    flags = flag_ref[...]
+        seen.append(before)
+    flags = jnp.concatenate(seen, axis=0)
+    zr_ref[...] = jnp.where(flags > 0.0, -1, jnp.bitwise_and(cell_ref[...], depth - 1))
     marks = flags.astype(BF16)
     inside = mm(marks, jnp.where(down <= along, 1.0, 0.0).astype(BF16))
     above = jnp.where(down < along, 1.0, 0.0)[:, 0:devices][0:devices]
@@ -479,7 +486,7 @@
         term_ref[:, span] = mm_tn(skip_ref[...], latent.astype(BF16)) + bias
 
 
-def pre_kernel(depth, rx_ref, lp_ref, term_ref, cell_ref, spec_ref, msg_ref, pre_ref, rt_ref):
+def pre_kernel(depth, rx_ref, lp_ref, term_ref, cell_ref, spec_ref, msg_ref, slope_ref, rt_ref):
     devices = rx_ref.shape[0]
     rows = lp_ref.shape[0]
     step = rows // devices
@@ -494,15 +501,16 @@
         for level in range(1, depth):
             total += jnp.where(zpos == level, field[level * WIDTH : (level + 1) * WIDTH], 0.0)
         pre = total + term_ref[:, cut]
-        pre_ref[:, cut] = pre
-        feats = gelu_value(pre).astype(BF16)
+        feats, slope = gelu_both(pre)
+        slope_ref[:, cut] = slope
+        feats = feats.astype(BF16)
         for half in range(2):
             dest = 2 * pair + half
             msg_ref[dest, 0:WIDTH, :] = feats[:, half * LANES : (half + 1) * LANES]
-            msg_ref[dest, WIDTH:, :] = spec_ref[dest]
-
-
-def head_kernel(rx_ref, point_ref, pw_ref, head_ref, bias_ref, out_ref, area_ref, normal_ref, pres_ref, msg_ref, spec_ref, value_ref, hot_ref, na_ref):
+            msg_ref[dest, WIDTH : WIDTH + 16, :] = spec_ref[dest, 0:16, :]
+
+
+def head_kernel(rx_ref, point_ref, pw_ref, head_ref, bias_ref, out_ref, area_ref, normal_ref, own_ref, pres_ref, msg_ref, spec_ref, value_ref, hot_ref):
     devices = rx_ref.shape[0]
     points = area_ref.shape[1]
     rows = short_rows(points)
@@ -518,11 +526,11 @@
     weight = head_ref[...]
     head_pre = mm_tn(weight, first) + mm_tn(weight, second) + mm_tn(weight, third) + column_of(bias_ref[...])
     out_column = column_of(out_ref[...])
-    head = gelu_value(head_pre)
+    head, head_slope = gelu_both(head_pre)
     pressure = jnp.sum(head * out_column, axis=0, keepdims=True)
     pres_ref[...] = pressure
     along = [normal_ref[which : which + 1, :] * area_ref[...] for which in range(2)]
-    first, second, third = three_parts(out_column * gelu_slope(head_pre))
+    first, second, third = three_parts(out_column * head_slope)
     grad = mm(weight, first) + mm(weight, second) + mm(weight, third)
     place = lax.broadcasted_iota(jnp.int32, (16, points), 0)
     extra = jnp.zeros((16, points), F32)
@@ -554,31 +562,35 @@
         out_parts[0].astype(F32),
         jnp.where(place == 5, out_parts[1].astype(F32), jnp.where(place == 6, force_row, 0.0)),
     )
+    found = ([], [])
     for pair in range(devices // 2):
         got = mm(table, hot_ref[:, pair * 2 * LANES : (pair + 1) * 2 * LANES])
         for half in range(2):
             block = 2 * pair + half
             cut = slice(half * LANES, (half + 1) * LANES)
             msg_ref[block, 0:WIDTH, :] = got[0:WIDTH, cut].astype(BF16)
-            spec_ref[block] = rx_ref[block, WIDTH:, :]
+            spec_ref[block] = rx_ref[block, WIDTH : WIDTH + 16, :]
             for which in range(2):
                 at = WIDTH + 3 * which
-                na_ref[which, block : block + 1, :] = (
+                found[which].append(
                     got[at : at + 1, cut] + got[at + 1 : at + 2, cut] + got[at + 2 : at + 3, cut]
                 )
-    scaled = [three_parts(pw_ref[...] * na_ref[which]) for which in range(2)]
+    scaled = [
+        three_parts(pw_ref[...] * jnp.concatenate(found[which], axis=0)) for which in range(2)
+    ]
     rows = [scaled[which][index].astype(F32) for which in range(2) for index in range(2)]
     for block in range(devices):
         tail = common
         for index, row in enumerate(rows):
             tail = jnp.where(place == index, row[block : block + 1, :], tail)
-        msg_ref[block, WIDTH : WIDTH + 8, :] = tail.astype(BF16)
-
-
-def back_kernel(depth, scale, rx_ref, target_ref, cell_ref, lp_ref, lat_ref, pre_ref, msg_ref, force_ref, outg_ref, pg_ref, rp_ref):
+        tail = jnp.concatenate([tail, own_ref[block, 16:32, :].astype(F32)[0:8]], axis=0)
+        msg_ref[block, WIDTH : WIDTH + 16, :] = tail.astype(BF16)
+
+
+def back_kernel(depth, scale, rx_ref, target_ref, cell_ref, lp_ref, lat_ref, slope_ref, msg_ref, force_ref, outg_ref, spec_ref, pg_ref, rp_ref):
     devices = rx_ref.shape[0]
-    main = msg_ref.shape[1] - 8
-    extra = slice(WIDTH, WIDTH + 8)
+    main = msg_ref.shape[1] - 16
+    extra = slice(WIDTH, WIDTH + 16)
     total = rx_ref[0, extra, :].astype(F32)
     for block in range(1, devices):
         total += rx_ref[block, extra, :].astype(F32)
@@ -596,10 +608,10 @@
     outg_ref[...] = drag * out_row[:, 0:WIDTH] + lift * out_row[:, WIDTH : 2 * WIDTH]
     for block in range(devices):
         tail = rx_ref[block, extra, :].astype(F32)
+        spec_ref[block] = tail[8:16]
         factor = drag * (tail[0:1] + tail[1:2]) + lift * (tail[2:3] + tail[3:4])
         cut = slice(block * LANES, (block + 1) * LANES)
-        slope = gelu_slope(pre_ref[:, cut])
-        grad = factor * rx_ref[block, 0:WIDTH, :].astype(F32) * slope
+        grad = factor * rx_ref[block, 0:WIDTH, :].astype(F32) * slope_ref[:, cut]
         pg_ref[:, cut] = grad.astype(BF16)
     slab_rows(
         pg_ref,
@@ -608,7 +620,9 @@
     )
     skip = mm_nt(lat_ref[...], pg_ref[...])
     for dest in range(msg_ref.shape[0]):
-        msg_ref[dest, main : main + 8, :] = two_parts(skip[8 * dest : 8 * dest + 8]).astype(BF16)
+        rows = two_parts(skip[8 * dest : 8 * dest + 8])
+        rows = jnp.concatenate([rows, jnp.zeros_like(rows)], axis=0)
+        msg_ref[dest, main : main + 16, :] = rows.astype(BF16)
 
 
 def two_parts(values):
@@ -616,31 +630,37 @@
     return jnp.concatenate([first.astype(F32), second.astype(F32)], axis=1)
 
 
-def spec_kernel(half_ref, rx_ref, table_ref, msg_ref, sp_ref):
+def spec_kernel(half_ref, rx_ref, table_ref, own_ref, msg_ref, sp_ref):
     peers, devices = rx_ref.shape[0], msg_ref.shape[0]
     part_rows = sp_ref.shape[0] // devices
-    main = rx_ref.shape[1] - 8
+    main = rx_ref.shape[1] - 16
     to_modes(rx_ref, table_ref[half_ref[0]], sp_ref)
-    total = rx_ref[0, main : main + 8, :].astype(F32)
+    total = rx_ref[0, main : main + 16, :].astype(F32)
     for source in range(1, peers):
-        total += rx_ref[source, main : main + 8, :].astype(F32)
-    total = two_parts((total + swap_halves(total))[:, 0:WIDTH]).astype(BF16)
+        total += rx_ref[source, main : main + 16, :].astype(F32)
+    total = total[0:8]
+    total = two_parts((total + swap_halves(total))[:, 0:WIDTH])
     for dest in range(devices):
         msg_ref[dest, 0:part_rows, :] = sp_ref[dest * part_rows : (dest + 1) * part_rows, :].astype(BF16)
-        msg_ref[dest, part_rows : part_rows + 8, :] = total
-
-
-def final_kernel(peers, rx_ref, own_ref, spec_ref, skip_ref):
+        rows = jnp.concatenate([total, own_ref[dest, 16:32, :].astype(F32)[8:16]], axis=0)
+        msg_ref[dest, part_rows : part_rows + 16, :] = rows.astype(BF16)
+
+
+def final_kernel(peers, rx_ref, own_ref, next_ref, spec_ref, skip_ref):
     devices = rx_ref.shape[0]
     low = MODES // devices
     high = MODES // peers
     owned = spec_ref.shape[0] // MODES
     left = lax.broadcasted_iota(jnp.int32, (8, LANES), 1) < WIDTH
+    main = rx_ref.shape[1] - 16
     for which in range(owned):
         for source in range(devices):
-            at = which * 8 * low
-            coeffs = own_ref[source, at : at + 8 * low, :].astype(F32)
-            first, second = coeffs[0:8], coeffs[8:16]
+            if which == 0:
+                coeffs = own_ref[source].astype(F32)
+                first, second = coeffs[0:8], coeffs[8:16]
+            else:
+                first = next_ref[source]
+                second = rx_ref[source, main : main + 16, :].astype(F32)[8:16]
             block = [
                 jnp.where(left, first, 0.0),
                 jnp.where(left, swap_halves(first), 0.0),
@@ -659,11 +679,11 @@
             mode = which * MODES + low * source
             spec_ref[mode] = found[0:WIDTH]
             spec_ref[mode + 1] = found[WIDTH : 2 * WIDTH]
-    main = rx_ref.shape[1] - 8
     for peer in range(peers):
-        rows = rx_ref[peer, main : main + 8, :].astype(F32)
+        rows = rx_ref[peer, main : main + 16, :].astype(F32)
         for shift in range(peers, devices, peers):
-            rows += rx_ref[peer + shift, main : main + 8, :].astype(F32)
+            rows += rx_ref[peer + shift, main : main + 16, :].astype(F32)
+        rows = rows[0:8]
         skip_ref[8 * peer : 8 * peer + 8, :] = (rows + swap_halves(rows))[:, 0:WIDTH]
 
 
@@ -775,7 +795,6 @@
         2 * rows * LANES * slots,
         scratch=[
             pltpu.VMEM((slots, LANES), F32),
-            pltpu.VMEM((n, LANES), F32),
             pltpu.VMEM((shared, slots), BF16),
             pltpu.VMEM((16, slots), BF16),
         ],
@@ -828,40 +847,40 @@
     )
     msg, pre = run(
         functools.partial(pre_kernel, depth),
-        [shape((n, WIDTH + own_rows, LANES), BF16), shape((WIDTH, slots), F32)],
+        [shape((n, WIDTH + 16, LANES), BF16), shape((WIDTH, slots), F32)],
         [slabs, lp, term, cells, spec],
         2 * rows * slots * depth * WIDTH,
         scratch=[pltpu.VMEM((depth * WIDTH, rows), BF16)],
     )
-    returned, pre, lat, cells, pw = exchange_alone(
-        msg, pre, lat, cells, pw
+    returned, pre, lat, cells, pw, spec = exchange_alone(
+        msg, pre, lat, cells, pw, spec
     )
     out_row = out_weight.reshape(1, WIDTH)
     pressure, msg, own_spec = run(
         head_kernel,
         [
             shape((1, points), F32),
-            shape((n, WIDTH + 8, LANES), BF16),
-            shape((n, own_rows, LANES), BF16),
+            shape((n, WIDTH + 16, LANES), BF16),
+            shape((n, 16, LANES), BF16),
         ],
-        [returned, point_rows, pw, head_weight, head_bias.reshape(1, WIDTH), out_row, area_row, normals],
+        [returned, point_rows, pw, head_weight, head_bias.reshape(1, WIDTH), out_row, area_row, normals, spec],
         2 * 3 * WIDTH * points * slots,
         scratch=[
             pltpu.VMEM((2 * WIDTH, slots), BF16),
             pltpu.VMEM((points, slots), BF16),
-            pltpu.VMEM((2, n, LANES), F32),
         ],
     )
-    grads, pressure, own_spec, pre, lat, cells = exchange_alone(
-        msg, pressure, own_spec, pre, lat, cells
+    grads, pressure, own_spec, pre, lat, cells, spec = exchange_alone(
+        msg, pressure, own_spec, pre, lat, cells, spec
     )
     scale = 1.0 / math.sqrt(points * n)
-    msg, forces, out_grad = run(
+    msg, forces, out_grad, next_spec = run(
         functools.partial(back_kernel, depth, scale),
         [
-            shape((peers, halves * main + 8, LANES), BF16),
+            shape((peers, halves * main + 16, LANES), BF16),
             shape((1, 2), F32),
             shape((1, WIDTH), F32),
+            shape((n, 8, LANES), F32),
         ],
         [grads, targets.reshape(1, 2), cells, lp, lat, pre],
         2 * rows * slots * depth * WIDTH,
@@ -881,8 +900,8 @@
     part_rows = MODES * high * levels // n
     (msg,) = run(
         spec_kernel,
-        [shape((n, part_rows + 8, LANES), BF16)],
-        [half, grad_columns, part_table],
+        [shape((n, part_rows + 16, LANES), BF16)],
+        [half, grad_columns, part_table, spec],
         2 * MODES * high * rows * depth * WIDTH,
         scratch=[pltpu.VMEM((MODES * high * levels, LANES), F32)],
         smem=1,
@@ -891,7 +910,7 @@
     spec_grad, skip_grad = run(
         functools.partial(final_kernel, peers),
         [shape((spec_weight.shape[0], WIDTH, WIDTH), F32), shape((WIDTH, WIDTH), F32)],
-        [finals, own_spec],
+        [finals, own_spec, next_spec],
         2 * NMODE * WIDTH * WIDTH * depth // n,
     )
     return (pressure.reshape(points), forces.reshape(2), spec_grad, skip_grad, out_grad.reshape(WIDTH))

time: 130 us -> 130 us (level)
  no operation moved by 1% of the time
where the time goes in v12:
time: 130 us; the launch traced here: 129 us
  blocking collectives  73.8 us (57%)
  waiting for transfers between devices  22.9 us (18%)
  Pallas kernels  18.2 us (14%)
  starting transfers between devices  13.2 us (10%)
    all_to_all x4, blocking collectives, exchange(): lax.all_to_all(message, 'gx', split_axis=0, concat_axis=0, tiled=True)  61.3 us
    pallas_call x11, Pallas kernels, run(): pl.pallas_call(kernel, out_shape=tuple(outs), in_specs=[scalar] * smem +...  18.2 us
    all_to_all x2, waiting for transfers between devices, exchange(): lax.all_to_all(message, 'gx', split_axis=0, concat_axis=0, tiled=True)  17.9 us
    all_to_all x1, blocking collectives, slab_step(): lax.all_to_all(msg, 'gx', split_axis=0, concat_axis=0, tiled=True, axis_i...  12.5 us
    all_to_all x2, starting transfers between devices, exchange(): lax.all_to_all(message, 'gx', split_axis=0, concat_axis=0, tiled=True)  11.6 us
    ppermute x1, waiting for transfers between devices, slab_step(): other = lax.ppermute(own, 'groups', [(0, 1), (1, 0)])  5.01 us
  transfers between devices with their start and end apart: 3, of which 3 were waited for; matrix products, arithmetic and copies ran while one was open for 0% of the time, Pallas kernels for 3%

profile of v12, /device:TPU:0, one launch (start us, length us, event | category | flops | bytes accessed | tf_op | source)
XLA Modules:
  0.0 129.0 jit_solution(11163832923115957274)
XLA Ops:
  0.6 0.0 copy-start.14
  0.6 0.0 copy-start.5
  0.7 2.4 %shard_map.209 = (bf16[16,128,128]{2,1,0:T(8,128)(2,1)}, f32[16,128]{1,0:T(8,128)}) custom-call(s32[1]{0:T(128)} %bitcast.group_ref, s32[1]{0:T(128)} %bitcast.1.half_ref, s32[1,16]{1,0:T(1,128)} %count_hbm.1, s32[16,128]{1,0:T(8,128)} %bitcast.14, f32[16,128]{1,0:T(8,128)} %bitcast.28, f32[1,512]{1,0:T(1,128)} %bitcast.21, bf16[64,512]{1,0:T(8,128)(2,1)} %bitcast.27, ...), custom_call_target="tpu_custom_call" | custom-call | flops 167772160 | bytes 1140808 | tf_op jit(solution)/shard_map/pallas_call | solution.py:695
  3.1 7.4 %all-to-all-start = ((bf16[16,128,128]{2,1,0:T(8,128)(2,1)}), bf16[16,128,128]{2,1,0:T(8,128)(2,1)S(1)}, u32[]{:S(2)}, u32[]{:S(2)}) async-start(bf16[16,128,128]{2,1,0:T(8,128)(2,1)} %get-tuple-element.55), calls=%async_computation | async-start | bytes 1048576 | tf_op jit(solution)/shard_map/all_to_all | solution.py:757
  10.5 0.0 copy-done.14
  10.5 0.0 copy-done.5
  10.5 2.2 %shard_map.210 = (s32[16,128]{1,0:T(8,128)S(1)}, s32[16,128]{1,0:T(8,128)S(1)}, f32[256,128]{1,0:T(8,128)S(1)}, bf16[256,2048]{1,0:T(8,128)(2,1)S(1)}) custom-call(s32[16,128]{1,0:T(8,128)S(1)} %bitcast.16, bf16[256,128]{1,0:T(8,128)(2,1)S(1)} %copy-done.14), custom_call_target="tpu_custom_call" | custom-call | flops 134217728 | bytes 1269760 | tf_op jit(solution)/shard_map/pallas_call | solution.py:695
  12.7 12.2 %all-to-all-done.rx_ref = bf16[16,128,128]{2,1,0:T(8,128)(2,1)S(1)} async-done(((bf16[16,128,128]{2,1,0:T(8,128)(2,1)}), bf16[16,128,128]{2,1,0:T(8,128)(2,1)S(1)}, u32[]{:S(2)}, u32[]{:S(2)}) %all-to-all-start) | async-done | bytes 524320 | tf_op jit(solution)/shard_map/all_to_all | solution.py:757
  24.9 3.3 %shard_map.211 = (bf16[16,128,128]{2,1,0:T(8,128)(2,1)}, bf16[64,2048]{1,0:T(8,128)(2,1)S(1)}) custom-call(bf16[16,128,128]{2,1,0:T(8,128)(2,1)S(1)} %all-to-all-done.rx_ref, s32[16,128]{1,0:T(8,128)S(1)} %bitcast.17, s32[16,128]{1,0:T(8,128)S(1)} %get-tuple-element.56.rank_ref, s32[16,128]{1,0:T(8,128)S(1)} %get-tuple-element.57.zr_ref, ...), custom_call_target="tpu_custom_call" | custom-call | flops 1610612736 | bytes 2514944 | tf_op jit(solution)/shard_map/pallas_call | solution.py:695
  28.2 4.2 %all-to-all-start.1 = ((bf16[16,128,128]{2,1,0:T(8,128)(2,1)}), bf16[16,128,128]{2,1,0:T(8,128)(2,1)S(1)}, u32[]{:S(2)}, u32[]{:S(2)}) async-start(bf16[16,128,128]{2,1,0:T(8,128)(2,1)} %get-tuple-element.60), calls=%async_computation.1 | async-start | bytes 1048576 | tf_op jit(solution)/shard_map/all_to_all | solution.py:757
  32.5 1.6 %collective-permute-start = (bf16[16,64,128]{2,1,0:T(8,128)(2,1)S(1)}, bf16[16,64,128]{2,1,0:T(8,128)(2,1)S(1)}, u32[]{:S(2)}, u32[]{:S(2)}) collective-permute-start(bf16[16,64,128]{2,1,0:T(8,128)(2,1)S(1)} %slice.4.own_ref), channel_id=1, source_target_pairs={{0,16},{16,0},{1,17},{17,1},{2,18},{18,2},{3,19},{19,3},{4,20},{20... | collective-permute-start | bytes 786440 | tf_op jit(solution)/shard_map/ppermute | solution.py:810
  34.1 0.0 copy-done.7
  34.1 2.1 %shard_map.213 = (f32[64,2048]{1,0:T(8,128)S(1)}, bf16[64,2048]{1,0:T(8,128)(2,1)S(1)}) custom-call(s32[16,128]{1,0:T(8,128)S(1)} %bitcast.18, s32[16,128]{1,0:T(8,128)S(1)} %get-tuple-element.56.rank_ref, s32[16,128]{1,0:T(8,128)S(1)} %get-tuple-element.57.zr_ref, f32[256,128]{1,0:T(8,128)S(1)} %get-tuple-element.58.home_ref, ...), custom_call_target="tpu_custom_call" | custom-call | flops 67108864 | bytes 1212672 | tf_op jit(solution)/shard_map/pallas_call | solution.py:695
  36.2 5.0 %collective-permute-done.other_ref = bf16[16,64,128]{2,1,0:T(8,128)(2,1)S(1)} collective-permute-done((bf16[16,64,128]{2,1,0:T(8,128)(2,1)S(1)}, bf16[16,64,128]{2,1,0:T(8,128)(2,1)S(1)}, u32[]{:S(2)}, u32[]{:S(2)}) %collective-permute-start) | collective-permute-done | bytes 262176 | tf_op jit(solution)/shard_map/ppermute | solution.py:810
  41.2 0.1 shard_map.212.weight_ref
  41.3 5.6 %all-to-all-done.1.rx_ref = bf16[16,128,128]{2,1,0:T(8,128)(2,1)S(1)} async-done(((bf16[16,128,128]{2,1,0:T(8,128)(2,1)}), bf16[16,128,128]{2,1,0:T(8,128)(2,1)S(1)}, u32[]{:S(2)}, u32[]{:S(2)}) %all-to-all-start.1) | async-done | bytes 524320 | tf_op jit(solution)/shard_map/all_to_all | solution.py:757
  46.9 0.0 copy-done.2
  46.9 0.9 shard_map.214
  47.8 18.4 %all_to_all.35.rx_ref = bf16[16,128,128]{2,1,0:T(8,128)(2,1)S(1)} all-to-all(bf16[16,128,128]{2,1,0:T(8,128)(2,1)S(1)} %get-tuple-element.63), channel_id=1, replica_groups=mesh['groups'=2,'gx'=16] {'gx'}, dimensions={0} | all-to-all | bytes 1048576 | tf_op jit(solution)/shard_map/all_to_all | solution.py:757
  66.2 0.0 copy-start.10
  66.2 0.0 copy-start.11
  66.3 0.0 copy-start.12
  66.3 1.4 %shard_map.215 = (bf16[16,80,128]{2,1,0:T(8,128)(2,1)S(1)}, f32[64,2048]{1,0:T(8,128)S(1)}) custom-call(bf16[16,128,128]{2,1,0:T(8,128)(2,1)S(1)} %all_to_all.35.rx_ref, bf16[256,2048]{1,0:T(8,128)(2,1)S(1)} %get-tuple-element.59.lp_ref, f32[64,2048]{1,0:T(8,128)S(1)} %get-tuple-element.68.term_ref, s32[16,128]{1,0:T(8,128)S(1)} %bitcast.19, ...), custom_call_target="tpu_custom_call" | custom-call | flops 1073741824 | bytes 3088384 | tf_op jit(solution)/shard_map/pallas_call | solution.py:695
  67.7 0.0 copy-start.13
  67.7 15.0 %all_to_all.36.rx_ref = bf16[16,80,128]{2,1,0:T(8,128)(2,1)S(1)} all-to-all(bf16[16,80,128]{2,1,0:T(8,128)(2,1)S(1)} %get-tuple-element.71), channel_id=1, replica_groups=mesh['groups'=2,'gx'=16] {'gx'}, dimensions={0} | all-to-all | bytes 655360 | tf_op jit(solution)/shard_map/all_to_all | solution.py:757
  82.7 1.9 %shard_map.216 = (f32[1,512]{1,0:T(1,128)}, bf16[16,80,128]{2,1,0:T(8,128)(2,1)S(1)}, bf16[16,16,128]{2,1,0:T(8,128)(2,1)S(1)}) custom-call(bf16[16,80,128]{2,1,0:T(8,128)(2,1)S(1)} %all_to_all.36.rx_ref, s32[16,128]{1,0:T(8,128)S(1)} %bitcast.15, f32[16,128]{1,0:T(8,128)S(1)} %copy-done.9, bf16[64,64]{1,0:T(8,128)(2,1)S(1)} %copy-done.8, ...), custom_call_target="tpu_custom_call" | custom-call | flops 402653184 | bytes 885248 | tf_op jit(solution)/shard_map/pallas_call | solution.py:695
  84.6 14.1 %all_to_all.37.rx_ref = bf16[16,80,128]{2,1,0:T(8,128)(2,1)S(1)} all-to-all(bf16[16,80,128]{2,1,0:T(8,128)(2,1)S(1)} %get-tuple-element.78), channel_id=1, replica_groups=mesh['groups'=2,'gx'=16] {'gx'}, dimensions={0} | all-to-all | bytes 655360 | tf_op jit(solution)/shard_map/all_to_all | solution.py:757
  98.8 1.7 %shard_map.217 = (bf16[8,272,128]{2,1,0:T(8,128)(2,1)S(1)}, f32[1,2]{1,0:T(1,128)}, f32[1,64]{1,0:T(1,128)}, f32[16,8,128]{2,1,0:T(8,128)S(1)}) custom-call(bf16[16,80,128]{2,1,0:T(8,128)(2,1)S(1)} %all_to_all.37.rx_ref, f32[1,2]{1,0:T(1,128)S(1)} %bitcast.26, s32[16,128]{1,0:T(8,128)S(1)} %bitcast.20, bf16[256,2048]{1,0:T(8,128)(2,1)S(1)} %get-tuple-element.59.lp_ref, ...), custom_call_target="tpu_custom_call" | custom-call | flops 1073741824 | bytes 2793744 | tf_op jit(solution)/shard_map/pallas_call | solution.py:695
  100.5 12.5 %all_to_all.38.rx_ref = bf16[8,272,128]{2,1,0:T(8,128)(2,1)S(1)} all-to-all(bf16[8,272,128]{2,1,0:T(8,128)(2,1)S(1)} %get-tuple-element.89), channel_id=1, replica_groups={{0,1,2,3,4,5,6,7},{8,9,10,11,12,13,14,15},{16,17,18,19,20,21,22,23},{24..., dimensions={0} | all-to-all | bytes 1114112 | tf_op jit(solution)/shard_map/all_to_all | solution.py:892
  113.0 0.3 shard_map.218
  113.3 13.8 %all_to_all.39.rx_ref = bf16[16,80,128]{2,1,0:T(8,128)(2,1)S(1)} all-to-all(bf16[16,80,128]{2,1,0:T(8,128)(2,1)S(1)} %shard_map.218), channel_id=1, replica_groups=mesh['groups'=2,'gx'=16] {'gx'}, dimensions={0} | all-to-all | bytes 655360 | tf_op jit(solution)/shard_map/all_to_all | solution.py:757
  127.1 2.0 %shard_map.219 = (f32[64,64,64]{2,1,0:T(8,128)}, f32[64,64]{1,0:T(8,128)}) custom-call(bf16[16,80,128]{2,1,0:T(8,128)(2,1)S(1)} %all_to_all.39.rx_ref, bf16[16,16,128]{2,1,0:T(8,128)(2,1)S(1)} %get-tuple-element.100.own_ref, f32[16,8,128]{2,1,0:T(8,128)S(1)} %get-tuple-element.101.next_ref), custom_call_target="tpu_custom_call" | custom-call | flops 8388608 | bytes 1523712 | tf_op jit(solution)/shard_map/pallas_call | solution.py:695
  (21 shorter events, 0.1 us)
Async XLA Ops:
  0.6 9.8 %copy-start.14 = (bf16[256,128]{1,0:T(8,128)(2,1)S(1)}, bf16[256,128]{1,0:T(8,128)(2,1)}, u32[]{:S(2)}) copy-start(bf16[256,128]{1,0:T(8,128)(2,1)} %constant.19.clone.by_ref) | copy-start | bytes 196612
  0.6 9.8 %copy-start.5 = (s32[16,1,128]{2,1,0:T(1,128)S(1)}, s32[16,1,128]{2,1,0:T(1,128)}, u32[]{:S(2)}) copy-start(s32[16,1,128]{2,1,0:T(1,128)} %param.20) | copy-start | bytes 24580
  3.1 21.9 %all-to-all-start = ((bf16[16,128,128]{2,1,0:T(8,128)(2,1)}), bf16[16,128,128]{2,1,0:T(8,128)(2,1)S(1)}, u32[]{:S(2)}, u32[]{:S(2)}) async-start(bf16[16,128,128]{2,1,0:T(8,128)(2,1)} %get-tuple-element.55), calls=%async_computation | async-start | bytes 1048576 | tf_op jit(solution)/shard_map/all_to_all | solution.py:757
  24.9 9.1 %copy-start.3 = (bf16[64,64]{1,0:T(8,128)(2,1)S(1)}, bf16[64,64]{1,0:T(8,128)(2,1)}, u32[]{:S(2)}) copy-start(bf16[64,64]{1,0:T(8,128)(2,1)} %skip_ref.1) | copy-start | bytes 24580
  24.9 9.1 %copy-start.7 = (f32[64]{0:T(128)S(1)}, f32[64]{0:T(128)}, u32[]{:S(2)}) copy-start(f32[64]{0:T(128)} %param.28) | copy-start | bytes 772
  28.2 18.7 %copy-start.1 = (bf16[256,64]{1,0:T(8,128)(2,1)S(1)}, bf16[256,64]{1,0:T(8,128)(2,1)}, u32[]{:S(2)}) copy-start(bf16[256,64]{1,0:T(8,128)(2,1)} %constant.20.clone.back_ref) | copy-start | bytes 98308
  28.2 18.7 %copy-start.2 = (bf16[64,256]{1,0:T(8,128)(2,1)S(1)}, bf16[64,256]{1,0:T(8,128)(2,1)}, u32[]{:S(2)}) copy-start(bf16[64,256]{1,0:T(8,128)(2,1)} %constant.21.clone.table_ref) | copy-start | bytes 98308
  28.2 18.7 %all-to-all-start.1 = ((bf16[16,128,128]{2,1,0:T(8,128)(2,1)}), bf16[16,128,128]{2,1,0:T(8,128)(2,1)S(1)}, u32[]{:S(2)}, u32[]{:S(2)}) async-start(bf16[16,128,128]{2,1,0:T(8,128)(2,1)} %get-tuple-element.60), calls=%async_computation.1 | async-start | bytes 1048576 | tf_op jit(solution)/shard_map/all_to_all | solution.py:757
  32.5 8.7 %collective-permute-start = (bf16[16,64,128]{2,1,0:T(8,128)(2,1)S(1)}, bf16[16,64,128]{2,1,0:T(8,128)(2,1)S(1)}, u32[]{:S(2)}, u32[]{:S(2)}) collective-permute-start(bf16[16,64,128]{2,1,0:T(8,128)(2,1)S(1)} %slice.4.own_ref), channel_id=1, source_target_pairs={{0,16},{16,0},{1,17},{17,1},{2,18},{18,2},{3,19},{19,3},{4,20},{20... | collective-permute-start | bytes 786440 | tf_op jit(solution)/shard_map/ppermute | solution.py:810
  66.2 16.5 %copy-start.4 = (s32[1,16,128]{2,1,0:T(8,128)S(1)}, s32[1,16,128]{2,1,0:T(8,128)}, u32[]{:S(2)}) copy-start(s32[1,16,128]{2,1,0:T(8,128)} %param.19) | copy-start | bytes 24580
  66.2 16.5 %copy-start.6 = (f32[512]{0:T(512)S(1)}, f32[512]{0:T(512)}, u32[]{:S(2)}) copy-start(f32[512]{0:T(512)} %param.23) | copy-start | bytes 6148
  66.2 16.5 %copy-start.8 = (bf16[64,64]{1,0:T(8,128)(2,1)S(1)}, bf16[64,64]{1,0:T(8,128)(2,1)}, u32[]{:S(2)}) copy-start(bf16[64,64]{1,0:T(8,128)(2,1)} %head_ref.1) | copy-start | bytes 24580
  66.2 16.5 %copy-start.9 = (f32[16,128]{1,0:T(8,128)S(1)}, f32[16,128]{1,0:T(8,128)}, u32[]{:S(2)}) copy-start(f32[16,128]{1,0:T(8,128)} %get-tuple-element.76.pw_ref) | copy-start | bytes 24580
  66.2 16.5 %copy-start.10 = (f32[2,512]{1,0:T(2,128)S(1)}, f32[2,512]{1,0:T(2,128)}, u32[]{:S(2)}) copy-start(f32[2,512]{1,0:T(2,128)} %normal_ref.1) | copy-start | bytes 12292
  66.2 16.5 %copy-start.11 = (f32[64]{0:T(128)S(1)}, f32[64]{0:T(128)}, u32[]{:S(2)}) copy-start(f32[64]{0:T(128)} %param.30) | copy-start | bytes 772
  66.3 16.5 %copy-start.12 = (f32[64]{0:T(128)S(1)}, f32[64]{0:T(128)}, u32[]{:S(2)}) copy-start(f32[64]{0:T(128)} %param.31) | copy-start | bytes 772
  67.7 31.1 %copy-start.13 = (f32[2]{0:T(128)S(1)}, f32[2]{0:T(128)}, u32[]{:S(2)}) copy-start(f32[2]{0:T(128)} %param.25) | copy-start | bytes 28
  98.8 14.2 %copy-start = (bf16[2,128,256]{2,1,0:T(8,128)(2,1)S(1)}, bf16[2,128,256]{2,1,0:T(8,128)(2,1)}, u32[]{:S(2)}) copy-start(bf16[2,128,256]{2,1,0:T(8,128)(2,1)} %constant.22.clone.table_ref) | copy-start | bytes 393220

commit v13 on v12

--- a/solution.py
+++ b/solution.py
@@ -338,9 +338,11 @@
     pick_rows(rank_ref, pick_ref)
     found = mm_nt(part_ref[...], pick_ref[...])
     found = found[0:1] * 128.0 + found[1:2]
-    for block in range(home_ref.shape[0] // LANES):
-        cut = slice(block * LANES, (block + 1) * LANES)
-        home_ref[cut, :] = columns_of(found[:, cut])
+    shared = home_ref.shape[0]
+    found = jnp.concatenate([found, jnp.zeros((1, -shared % LANES), F32)], axis=1)
+    for at in range(0, shared, LANES):
+        rows = min(LANES, shared - at)
+        home_ref[at : at + rows, :] = columns_of(found[:, at : at + LANES])[0:rows]
 
 
 def first_rows(cell_ref, zr_ref, home_ref, first_ref):
@@ -782,7 +784,7 @@
         grant=60,
     )
     rx = exchange(msg)
-    shared = 256
+    shared = 192
     zr, rank, home, lp = run(
         functools.partial(place_kernel, depth),
         [

time: 130 us -> 129 us (level)
  no operation moved by 1% of the time
where the time goes in v13:
time: 129 us
  blocking collectives  73.8 us (57%)
  waiting for transfers between devices  23.4 us (18%)
  Pallas kernels  17.6 us (14%)
  starting transfers between devices  13.2 us (10%)
    all_to_all x4, blocking collectives, exchange(): lax.all_to_all(message, 'gx', split_axis=0, concat_axis=0, tiled=True)  61.3 us
    all_to_all x2, waiting for transfers between devices, exchange(): lax.all_to_all(message, 'gx', split_axis=0, concat_axis=0, tiled=True)  18.1 us
    pallas_call x11, Pallas kernels, run(): pl.pallas_call(kernel, out_shape=tuple(outs), in_specs=[scalar] * smem +...  17.6 us
    all_to_all x1, blocking collectives, slab_step(): lax.all_to_all(msg, 'gx', split_axis=0, concat_axis=0, tiled=True, axis_i...  12.5 us
    all_to_all x2, starting transfers between devices, exchange(): lax.all_to_all(message, 'gx', split_axis=0, concat_axis=0, tiled=True)  11.6 us
    ppermute x1, waiting for transfers between devices, slab_step(): other = lax.ppermute(own, 'groups', [(0, 1), (1, 0)])  5.33 us
  transfers between devices with their start and end apart: 3, of which 3 were waited for; matrix products, arithmetic and copies ran while one was open for 0% of the time, Pallas kernels for 3%

profile of v13, /device:TPU:0, one launch (start us, length us, event | category | flops | bytes accessed | tf_op | source)
XLA Modules:
  0.0 128.8 jit_solution(8168111694912016603)
XLA Ops:
  0.6 0.0 copy-start.14
  0.6 0.0 copy-start.5
  0.7 2.4 %shard_map.209 = (bf16[16,128,128]{2,1,0:T(8,128)(2,1)}, f32[16,128]{1,0:T(8,128)}) custom-call(s32[1]{0:T(128)} %bitcast.group_ref, s32[1]{0:T(128)} %bitcast.1.half_ref, s32[1,16]{1,0:T(1,128)} %count_hbm.1, s32[16,128]{1,0:T(8,128)} %bitcast.14, f32[16,128]{1,0:T(8,128)} %bitcast.28, f32[1,512]{1,0:T(1,128)} %bitcast.21, bf16[64,512]{1,0:T(8,128)(2,1)} %bitcast.27, ...), custom_call_target="tpu_custom_call" | custom-call | flops 167772160 | bytes 1140808 | tf_op jit(solution)/shard_map/pallas_call | solution.py:697
  3.1 7.4 %all-to-all-start = ((bf16[16,128,128]{2,1,0:T(8,128)(2,1)}), bf16[16,128,128]{2,1,0:T(8,128)(2,1)S(1)}, u32[]{:S(2)}, u32[]{:S(2)}) async-start(bf16[16,128,128]{2,1,0:T(8,128)(2,1)} %get-tuple-element.55), calls=%async_computation | async-start | bytes 1048576 | tf_op jit(solution)/shard_map/all_to_all | solution.py:759
  10.5 0.0 copy-done.14
  10.5 0.0 copy-done.5
  10.5 2.0 %shard_map.210 = (s32[16,128]{1,0:T(8,128)S(1)}, s32[16,128]{1,0:T(8,128)S(1)}, f32[192,128]{1,0:T(8,128)S(1)}, bf16[256,2048]{1,0:T(8,128)(2,1)S(1)}) custom-call(s32[16,128]{1,0:T(8,128)S(1)} %bitcast.16, bf16[256,128]{1,0:T(8,128)(2,1)S(1)} %copy-done.14), custom_call_target="tpu_custom_call" | custom-call | flops 134217728 | bytes 1236992 | tf_op jit(solution)/shard_map/pallas_call | solution.py:697
  12.5 12.4 %all-to-all-done.rx_ref = bf16[16,128,128]{2,1,0:T(8,128)(2,1)S(1)} async-done(((bf16[16,128,128]{2,1,0:T(8,128)(2,1)}), bf16[16,128,128]{2,1,0:T(8,128)(2,1)S(1)}, u32[]{:S(2)}, u32[]{:S(2)}) %all-to-all-start) | async-done | bytes 524320 | tf_op jit(solution)/shard_map/all_to_all | solution.py:759
  24.9 3.1 %shard_map.211 = (bf16[16,128,128]{2,1,0:T(8,128)(2,1)}, bf16[64,2048]{1,0:T(8,128)(2,1)S(1)}) custom-call(bf16[16,128,128]{2,1,0:T(8,128)(2,1)S(1)} %all-to-all-done.rx_ref, s32[16,128]{1,0:T(8,128)S(1)} %bitcast.17, s32[16,128]{1,0:T(8,128)S(1)} %get-tuple-element.56.rank_ref, s32[16,128]{1,0:T(8,128)S(1)} %get-tuple-element.57.zr_ref, ...), custom_call_target="tpu_custom_call" | custom-call | flops 1610612736 | bytes 2482176 | tf_op jit(solution)/shard_map/pallas_call | solution.py:697
  28.0 4.2 %all-to-all-start.1 = ((bf16[16,128,128]{2,1,0:T(8,128)(2,1)}), bf16[16,128,128]{2,1,0:T(8,128)(2,1)S(1)}, u32[]{:S(2)}, u32[]{:S(2)}) async-start(bf16[16,128,128]{2,1,0:T(8,128)(2,1)} %get-tuple-element.60), calls=%async_computation.1 | async-start | bytes 1048576 | tf_op jit(solution)/shard_map/all_to_all | solution.py:759
  32.3 1.6 %collective-permute-start = (bf16[16,64,128]{2,1,0:T(8,128)(2,1)S(1)}, bf16[16,64,128]{2,1,0:T(8,128)(2,1)S(1)}, u32[]{:S(2)}, u32[]{:S(2)}) collective-permute-start(bf16[16,64,128]{2,1,0:T(8,128)(2,1)S(1)} %slice.4.own_ref), channel_id=1, source_target_pairs={{0,16},{16,0},{1,17},{17,1},{2,18},{18,2},{3,19},{19,3},{4,20},{20... | collective-permute-start | bytes 786440 | tf_op jit(solution)/shard_map/ppermute | solution.py:812
  33.9 0.0 copy-done.7
  33.9 1.8 %shard_map.213 = (f32[64,2048]{1,0:T(8,128)S(1)}, bf16[64,2048]{1,0:T(8,128)(2,1)S(1)}) custom-call(s32[16,128]{1,0:T(8,128)S(1)} %bitcast.18, s32[16,128]{1,0:T(8,128)S(1)} %get-tuple-element.56.rank_ref, s32[16,128]{1,0:T(8,128)S(1)} %get-tuple-element.57.zr_ref, f32[192,128]{1,0:T(8,128)S(1)} %get-tuple-element.58.home_ref, ...), custom_call_target="tpu_custom_call" | custom-call | flops 50331648 | bytes 1179904 | tf_op jit(solution)/shard_map/pallas_call | solution.py:697
  35.7 5.3 %collective-permute-done.other_ref = bf16[16,64,128]{2,1,0:T(8,128)(2,1)S(1)} collective-permute-done((bf16[16,64,128]{2,1,0:T(8,128)(2,1)S(1)}, bf16[16,64,128]{2,1,0:T(8,128)(2,1)S(1)}, u32[]{:S(2)}, u32[]{:S(2)}) %collective-permute-start) | collective-permute-done | bytes 262176 | tf_op jit(solution)/shard_map/ppermute | solution.py:812
  41.0 0.1 shard_map.212.weight_ref
  41.1 5.6 %all-to-all-done.1.rx_ref = bf16[16,128,128]{2,1,0:T(8,128)(2,1)S(1)} async-done(((bf16[16,128,128]{2,1,0:T(8,128)(2,1)}), bf16[16,128,128]{2,1,0:T(8,128)(2,1)S(1)}, u32[]{:S(2)}, u32[]{:S(2)}) %all-to-all-start.1) | async-done | bytes 524320 | tf_op jit(solution)/shard_map/all_to_all | solution.py:759
  46.7 0.0 copy-done.2
  46.7 0.9 shard_map.214
  47.6 18.4 %all_to_all.35.rx_ref = bf16[16,128,128]{2,1,0:T(8,128)(2,1)S(1)} all-to-all(bf16[16,128,128]{2,1,0:T(8,128)(2,1)S(1)} %get-tuple-element.63), channel_id=1, replica_groups=mesh['groups'=2,'gx'=16] {'gx'}, dimensions={0} | all-to-all | bytes 1048576 | tf_op jit(solution)/shard_map/all_to_all | solution.py:759
  66.0 0.0 copy-start.10
  66.0 0.0 copy-start.11
  66.1 0.0 copy-start.12
  66.1 1.4 %shard_map.215 = (bf16[16,80,128]{2,1,0:T(8,128)(2,1)S(1)}, f32[64,2048]{1,0:T(8,128)S(1)}) custom-call(bf16[16,128,128]{2,1,0:T(8,128)(2,1)S(1)} %all_to_all.35.rx_ref, bf16[256,2048]{1,0:T(8,128)(2,1)S(1)} %get-tuple-element.59.lp_ref, f32[64,2048]{1,0:T(8,128)S(1)} %get-tuple-element.68.term_ref, s32[16,128]{1,0:T(8,128)S(1)} %bitcast.19, ...), custom_call_target="tpu_custom_call" | custom-call | flops 1073741824 | bytes 3088384 | tf_op jit(solution)/shard_map/pallas_call | solution.py:697
  67.5 0.0 copy-start.13
  67.5 15.0 %all_to_all.36.rx_ref = bf16[16,80,128]{2,1,0:T(8,128)(2,1)S(1)} all-to-all(bf16[16,80,128]{2,1,0:T(8,128)(2,1)S(1)} %get-tuple-element.71), channel_id=1, replica_groups=mesh['groups'=2,'gx'=16] {'gx'}, dimensions={0} | all-to-all | bytes 655360 | tf_op jit(solution)/shard_map/all_to_all | solution.py:759
  82.5 1.9 %shard_map.216 = (f32[1,512]{1,0:T(1,128)}, bf16[16,80,128]{2,1,0:T(8,128)(2,1)S(1)}, bf16[16,16,128]{2,1,0:T(8,128)(2,1)S(1)}) custom-call(bf16[16,80,128]{2,1,0:T(8,128)(2,1)S(1)} %all_to_all.36.rx_ref, s32[16,128]{1,0:T(8,128)S(1)} %bitcast.15, f32[16,128]{1,0:T(8,128)S(1)} %copy-done.9, bf16[64,64]{1,0:T(8,128)(2,1)S(1)} %copy-done.8, ...), custom_call_target="tpu_custom_call" | custom-call | flops 402653184 | bytes 885248 | tf_op jit(solution)/shard_map/pallas_call | solution.py:697
  84.4 14.1 %all_to_all.37.rx_ref = bf16[16,80,128]{2,1,0:T(8,128)(2,1)S(1)} all-to-all(bf16[16,80,128]{2,1,0:T(8,128)(2,1)S(1)} %get-tuple-element.78), channel_id=1, replica_groups=mesh['groups'=2,'gx'=16] {'gx'}, dimensions={0} | all-to-all | bytes 655360 | tf_op jit(solution)/shard_map/all_to_all | solution.py:759
  98.6 1.7 %shard_map.217 = (bf16[8,272,128]{2,1,0:T(8,128)(2,1)S(1)}, f32[1,2]{1,0:T(1,128)}, f32[1,64]{1,0:T(1,128)}, f32[16,8,128]{2,1,0:T(8,128)S(1)}) custom-call(bf16[16,80,128]{2,1,0:T(8,128)(2,1)S(1)} %all_to_all.37.rx_ref, f32[1,2]{1,0:T(1,128)S(1)} %bitcast.26, s32[16,128]{1,0:T(8,128)S(1)} %bitcast.20, bf16[256,2048]{1,0:T(8,128)(2,1)S(1)} %get-tuple-element.59.lp_ref, ...), custom_call_target="tpu_custom_call" | custom-call | flops 1073741824 | bytes 2793744 | tf_op jit(solution)/shard_map/pallas_call | solution.py:697
  100.3 12.5 %all_to_all.38.rx_ref = bf16[8,272,128]{2,1,0:T(8,128)(2,1)S(1)} all-to-all(bf16[8,272,128]{2,1,0:T(8,128)(2,1)S(1)} %get-tuple-element.89), channel_id=1, replica_groups={{0,1,2,3,4,5,6,7},{8,9,10,11,12,13,14,15},{16,17,18,19,20,21,22,23},{24..., dimensions={0} | all-to-all | bytes 1114112 | tf_op jit(solution)/shard_map/all_to_all | solution.py:894
  112.8 0.3 shard_map.218
  113.1 13.8 %all_to_all.39.rx_ref = bf16[16,80,128]{2,1,0:T(8,128)(2,1)S(1)} all-to-all(bf16[16,80,128]{2,1,0:T(8,128)(2,1)S(1)} %shard_map.218), channel_id=1, replica_groups=mesh['groups'=2,'gx'=16] {'gx'}, dimensions={0} | all-to-all | bytes 655360 | tf_op jit(solution)/shard_map/all_to_all | solution.py:759
  126.9 2.0 %shard_map.219 = (f32[64,64,64]{2,1,0:T(8,128)}, f32[64,64]{1,0:T(8,128)}) custom-call(bf16[16,80,128]{2,1,0:T(8,128)(2,1)S(1)} %all_to_all.39.rx_ref, bf16[16,16,128]{2,1,0:T(8,128)(2,1)S(1)} %get-tuple-element.100.own_ref, f32[16,8,128]{2,1,0:T(8,128)S(1)} %get-tuple-element.101.next_ref), custom_call_target="tpu_custom_call" | custom-call | flops 8388608 | bytes 1523712 | tf_op jit(solution)/shard_map/pallas_call | solution.py:697
  (21 shorter events, 0.1 us)
Async XLA Ops:
  0.6 9.8 %copy-start.14 = (bf16[256,128]{1,0:T(8,128)(2,1)S(1)}, bf16[256,128]{1,0:T(8,128)(2,1)}, u32[]{:S(2)}) copy-start(bf16[256,128]{1,0:T(8,128)(2,1)} %constant.19.clone.by_ref) | copy-start | bytes 196612
  0.6 9.8 %copy-start.5 = (s32[16,1,128]{2,1,0:T(1,128)S(1)}, s32[16,1,128]{2,1,0:T(1,128)}, u32[]{:S(2)}) copy-start(s32[16,1,128]{2,1,0:T(1,128)} %param.20) | copy-start | bytes 24580
  3.1 21.9 %all-to-all-start = ((bf16[16,128,128]{2,1,0:T(8,128)(2,1)}), bf16[16,128,128]{2,1,0:T(8,128)(2,1)S(1)}, u32[]{:S(2)}, u32[]{:S(2)}) async-start(bf16[16,128,128]{2,1,0:T(8,128)(2,1)} %get-tuple-element.55), calls=%async_computation | async-start | bytes 1048576 | tf_op jit(solution)/shard_map/all_to_all | solution.py:759
  24.9 8.9 %copy-start.3 = (bf16[64,64]{1,0:T(8,128)(2,1)S(1)}, bf16[64,64]{1,0:T(8,128)(2,1)}, u32[]{:S(2)}) copy-start(bf16[64,64]{1,0:T(8,128)(2,1)} %skip_ref.1) | copy-start | bytes 24580
  24.9 8.9 %copy-start.7 = (f32[64]{0:T(128)S(1)}, f32[64]{0:T(128)}, u32[]{:S(2)}) copy-start(f32[64]{0:T(128)} %param.28) | copy-start | bytes 772
  28.0 18.7 %copy-start.1 = (bf16[256,64]{1,0:T(8,128)(2,1)S(1)}, bf16[256,64]{1,0:T(8,128)(2,1)}, u32[]{:S(2)}) copy-start(bf16[256,64]{1,0:T(8,128)(2,1)} %constant.20.clone.back_ref) | copy-start | bytes 98308
  28.0 18.7 %copy-start.2 = (bf16[64,256]{1,0:T(8,128)(2,1)S(1)}, bf16[64,256]{1,0:T(8,128)(2,1)}, u32[]{:S(2)}) copy-start(bf16[64,256]{1,0:T(8,128)(2,1)} %constant.21.clone.table_ref) | copy-start | bytes 98308
  28.0 18.7 %all-to-all-start.1 = ((bf16[16,128,128]{2,1,0:T(8,128)(2,1)}), bf16[16,128,128]{2,1,0:T(8,128)(2,1)S(1)}, u32[]{:S(2)}, u32[]{:S(2)}) async-start(bf16[16,128,128]{2,1,0:T(8,128)(2,1)} %get-tuple-element.60), calls=%async_computation.1 | async-start | bytes 1048576 | tf_op jit(solution)/shard_map/all_to_all | solution.py:759
  32.3 8.7 %collective-permute-start = (bf16[16,64,128]{2,1,0:T(8,128)(2,1)S(1)}, bf16[16,64,128]{2,1,0:T(8,128)(2,1)S(1)}, u32[]{:S(2)}, u32[]{:S(2)}) collective-permute-start(bf16[16,64,128]{2,1,0:T(8,128)(2,1)S(1)} %slice.4.own_ref), channel_id=1, source_target_pairs={{0,16},{16,0},{1,17},{17,1},{2,18},{18,2},{3,19},{19,3},{4,20},{20... | collective-permute-start | bytes 786440 | tf_op jit(solution)/shard_map/ppermute | solution.py:812
  66.0 16.5 %copy-start.4 = (s32[1,16,128]{2,1,0:T(8,128)S(1)}, s32[1,16,128]{2,1,0:T(8,128)}, u32[]{:S(2)}) copy-start(s32[1,16,128]{2,1,0:T(8,128)} %param.19) | copy-start | bytes 24580
  66.0 16.5 %copy-start.6 = (f32[512]{0:T(512)S(1)}, f32[512]{0:T(512)}, u32[]{:S(2)}) copy-start(f32[512]{0:T(512)} %param.23) | copy-start | bytes 6148
  66.0 16.5 %copy-start.8 = (bf16[64,64]{1,0:T(8,128)(2,1)S(1)}, bf16[64,64]{1,0:T(8,128)(2,1)}, u32[]{:S(2)}) copy-start(bf16[64,64]{1,0:T(8,128)(2,1)} %head_ref.1) | copy-start | bytes 24580
  66.0 16.5 %copy-start.9 = (f32[16,128]{1,0:T(8,128)S(1)}, f32[16,128]{1,0:T(8,128)}, u32[]{:S(2)}) copy-start(f32[16,128]{1,0:T(8,128)} %get-tuple-element.76.pw_ref) | copy-start | bytes 24580
  66.0 16.5 %copy-start.10 = (f32[2,512]{1,0:T(2,128)S(1)}, f32[2,512]{1,0:T(2,128)}, u32[]{:S(2)}) copy-start(f32[2,512]{1,0:T(2,128)} %normal_ref.1) | copy-start | bytes 12292
  66.0 16.5 %copy-start.11 = (f32[64]{0:T(128)S(1)}, f32[64]{0:T(128)}, u32[]{:S(2)}) copy-start(f32[64]{0:T(128)} %param.30) | copy-start | bytes 772
  66.1 16.5 %copy-start.12 = (f32[64]{0:T(128)S(1)}, f32[64]{0:T(128)}, u32[]{:S(2)}) copy-start(f32[64]{0:T(128)} %param.31) | copy-start | bytes 772
  67.5 31.1 %copy-start.13 = (f32[2]{0:T(128)S(1)}, f32[2]{0:T(128)}, u32[]{:S(2)}) copy-start(f32[2]{0:T(128)} %param.25) | copy-start | bytes 28
  98.6 14.2 %copy-start = (bf16[2,128,256]{2,1,0:T(8,128)(2,1)S(1)}, bf16[2,128,256]{2,1,0:T(8,128)(2,1)}, u32[]{:S(2)}) copy-start(bf16[2,128,256]{2,1,0:T(8,128)(2,1)} %constant.22.clone.table_ref) | copy-start | bytes 393220
